TPU v7x, 32 devices: a whole 2x2x4 slice. The times are simulated.
32 devices in a mesh: wide: 16 (over z, y, x), narrow: 2 (over core).
Axes of the slice: x: 2, y: 2, z: 4, core: 2. Of those that a mesh axis runs over, the one named last changes fastest.
Arguments:
- inverse: bfloat16 [4096, 4096], P('wide', 'narrow')
- panel: bfloat16 [2, 4096, 4096], P(None, 'narrow', 'wide'), may hold values from -0.109375 to 0.109375
- factor_inv: bfloat16 [2, 4096, 4096], P(None, 'wide', 'narrow')
- structure: int32 [2, 12], replicated, may hold values from 0 to 15, as said below
Outputs:
- cross: bfloat16 [4096, 2, 4096], P('narrow', None, 'wide')
- variance: float32 [2, 4096], P(None, 'narrow')
Inputs may be any that keep to these rules, and one draw needn't show every extreme that they name: `structure`: row k lists 12 distinct block indices in increasing order; the last, 15, is always listed.
All inputs are finite; a program needn't handle non-finite values.
Results may differ from a plain program's by a relative error of at most 0.0013.
Values may be sent and summed in bfloat16 or wider, within the bound.
No kernel may reach another device: no remote copies, remote signals or barrier semaphores. Data moves between devices by JAX's collectives and lax.ppermute only.
A program may use at most 192 MiB of HBM per device.

v0:
```python
import jax
import jax.numpy as jnp
from jax import lax
from jax.sharding import PartitionSpec as P

BLK = 256


def spread(value, axis, source):
    kept = jnp.where(lax.axis_index(axis) == source, value, 0).astype(value.dtype)
    return lax.psum(kept, axis)


def block_partial(gathered, inverse, row_inside, col_inside, first_row, row_count):
    local_blocks = inverse.shape[1] // BLK
    running = jnp.zeros((row_count, BLK), jnp.float32)
    for blk_index in range(local_blocks):

        def product(blk_index=blk_index):
            panel_piece = lax.dynamic_slice(
                gathered, (blk_index * BLK, first_row), (BLK, row_count)
            )
            block_z = inverse[:, blk_index * BLK : (blk_index + 1) * BLK]
            return lax.dot_general(
                panel_piece, block_z, (((0,), (1,)), ((), ())), preferred_element_type=jnp.float32
            )

        def skipped():
            return jnp.zeros((row_count, BLK), jnp.float32)

        running = running + lax.cond(row_inside & col_inside[blk_index], product, skipped)
    return -running


def per_device(inverse, panel, factor_inv, structure):
    wide_count = lax.axis_size("wide")
    narrow_count = lax.axis_size("narrow")
    nsup_count = panel.shape[0]
    kw_total = panel.shape[2] * wide_count
    kw_local = kw_total // narrow_count
    local_blocks = inverse.shape[1] // BLK
    row_index = lax.axis_index("wide")
    col_first = lax.axis_index("narrow") * local_blocks
    col_ids = col_first + jnp.arange(local_blocks, dtype=jnp.int32)
    row_inside = jnp.any(structure == row_index, axis=1)
    col_inside = jnp.any(structure[:, :, None] == col_ids[None, None, :], axis=1)
    root_index = row_index // local_blocks
    offset = (row_index - root_index * local_blocks) * BLK
    cross_parts = []
    own_parts = []
    for sup_index in range(nsup_count):
        gathered_one = lax.all_gather(panel[sup_index], "wide", axis=1, tiled=True)

        def one_term(first_row, row_count, gathered_one=gathered_one, sup_index=sup_index):
            return block_partial(
                gathered_one,
                inverse,
                row_inside[sup_index],
                col_inside[sup_index],
                first_row,
                row_count,
            )

        cross_parts.append(
            lax.psum_scatter(
                one_term(jnp.int32(0), kw_local * lax.axis_size("narrow")),
                "narrow",
                scatter_dimension=0,
                tiled=True,
            )
        )
        own_parts.append(lax.dynamic_slice_in_dim(gathered_one, offset, BLK, axis=0))
    cross_f = jnp.stack(cross_parts, axis=1)
    own_rows = jnp.stack(own_parts)
    owner_panel = spread(own_rows, "narrow", root_index)
    owner_slice = lax.dynamic_slice_in_dim(
        owner_panel, lax.axis_index("narrow") * kw_local, kw_local, axis=2
    )
    weighted = jnp.einsum("kia,aki->ka", owner_slice.astype(jnp.float32), cross_f)
    linv_part = jnp.sum(jnp.square(factor_inv.astype(jnp.float32)), axis=1)
    variance = lax.psum(linv_part - weighted, "wide")
    return (cross_f.astype(jnp.bfloat16), variance)


def solution(mesh):
    in_specs = (P("wide", "narrow"), P(None, "narrow", "wide"), P(None, "wide", "narrow"), P())
    out_specs = (P("narrow", None, "wide"), P(None, "narrow"))
    return jax.shard_map(
        per_device, mesh=mesh, in_specs=in_specs, out_specs=out_specs, check_vma=False
    )
```

profile of v0, /device:TPU:0, one launch (start us, length us, event | category | flops | bytes accessed | tf_op | source)
XLA Modules:
  0.0 717.6 jit_solution(15447077035410899923)
XLA Ops:
  7.2 3.0 fusion.49
  11.1 237.6 %all-gather.7.cloned.1.call-done = bf16[1,2048,4096]{2,1,0:T(8,128)(2,1)} async-done(((bf16[1,2048,256]{2,1,0:T(8,128)(2,1)}), bf16[1,2048,4096]{2,1,0:T(8,128)(2,1)}) %all-gather.7.cloned.1.call-update) | async-done | bytes 16777232 | tf_op jit(solution)/shard_map/all_gather | solution.py:52
  250.4 235.0 %all-gather.5.cloned.1.call-done = bf16[1,2048,4096]{2,1,0:T(8,128)(2,1)} async-done(((bf16[1,2048,256]{2,1,0:T(8,128)(2,1)}), bf16[1,2048,4096]{2,1,0:T(8,128)(2,1)}) %all-gather.5.cloned.1.call-update) | async-done | bytes 16777232 | tf_op jit(solution)/shard_map/all_gather | solution.py:52
  502.1 4.3 conditional.16
  502.1 4.3 fusion
  508.6 4.6 conditional.18
  508.6 4.6 fusion.6
  513.3 4.6 conditional.19
  513.3 4.6 fusion.9
  517.8 4.3 conditional.20
  517.8 4.3 fusion.12
  522.1 4.3 conditional.21
  522.1 4.3 fusion.15
  530.9 13.8 %add_negate_fusion.1 = f32[4096,256]{1,0:T(8,128)} fusion(f32[4096,256]{1,0:T(8,128)} %get-tuple-element.177, f32[4096,256]{1,0:T(8,128)} %get-tuple-element.176, f32[4096,256]{1,0:T(8,128)} %get-tuple-element.175, f32[4096,256]{1,0:T(8,128)} %get-tuple-element.174, f32[4096,256]{1,0:T(8,128)} %get-tuple-element.173, f32[4096,256]{1,0:T(8,128)} %get-tuple-element.172, ...), kind=kLoop, calls=%fused_computation.53 | loop fusion | flops 8388608 | bytes 37748736 | tf_op jit(solution)/shard_map/neg | solution.py:32
  554.8 2.5 conditional.24
  554.8 2.5 broadcast.46
  564.0 2.3 conditional.28
  573.1 13.9 %add_negate_fusion = f32[4096,256]{1,0:T(8,128)} fusion(f32[4096,256]{1,0:T(8,128)} %get-tuple-element.185, f32[4096,256]{1,0:T(8,128)} %get-tuple-element.184, f32[4096,256]{1,0:T(8,128)} %get-tuple-element.183, f32[4096,256]{1,0:T(8,128)} %get-tuple-element.182, f32[4096,256]{1,0:T(8,128)} %get-tuple-element.181, f32[4096,256]{1,0:T(8,128)} %get-tuple-element.180, ...), kind=kLoop, calls=%fused_computation.52 | loop fusion | flops 8388608 | bytes 37748736 | tf_op jit(solution)/shard_map/neg | solution.py:32
  589.0 4.1 bitcast_convert_fusion
  593.1 5.3 copy.13
  598.5 15.1 %reduce-scatter.5.cloned.1.call-done = f32[2048,256]{1,0:T(8,128)} async-done(((f32[4096,256]{1,0:T(8,128)}), f32[2048,256]{1,0:T(8,128)}) %reduce-scatter.5.cloned.1.call-update) | async-done | bytes 2097168 | tf_op jit(solution)/shard_map/reduce_scatter | solution.py:65
  613.5 2.7 fusion.48
  620.0 77.1 %psum.15 = f32[2,2048]{1,0:T(2,128)} all-reduce(f32[2,2048]{1,0:T(2,128)S(1)} %sub.12), channel_id=1, replica_groups=mesh['wide'=16,'narrow'=2] {'wide'}, use_global_device_ids=true, to_apply=%region_38.39 | all-reduce | flops 4096 | bytes 32768 | tf_op jit(solution)/shard_map/psum | solution.py:81
  697.1 14.0 %copy.7 = bf16[2048,2,256]{2,1,0:T(2,128)(2,1)} copy(bf16[2048,2,256]{2,0,1:T(8,128)(2,1)S(1)} %fusion.48) | data formatting | bytes 4194304
  (52 shorter events, 57.3 us)
Async XLA Ops:
  7.2 241.5 %all-gather.7.cloned.1.call-start = ((), (), s32[]{:S(2)}) async-start(), calls=%async_computation.6 | async-start | bytes 17825792 | tf_op jit(solution)/shard_map/all_gather | solution.py:52
  10.2 475.2 %all-gather.5.cloned.1.call-start = ((), (), s32[]{:S(2)}) async-start(), calls=%async_computation.5 | async-start | bytes 17825792 | tf_op jit(solution)/shard_map/all_gather | solution.py:52
  11.0 578.0 %all-reduce.2.cloned.1.call-start = ((), (), s32[]{:S(2)}) async-start(), calls=%async_computation.4 | async-start | bytes 8388608 | tf_op jit(solution)/shard_map/psum | solution.py:11
  489.5 0.7 copy-start.4
  489.5 12.6 %copy-start.2 = (bf16[256,2048]{1,0:T(8,128)(2,1)S(1)}, bf16[256,2048]{1,0:T(8,128)(2,1)}, u32[]{:S(2)}) copy-start(bf16[256,2048]{1,0:T(8,128)(2,1)} %param.36) | copy-start | bytes 3145732
  489.5 109.0 %reduce-scatter.3.cloned.1.call-start = ((), (), s32[]{:S(2)}) async-start(), calls=%async_computation.2 | async-start | bytes 6291456 | tf_op jit(solution)/shard_map/reduce_scatter | solution.py:65
  544.8 68.8 %reduce-scatter.5.cloned.1.call-start = ((), (), s32[]{:S(2)}) async-start(), calls=%async_computation.3 | async-start | bytes 6291456 | tf_op jit(solution)/shard_map/reduce_scatter | solution.py:65
  587.0 1.6 copy-start.3
  613.5 3.4 copy-start
  613.5 4.1 copy-start.1
Sparse Core Ops, SparseCore 0:
  10.7 237.9 all-gather.6
  252.0 233.4 all-gather.4
  489.6 26.5 all-reduce.1
  544.9 14.1 reduce-scatter.2
  587.1 26.3 reduce-scatter.4
where the time goes:
time: 720 us; the launch traced here: 718 us
  waiting for transfers between devices  488 us (68%)
  blocking collectives  77.1 us (11%)
  local copies, waits for them, and re-layouts  55.6 us (8%)
  other arithmetic  39.8 us (6%)
  between operations  34.1 us (5%)
  matrix products  22.1 us (3%)
    all_gather x2, waiting for transfers between devices, per_device(): gathered_one = lax.all_gather(panel[sup_index], 'wide', axis=1, tiled=True)  473 us
    psum x1, blocking collectives, per_device(): variance = lax.psum(linv_part - weighted, 'wide')  77.1 us
    neg x2, other arithmetic, block_partial(): return -running  27.6 us
    another operation x11, local copies, waits for them, and re-layouts  25 us
    unnamed x12, local copies, waits for them, and re-layouts  22.8 us
    dot_general x5, matrix products, product(): lax.dot_general(panel_piece, block_z, (((0,), (1,)), ((), ())), preferred...  22.1 us
    reduce_scatter x2, waiting for transfers between devices, per_device(): lax.psum_scatter(one_term(jnp.int32(0), kw_local * lax.axis_size('narrow'...  15.1 us
  transfers between devices with their start and end apart: 5, of which 3 were waited for; matrix products, arithmetic and copies ran while one was open for 12% of the time, Pallas kernels for 0%

commit v1 on v0

--- a/solution.py
+++ b/solution.py
@@ -1,9 +1,13 @@
 import jax
 import jax.numpy as jnp
 from jax import lax
+from jax.experimental import pallas as pl
+from jax.experimental.pallas import tpu as pltpu
 from jax.sharding import PartitionSpec as P
 
 BLK = 256
+LANES = 128
+ANY = pl.BlockSpec(memory_space=pl.ANY)
 
 
 def spread(value, axis, source):
@@ -32,7 +36,7 @@
     return -running
 
 
-def per_device(inverse, panel, factor_inv, structure):
+def per_device_general(inverse, panel, factor_inv, structure):
     wide_count = lax.axis_size("wide")
     narrow_count = lax.axis_size("narrow")
     nsup_count = panel.shape[0]
@@ -82,9 +86,296 @@
     return (cross_f.astype(jnp.bfloat16), variance)
 
 
+X, Y, ZL, ZH = 1, 2, 4, 8
+NGRP = 4
+
+
+def swap_cores(value):
+    return lax.ppermute(value, "narrow", [(0, 1), (1, 0)])
+
+
+def hop(value, mask):
+    size = lax.axis_size("wide")
+    return lax.ppermute(value, "wide", [(i, i ^ mask) for i in range(size)])
+
+
+def pack_panel(structure, panel, other):
+    nblocks = structure.shape[1]
+    half_blocks = panel.shape[1] // BLK
+
+    def body(st, panel_ref, other_ref, out0, out1, sem):
+        n = lax.axis_index("narrow")
+        outs = (out0, out1)
+
+        def copies(j):
+            b = st[n, j]
+            row = pl.multiple_of(lax.rem(b, half_blocks) * BLK, BLK)
+            mine = lax.div(b, half_blocks) == n
+            return mine, [
+                (
+                    pltpu.make_async_copy(
+                        panel_ref.at[n, pl.ds(row, BLK), pl.ds(c * LANES, LANES)],
+                        outs[c].at[pl.ds(j * BLK, BLK), :],
+                        sem.at[j, c],
+                    ),
+                    pltpu.make_async_copy(
+                        other_ref.at[pl.ds(row, BLK), pl.ds(c * LANES, LANES)],
+                        outs[c].at[pl.ds(j * BLK, BLK), :],
+                        sem.at[j, c],
+                    ),
+                )
+                for c in range(2)
+            ]
+
+        for j in range(nblocks):
+            mine, pairs = copies(j)
+            for own, oth in pairs:
+                pl.when(mine)(own.start)
+                pl.when(jnp.logical_not(mine))(oth.start)
+        for j in range(nblocks):
+            mine, pairs = copies(j)
+            for own, oth in pairs:
+                oth.wait()
+
+    shape = jax.ShapeDtypeStruct((nblocks * BLK, LANES), panel.dtype)
+    return pl.pallas_call(
+        body,
+        out_shape=(shape, shape),
+        grid_spec=pltpu.PrefetchScalarGridSpec(
+            num_scalar_prefetch=1,
+            grid=(1,),
+            in_specs=[ANY, ANY],
+            out_specs=[ANY, ANY],
+            scratch_shapes=[pltpu.SemaphoreType.DMA((nblocks, 2))],
+        ),
+        name="pack_panel",
+    )(structure, panel, other)
+
+
+def pack_inverse(structure, owns, others):
+    nblocks = structure.shape[1]
+    half_blocks = owns[0].shape[1] // BLK
+
+    def body(st, *refs):
+        own_refs, oth_refs = refs[:NGRP], refs[NGRP : 2 * NGRP]
+        out, sem = refs[2 * NGRP :]
+        n = lax.axis_index("narrow")
+        for start in (True, False):
+            for j in range(nblocks):
+                b = st[n, j]
+                col = pl.multiple_of(lax.rem(b, half_blocks) * BLK, BLK)
+                mine = lax.div(b, half_blocks) == n
+                for d in range(NGRP):
+                    own, oth = [
+                        pltpu.make_async_copy(
+                            ref.at[:, pl.ds(col, BLK)],
+                            out.at[d, :, pl.ds(j * BLK, BLK)],
+                            sem.at[j, d],
+                        )
+                        for ref in (own_refs[d], oth_refs[d])
+                    ]
+                    if start:
+                        pl.when(mine)(own.start)
+                        pl.when(jnp.logical_not(mine))(oth.start)
+                    else:
+                        oth.wait()
+
+    return pl.pallas_call(
+        body,
+        out_shape=jax.ShapeDtypeStruct((NGRP, BLK, nblocks * BLK), owns[0].dtype),
+        grid_spec=pltpu.PrefetchScalarGridSpec(
+            num_scalar_prefetch=1,
+            grid=(1,),
+            in_specs=[ANY] * (2 * NGRP),
+            out_specs=ANY,
+            scratch_shapes=[pltpu.SemaphoreType.DMA((nblocks, NGRP))],
+        ),
+        name="pack_inverse",
+    )(structure, *owns, *others)
+
+
+def products(structure, sel, pieces):
+    nblocks = structure.shape[1]
+    depth = nblocks * BLK
+
+    def body(st, sel_ref, b0, b1, b2, b3, out_ref, sum_ref):
+        d = pl.program_id(0)
+        n = lax.axis_index("narrow")
+        w = lax.axis_index("wide")
+        x = lax.bitwise_and(w, 1)
+        zh = lax.div(w, ZH)
+        mask = lax.rem(d, 2) * Y + lax.div(d, 2) * ZL
+        row = lax.bitwise_xor(w, mask)
+        pos = jnp.int32(0)
+        inside = jnp.int32(0)
+        for j in range(nblocks):
+            hit = (st[n, j] == row).astype(jnp.int32)
+            pos = pos + j * hit
+            inside = inside + hit
+        pos = pl.multiple_of(pos * BLK, BLK)
+        refs = (b0, b1, b2, b3)
+
+        @pl.when(d == 0)
+        def _():
+            sum_ref[...] = jnp.zeros_like(sum_ref)
+
+        @pl.when(inside == 0)
+        def _():
+            out_ref[...] = jnp.zeros_like(out_ref)
+
+        @pl.when(inside > 0)
+        def _():
+            for dz in range(2):
+                away = (lax.bitwise_xor(zh, dz) != n).astype(jnp.int32)
+                left, right = refs[2 * dz], refs[2 * dz + 1]
+                acc = jnp.zeros((BLK, 2 * LANES), jnp.float32)
+                acc = jnp.dot(
+                    sel_ref[0],
+                    jnp.concatenate([left[...], right[...]], axis=1),
+                    preferred_element_type=jnp.float32,
+                )
+                for dx in range(2):
+                    part = acc[:, dx * LANES : (dx + 1) * LANES]
+                    slot = lax.bitwise_xor(x, dx)
+                    rows = refs[2 * dz + dx][pl.ds(pos, BLK), :].astype(jnp.float32)
+                    sum_ref[away, slot] += jnp.sum(part * rows, axis=0, keepdims=True)
+                    out_ref[away, 0, slot] = (-part).T.astype(out_ref.dtype)
+
+    whole = pl.BlockSpec((depth, LANES), lambda d, st: (0, 0))
+    return pl.pallas_call(
+        body,
+        out_shape=(
+            jax.ShapeDtypeStruct((2, NGRP, 2, LANES, BLK), sel.dtype),
+            jax.ShapeDtypeStruct((2, 2, 1, LANES), jnp.float32),
+        ),
+        grid_spec=pltpu.PrefetchScalarGridSpec(
+            num_scalar_prefetch=1,
+            grid=(NGRP,),
+            in_specs=[pl.BlockSpec((1, BLK, depth), lambda d, st: (d, 0, 0))] + [whole] * 4,
+            out_specs=[
+                pl.BlockSpec((2, 1, 2, LANES, BLK), lambda d, st: (0, d, 0, 0, 0)),
+                pl.BlockSpec((2, 2, 1, LANES), lambda d, st: (0, 0, 0, 0)),
+            ],
+        ),
+        compiler_params=pltpu.CompilerParams(vmem_limit_bytes=40 * 1024 * 1024),
+        cost_estimate=pl.CostEstimate(
+            flops=2 * NGRP * BLK * depth * 4 * LANES,
+            bytes_accessed=2 * (NGRP * BLK * depth + 4 * depth * LANES),
+            transcendentals=0,
+        ),
+        name="products",
+    )(structure, sel, *pieces)
+
+
+def assemble(messages, chunk, held):
+    tall = 4 * LANES
+    rows_total = 2 * 2 * NGRP * tall
+
+    def body(*refs):
+        msg_refs = refs[:NGRP]
+        out, wide_buf, narrow_buf, sem = refs[-4:]
+        n = lax.axis_index("narrow")
+        w = lax.axis_index("wide")
+        copies = []
+        for d in range(NGRP):
+            source = lax.bitwise_xor(lax.rem(lax.div(w, Y), NGRP), d)
+            for xx in range(2):
+                slot = 2 * d + xx
+                for k in range(2):
+                    which = (n != k).astype(jnp.int32)
+                    value = msg_refs[d][which, xx].astype(jnp.float32)
+                    for lt in range(2):
+                        wide_buf[slot, pl.ds(2 * lt + k, LANES, stride=4), :] = value[
+                            :, lt * LANES : (lt + 1) * LANES
+                        ]
+                narrow_buf[slot] = wide_buf[slot].astype(narrow_buf.dtype)
+                row = pl.multiple_of(((source * 2 + xx) * 2 + chunk) * tall, tall)
+                copy = pltpu.make_async_copy(
+                    narrow_buf.at[slot], out.at[pl.ds(row, tall), :], sem.at[slot]
+                )
+                copy.start()
+                copies.append(copy)
+        for copy in copies:
+            copy.wait()
+
+    vmem = pl.BlockSpec(memory_space=pltpu.VMEM)
+    extra = () if held is None else (held,)
+    return pl.pallas_call(
+        body,
+        out_shape=jax.ShapeDtypeStruct((rows_total, LANES), messages[0].dtype),
+        in_specs=[vmem] * NGRP + [ANY] * len(extra),
+        out_specs=ANY,
+        scratch_shapes=[
+            pltpu.VMEM((2 * NGRP, tall, LANES), jnp.float32),
+            pltpu.VMEM((2 * NGRP, tall, LANES), messages[0].dtype),
+            pltpu.SemaphoreType.DMA((2 * NGRP,)),
+        ],
+        input_output_aliases={NGRP: 0} if extra else {},
+        compiler_params=pltpu.CompilerParams(vmem_limit_bytes=16 * 1024 * 1024),
+        name="assemble",
+    )(*messages, *extra)
+
+
+def per_device_grid(inverse, panel, factor_inv, structure):
+    n = lax.axis_index("narrow")
+    w = lax.axis_index("wide")
+    other = swap_cores(lax.dynamic_index_in_dim(panel, 1 - n, 0, keepdims=False))
+    a_y = hop(inverse, Y)
+    a_z = hop(inverse, ZL)
+    chunks = pack_panel(structure, panel, other)
+    a_yz = hop(a_z, Y)
+    owns = [inverse, a_y, a_z, a_yz]
+    others = [swap_cores(a) for a in owns]
+    linv_part = jnp.sum(jnp.square(factor_inv.astype(jnp.float32)), axis=1)
+    sel = pack_inverse(structure, owns, others)
+    held = None
+    sums = []
+    for c, mine in enumerate(chunks):
+        b_x = hop(mine, X)
+        b_z = hop(mine, ZH)
+        b_xz = hop(b_z, X)
+        out, sum_c = products(structure, sel, (mine, b_x, b_z, b_xz))
+        sums.append(sum_c)
+        kept, sent = out[0], out[1]
+        back = swap_cores(sent)
+        messages = []
+        for d in range(NGRP):
+            message = jnp.stack([kept[d], back[d]])
+            if d:
+                message = hop(message, (d % 2) * Y + (d // 2) * ZL)
+            messages.append(message)
+        held = assemble(messages, c, held)
+    half = panel.shape[2] * lax.axis_size("wide") // 2
+    cross = held.reshape(half, 2, 2, LANES).transpose(0, 2, 1, 3).reshape(half, 2, BLK)
+    both = jnp.concatenate(sums, axis=2)
+    kept, sent = both[0].reshape(-1), both[1].reshape(-1)
+    back = swap_cores(sent)
+    pair = jnp.where(n == 0, jnp.stack([kept, back]), jnp.stack([back, kept]))
+    group = lax.rem(lax.div(w, Y), NGRP)
+    spots = jnp.arange(NGRP, dtype=jnp.int32)[None, :, None] == group
+    placed = jnp.where(spots, pair[:, None, :], 0.0).reshape(2, half)
+    variance = linv_part + placed
+    for mask in (Y, ZL, X, ZH):
+        variance = variance + hop(variance, mask)
+    return cross, variance
+
+
 def solution(mesh):
     in_specs = (P("wide", "narrow"), P(None, "narrow", "wide"), P(None, "wide", "narrow"), P())
     out_specs = (P("narrow", None, "wide"), P(None, "narrow"))
-    return jax.shard_map(
-        per_device, mesh=mesh, in_specs=in_specs, out_specs=out_specs, check_vma=False
-    )
+
+    def run(inverse, panel, factor_inv, structure):
+        fits = (
+            mesh.shape["wide"] == 16
+            and mesh.shape["narrow"] == 2 == panel.shape[0]
+            and panel.shape[2] == 16 * BLK == inverse.shape[0]
+        )
+        return jax.shard_map(
+            per_device_grid if fits else per_device_general,
+            mesh=mesh,
+            in_specs=in_specs,
+            out_specs=out_specs,
+            check_vma=False,
+        )(inverse, panel, factor_inv, structure)
+
+    return run

time: 720 us -> 408 us (0.57)
  waiting for transfers between devices: 488 us -> 113 us
  Pallas kernels: 0 us -> 256 us
  blocking collectives: 77.1 us -> 0 us
  local copies, waits for them, and re-layouts: 55.6 us -> 5.37 us
  other arithmetic: 39.8 us -> 2.95 us
  between operations: 34.1 us -> 0.98 us
  starting transfers between devices: 0.2 us -> 29.1 us
  matrix products: 22.1 us -> 0 us
    all_gather x2 -> x0, waiting for transfers between devices: 473 us -> none  [per_device(): gathered_one = lax.all_gather(panel[sup_index], 'wide', axis=1, tiled=True)]
    pallas_call x0 -> x6, Pallas kernels: none -> 256 us  [the longest x1 193 us: pack_inverse(): pl.pallas_call(body, out_shape=jax.ShapeDtypeStruct((NGRP, BLK, nblocks *...]
    ppermute x0 -> x27, waiting for transfers between devices: none -> 113 us  [the longest x19 112 us: hop(): return lax.ppermute(value, 'wide', [(i, i ^ mask) for i in range(size)])]
    psum x1 -> x0, blocking collectives: 77.1 us -> none  [per_device(): variance = lax.psum(linv_part - weighted, 'wide')]
    ppermute x0 -> x27, starting transfers between devices: none -> 29.1 us  [the longest x19 27.3 us: hop(): return lax.ppermute(value, 'wide', [(i, i ^ mask) for i in range(size)])]
    neg x2 -> x0, other arithmetic: 27.6 us -> none  [block_partial(): return -running]
    another operation x11 -> x0, local copies, waits for them, and re-layouts: 25 us -> none
    dot_general x5 -> x0, matrix products: 22.1 us -> none  [product(): lax.dot_general(panel_piece, block_z, (((0,), (1,)), ((), ())), preferred...]
  transfers between devices with their start and end apart: 5 -> 27, of which waited for: 3 -> 10; matrix products, arithmetic and copies ran while one was open for 12% -> 1% of each run, Pallas kernels for 0% -> 61%
where the time goes in v1:
time: 408 us; the launch traced here: 407 us
  Pallas kernels  256 us (63%)
  waiting for transfers between devices  113 us (28%)
  starting transfers between devices  29.1 us (7%)
  local copies, waits for them, and re-layouts  5.37 us (1%)
    pallas_call x1, Pallas kernels, pack_inverse(): pl.pallas_call(body, out_shape=jax.ShapeDtypeStruct((NGRP, BLK, nblocks *...  193 us
    ppermute x19, waiting for transfers between devices, hop(): return lax.ppermute(value, 'wide', [(i, i ^ mask) for i in range(size)])  112 us
    pallas_call x1, Pallas kernels, pack_panel(): pl.pallas_call(body, out_shape=(shape, shape), grid_spec=pltpu.PrefetchSc...  49.7 us
    ppermute x19, starting transfers between devices, hop(): return lax.ppermute(value, 'wide', [(i, i ^ mask) for i in range(size)])  27.3 us
    pallas_call x2, Pallas kernels, products(): pl.pallas_call(body, out_shape=(jax.ShapeDtypeStruct((2, NGRP, 2, LANES,...  11.3 us
  transfers between devices with their start and end apart: 27, of which 10 were waited for; matrix products, arithmetic and copies ran while one was open for 1% of the time, Pallas kernels for 61%

profile of v1, /device:TPU:0, one launch (start us, length us, event | category | flops | bytes accessed | tf_op | source)
XLA Modules:
  0.0 407.0 jit_solution(8130059628435693478)
XLA Ops:
  0.6 3.1 collective-permute-start.1
  3.7 1.5 collective-permute-start
  7.1 20.1 %collective-permute-done.1.refs_2_ = bf16[256,2048]{1,0:T(8,128)(2,1)} collective-permute-done((bf16[256,2048]{1,0:T(8,128)(2,1)}, bf16[256,2048]{1,0:T(8,128)(2,1)}, u32[]{:S(2)}, u32[]{:S(2)}) %collective-permute-start.1) | collective-permute-done | bytes 1048608 | tf_op jit(solution)/shard_map/ppermute | solution.py:99
  27.2 1.7 collective-permute-start.2
  30.4 49.7 %pack_panel.1 = (bf16[3072,128]{1,0:T(8,128)(2,1)}, bf16[3072,128]{1,0:T(8,128)(2,1)}) custom-call(s32[2,12]{1,0:T(2,128)} %st.7, bf16[2,2048,256]{2,1,0:T(8,128)(2,1)} %panel_ref.1, bf16[2048,256]{1,0:T(8,128)(2,1)} %copy-done.4), custom_call_target="tpu_custom_call" | custom-call | tf_op jit(solution)/shard_map/pack_panel/pallas_call | solution.py:141
  80.0 2.7 collective-permute-start.9
  83.0 52.3 %collective-permute-done.9.b2 = bf16[3072,128]{1,0:T(8,128)(2,1)S(1)} collective-permute-done((bf16[3072,128]{1,0:T(8,128)(2,1)}, bf16[3072,128]{1,0:T(8,128)(2,1)S(1)}, u32[]{:S(2)}, u32[]{:S(2)}) %collective-permute-start.9) | collective-permute-done | bytes 786464 | tf_op jit(solution)/shard_map/ppermute | solution.py:99
  135.3 1.5 collective-permute-start.8
  136.8 14.4 %collective-permute-done.16.b2 = bf16[3072,128]{1,0:T(8,128)(2,1)S(1)} collective-permute-done((bf16[3072,128]{1,0:T(8,128)(2,1)}, bf16[3072,128]{1,0:T(8,128)(2,1)S(1)}, u32[]{:S(2)}, u32[]{:S(2)}) %collective-permute-start.16) | collective-permute-done | bytes 786464 | tf_op jit(solution)/shard_map/ppermute | solution.py:99
  151.2 1.5 collective-permute-start.10
  153.3 1.5 collective-permute-start.17
  154.9 2.0 multiply_reduce_fusion
  156.9 193.0 %pack_inverse.1.sel_ref = bf16[4,256,3072]{2,1,0:T(8,128)(2,1)} custom-call(s32[2,12]{1,0:T(2,128)} %st.7, bf16[256,2048]{1,0:T(8,128)(2,1)} %refs_0_.1, bf16[256,2048]{1,0:T(8,128)(2,1)} %collective-permute-done.refs_1_, bf16[256,2048]{1,0:T(8,128)(2,1)} %collective-permute-done.1.refs_2_, bf16[256,2048]{1,0:T(8,128)(2,1)} %collective-permute-done.2.refs_3_, ...), custom_call_target="tpu_custom_call" | custom-call | tf_op jit(solution)/shard_map/pack_inverse/pallas_call | solution.py:183
  350.0 2.8 copy-done
  352.7 5.6 %products.2 = (bf16[2,4,2,128,256]{4,3,2,1,0:T(8,128)(2,1)S(1)}, f32[2,2,1,128]{3,2,1,0:T(1,128)S(1)}) custom-call(s32[2,12]{1,0:T(2,128)S(1)} %copy-done.1, bf16[4,256,3072]{2,1,0:T(8,128)(2,1)S(1)} %copy-done, bf16[3072,128]{1,0:T(8,128)(2,1)S(1)} %copy-done.3, bf16[3072,128]{1,0:T(8,128)(2,1)} %collective-permute-done.8.b1, ...), custom_call_target="tpu_custom_call" | custom-call | flops 3221225472 | bytes 9437184 | tf_op jit(solution)/shard_map/products/pallas_call | solution.py:245
  358.4 5.7 %products.3 = (bf16[2,4,2,128,256]{4,3,2,1,0:T(8,128)(2,1)S(1)}, f32[2,2,1,128]{3,2,1,0:T(1,128)S(1)}) custom-call(s32[2,12]{1,0:T(2,128)S(1)} %copy-done.1, bf16[4,256,3072]{2,1,0:T(8,128)(2,1)S(1)} %copy-done, bf16[3072,128]{1,0:T(8,128)(2,1)S(1)} %copy-done.2, bf16[3072,128]{1,0:T(8,128)(2,1)} %collective-permute-done.15.b1, ...), custom_call_target="tpu_custom_call" | custom-call | flops 3221225472 | bytes 9437184 | tf_op jit(solution)/shard_map/products/pallas_call | solution.py:245
  366.8 2.4 collective-permute-done.23
  370.2 2.8 collective-permute-done.24
  373.9 3.0 collective-permute-done.25
  376.8 2.8 collective-permute-start.26
  382.0 2.1 collective-permute-start.20
  384.3 2.1 collective-permute-start.13
  386.4 12.3 %collective-permute-done.19.refs_1_ = bf16[2,2,128,256]{3,2,1,0:T(8,128)(2,1)S(1)} collective-permute-done((bf16[2,2,128,256]{3,2,1,0:T(8,128)(2,1)S(1)}, bf16[2,2,128,256]{3,2,1,0:T(8,128)(2,1)S(1)}, u32[]{:S(2)}, u32[]{:S(2)}) %collective-permute-start.19) | collective-permute-done | bytes 262176 | tf_op jit(solution)/shard_map/ppermute | solution.py:99
  401.6 4.4 %collective-permute-done.14.refs_3_ = bf16[2,2,128,256]{3,2,1,0:T(8,128)(2,1)S(1)} collective-permute-done((bf16[2,2,128,256]{3,2,1,0:T(8,128)(2,1)S(1)}, bf16[2,2,128,256]{3,2,1,0:T(8,128)(2,1)S(1)}, u32[]{:S(2)}, u32[]{:S(2)}) %collective-permute-start.14) | collective-permute-done | bytes 262176 | tf_op jit(solution)/shard_map/ppermute | solution.py:99
  (76 shorter events, 15.3 us)
Async XLA Ops:
  0.6 26.6 %collective-permute-start.1 = (bf16[256,2048]{1,0:T(8,128)(2,1)}, bf16[256,2048]{1,0:T(8,128)(2,1)}, u32[]{:S(2)}, u32[]{:S(2)}) collective-permute-start(bf16[256,2048]{1,0:T(8,128)(2,1)} %refs_0_.1), channel_id=1, source_target_pairs={{0,8},{2,10},{4,12},{6,14},{8,0},{10,2},{12,4},{14,6},{16,24},{18,... | collective-permute-start | bytes 3145736 | tf_op jit(solution)/shard_map/ppermute | solution.py:99
  3.7 25.2 %collective-permute-start = (bf16[256,2048]{1,0:T(8,128)(2,1)}, bf16[256,2048]{1,0:T(8,128)(2,1)}, u32[]{:S(2)}, u32[]{:S(2)}) collective-permute-start(bf16[256,2048]{1,0:T(8,128)(2,1)} %refs_0_.1), channel_id=1, source_target_pairs={{0,4},{2,6},{4,0},{6,2},{8,12},{10,14},{12,8},{14,10},{16,20},{18,... | collective-permute-start | bytes 3145736 | tf_op jit(solution)/shard_map/ppermute | solution.py:99
  6.5 22.9 %collective-permute-start.7 = (bf16[2048,256]{1,0:T(8,128)(2,1)S(1)}, bf16[2048,256]{1,0:T(8,128)(2,1)S(1)}, u32[]{:S(2)}, u32[]{:S(2)}) collective-permute-start(bf16[2048,256]{1,0:T(8,128)(2,1)S(1)} %dynamic-slice_bitcast_fusion), channel_id=1, source_target_pairs={{0,1},{1,0},{2,3},{3,2},{4,5},{5,4},{6,7},{7,6},{8,9},{9,8},{10,11... | collective-permute-start | bytes 3145736 | tf_op jit(solution)/shard_map/ppermute | solution.py:94
  6.6 76.1 %collective-permute-start.3 = (bf16[256,2048]{1,0:T(8,128)(2,1)S(1)}, bf16[256,2048]{1,0:T(8,128)(2,1)}, u32[]{:S(2)}, u32[]{:S(2)}) collective-permute-start(bf16[256,2048]{1,0:T(8,128)(2,1)S(1)} %copy-done.5), channel_id=1, source_target_pairs={{0,1},{1,0},{2,3},{3,2},{4,5},{5,4},{6,7},{7,6},{8,9},{9,8},{10,11... | collective-permute-start | bytes 3145736 | tf_op jit(solution)/shard_map/ppermute | solution.py:94
  27.2 55.8 %collective-permute-start.2 = (bf16[256,2048]{1,0:T(8,128)(2,1)}, bf16[256,2048]{1,0:T(8,128)(2,1)}, u32[]{:S(2)}, u32[]{:S(2)}) collective-permute-start(bf16[256,2048]{1,0:T(8,128)(2,1)} %collective-permute-done.1.refs_2_), channel_id=1, source_target_pairs={{0,4},{2,6},{4,0},{6,2},{8,12},{10,14},{12,8},{14,10},{16,20},{18,... | collective-permute-start | bytes 3145736 | tf_op jit(solution)/shard_map/ppermute | solution.py:99
  28.9 123.8 %collective-permute-start.4 = (bf16[256,2048]{1,0:T(8,128)(2,1)}, bf16[256,2048]{1,0:T(8,128)(2,1)}, u32[]{:S(2)}, u32[]{:S(2)}) collective-permute-start(bf16[256,2048]{1,0:T(8,128)(2,1)} %collective-permute-done.refs_1_), channel_id=1, source_target_pairs={{0,1},{1,0},{2,3},{3,2},{4,5},{5,4},{6,7},{7,6},{8,9},{9,8},{10,11... | collective-permute-start | bytes 3145736 | tf_op jit(solution)/shard_map/ppermute | solution.py:94
  28.9 124.4 %collective-permute-start.5 = (bf16[256,2048]{1,0:T(8,128)(2,1)}, bf16[256,2048]{1,0:T(8,128)(2,1)}, u32[]{:S(2)}, u32[]{:S(2)}) collective-permute-start(bf16[256,2048]{1,0:T(8,128)(2,1)} %collective-permute-done.1.refs_2_), channel_id=1, source_target_pairs={{0,1},{1,0},{2,3},{3,2},{4,5},{5,4},{6,7},{7,6},{8,9},{9,8},{10,11... | collective-permute-start | bytes 3145736 | tf_op jit(solution)/shard_map/ppermute | solution.py:94
  80.0 55.3 %collective-permute-start.9 = (bf16[3072,128]{1,0:T(8,128)(2,1)}, bf16[3072,128]{1,0:T(8,128)(2,1)S(1)}, u32[]{:S(2)}, u32[]{:S(2)}) collective-permute-start(bf16[3072,128]{1,0:T(8,128)(2,1)} %get-tuple-element.8.b0), channel_id=1, source_target_pairs={{0,16},{2,18},{4,20},{6,22},{8,24},{10,26},{12,28},{14,30},{16,0},... | collective-permute-start | bytes 2359304 | tf_op jit(solution)/shard_map/ppermute | solution.py:99
  82.7 68.5 %collective-permute-start.16 = (bf16[3072,128]{1,0:T(8,128)(2,1)}, bf16[3072,128]{1,0:T(8,128)(2,1)S(1)}, u32[]{:S(2)}, u32[]{:S(2)}) collective-permute-start(bf16[3072,128]{1,0:T(8,128)(2,1)} %get-tuple-element.10.b0), channel_id=1, source_target_pairs={{0,16},{2,18},{4,20},{6,22},{8,24},{10,26},{12,28},{14,30},{16,0},... | collective-permute-start | bytes 2359304 | tf_op jit(solution)/shard_map/ppermute | solution.py:99
  83.0 73.9 %collective-permute-start.6 = (bf16[256,2048]{1,0:T(8,128)(2,1)}, bf16[256,2048]{1,0:T(8,128)(2,1)}, u32[]{:S(2)}, u32[]{:S(2)}) collective-permute-start(bf16[256,2048]{1,0:T(8,128)(2,1)} %collective-permute-done.2.refs_3_), channel_id=1, source_target_pairs={{0,1},{1,0},{2,3},{3,2},{4,5},{5,4},{6,7},{7,6},{8,9},{9,8},{10,11... | collective-permute-start | bytes 3145736 | tf_op jit(solution)/shard_map/ppermute | solution.py:94
  135.3 214.6 %collective-permute-start.8 = (bf16[3072,128]{1,0:T(8,128)(2,1)}, bf16[3072,128]{1,0:T(8,128)(2,1)}, u32[]{:S(2)}, u32[]{:S(2)}) collective-permute-start(bf16[3072,128]{1,0:T(8,128)(2,1)} %get-tuple-element.8.b0), channel_id=1, source_target_pairs={{0,2},{2,0},{4,6},{6,4},{8,10},{10,8},{12,14},{14,12},{16,18},{18,... | collective-permute-start | bytes 2359304 | tf_op jit(solution)/shard_map/ppermute | solution.py:99
  151.2 198.7 %collective-permute-start.10 = (bf16[3072,128]{1,0:T(8,128)(2,1)S(1)}, bf16[3072,128]{1,0:T(8,128)(2,1)}, u32[]{:S(2)}, u32[]{:S(2)}) collective-permute-start(bf16[3072,128]{1,0:T(8,128)(2,1)S(1)} %collective-permute-done.9.b2), channel_id=1, source_target_pairs={{0,2},{2,0},{4,6},{6,4},{8,10},{10,8},{12,14},{14,12},{16,18},{18,... | collective-permute-start | bytes 2359304 | tf_op jit(solution)/shard_map/ppermute | solution.py:99
  152.7 205.7 %collective-permute-start.15 = (bf16[3072,128]{1,0:T(8,128)(2,1)}, bf16[3072,128]{1,0:T(8,128)(2,1)}, u32[]{:S(2)}, u32[]{:S(2)}) collective-permute-start(bf16[3072,128]{1,0:T(8,128)(2,1)} %get-tuple-element.10.b0), channel_id=1, source_target_pairs={{0,2},{2,0},{4,6},{6,4},{8,10},{10,8},{12,14},{14,12},{16,18},{18,... | collective-permute-start | bytes 2359304 | tf_op jit(solution)/shard_map/ppermute | solution.py:99
  153.3 205.1 %collective-permute-start.17 = (bf16[3072,128]{1,0:T(8,128)(2,1)S(1)}, bf16[3072,128]{1,0:T(8,128)(2,1)}, u32[]{:S(2)}, u32[]{:S(2)}) collective-permute-start(bf16[3072,128]{1,0:T(8,128)(2,1)S(1)} %collective-permute-done.16.b2), channel_id=1, source_target_pairs={{0,2},{2,0},{4,6},{6,4},{8,10},{10,8},{12,14},{14,12},{16,18},{18,... | collective-permute-start | bytes 2359304 | tf_op jit(solution)/shard_map/ppermute | solution.py:99
  364.2 15.5 %collective-permute-start.11 = (bf16[4,2,128,256]{3,2,1,0:T(8,128)(2,1)S(1)}, bf16[4,2,128,256]{3,2,1,0:T(8,128)(2,1)S(1)}, u32[]{:S(2)}, u32[]{:S(2)}) collective-permute-start(bf16[4,2,128,256]{3,2,1,0:T(8,128)(2,1)S(1)} %slice_bitcast_fusion.1), channel_id=1, source_target_pairs={{0,1},{1,0},{2,3},{3,2},{4,5},{5,4},{6,7},{7,6},{8,9},{9,8},{10,11... | collective-permute-start | bytes 1572872 | tf_op jit(solution)/shard_map/ppermute | solution.py:94
  365.4 3.8 collective-permute-start.23
  370.1 10.3 %collective-permute-start.18 = (bf16[4,2,128,256]{3,2,1,0:T(8,128)(2,1)S(1)}, bf16[4,2,128,256]{3,2,1,0:T(8,128)(2,1)S(1)}, u32[]{:S(2)}, u32[]{:S(2)}) collective-permute-start(bf16[4,2,128,256]{3,2,1,0:T(8,128)(2,1)S(1)} %slice_bitcast_fusion), channel_id=1, source_target_pairs={{0,1},{1,0},{2,3},{3,2},{4,5},{5,4},{6,7},{7,6},{8,9},{9,8},{10,11... | collective-permute-start | bytes 1572872 | tf_op jit(solution)/shard_map/ppermute | solution.py:94
  376.8 7.5 %collective-permute-start.26 = (f32[2,2048]{1,0:T(2,128)S(1)}, f32[2,2048]{1,0:T(2,128)S(1)}, u32[]{:S(2)}, u32[]{:S(2)}) collective-permute-start(f32[2,2048]{1,0:T(2,128)S(1)} %add.24), channel_id=1, source_target_pairs={{0,16},{2,18},{4,20},{6,22},{8,24},{10,26},{12,28},{14,30},{16,0},... | collective-permute-start | bytes 49160 | tf_op jit(solution)/shard_map/ppermute | solution.py:99
  379.7 21.5 %collective-permute-start.12 = (bf16[2,2,128,256]{3,2,1,0:T(8,128)(2,1)S(1)}, bf16[2,2,128,256]{3,2,1,0:T(8,128)(2,1)S(1)}, u32[]{:S(2)}, u32[]{:S(2)}) collective-permute-start(bf16[2,2,128,256]{3,2,1,0:T(8,128)(2,1)S(1)} %pad_maximum_fusion.1), channel_id=1, source_target_pairs={{0,4},{2,6},{4,0},{6,2},{8,12},{10,14},{12,8},{14,10},{16,20},{18,... | collective-permute-start | bytes 786440 | tf_op jit(solution)/shard_map/ppermute | solution.py:99
  380.5 18.2 %collective-permute-start.19 = (bf16[2,2,128,256]{3,2,1,0:T(8,128)(2,1)S(1)}, bf16[2,2,128,256]{3,2,1,0:T(8,128)(2,1)S(1)}, u32[]{:S(2)}, u32[]{:S(2)}) collective-permute-start(bf16[2,2,128,256]{3,2,1,0:T(8,128)(2,1)S(1)} %pad_maximum_fusion.5), channel_id=1, source_target_pairs={{0,4},{2,6},{4,0},{6,2},{8,12},{10,14},{12,8},{14,10},{16,20},{18,... | collective-permute-start | bytes 786440 | tf_op jit(solution)/shard_map/ppermute | solution.py:99
  382.0 18.1 %collective-permute-start.20 = (bf16[2,2,128,256]{3,2,1,0:T(8,128)(2,1)S(1)}, bf16[2,2,128,256]{3,2,1,0:T(8,128)(2,1)S(1)}, u32[]{:S(2)}, u32[]{:S(2)}) collective-permute-start(bf16[2,2,128,256]{3,2,1,0:T(8,128)(2,1)S(1)} %pad_maximum_fusion.6), channel_id=1, source_target_pairs={{0,8},{2,10},{4,12},{6,14},{8,0},{10,2},{12,4},{14,6},{16,24},{18,... | collective-permute-start | bytes 786440 | tf_op jit(solution)/shard_map/ppermute | solution.py:99
  384.1 16.0 %collective-permute-start.21 = (bf16[2,2,128,256]{3,2,1,0:T(8,128)(2,1)S(1)}, bf16[2,2,128,256]{3,2,1,0:T(8,128)(2,1)S(1)}, u32[]{:S(2)}, u32[]{:S(2)}) collective-permute-start(bf16[2,2,128,256]{3,2,1,0:T(8,128)(2,1)S(1)} %pad_maximum_fusion.7), channel_id=1, source_target_pairs={{0,12},{2,14},{4,8},{6,10},{8,4},{10,6},{12,0},{14,2},{16,28},{18,... | collective-permute-start | bytes 786440 | tf_op jit(solution)/shard_map/ppermute | solution.py:99
  384.3 17.3 %collective-permute-start.13 = (bf16[2,2,128,256]{3,2,1,0:T(8,128)(2,1)S(1)}, bf16[2,2,128,256]{3,2,1,0:T(8,128)(2,1)S(1)}, u32[]{:S(2)}, u32[]{:S(2)}) collective-permute-start(bf16[2,2,128,256]{3,2,1,0:T(8,128)(2,1)S(1)} %pad_maximum_fusion.2), channel_id=1, source_target_pairs={{0,8},{2,10},{4,12},{6,14},{8,0},{10,2},{12,4},{14,6},{16,24},{18,... | collective-permute-start | bytes 786440 | tf_op jit(solution)/shard_map/ppermute | solution.py:99
  398.7 7.3 %collective-permute-start.14 = (bf16[2,2,128,256]{3,2,1,0:T(8,128)(2,1)S(1)}, bf16[2,2,128,256]{3,2,1,0:T(8,128)(2,1)S(1)}, u32[]{:S(2)}, u32[]{:S(2)}) collective-permute-start(bf16[2,2,128,256]{3,2,1,0:T(8,128)(2,1)S(1)} %pad_maximum_fusion.3), channel_id=1, source_target_pairs={{0,12},{2,14},{4,8},{6,10},{8,4},{10,6},{12,0},{14,2},{16,28},{18,... | collective-permute-start | bytes 786440 | tf_op jit(solution)/shard_map/ppermute | solution.py:99
  (9 other events, 606.1 us)

commit v2 on v1

v2 whole, which is shorter than its diff:
```python
import jax
import jax.numpy as jnp
from jax import lax
from jax.experimental import pallas as pl
from jax.experimental.pallas import tpu as pltpu
from jax.sharding import PartitionSpec as P

BLK = 256
LANES = 128
ANY = pl.BlockSpec(memory_space=pl.ANY)
VMEM = pl.BlockSpec(memory_space=pltpu.VMEM)
SMEM = pl.BlockSpec(memory_space=pltpu.SMEM)


def spread(value, axis, source):
    kept = jnp.where(lax.axis_index(axis) == source, value, 0).astype(value.dtype)
    return lax.psum(kept, axis)


def block_partial(gathered, inverse, row_inside, col_inside, first_row, row_count):
    local_blocks = inverse.shape[1] // BLK
    running = jnp.zeros((row_count, BLK), jnp.float32)
    for blk_index in range(local_blocks):

        def product(blk_index=blk_index):
            panel_piece = lax.dynamic_slice(
                gathered, (blk_index * BLK, first_row), (BLK, row_count)
            )
            block_z = inverse[:, blk_index * BLK : (blk_index + 1) * BLK]
            return lax.dot_general(
                panel_piece, block_z, (((0,), (1,)), ((), ())), preferred_element_type=jnp.float32
            )

        def skipped():
            return jnp.zeros((row_count, BLK), jnp.float32)

        running = running + lax.cond(row_inside & col_inside[blk_index], product, skipped)
    return -running


def per_device_general(inverse, panel, factor_inv, structure):
    wide_count = lax.axis_size("wide")
    narrow_count = lax.axis_size("narrow")
    nsup_count = panel.shape[0]
    kw_total = panel.shape[2] * wide_count
    kw_local = kw_total // narrow_count
    local_blocks = inverse.shape[1] // BLK
    row_index = lax.axis_index("wide")
    col_first = lax.axis_index("narrow") * local_blocks
    col_ids = col_first + jnp.arange(local_blocks, dtype=jnp.int32)
    row_inside = jnp.any(structure == row_index, axis=1)
    col_inside = jnp.any(structure[:, :, None] == col_ids[None, None, :], axis=1)
    root_index = row_index // local_blocks
    offset = (row_index - root_index * local_blocks) * BLK
    cross_parts = []
    own_parts = []
    for sup_index in range(nsup_count):
        gathered_one = lax.all_gather(panel[sup_index], "wide", axis=1, tiled=True)

        def one_term(first_row, row_count, gathered_one=gathered_one, sup_index=sup_index):
            return block_partial(
                gathered_one,
                inverse,
                row_inside[sup_index],
                col_inside[sup_index],
                first_row,
                row_count,
            )

        cross_parts.append(
            lax.psum_scatter(
                one_term(jnp.int32(0), kw_local * lax.axis_size("narrow")),
                "narrow",
                scatter_dimension=0,
                tiled=True,
            )
        )
        own_parts.append(lax.dynamic_slice_in_dim(gathered_one, offset, BLK, axis=0))
    cross_f = jnp.stack(cross_parts, axis=1)
    own_rows = jnp.stack(own_parts)
    owner_panel = spread(own_rows, "narrow", root_index)
    owner_slice = lax.dynamic_slice_in_dim(
        owner_panel, lax.axis_index("narrow") * kw_local, kw_local, axis=2
    )
    weighted = jnp.einsum("kia,aki->ka", owner_slice.astype(jnp.float32), cross_f)
    linv_part = jnp.sum(jnp.square(factor_inv.astype(jnp.float32)), axis=1)
    variance = lax.psum(linv_part - weighted, "wide")
    return (cross_f.astype(jnp.bfloat16), variance)


X, Y, ZL, ZH = 1, 2, 4, 8
NGRP = 4


def swap_cores(value, name):
    with jax.named_scope(name):
        return lax.ppermute(value, "narrow", [(0, 1), (1, 0)])


def hop(value, mask, name):
    size = lax.axis_size("wide")
    with jax.named_scope(name):
        return lax.ppermute(value, "wide", [(i, i ^ mask) for i in range(size)])


def after(value, *earlier):
    return lax.optimization_barrier((value, *earlier))[0]


def pick(structure_ref, n, j, first):
    nblocks = structure_ref.shape[1]
    start = jnp.where(n == 0, 0, nblocks - first)
    return structure_ref[n, lax.rem(start + j, nblocks)]


def pack_first(structure, panel, first):
    half_blocks = panel.shape[1] // BLK

    def body(st, panel_ref, out):
        n = lax.axis_index("narrow")
        for j in range(first):
            row = pl.multiple_of(lax.rem(pick(st, n, j, first), half_blocks) * BLK, BLK)
            out[j * BLK : (j + 1) * BLK, :] = panel_ref[n, pl.ds(row, BLK), :]

    return pl.pallas_call(
        body,
        out_shape=jax.ShapeDtypeStruct((first * BLK, panel.shape[2]), panel.dtype),
        in_specs=[SMEM, VMEM],
        out_specs=VMEM,
        compiler_params=pltpu.CompilerParams(vmem_limit_bytes=16 * 1024 * 1024),
        name="pack_first",
    )(structure, panel)


def pack_rest(structure, panel, other, first):
    nblocks = structure.shape[1]
    half_blocks = panel.shape[1] // BLK

    def body(st, panel_ref, other_ref, out0, out1):
        n = lax.axis_index("narrow")
        for j in range(nblocks - first):
            b = pick(st, n, first + j, first)
            row = pl.multiple_of(lax.rem(b, half_blocks) * BLK, BLK)
            mine = lax.div(b, half_blocks) == n
            rows = slice(j * BLK, (j + 1) * BLK)

            @pl.when(mine)
            def _():
                out0[rows, :] = panel_ref[n, pl.ds(row, BLK), :LANES]
                out1[rows, :] = panel_ref[n, pl.ds(row, BLK), LANES:]

            @pl.when(jnp.logical_not(mine))
            def _():
                out0[rows, :] = other_ref[pl.ds(row, BLK), :LANES]
                out1[rows, :] = other_ref[pl.ds(row, BLK), LANES:]

    shape = jax.ShapeDtypeStruct(((nblocks - first) * BLK, LANES), panel.dtype)
    return pl.pallas_call(
        body,
        out_shape=(shape, shape),
        in_specs=[SMEM, VMEM, VMEM],
        out_specs=[VMEM, VMEM],
        compiler_params=pltpu.CompilerParams(vmem_limit_bytes=16 * 1024 * 1024),
        cost_estimate=pl.CostEstimate(flops=2 * 10**10, bytes_accessed=0, transcendentals=0),
        name="pack_rest",
    )(structure, panel, other)


def pack_inverse(structure, owns, others, first):
    nblocks = structure.shape[1]
    half_blocks = owns[0].shape[1] // BLK

    def body(st, *refs):
        own_refs, oth_refs = refs[:NGRP], refs[NGRP : 2 * NGRP]
        out = refs[2 * NGRP]
        n = lax.axis_index("narrow")
        for j in range(nblocks):
            b = pick(st, n, j, first)
            col = pl.multiple_of(lax.rem(b, half_blocks) * BLK, BLK)
            mine = lax.div(b, half_blocks) == n

            def move(sources, j=j, col=col):
                for d in range(NGRP):
                    out[d, :, j * BLK : (j + 1) * BLK] = sources[d][:, pl.ds(col, BLK)]

            pl.when(mine)(lambda move=move: move(own_refs))
            pl.when(jnp.logical_not(mine))(lambda move=move: move(oth_refs))

    return pl.pallas_call(
        body,
        out_shape=jax.ShapeDtypeStruct((NGRP, BLK, nblocks * BLK), owns[0].dtype),
        in_specs=[SMEM] + [VMEM] * (2 * NGRP),
        out_specs=VMEM,
        compiler_params=pltpu.CompilerParams(vmem_limit_bytes=32 * 1024 * 1024),
        name="pack_inverse",
    )(structure, *owns, *others)


def products(structure, sel, firsts, rests, chunk, dz):
    nblocks = structure.shape[1]
    early = firsts[0].shape[0]
    late = rests[0].shape[0]
    first = early // BLK

    def body(st, sel_ref, f0, f1, r0, r1, out_ref, sum_ref):
        d = pl.program_id(0)
        n = lax.axis_index("narrow")
        w = lax.axis_index("wide")
        x = lax.bitwise_and(w, 1)
        mask = lax.rem(d, 2) * Y + lax.div(d, 2) * ZL
        row = lax.bitwise_xor(w, mask)
        pos = jnp.int32(0)
        inside = jnp.int32(0)
        for j in range(nblocks):
            hit = (pick(st, n, j, first) == row).astype(jnp.int32)
            pos = pos + j * hit
            inside = inside + hit

        @pl.when(d == 0)
        def _():
            sum_ref[...] = jnp.zeros_like(sum_ref)

        @pl.when(inside == 0)
        def _():
            out_ref[...] = jnp.zeros_like(out_ref)

        @pl.when(inside > 0)
        def _():
            acc = jnp.dot(
                sel_ref[0, :, :early],
                jnp.concatenate([f0[...], f1[...]], axis=1),
                preferred_element_type=jnp.float32,
            ) + jnp.dot(
                sel_ref[0, :, early:],
                jnp.concatenate([r0[...], r1[...]], axis=1),
                preferred_element_type=jnp.float32,
            )
            for dx in range(2):
                part = acc[:, dx * LANES : (dx + 1) * LANES]
                slot = lax.bitwise_xor(x, dx)

                def weigh(rows, part=part, slot=slot):
                    total = jnp.sum(part * rows.astype(jnp.float32), axis=0, keepdims=True)
                    sum_ref[slot] += total

                @pl.when(pos < first)
                def _():
                    at = pl.multiple_of(pos * BLK, BLK)
                    weigh((f0, f1)[dx][pl.ds(at, BLK), :])

                @pl.when(pos >= first)
                def _():
                    at = pl.multiple_of((pos - first) * BLK, BLK)
                    weigh((r0, r1)[dx][pl.ds(at, BLK), :])

                out_ref[0, slot] = (-part).T.astype(out_ref.dtype)

    front = pl.BlockSpec((early, LANES), lambda d, st: (0, chunk))
    back = pl.BlockSpec((late, LANES), lambda d, st: (0, 0))
    return pl.pallas_call(
        body,
        out_shape=(
            jax.ShapeDtypeStruct((NGRP, 2, LANES, BLK), sel.dtype),
            jax.ShapeDtypeStruct((2, 1, LANES), jnp.float32),
        ),
        grid_spec=pltpu.PrefetchScalarGridSpec(
            num_scalar_prefetch=1,
            grid=(NGRP,),
            in_specs=[
                pl.BlockSpec((1, BLK, early + late), lambda d, st: (d, 0, 0)),
                front,
                front,
                back,
                back,
            ],
            out_specs=[
                pl.BlockSpec((1, 2, LANES, BLK), lambda d, st: (d, 0, 0, 0)),
                pl.BlockSpec((2, 1, LANES), lambda d, st: (0, 0, 0)),
            ],
        ),
        compiler_params=pltpu.CompilerParams(vmem_limit_bytes=32 * 1024 * 1024),
        cost_estimate=pl.CostEstimate(
            flops=2 * NGRP * BLK * (early + late) * 2 * LANES,
            bytes_accessed=2 * (NGRP * BLK + 2 * LANES) * (early + late),
            transcendentals=0,
        ),
        name="products",
    )(structure, sel, *firsts, *rests)


def assemble(messages, chunk, held):
    tall = 4 * LANES
    rows_total = 2 * 2 * NGRP * tall

    def body(*refs):
        msg_refs = refs[:NGRP]
        out, wide_buf, narrow_buf, sem = refs[-4:]
        n = lax.axis_index("narrow")
        w = lax.axis_index("wide")
        copies = []
        for d in range(NGRP):
            source = lax.bitwise_xor(lax.rem(lax.div(w, Y), NGRP), d)
            for xx in range(2):
                slot = 2 * d + xx
                for k in range(2):
                    which = (n != k).astype(jnp.int32)
                    value = msg_refs[d][which, xx].astype(jnp.float32)
                    for lt in range(2):
                        wide_buf[slot, pl.ds(2 * lt + k, LANES, stride=4), :] = value[
                            :, lt * LANES : (lt + 1) * LANES
                        ]
                narrow_buf[slot] = wide_buf[slot].astype(narrow_buf.dtype)
                row = pl.multiple_of(((source * 2 + xx) * 2 + chunk) * tall, tall)
                copy = pltpu.make_async_copy(
                    narrow_buf.at[slot], out.at[pl.ds(row, tall), :], sem.at[slot]
                )
                copy.start()
                copies.append(copy)
        for copy in copies:
            copy.wait()

    extra = () if held is None else (held,)
    return pl.pallas_call(
        body,
        out_shape=jax.ShapeDtypeStruct((rows_total, LANES), messages[0].dtype),
        in_specs=[VMEM] * NGRP + [ANY] * len(extra),
        out_specs=ANY,
        scratch_shapes=[
            pltpu.VMEM((2 * NGRP, tall, LANES), jnp.float32),
            pltpu.VMEM((2 * NGRP, tall, LANES), messages[0].dtype),
            pltpu.SemaphoreType.DMA((2 * NGRP,)),
        ],
        input_output_aliases={NGRP: 0} if extra else {},
        compiler_params=pltpu.CompilerParams(vmem_limit_bytes=16 * 1024 * 1024),
        name="assemble",
    )(*messages, *extra)


def per_device_grid(inverse, panel, factor_inv, structure):
    n = lax.axis_index("narrow")
    w = lax.axis_index("wide")
    zh = lax.div(w, ZH)
    first = structure.shape[1] - panel.shape[1] // BLK
    f_own = pack_first(structure, panel, first)
    other = swap_cores(lax.dynamic_index_in_dim(panel, 1 - n, 0, keepdims=False), "panel_swap")
    r_own = pack_rest(structure, panel, after(other, f_own), first)
    f_z = hop(f_own, ZH, "first_z")
    f_x = hop(f_own, X, "first_x")
    ahead = after(inverse, f_own)
    a_y = hop(ahead, Y, "inv_y")
    a_z = hop(ahead, ZL, "inv_z")
    s_own = swap_cores(after(inverse, *r_own), "inv_swap")
    r_x0 = hop(after(r_own[0], f_x, s_own), X, "rest0_x")
    f_z, r_x0, a_y, a_z = lax.optimization_barrier((f_z, r_x0, a_y, a_z))
    r_z0 = hop(after(r_own[0], f_z), ZH, "rest0_z")
    r_x1 = hop(after(r_own[1], f_z), X, "rest1_x")
    f_xz = hop(f_z, X, "first_xz")
    a_yz = hop(a_z, Y, "inv_yz")
    s_y = swap_cores(a_y, "inv_swap_y")
    r_z0, r_x1, f_xz, a_yz, s_y = lax.optimization_barrier((r_z0, r_x1, f_xz, a_yz, s_y))
    r_z1 = hop(after(r_own[1], r_z0), ZH, "rest1_z")
    r_xz0 = hop(r_z0, X, "rest0_xz")
    s_z = swap_cores(after(a_z, r_z0), "inv_swap_z")
    s_yz = swap_cores(a_yz, "inv_swap_yz")
    owns = [inverse, a_y, a_z, a_yz]
    others = [s_own, s_y, s_z, s_yz]
    linv_part = jnp.sum(jnp.square(factor_inv.astype(jnp.float32)), axis=1)
    sel = pack_inverse(structure, owns, others, first)
    stay = n == zh

    def parts(near, far):
        return jnp.where(stay, near, far), jnp.where(stay, far, near)

    def deliver(near, far, c):
        kept, sent = parts(near, far)
        back = swap_cores(sent, f"cross{c}_swap")
        messages = [jnp.stack([kept[d], back[d]]) for d in range(NGRP)]
        return messages[:1] + [
            hop(messages[d], (d % 2) * Y + (d // 2) * ZL, f"cross{c}_{d}") for d in range(1, NGRP)
        ]

    near, near_sum = products(structure, sel, (f_own, f_x), (r_own[0], r_x0), 0, 0)
    far, far_sum = products(structure, sel, (f_z, f_xz), (r_z0, r_xz0), 0, 1)
    sums = [parts(near_sum, far_sum)]
    messages = deliver(near, far, 0)
    near, near_sum = products(structure, sel, (f_own, f_x), (r_own[1], r_x1), 1, 0)
    r_xz1 = hop(after(r_z1, near), X, "rest1_xz")
    r_xz1, *messages = lax.optimization_barrier((r_xz1, *messages))
    far, far_sum = products(structure, sel, (f_z, f_xz), (r_z1, r_xz1), 1, 1)
    sums.append(parts(near_sum, far_sum))
    held = assemble(messages, 0, None)
    held = assemble(deliver(near, far, 1), 1, held)
    half = panel.shape[2] * lax.axis_size("wide") // 2
    cross = held.reshape(half, 2, 2, LANES).transpose(0, 2, 1, 3).reshape(half, 2, BLK)
    kept, sent = [jnp.concatenate([sums[0][i], sums[1][i]], axis=1).reshape(-1) for i in (0, 1)]
    back = swap_cores(sent, "sums_swap")
    pair = jnp.where(n == 0, jnp.stack([kept, back]), jnp.stack([back, kept]))
    group = lax.rem(lax.div(w, Y), NGRP)
    spots = jnp.arange(NGRP, dtype=jnp.int32)[None, :, None] == group
    placed = jnp.where(spots, pair[:, None, :], 0.0).reshape(2, half)
    variance = linv_part + placed
    for mask in (Y, ZL, X, ZH):
        variance = variance + hop(variance, mask, f"variance_{mask}")
    return cross, variance


def solution(mesh):
    in_specs = (P("wide", "narrow"), P(None, "narrow", "wide"), P(None, "wide", "narrow"), P())
    out_specs = (P("narrow", None, "wide"), P(None, "narrow"))

    def run(inverse, panel, factor_inv, structure):
        fits = (
            mesh.shape["wide"] == 16
            and mesh.shape["narrow"] == 2 == panel.shape[0]
            and panel.shape[2] == 16 * BLK == inverse.shape[0]
        )
        return jax.shard_map(
            per_device_grid if fits else per_device_general,
            mesh=mesh,
            in_specs=in_specs,
            out_specs=out_specs,
            check_vma=False,
        )(inverse, panel, factor_inv, structure)

    return run
```

time: 408 us -> 159 us (0.39)
  Pallas kernels: 256 us -> 21.2 us
  waiting for transfers between devices: 113 us -> 87.5 us
  starting transfers between devices: 29.1 us -> 37.9 us
  local copies, waits for them, and re-layouts: 5.37 us -> 9.77 us
    pallas_call x1, Pallas kernels: 193 us -> 3.37 us  [pack_inverse(): pl.pallas_call(body, out_shape=jax.ShapeDtypeStruct((NGRP, BLK, nblocks *...]
    pallas_call x3 -> x6, Pallas kernels: 61 us -> 15.7 us  [the longest x4 13.3 us: products(): pl.pallas_call(body, out_shape=(jax.ShapeDtypeStruct((NGRP, 2, LANES, BLK...]
    ppermute x19 -> x22, waiting for transfers between devices: 112 us -> 82.2 us  [hop(): return lax.ppermute(value, 'wide', [(i, i ^ mask) for i in range(size)])]
    ppermute x19 -> x22, starting transfers between devices: 27.3 us -> 33.6 us  [hop(): return lax.ppermute(value, 'wide', [(i, i ^ mask) for i in range(size)])]
    ppermute x8, waiting for transfers between devices: 0.56 us -> 5.32 us  [swap_cores(): return lax.ppermute(value, 'narrow', [(0, 1), (1, 0)])]
    unnamed x16 -> x34, local copies, waits for them, and re-layouts: 3.87 us -> 8.18 us
  transfers between devices with their start and end apart: 27 -> 30, of which waited for: 10 -> 18; matrix products, arithmetic and copies ran while one was open for 1% -> 1% of each run, Pallas kernels for 61% -> 10%
where the time goes in v2:
time: 159 us
  waiting for transfers between devices  87.5 us (55%)
  starting transfers between devices  37.9 us (24%)
  Pallas kernels  21.2 us (13%)
  local copies, waits for them, and re-layouts  9.77 us (6%)
    ppermute x22, waiting for transfers between devices, hop(): return lax.ppermute(value, 'wide', [(i, i ^ mask) for i in range(size)])  82.2 us
    ppermute x22, starting transfers between devices, hop(): return lax.ppermute(value, 'wide', [(i, i ^ mask) for i in range(size)])  33.6 us
    pallas_call x4, Pallas kernels, products(): pl.pallas_call(body, out_shape=(jax.ShapeDtypeStruct((NGRP, 2, LANES, BLK...  13.3 us
    unnamed x34, local copies, waits for them, and re-layouts  8.18 us
    ppermute x8, waiting for transfers between devices, swap_cores(): return lax.ppermute(value, 'narrow', [(0, 1), (1, 0)])  5.32 us
    ppermute x8, starting transfers between devices, swap_cores(): return lax.ppermute(value, 'narrow', [(0, 1), (1, 0)])  4.24 us
    pallas_call x1, Pallas kernels, pack_inverse(): pl.pallas_call(body, out_shape=jax.ShapeDtypeStruct((NGRP, BLK, nblocks *...  3.37 us
  transfers between devices with their start and end apart: 30, of which 18 were waited for; matrix products, arithmetic and copies ran while one was open for 1% of the time, Pallas kernels for 10%

profile of v2, /device:TPU:0, one launch (start us, length us, event | category | flops | bytes accessed | tf_op | source)
XLA Modules:
  0.0 158.8 jit_solution(6373553613831120296)
XLA Ops:
  4.9 1.7 %pack_rest.1 = (bf16[2048,128]{1,0:T(8,128)(2,1)S(1)}, bf16[2048,128]{1,0:T(8,128)(2,1)}) custom-call(s32[2,12]{1,0:T(2,128)S(1)} %copy-done.13, bf16[2,2048,256]{2,1,0:T(8,128)(2,1)S(1)} %copy-done, bf16[2048,256]{1,0:T(8,128)(2,1)S(1)} %collective-permute-done.1.other_ref), custom_call_target="tpu_custom_call" | custom-call | flops 20000000000 | tf_op jit(solution)/shard_map/pack_rest/pallas_call | solution.py:158
  7.0 2.6 %collective-permute-start.2 = (bf16[1024,256]{1,0:T(8,128)(2,1)S(1)}, bf16[1024,256]{1,0:T(8,128)(2,1)S(1)}, u32[]{:S(2)}, u32[]{:S(2)}) collective-permute-start(bf16[1024,256]{1,0:T(8,128)(2,1)S(1)} %pack_first.1.f0), channel_id=1, source_target_pairs={{0,2},{2,0},{4,6},{6,4},{8,10},{10,8},{12,14},{14,12},{16,18},{18,... | collective-permute-start | bytes 1572872 | tf_op jit(solution)/shard_map/first_x/ppermute | solution.py:103
  12.8 2.6 %collective-permute-start = (bf16[1024,256]{1,0:T(8,128)(2,1)S(1)}, bf16[1024,256]{1,0:T(8,128)(2,1)S(1)}, u32[]{:S(2)}, u32[]{:S(2)}) collective-permute-start(bf16[1024,256]{1,0:T(8,128)(2,1)S(1)} %pack_first.1.f0), channel_id=1, source_target_pairs={{0,16},{2,18},{4,20},{6,22},{8,24},{10,26},{12,28},{14,30},{16,0},... | collective-permute-start | bytes 1572872 | tf_op jit(solution)/shard_map/first_z/ppermute | solution.py:103
  15.3 6.8 %collective-permute-done.2.f1 = bf16[1024,256]{1,0:T(8,128)(2,1)S(1)} collective-permute-done((bf16[1024,256]{1,0:T(8,128)(2,1)S(1)}, bf16[1024,256]{1,0:T(8,128)(2,1)S(1)}, u32[]{:S(2)}, u32[]{:S(2)}) %collective-permute-start.2) | collective-permute-done | bytes 524320 | tf_op jit(solution)/shard_map/first_x/ppermute | solution.py:103
  22.1 1.7 %collective-permute-start.4 = (bf16[2048,128]{1,0:T(8,128)(2,1)S(1)}, bf16[2048,128]{1,0:T(8,128)(2,1)S(1)}, u32[]{:S(2)}, u32[]{:S(2)}) collective-permute-start(bf16[2048,128]{1,0:T(8,128)(2,1)S(1)} %get-tuple-element.44.r0), channel_id=1, source_target_pairs={{0,2},{2,0},{4,6},{6,4},{8,10},{10,8},{12,14},{14,12},{16,18},{18,... | collective-permute-start | bytes 1572872 | tf_op jit(solution)/shard_map/rest0_x/ppermute | solution.py:103
  23.8 22.5 %collective-permute-done.f0 = bf16[1024,256]{1,0:T(8,128)(2,1)S(1)} collective-permute-done((bf16[1024,256]{1,0:T(8,128)(2,1)S(1)}, bf16[1024,256]{1,0:T(8,128)(2,1)S(1)}, u32[]{:S(2)}, u32[]{:S(2)}) %collective-permute-start) | collective-permute-done | bytes 524320 | tf_op jit(solution)/shard_map/first_z/ppermute | solution.py:103
  50.0 2.5 %collective-permute-start.7 = (bf16[2048,128]{1,0:T(8,128)(2,1)S(1)}, bf16[2048,128]{1,0:T(8,128)(2,1)}, u32[]{:S(2)}, u32[]{:S(2)}) collective-permute-start(bf16[2048,128]{1,0:T(8,128)(2,1)S(1)} %get-tuple-element.44.r0), channel_id=1, source_target_pairs={{0,16},{2,18},{4,20},{6,22},{8,24},{10,26},{12,28},{14,30},{16,0},... | collective-permute-start | bytes 1572872 | tf_op jit(solution)/shard_map/rest0_z/ppermute | solution.py:103
  54.9 9.7 %collective-permute-done.8.r1 = bf16[2048,128]{1,0:T(8,128)(2,1)S(1)} collective-permute-done((bf16[2048,128]{1,0:T(8,128)(2,1)}, bf16[2048,128]{1,0:T(8,128)(2,1)S(1)}, u32[]{:S(2)}, u32[]{:S(2)}) %collective-permute-start.8) | collective-permute-done | bytes 524320 | tf_op jit(solution)/shard_map/rest1_x/ppermute | solution.py:103
  65.4 10.9 %collective-permute-done.7.r0 = bf16[2048,128]{1,0:T(8,128)(2,1)} collective-permute-done((bf16[2048,128]{1,0:T(8,128)(2,1)S(1)}, bf16[2048,128]{1,0:T(8,128)(2,1)}, u32[]{:S(2)}, u32[]{:S(2)}) %collective-permute-start.7) | collective-permute-done | bytes 524320 | tf_op jit(solution)/shard_map/rest0_z/ppermute | solution.py:103
  77.8 1.7 %collective-permute-start.16 = (bf16[2048,128]{1,0:T(8,128)(2,1)}, bf16[2048,128]{1,0:T(8,128)(2,1)}, u32[]{:S(2)}, u32[]{:S(2)}) collective-permute-start(bf16[2048,128]{1,0:T(8,128)(2,1)} %collective-permute-done.7.r0), channel_id=1, source_target_pairs={{0,2},{2,0},{4,6},{6,4},{8,10},{10,8},{12,14},{14,12},{16,18},{18,... | collective-permute-start | bytes 1572872 | tf_op jit(solution)/shard_map/rest0_xz/ppermute | solution.py:103
  85.5 3.4 %pack_inverse.1.sel_ref = bf16[4,256,3072]{2,1,0:T(8,128)(2,1)S(1)} custom-call(s32[2,12]{1,0:T(2,128)S(1)} %copy-done.13, bf16[256,2048]{1,0:T(8,128)(2,1)S(1)} %copy-done.2, bf16[256,2048]{1,0:T(8,128)(2,1)S(1)} %copy-done.4, bf16[256,2048]{1,0:T(8,128)(2,1)} %collective-permute-done.6.refs_2_, bf16[256,2048]{1,0:T(8,128)(2,1)} %collective-permute-done.10.refs_3_, ...), custom_call_target="tpu_custom_call" | custom-call | tf_op jit(solution)/shard_map/pack_inverse/pallas_call | solution.py:189
  88.9 2.8 %products.5 = (bf16[4,2,128,256]{3,2,1,0:T(8,128)(2,1)S(1)}, f32[2,1,128]{2,1,0:T(1,128)S(1)}) custom-call(s32[2,12]{1,0:T(2,128)S(1)} %copy-done.13, bf16[4,256,3072]{2,1,0:T(8,128)(2,1)S(1)} %pack_inverse.1.sel_ref, bf16[1024,256]{1,0:T(8,128)(2,1)S(1)} %pack_first.1.f0, bf16[1024,256]{1,0:T(8,128)(2,1)S(1)} %collective-permute-done.2.f1, ...), custom_call_target="tpu_custom_call" | custom-call | flops 1610612736 | bytes 7864320 | tf_op jit(solution)/shard_map/products/pallas_call | solution.py:260
  92.0 3.9 %products.6 = (bf16[4,2,128,256]{3,2,1,0:T(8,128)(2,1)S(1)}, f32[2,1,128]{2,1,0:T(1,128)S(1)}) custom-call(s32[2,12]{1,0:T(2,128)S(1)} %copy-done.13, bf16[4,256,3072]{2,1,0:T(8,128)(2,1)S(1)} %pack_inverse.1.sel_ref, bf16[1024,256]{1,0:T(8,128)(2,1)S(1)} %collective-permute-done.f0, bf16[1024,256]{1,0:T(8,128)(2,1)S(1)} %collective-permute-done.9.f1, ...), custom_call_target="tpu_custom_call" | custom-call | flops 1610612736 | bytes 7864320 | tf_op jit(solution)/shard_map/products/pallas_call | solution.py:260
  96.0 1.9 %collective-permute-start.17 = (bf16[4,2,128,256]{3,2,1,0:T(8,128)(2,1)S(1)}, bf16[4,2,128,256]{3,2,1,0:T(8,128)(2,1)S(1)}, u32[]{:S(2)}, u32[]{:S(2)}) collective-permute-start(bf16[4,2,128,256]{3,2,1,0:T(8,128)(2,1)S(1)} %get-tuple-element.71), channel_id=1, source_target_pairs={{0,1},{1,0},{2,3},{3,2},{4,5},{5,4},{6,7},{7,6},{8,9},{9,8},{10,11... | collective-permute-start | bytes 1572872 | tf_op jit(solution)/shard_map/cross0_swap/ppermute | solution.py:97
  98.4 3.8 %products.4 = (bf16[4,2,128,256]{3,2,1,0:T(8,128)(2,1)S(1)}, f32[2,1,128]{2,1,0:T(1,128)S(1)}) custom-call(s32[2,12]{1,0:T(2,128)S(1)} %copy-done.13, bf16[4,256,3072]{2,1,0:T(8,128)(2,1)S(1)} %pack_inverse.1.sel_ref, bf16[1024,256]{1,0:T(8,128)(2,1)S(1)} %pack_first.1.f0, bf16[1024,256]{1,0:T(8,128)(2,1)S(1)} %collective-permute-done.2.f1, ...), custom_call_target="tpu_custom_call" | custom-call | flops 1610612736 | bytes 7864320 | tf_op jit(solution)/shard_map/products/pallas_call | solution.py:260
  102.2 3.3 %collective-permute-done.14.r0 = bf16[2048,128]{1,0:T(8,128)(2,1)S(1)} collective-permute-done((bf16[2048,128]{1,0:T(8,128)(2,1)}, bf16[2048,128]{1,0:T(8,128)(2,1)S(1)}, u32[]{:S(2)}, u32[]{:S(2)}) %collective-permute-start.14) | collective-permute-done | bytes 524320 | tf_op jit(solution)/shard_map/rest1_z/ppermute | solution.py:103
  107.6 1.7 %collective-permute-start.19 = (bf16[2,2,128,256]{3,2,1,0:T(8,128)(2,1)S(1)}, bf16[2,2,128,256]{3,2,1,0:T(8,128)(2,1)S(1)}, u32[]{:S(2)}, u32[]{:S(2)}) collective-permute-start(bf16[2,2,128,256]{3,2,1,0:T(8,128)(2,1)S(1)} %pad_maximum_fusion.2), channel_id=1, source_target_pairs={{0,8},{2,10},{4,12},{6,14},{8,0},{10,2},{12,4},{14,6},{16,24},{18,... | collective-permute-start | bytes 786440 | tf_op jit(solution)/shard_map/cross0_2/ppermute | solution.py:103
  109.8 8.8 %collective-permute-done.15.r1 = bf16[2048,128]{1,0:T(8,128)(2,1)S(1)} collective-permute-done((bf16[2048,128]{1,0:T(8,128)(2,1)S(1)}, bf16[2048,128]{1,0:T(8,128)(2,1)S(1)}, u32[]{:S(2)}, u32[]{:S(2)}) %collective-permute-start.15) | collective-permute-done | bytes 524320 | tf_op jit(solution)/shard_map/rest1_xz/ppermute | solution.py:103
  118.6 2.4 %collective-permute-done.19.refs_2_ = bf16[2,2,128,256]{3,2,1,0:T(8,128)(2,1)S(1)} collective-permute-done((bf16[2,2,128,256]{3,2,1,0:T(8,128)(2,1)S(1)}, bf16[2,2,128,256]{3,2,1,0:T(8,128)(2,1)S(1)}, u32[]{:S(2)}, u32[]{:S(2)}) %collective-permute-start.19) | collective-permute-done | bytes 262176 | tf_op jit(solution)/shard_map/cross0_2/ppermute | solution.py:103
  121.0 2.8 %products.7 = (bf16[4,2,128,256]{3,2,1,0:T(8,128)(2,1)S(1)}, f32[2,1,128]{2,1,0:T(1,128)S(1)}) custom-call(s32[2,12]{1,0:T(2,128)S(1)} %copy-done.13, bf16[4,256,3072]{2,1,0:T(8,128)(2,1)S(1)} %pack_inverse.1.sel_ref, bf16[1024,256]{1,0:T(8,128)(2,1)S(1)} %collective-permute-done.f0, bf16[1024,256]{1,0:T(8,128)(2,1)S(1)} %collective-permute-done.9.f1, ...), custom_call_target="tpu_custom_call" | custom-call | flops 1610612736 | bytes 7864320 | tf_op jit(solution)/shard_map/products/pallas_call | solution.py:260
  132.2 9.9 %collective-permute-done.26 = f32[2,2048]{1,0:T(2,128)S(1)} collective-permute-done((f32[2,2048]{1,0:T(2,128)S(1)}, f32[2,2048]{1,0:T(2,128)S(1)}, u32[]{:S(2)}, u32[]{:S(2)}) %collective-permute-start.26) | collective-permute-done | bytes 16416 | tf_op jit(solution)/shard_map/variance_2/ppermute | solution.py:103
  142.7 3.2 %collective-permute-done.27 = f32[2,2048]{1,0:T(2,128)S(1)} collective-permute-done((f32[2,2048]{1,0:T(2,128)S(1)}, f32[2,2048]{1,0:T(2,128)S(1)}, u32[]{:S(2)}, u32[]{:S(2)}) %collective-permute-start.27) | collective-permute-done | bytes 16416 | tf_op jit(solution)/shard_map/variance_4/ppermute | solution.py:103
  147.0 2.7 %collective-permute-done.28 = f32[2,2048]{1,0:T(2,128)S(1)} collective-permute-done((f32[2,2048]{1,0:T(2,128)S(1)}, f32[2,2048]{1,0:T(2,128)S(1)}, u32[]{:S(2)}, u32[]{:S(2)}) %collective-permute-start.28) | collective-permute-done | bytes 16416 | tf_op jit(solution)/shard_map/variance_1/ppermute | solution.py:103
  149.8 5.6 %collective-permute-start.29 = (f32[2,2048]{1,0:T(2,128)S(1)}, f32[2,2048]{1,0:T(2,128)S(1)}, u32[]{:S(2)}, u32[]{:S(2)}) collective-permute-start(f32[2,2048]{1,0:T(2,128)S(1)} %add.24), channel_id=1, source_target_pairs={{0,16},{2,18},{4,20},{6,22},{8,24},{10,26},{12,28},{14,30},{16,0},... | collective-permute-start | bytes 49160 | tf_op jit(solution)/shard_map/variance_8/ppermute | solution.py:103
  (106 shorter events, 38.8 us)
Async XLA Ops:
  6.6 15.5 %collective-permute-start.3 = (bf16[256,2048]{1,0:T(8,128)(2,1)S(1)}, bf16[256,2048]{1,0:T(8,128)(2,1)S(1)}, u32[]{:S(2)}, u32[]{:S(2)}) collective-permute-start(bf16[256,2048]{1,0:T(8,128)(2,1)S(1)} %copy-done.1), channel_id=1, source_target_pairs={{0,1},{1,0},{2,3},{3,2},{4,5},{5,4},{6,7},{7,6},{8,9},{9,8},{10,11... | collective-permute-start | bytes 3145736 | tf_op jit(solution)/shard_map/inv_swap/ppermute | solution.py:97
  7.0 15.1 %collective-permute-start.2 = (bf16[1024,256]{1,0:T(8,128)(2,1)S(1)}, bf16[1024,256]{1,0:T(8,128)(2,1)S(1)}, u32[]{:S(2)}, u32[]{:S(2)}) collective-permute-start(bf16[1024,256]{1,0:T(8,128)(2,1)S(1)} %pack_first.1.f0), channel_id=1, source_target_pairs={{0,2},{2,0},{4,6},{6,4},{8,10},{10,8},{12,14},{14,12},{16,18},{18,... | collective-permute-start | bytes 1572872 | tf_op jit(solution)/shard_map/first_x/ppermute | solution.py:103
  9.7 36.7 %collective-permute-start.5 = (bf16[256,2048]{1,0:T(8,128)(2,1)S(1)}, bf16[256,2048]{1,0:T(8,128)(2,1)S(1)}, u32[]{:S(2)}, u32[]{:S(2)}) collective-permute-start(bf16[256,2048]{1,0:T(8,128)(2,1)S(1)} %copy-done.1), channel_id=1, source_target_pairs={{0,4},{2,6},{4,0},{6,2},{8,12},{10,14},{12,8},{14,10},{16,20},{18,... | collective-permute-start | bytes 3145736 | tf_op jit(solution)/shard_map/inv_y/ppermute | solution.py:103
  11.2 36.2 %collective-permute-start.6 = (bf16[256,2048]{1,0:T(8,128)(2,1)S(1)}, bf16[256,2048]{1,0:T(8,128)(2,1)}, u32[]{:S(2)}, u32[]{:S(2)}) collective-permute-start(bf16[256,2048]{1,0:T(8,128)(2,1)S(1)} %copy-done.1), channel_id=1, source_target_pairs={{0,8},{2,10},{4,12},{6,14},{8,0},{10,2},{12,4},{14,6},{16,24},{18,... | collective-permute-start | bytes 3145736 | tf_op jit(solution)/shard_map/inv_z/ppermute | solution.py:103
  12.8 33.6 %collective-permute-start = (bf16[1024,256]{1,0:T(8,128)(2,1)S(1)}, bf16[1024,256]{1,0:T(8,128)(2,1)S(1)}, u32[]{:S(2)}, u32[]{:S(2)}) collective-permute-start(bf16[1024,256]{1,0:T(8,128)(2,1)S(1)} %pack_first.1.f0), channel_id=1, source_target_pairs={{0,16},{2,18},{4,20},{6,22},{8,24},{10,26},{12,28},{14,30},{16,0},... | collective-permute-start | bytes 1572872 | tf_op jit(solution)/shard_map/first_z/ppermute | solution.py:103
  22.1 25.3 %collective-permute-start.4 = (bf16[2048,128]{1,0:T(8,128)(2,1)S(1)}, bf16[2048,128]{1,0:T(8,128)(2,1)S(1)}, u32[]{:S(2)}, u32[]{:S(2)}) collective-permute-start(bf16[2048,128]{1,0:T(8,128)(2,1)S(1)} %get-tuple-element.44.r0), channel_id=1, source_target_pairs={{0,2},{2,0},{4,6},{6,4},{8,10},{10,8},{12,14},{14,12},{16,18},{18,... | collective-permute-start | bytes 1572872 | tf_op jit(solution)/shard_map/rest0_x/ppermute | solution.py:103
  48.2 28.2 %collective-permute-start.10 = (bf16[256,2048]{1,0:T(8,128)(2,1)}, bf16[256,2048]{1,0:T(8,128)(2,1)}, u32[]{:S(2)}, u32[]{:S(2)}) collective-permute-start(bf16[256,2048]{1,0:T(8,128)(2,1)} %collective-permute-done.6.refs_2_), channel_id=1, source_target_pairs={{0,4},{2,6},{4,0},{6,2},{8,12},{10,14},{12,8},{14,10},{16,20},{18,... | collective-permute-start | bytes 3145736 | tf_op jit(solution)/shard_map/inv_yz/ppermute | solution.py:103
  48.7 27.6 %collective-permute-start.11 = (bf16[256,2048]{1,0:T(8,128)(2,1)S(1)}, bf16[256,2048]{1,0:T(8,128)(2,1)S(1)}, u32[]{:S(2)}, u32[]{:S(2)}) collective-permute-start(bf16[256,2048]{1,0:T(8,128)(2,1)S(1)} %collective-permute-done.5.refs_1_), channel_id=1, source_target_pairs={{0,1},{1,0},{2,3},{3,2},{4,5},{5,4},{6,7},{7,6},{8,9},{9,8},{10,11... | collective-permute-start | bytes 3145736 | tf_op jit(solution)/shard_map/inv_swap_y/ppermute | solution.py:97
  49.7 14.9 %collective-permute-start.8 = (bf16[2048,128]{1,0:T(8,128)(2,1)}, bf16[2048,128]{1,0:T(8,128)(2,1)S(1)}, u32[]{:S(2)}, u32[]{:S(2)}) collective-permute-start(bf16[2048,128]{1,0:T(8,128)(2,1)} %get-tuple-element.53.r0), channel_id=1, source_target_pairs={{0,2},{2,0},{4,6},{6,4},{8,10},{10,8},{12,14},{14,12},{16,18},{18,... | collective-permute-start | bytes 1572872 | tf_op jit(solution)/shard_map/rest1_x/ppermute | solution.py:103
  50.0 26.3 %collective-permute-start.7 = (bf16[2048,128]{1,0:T(8,128)(2,1)S(1)}, bf16[2048,128]{1,0:T(8,128)(2,1)}, u32[]{:S(2)}, u32[]{:S(2)}) collective-permute-start(bf16[2048,128]{1,0:T(8,128)(2,1)S(1)} %get-tuple-element.44.r0), channel_id=1, source_target_pairs={{0,16},{2,18},{4,20},{6,22},{8,24},{10,26},{12,28},{14,30},{16,0},... | collective-permute-start | bytes 1572872 | tf_op jit(solution)/shard_map/rest0_z/ppermute | solution.py:103
  53.4 22.9 %collective-permute-start.9 = (bf16[1024,256]{1,0:T(8,128)(2,1)S(1)}, bf16[1024,256]{1,0:T(8,128)(2,1)S(1)}, u32[]{:S(2)}, u32[]{:S(2)}) collective-permute-start(bf16[1024,256]{1,0:T(8,128)(2,1)S(1)} %collective-permute-done.f0), channel_id=1, source_target_pairs={{0,2},{2,0},{4,6},{6,4},{8,10},{10,8},{12,14},{14,12},{16,18},{18,... | collective-permute-start | bytes 1572872 | tf_op jit(solution)/shard_map/first_xz/ppermute | solution.py:103
  77.3 4.5 %collective-permute-start.13 = (bf16[256,2048]{1,0:T(8,128)(2,1)}, bf16[256,2048]{1,0:T(8,128)(2,1)}, u32[]{:S(2)}, u32[]{:S(2)}) collective-permute-start(bf16[256,2048]{1,0:T(8,128)(2,1)} %collective-permute-done.10.refs_3_), channel_id=1, source_target_pairs={{0,1},{1,0},{2,3},{3,2},{4,5},{5,4},{6,7},{7,6},{8,9},{9,8},{10,11... | collective-permute-start | bytes 3145736 | tf_op jit(solution)/shard_map/inv_swap_yz/ppermute | solution.py:97
  77.8 14.1 %collective-permute-start.16 = (bf16[2048,128]{1,0:T(8,128)(2,1)}, bf16[2048,128]{1,0:T(8,128)(2,1)}, u32[]{:S(2)}, u32[]{:S(2)}) collective-permute-start(bf16[2048,128]{1,0:T(8,128)(2,1)} %collective-permute-done.7.r0), channel_id=1, source_target_pairs={{0,2},{2,0},{4,6},{6,4},{8,10},{10,8},{12,14},{14,12},{16,18},{18,... | collective-permute-start | bytes 1572872 | tf_op jit(solution)/shard_map/rest0_xz/ppermute | solution.py:103
  79.6 25.9 %collective-permute-start.14 = (bf16[2048,128]{1,0:T(8,128)(2,1)}, bf16[2048,128]{1,0:T(8,128)(2,1)S(1)}, u32[]{:S(2)}, u32[]{:S(2)}) collective-permute-start(bf16[2048,128]{1,0:T(8,128)(2,1)} %get-tuple-element.53.r0), channel_id=1, source_target_pairs={{0,16},{2,18},{4,20},{6,22},{8,24},{10,26},{12,28},{14,30},{16,0},... | collective-permute-start | bytes 1572872 | tf_op jit(solution)/shard_map/rest1_z/ppermute | solution.py:103
  96.0 9.9 %collective-permute-start.17 = (bf16[4,2,128,256]{3,2,1,0:T(8,128)(2,1)S(1)}, bf16[4,2,128,256]{3,2,1,0:T(8,128)(2,1)S(1)}, u32[]{:S(2)}, u32[]{:S(2)}) collective-permute-start(bf16[4,2,128,256]{3,2,1,0:T(8,128)(2,1)S(1)} %get-tuple-element.71), channel_id=1, source_target_pairs={{0,1},{1,0},{2,3},{3,2},{4,5},{5,4},{6,7},{7,6},{8,9},{9,8},{10,11... | collective-permute-start | bytes 1572872 | tf_op jit(solution)/shard_map/cross0_swap/ppermute | solution.py:97
  105.5 13.1 %collective-permute-start.15 = (bf16[2048,128]{1,0:T(8,128)(2,1)S(1)}, bf16[2048,128]{1,0:T(8,128)(2,1)S(1)}, u32[]{:S(2)}, u32[]{:S(2)}) collective-permute-start(bf16[2048,128]{1,0:T(8,128)(2,1)S(1)} %collective-permute-done.14.r0), channel_id=1, source_target_pairs={{0,2},{2,0},{4,6},{6,4},{8,10},{10,8},{12,14},{14,12},{16,18},{18,... | collective-permute-start | bytes 1572872 | tf_op jit(solution)/shard_map/rest1_xz/ppermute | solution.py:103
  106.0 12.6 %collective-permute-start.20 = (bf16[2,2,128,256]{3,2,1,0:T(8,128)(2,1)S(1)}, bf16[2,2,128,256]{3,2,1,0:T(8,128)(2,1)S(1)}, u32[]{:S(2)}, u32[]{:S(2)}) collective-permute-start(bf16[2,2,128,256]{3,2,1,0:T(8,128)(2,1)S(1)} %pad_maximum_fusion.3), channel_id=1, source_target_pairs={{0,12},{2,14},{4,8},{6,10},{8,4},{10,6},{12,0},{14,2},{16,28},{18,... | collective-permute-start | bytes 786440 | tf_op jit(solution)/shard_map/cross0_3/ppermute | solution.py:103
  107.6 13.4 %collective-permute-start.19 = (bf16[2,2,128,256]{3,2,1,0:T(8,128)(2,1)S(1)}, bf16[2,2,128,256]{3,2,1,0:T(8,128)(2,1)S(1)}, u32[]{:S(2)}, u32[]{:S(2)}) collective-permute-start(bf16[2,2,128,256]{3,2,1,0:T(8,128)(2,1)S(1)} %pad_maximum_fusion.2), channel_id=1, source_target_pairs={{0,8},{2,10},{4,12},{6,14},{8,0},{10,2},{12,4},{14,6},{16,24},{18,... | collective-permute-start | bytes 786440 | tf_op jit(solution)/shard_map/cross0_2/ppermute | solution.py:103
  109.3 11.7 %collective-permute-start.18 = (bf16[2,2,128,256]{3,2,1,0:T(8,128)(2,1)S(1)}, bf16[2,2,128,256]{3,2,1,0:T(8,128)(2,1)S(1)}, u32[]{:S(2)}, u32[]{:S(2)}) collective-permute-start(bf16[2,2,128,256]{3,2,1,0:T(8,128)(2,1)S(1)} %pad_maximum_fusion.1), channel_id=1, source_target_pairs={{0,4},{2,6},{4,0},{6,2},{8,12},{10,14},{12,8},{14,10},{16,20},{18,... | collective-permute-start | bytes 786440 | tf_op jit(solution)/shard_map/cross0_1/ppermute | solution.py:103
  126.8 30.9 %collective-permute-start.24 = (bf16[2,2,128,256]{3,2,1,0:T(8,128)(2,1)S(1)}, bf16[2,2,128,256]{3,2,1,0:T(8,128)(2,1)S(1)}, u32[]{:S(2)}, u32[]{:S(2)}) collective-permute-start(bf16[2,2,128,256]{3,2,1,0:T(8,128)(2,1)S(1)} %pad_maximum_fusion.7), channel_id=1, source_target_pairs={{0,12},{2,14},{4,8},{6,10},{8,4},{10,6},{12,0},{14,2},{16,28},{18,... | collective-permute-start | bytes 786440 | tf_op jit(solution)/shard_map/cross1_3/ppermute | solution.py:103
  128.3 29.4 %collective-permute-start.23 = (bf16[2,2,128,256]{3,2,1,0:T(8,128)(2,1)S(1)}, bf16[2,2,128,256]{3,2,1,0:T(8,128)(2,1)S(1)}, u32[]{:S(2)}, u32[]{:S(2)}) collective-permute-start(bf16[2,2,128,256]{3,2,1,0:T(8,128)(2,1)S(1)} %pad_maximum_fusion.6), channel_id=1, source_target_pairs={{0,8},{2,10},{4,12},{6,14},{8,0},{10,2},{12,4},{14,6},{16,24},{18,... | collective-permute-start | bytes 786440 | tf_op jit(solution)/shard_map/cross1_2/ppermute | solution.py:103
  130.0 27.7 %collective-permute-start.22 = (bf16[2,2,128,256]{3,2,1,0:T(8,128)(2,1)S(1)}, bf16[2,2,128,256]{3,2,1,0:T(8,128)(2,1)S(1)}, u32[]{:S(2)}, u32[]{:S(2)}) collective-permute-start(bf16[2,2,128,256]{3,2,1,0:T(8,128)(2,1)S(1)} %pad_maximum_fusion.5), channel_id=1, source_target_pairs={{0,4},{2,6},{4,0},{6,2},{8,12},{10,14},{12,8},{14,10},{16,20},{18,... | collective-permute-start | bytes 786440 | tf_op jit(solution)/shard_map/cross1_1/ppermute | solution.py:103
  130.6 11.5 %collective-permute-start.26 = (f32[2,2048]{1,0:T(2,128)S(1)}, f32[2,2048]{1,0:T(2,128)S(1)}, u32[]{:S(2)}, u32[]{:S(2)}) collective-permute-start(f32[2,2048]{1,0:T(2,128)S(1)} %select_add_fusion), channel_id=1, source_target_pairs={{0,4},{2,6},{4,0},{6,2},{8,12},{10,14},{12,8},{14,10},{16,20},{18,... | collective-permute-start | bytes 49160 | tf_op jit(solution)/shard_map/variance_2/ppermute | solution.py:103
  149.8 7.3 %collective-permute-start.29 = (f32[2,2048]{1,0:T(2,128)S(1)}, f32[2,2048]{1,0:T(2,128)S(1)}, u32[]{:S(2)}, u32[]{:S(2)}) collective-permute-start(f32[2,2048]{1,0:T(2,128)S(1)} %add.24), channel_id=1, source_target_pairs={{0,16},{2,18},{4,20},{6,22},{8,24},{10,26},{12,28},{14,30},{16,0},... | collective-permute-start | bytes 49160 | tf_op jit(solution)/shard_map/variance_8/ppermute | solution.py:103
  (21 other events, 43.7 us)

commit v3 on v2

--- a/solution.py
+++ b/solution.py
@@ -90,6 +90,7 @@
 
 X, Y, ZL, ZH = 1, 2, 4, 8
 NGRP = 4
+SPLIT = 192
 
 
 def swap_cores(value, name):
@@ -127,7 +128,7 @@
         out_shape=jax.ShapeDtypeStruct((first * BLK, panel.shape[2]), panel.dtype),
         in_specs=[SMEM, VMEM],
         out_specs=VMEM,
-        compiler_params=pltpu.CompilerParams(vmem_limit_bytes=16 * 1024 * 1024),
+        compiler_params=pltpu.CompilerParams(vmem_limit_bytes=6 * 1024 * 1024),
         name="pack_first",
     )(structure, panel)
 
@@ -160,8 +161,7 @@
         out_shape=(shape, shape),
         in_specs=[SMEM, VMEM, VMEM],
         out_specs=[VMEM, VMEM],
-        compiler_params=pltpu.CompilerParams(vmem_limit_bytes=16 * 1024 * 1024),
-        cost_estimate=pl.CostEstimate(flops=2 * 10**10, bytes_accessed=0, transcendentals=0),
+        compiler_params=pltpu.CompilerParams(vmem_limit_bytes=8 * 1024 * 1024),
         name="pack_rest",
     )(structure, panel, other)
 
@@ -169,10 +169,10 @@
 def pack_inverse(structure, owns, others, first):
     nblocks = structure.shape[1]
     half_blocks = owns[0].shape[1] // BLK
+    count = len(owns)
 
     def body(st, *refs):
-        own_refs, oth_refs = refs[:NGRP], refs[NGRP : 2 * NGRP]
-        out = refs[2 * NGRP]
+        own_refs, oth_refs, out = refs[:count], refs[count : 2 * count], refs[2 * count]
         n = lax.axis_index("narrow")
         for j in range(nblocks):
             b = pick(st, n, j, first)
@@ -180,8 +180,11 @@
             mine = lax.div(b, half_blocks) == n
 
             def move(sources, j=j, col=col):
-                for d in range(NGRP):
-                    out[d, :, j * BLK : (j + 1) * BLK] = sources[d][:, pl.ds(col, BLK)]
+                d = 0
+                for source in sources:
+                    for at in range(0, source.shape[0], BLK):
+                        out[d, :, j * BLK : (j + 1) * BLK] = source[at : at + BLK, pl.ds(col, BLK)]
+                        d += 1
 
             pl.when(mine)(lambda move=move: move(own_refs))
             pl.when(jnp.logical_not(mine))(lambda move=move: move(oth_refs))
@@ -189,9 +192,9 @@
     return pl.pallas_call(
         body,
         out_shape=jax.ShapeDtypeStruct((NGRP, BLK, nblocks * BLK), owns[0].dtype),
-        in_specs=[SMEM] + [VMEM] * (2 * NGRP),
+        in_specs=[SMEM] + [VMEM] * (2 * count),
         out_specs=VMEM,
-        compiler_params=pltpu.CompilerParams(vmem_limit_bytes=32 * 1024 * 1024),
+        compiler_params=pltpu.CompilerParams(vmem_limit_bytes=20 * 1024 * 1024),
         name="pack_inverse",
     )(structure, *owns, *others)
 
@@ -278,12 +281,8 @@
                 pl.BlockSpec((2, 1, LANES), lambda d, st: (0, 0, 0)),
             ],
         ),
-        compiler_params=pltpu.CompilerParams(vmem_limit_bytes=32 * 1024 * 1024),
-        cost_estimate=pl.CostEstimate(
-            flops=2 * NGRP * BLK * (early + late) * 2 * LANES,
-            bytes_accessed=2 * (NGRP * BLK + 2 * LANES) * (early + late),
-            transcendentals=0,
-        ),
+        compiler_params=pltpu.CompilerParams(vmem_limit_bytes=16 * 1024 * 1024),
+        cost_estimate=pl.CostEstimate(flops=0, bytes_accessed=0, transcendentals=0),
         name="products",
     )(structure, sel, *firsts, *rests)
 
@@ -342,28 +341,33 @@
     zh = lax.div(w, ZH)
     first = structure.shape[1] - panel.shape[1] // BLK
     f_own = pack_first(structure, panel, first)
-    other = swap_cores(lax.dynamic_index_in_dim(panel, 1 - n, 0, keepdims=False), "panel_swap")
-    r_own = pack_rest(structure, panel, after(other, f_own), first)
+    other = swap_cores(
+        lax.dynamic_index_in_dim(after(panel, f_own), 1 - n, 0, keepdims=False), "panel_swap"
+    )
+    r_own = pack_rest(structure, panel, other, first)
     f_z = hop(f_own, ZH, "first_z")
     f_x = hop(f_own, X, "first_x")
     ahead = after(inverse, f_own)
+    top, bottom = ahead[:SPLIT], ahead[SPLIT:]
     a_y = hop(ahead, Y, "inv_y")
-    a_z = hop(ahead, ZL, "inv_z")
-    s_own = swap_cores(after(inverse, *r_own), "inv_swap")
-    r_x0 = hop(after(r_own[0], f_x, s_own), X, "rest0_x")
-    f_z, r_x0, a_y, a_z = lax.optimization_barrier((f_z, r_x0, a_y, a_z))
-    r_z0 = hop(after(r_own[0], f_z), ZH, "rest0_z")
-    r_x1 = hop(after(r_own[1], f_z), X, "rest1_x")
+    a_z0 = hop(top, ZL, "inv_z0")
+    s_own = swap_cores(after(inverse, other), "inv_swap")
+    f_z, f_x, a_y, a_z0, s_own, *r_own = lax.optimization_barrier(
+        (f_z, f_x, a_y, a_z0, s_own, *r_own)
+    )
+    r_z0 = hop(r_own[0], ZH, "rest0_z")
+    a_z1 = hop(after(bottom, f_z), ZL, "inv_z1")
     f_xz = hop(f_z, X, "first_xz")
-    a_yz = hop(a_z, Y, "inv_yz")
-    s_y = swap_cores(a_y, "inv_swap_y")
-    r_z0, r_x1, f_xz, a_yz, s_y = lax.optimization_barrier((r_z0, r_x1, f_xz, a_yz, s_y))
+    a_yz0 = hop(a_z0, Y, "inv_yz0")
+    a_yz1 = hop(a_z1, Y, "inv_yz1")
+    r_x0 = hop(after(r_own[0], f_z), X, "rest0_x")
+    r_z0, f_xz, a_yz0, a_yz1, r_x0 = lax.optimization_barrier((r_z0, f_xz, a_yz0, a_yz1, r_x0))
     r_z1 = hop(after(r_own[1], r_z0), ZH, "rest1_z")
     r_xz0 = hop(r_z0, X, "rest0_xz")
-    s_z = swap_cores(after(a_z, r_z0), "inv_swap_z")
-    s_yz = swap_cores(a_yz, "inv_swap_yz")
-    owns = [inverse, a_y, a_z, a_yz]
-    others = [s_own, s_y, s_z, s_yz]
+    more = jnp.concatenate([after(a_y, r_z0), a_z0, a_z1, a_yz0, a_yz1])
+    s_more = swap_cores(more, "inv_swap_more")
+    owns = [inverse, more]
+    others = [s_own, s_more]
     linv_part = jnp.sum(jnp.square(factor_inv.astype(jnp.float32)), axis=1)
     sel = pack_inverse(structure, owns, others, first)
     stay = n == zh
@@ -383,8 +387,9 @@
     far, far_sum = products(structure, sel, (f_z, f_xz), (r_z0, r_xz0), 0, 1)
     sums = [parts(near_sum, far_sum)]
     messages = deliver(near, far, 0)
+    r_x1 = hop(after(r_own[1], sel), X, "rest1_x")
     near, near_sum = products(structure, sel, (f_own, f_x), (r_own[1], r_x1), 1, 0)
-    r_xz1 = hop(after(r_z1, near), X, "rest1_xz")
+    r_xz1 = hop(r_z1, X, "rest1_xz")
     r_xz1, *messages = lax.optimization_barrier((r_xz1, *messages))
     far, far_sum = products(structure, sel, (f_z, f_xz), (r_z1, r_xz1), 1, 1)
     sums.append(parts(near_sum, far_sum))
@@ -399,7 +404,7 @@
     spots = jnp.arange(NGRP, dtype=jnp.int32)[None, :, None] == group
     placed = jnp.where(spots, pair[:, None, :], 0.0).reshape(2, half)
     variance = linv_part + placed
-    for mask in (Y, ZL, X, ZH):
+    for mask in (X, ZH, Y, ZL):
         variance = variance + hop(variance, mask, f"variance_{mask}")
     return cross, variance
 

time: 159 us -> 165 us (1.038)
  local copies, waits for them, and re-layouts: 9.77 us -> 17.4 us
  waiting for transfers between devices: 87.5 us -> 81 us
  other arithmetic: 1.52 us -> 3.98 us
  Pallas kernels: 21.2 us -> 23.6 us
    ppermute x22 -> x24, waiting for transfers between devices: 82.2 us -> 75.3 us  [hop(): return lax.ppermute(value, 'wide', [(i, i ^ mask) for i in range(size)])]
    unnamed x34 -> x58, local copies, waits for them, and re-layouts: 8.18 us -> 13.9 us
    pallas_call x4, Pallas kernels: 13.3 us -> 16.6 us  [products(): pl.pallas_call(body, out_shape=(jax.ShapeDtypeStruct((NGRP, 2, LANES, BLK...]
    ppermute x8 -> x6, starting transfers between devices: 4.24 us -> 1.39 us  [swap_cores(): return lax.ppermute(value, 'narrow', [(0, 1), (1, 0)])]
    ppermute x22 -> x24, starting transfers between devices: 33.6 us -> 36.1 us  [hop(): return lax.ppermute(value, 'wide', [(i, i ^ mask) for i in range(size)])]
    slice x0 -> x2, local copies, waits for them, and re-layouts: none -> 2.16 us  [per_device_grid(): top, bottom = (ahead[:SPLIT], ahead[SPLIT:])]
    reduce_sum x1, other arithmetic: 0.46 us -> 2.12 us  [per_device_grid(): linv_part = jnp.sum(jnp.square(factor_inv.astype(jnp.float32)), axis=1)]
    ppermute x8 -> x6, waiting for transfers between devices: 5.32 us -> 5.65 us  [swap_cores(): return lax.ppermute(value, 'narrow', [(0, 1), (1, 0)])]
  transfers between devices with their start and end apart: 30 -> 30, of which waited for: 18 -> 14; matrix products, arithmetic and copies ran while one was open for 1% -> 4% of each run, Pallas kernels for 10% -> 10%
where the time goes in v3:
time: 165 us; the launch traced here: 164 us
  waiting for transfers between devices  81 us (49%)
  starting transfers between devices  37.5 us (23%)
  Pallas kernels  23.6 us (14%)
  local copies, waits for them, and re-layouts  17.4 us (11%)
  other arithmetic  3.98 us (2%)
    ppermute x24, waiting for transfers between devices, hop(): return lax.ppermute(value, 'wide', [(i, i ^ mask) for i in range(size)])  75.3 us
    ppermute x24, starting transfers between devices, hop(): return lax.ppermute(value, 'wide', [(i, i ^ mask) for i in range(size)])  36.1 us
    pallas_call x4, Pallas kernels, products(): pl.pallas_call(body, out_shape=(jax.ShapeDtypeStruct((NGRP, 2, LANES, BLK...  16.6 us
    unnamed x58, local copies, waits for them, and re-layouts  13.9 us
    ppermute x6, waiting for transfers between devices, swap_cores(): return lax.ppermute(value, 'narrow', [(0, 1), (1, 0)])  5.65 us
  transfers between devices with their start and end apart: 30, of which 14 were waited for; matrix products, arithmetic and copies ran while one was open for 4% of the time, Pallas kernels for 10%

profile of v3, /device:TPU:0, one launch (start us, length us, event | category | flops | bytes accessed | tf_op | source)
XLA Modules:
  0.0 164.5 jit_solution(75714562677002721)
XLA Ops:
  5.1 2.6 %collective-permute-start.2 = (bf16[256,2048]{1,0:T(8,128)(2,1)}, bf16[256,2048]{1,0:T(8,128)(2,1)S(1)}, u32[]{:S(2)}, u32[]{:S(2)}) collective-permute-start(bf16[256,2048]{1,0:T(8,128)(2,1)} %refs_0_.1), channel_id=1, source_target_pairs={{0,4},{2,6},{4,0},{6,2},{8,12},{10,14},{12,8},{14,10},{16,20},{18,... | collective-permute-start | bytes 3145736 | tf_op jit(solution)/shard_map/inv_y/ppermute | solution.py:104
  9.1 2.7 %collective-permute-start.3 = (bf16[192,2048]{1,0:T(8,128)(2,1)S(1)}, bf16[192,2048]{1,0:T(8,128)(2,1)S(1)}, u32[]{:S(2)}, u32[]{:S(2)}) collective-permute-start(bf16[192,2048]{1,0:T(8,128)(2,1)S(1)} %slice.54), channel_id=1, source_target_pairs={{0,8},{2,10},{4,12},{6,14},{8,0},{10,2},{12,4},{14,6},{16,24},{18,... | collective-permute-start | bytes 2359304 | tf_op jit(solution)/shard_map/inv_z0/ppermute | solution.py:104
  11.7 2.6 %collective-permute-start = (bf16[1024,256]{1,0:T(8,128)(2,1)S(1)}, bf16[1024,256]{1,0:T(8,128)(2,1)S(1)}, u32[]{:S(2)}, u32[]{:S(2)}) collective-permute-start(bf16[1024,256]{1,0:T(8,128)(2,1)S(1)} %pack_first.1.f0), channel_id=1, source_target_pairs={{0,16},{2,18},{4,20},{6,22},{8,24},{10,26},{12,28},{14,30},{16,0},... | collective-permute-start | bytes 1572872 | tf_op jit(solution)/shard_map/first_z/ppermute | solution.py:104
  17.6 22.7 %collective-permute-done.f0 = bf16[1024,256]{1,0:T(8,128)(2,1)S(1)} collective-permute-done((bf16[1024,256]{1,0:T(8,128)(2,1)S(1)}, bf16[1024,256]{1,0:T(8,128)(2,1)S(1)}, u32[]{:S(2)}, u32[]{:S(2)}) %collective-permute-start) | collective-permute-done | bytes 524320 | tf_op jit(solution)/shard_map/first_z/ppermute | solution.py:104
  44.7 3.5 %collective-permute-start.9 = (bf16[64,2048]{1,0:T(8,128)(2,1)S(1)}, bf16[64,2048]{1,0:T(8,128)(2,1)S(1)}, u32[]{:S(2)}, u32[]{:S(2)}) collective-permute-start(bf16[64,2048]{1,0:T(8,128)(2,1)S(1)} %slice.55), channel_id=1, source_target_pairs={{0,8},{2,10},{4,12},{6,14},{8,0},{10,2},{12,4},{14,6},{16,24},{18,... | collective-permute-start | bytes 786440 | tf_op jit(solution)/shard_map/inv_z1/ppermute | solution.py:104
  51.7 5.0 %collective-permute-done.9 = bf16[64,2048]{1,0:T(8,128)(2,1)S(1)} collective-permute-done((bf16[64,2048]{1,0:T(8,128)(2,1)S(1)}, bf16[64,2048]{1,0:T(8,128)(2,1)S(1)}, u32[]{:S(2)}, u32[]{:S(2)}) %collective-permute-start.9) | collective-permute-done | bytes 262176 | tf_op jit(solution)/shard_map/inv_z1/ppermute | solution.py:104
  57.2 9.7 %collective-permute-done.10 = bf16[64,2048]{1,0:T(8,128)(2,1)S(1)} collective-permute-done((bf16[64,2048]{1,0:T(8,128)(2,1)S(1)}, bf16[64,2048]{1,0:T(8,128)(2,1)S(1)}, u32[]{:S(2)}, u32[]{:S(2)}) %collective-permute-start.10) | collective-permute-done | bytes 262176 | tf_op jit(solution)/shard_map/inv_yz1/ppermute | solution.py:104
  67.7 4.5 %collective-permute-done.7.f1 = bf16[1024,256]{1,0:T(8,128)(2,1)S(1)} collective-permute-done((bf16[1024,256]{1,0:T(8,128)(2,1)S(1)}, bf16[1024,256]{1,0:T(8,128)(2,1)S(1)}, u32[]{:S(2)}, u32[]{:S(2)}) %collective-permute-start.7) | collective-permute-done | bytes 524320 | tf_op jit(solution)/shard_map/first_xz/ppermute | solution.py:104
  76.7 4.2 %collective-permute-done.12.refs_3_ = bf16[768,2048]{1,0:T(8,128)(2,1)} collective-permute-done((bf16[768,2048]{1,0:T(8,128)(2,1)S(1)}, bf16[768,2048]{1,0:T(8,128)(2,1)}, u32[]{:S(2)}, u32[]{:S(2)}) %collective-permute-start.12) | collective-permute-done | bytes 3145760 | tf_op jit(solution)/shard_map/inv_swap_more/ppermute | solution.py:98
  83.3 3.2 %pack_inverse.1.sel_ref = bf16[4,256,3072]{2,1,0:T(8,128)(2,1)S(1)} custom-call(s32[2,12]{1,0:T(2,128)S(1)} %copy-done.24, bf16[256,2048]{1,0:T(8,128)(2,1)S(1)} %copy-done.7, bf16[768,2048]{1,0:T(8,128)(2,1)S(1)} %constant_dynamic-update-slice_fusion.refs_1_, bf16[256,2048]{1,0:T(8,128)(2,1)S(1)} %copy-done.16, ...), custom_call_target="tpu_custom_call" | custom-call | tf_op jit(solution)/shard_map/pack_inverse/pallas_call | solution.py:192
  86.6 3.6 %products.5 = (bf16[4,2,128,256]{3,2,1,0:T(8,128)(2,1)S(1)}, f32[2,1,128]{2,1,0:T(1,128)S(1)}) custom-call(s32[2,12]{1,0:T(2,128)S(1)} %copy-done.24, bf16[4,256,3072]{2,1,0:T(8,128)(2,1)S(1)} %pack_inverse.1.sel_ref, bf16[1024,256]{1,0:T(8,128)(2,1)S(1)} %copy-done.5, bf16[1024,256]{1,0:T(8,128)(2,1)S(1)} %copy-done.11, bf16[2048,128]{1,0:T(8,128)(2,1)S(1)} %copy-done.20, ...), custom_call_target="tpu_custom_call" | custom-call | tf_op jit(solution)/shard_map/products/pallas_call | solution.py:263
  90.3 4.8 %products.6 = (bf16[4,2,128,256]{3,2,1,0:T(8,128)(2,1)S(1)}, f32[2,1,128]{2,1,0:T(1,128)S(1)}) custom-call(s32[2,12]{1,0:T(2,128)S(1)} %copy-done.24, bf16[4,256,3072]{2,1,0:T(8,128)(2,1)S(1)} %pack_inverse.1.sel_ref, bf16[1024,256]{1,0:T(8,128)(2,1)S(1)} %copy-done.9, bf16[1024,256]{1,0:T(8,128)(2,1)S(1)} %copy-done.14, ...), custom_call_target="tpu_custom_call" | custom-call | tf_op jit(solution)/shard_map/products/pallas_call | solution.py:263
  96.1 2.1 %multiply_reduce_fusion = f32[2,2048]{1,0:T(2,128)S(1)} fusion(bf16[2,256,2048]{2,1,0:T(8,128)(2,1)} %param.6), kind=kLoop, calls=%fused_computation | loop fusion | flops 3141632 | bytes 2113536 | tf_op jit(solution)/shard_map/reduce_sum | solution.py:371
  98.2 3.6 %collective-permute-done.14.r0 = bf16[2048,128]{1,0:T(8,128)(2,1)} collective-permute-done((bf16[2048,128]{1,0:T(8,128)(2,1)}, bf16[2048,128]{1,0:T(8,128)(2,1)}, u32[]{:S(2)}, u32[]{:S(2)}) %collective-permute-start.14) | collective-permute-done | bytes 524320 | tf_op jit(solution)/shard_map/rest1_z/ppermute | solution.py:104
  105.2 2.0 %collective-permute-start.19 = (bf16[2,2,128,256]{3,2,1,0:T(8,128)(2,1)S(1)}, bf16[2,2,128,256]{3,2,1,0:T(8,128)(2,1)S(1)}, u32[]{:S(2)}, u32[]{:S(2)}) collective-permute-start(bf16[2,2,128,256]{3,2,1,0:T(8,128)(2,1)S(1)} %pad_maximum_fusion.2), channel_id=1, source_target_pairs={{0,8},{2,10},{4,12},{6,14},{8,0},{10,2},{12,4},{14,6},{16,24},{18,... | collective-permute-start | bytes 786440 | tf_op jit(solution)/shard_map/cross0_2/ppermute | solution.py:104
  108.8 18.3 %collective-permute-done.13.r1 = bf16[2048,128]{1,0:T(8,128)(2,1)S(1)} collective-permute-done((bf16[2048,128]{1,0:T(8,128)(2,1)S(1)}, bf16[2048,128]{1,0:T(8,128)(2,1)S(1)}, u32[]{:S(2)}, u32[]{:S(2)}) %collective-permute-start.13) | collective-permute-done | bytes 524320 | tf_op jit(solution)/shard_map/rest1_x/ppermute | solution.py:104
  127.1 2.8 %copy-done.1 = bf16[4,256,3072]{2,1,0:T(8,128)(2,1)S(1)} copy-done((bf16[4,256,3072]{2,1,0:T(8,128)(2,1)S(1)}, bf16[4,256,3072]{2,1,0:T(8,128)(2,1)}, u32[]{:S(2)}) %copy-start.1) | copy-done | bytes 6291480
  129.9 3.6 %products.4 = (bf16[4,2,128,256]{3,2,1,0:T(8,128)(2,1)S(1)}, f32[2,1,128]{2,1,0:T(1,128)S(1)}) custom-call(s32[2,12]{1,0:T(2,128)S(1)} %copy-done.24, bf16[4,256,3072]{2,1,0:T(8,128)(2,1)S(1)} %copy-done.1, bf16[1024,256]{1,0:T(8,128)(2,1)S(1)} %copy-done.6, bf16[1024,256]{1,0:T(8,128)(2,1)S(1)} %copy-done.12, bf16[2048,128]{1,0:T(8,128)(2,1)S(1)} %copy-done.18, ...), custom_call_target="tpu_custom_call" | custom-call | tf_op jit(solution)/shard_map/products/pallas_call | solution.py:263
  133.6 4.6 %products.7 = (bf16[4,2,128,256]{3,2,1,0:T(8,128)(2,1)S(1)}, f32[2,1,128]{2,1,0:T(1,128)S(1)}) custom-call(s32[2,12]{1,0:T(2,128)S(1)} %copy-done.24, bf16[4,256,3072]{2,1,0:T(8,128)(2,1)S(1)} %copy-done.1, bf16[1024,256]{1,0:T(8,128)(2,1)S(1)} %copy-done.9, bf16[1024,256]{1,0:T(8,128)(2,1)S(1)} %copy-done.14, bf16[2048,128]{1,0:T(8,128)(2,1)} %collective-permute-done.14.r0, ...), custom_call_target="tpu_custom_call" | custom-call | tf_op jit(solution)/shard_map/products/pallas_call | solution.py:263
  140.7 2.0 %collective-permute-start.23 = (bf16[2,2,128,256]{3,2,1,0:T(8,128)(2,1)S(1)}, bf16[2,2,128,256]{3,2,1,0:T(8,128)(2,1)S(1)}, u32[]{:S(2)}, u32[]{:S(2)}) collective-permute-start(bf16[2,2,128,256]{3,2,1,0:T(8,128)(2,1)S(1)} %pad_maximum_fusion.6), channel_id=1, source_target_pairs={{0,8},{2,10},{4,12},{6,14},{8,0},{10,2},{12,4},{14,6},{16,24},{18,... | collective-permute-start | bytes 786440 | tf_op jit(solution)/shard_map/cross1_2/ppermute | solution.py:104
  145.0 3.2 %collective-permute-done.26 = f32[2,2048]{1,0:T(2,128)S(1)} collective-permute-done((f32[2,2048]{1,0:T(2,128)S(1)}, f32[2,2048]{1,0:T(2,128)S(1)}, u32[]{:S(2)}, u32[]{:S(2)}) %collective-permute-start.26) | collective-permute-done | bytes 16416 | tf_op jit(solution)/shard_map/variance_1/ppermute | solution.py:104
  150.1 3.0 %collective-permute-done.27 = f32[2,2048]{1,0:T(2,128)S(1)} collective-permute-done((f32[2,2048]{1,0:T(2,128)S(1)}, f32[2,2048]{1,0:T(2,128)S(1)}, u32[]{:S(2)}, u32[]{:S(2)}) %collective-permute-start.27) | collective-permute-done | bytes 16416 | tf_op jit(solution)/shard_map/variance_8/ppermute | solution.py:104
  154.0 2.9 %collective-permute-done.28 = f32[2,2048]{1,0:T(2,128)S(1)} collective-permute-done((f32[2,2048]{1,0:T(2,128)S(1)}, f32[2,2048]{1,0:T(2,128)S(1)}, u32[]{:S(2)}, u32[]{:S(2)}) %collective-permute-start.28) | collective-permute-done | bytes 16416 | tf_op jit(solution)/shard_map/variance_2/ppermute | solution.py:104
  156.9 4.1 %collective-permute-start.29 = (f32[2,2048]{1,0:T(2,128)S(1)}, f32[2,2048]{1,0:T(2,128)S(1)}, u32[]{:S(2)}, u32[]{:S(2)}) collective-permute-start(f32[2,2048]{1,0:T(2,128)S(1)} %add.24), channel_id=1, source_target_pairs={{0,8},{2,10},{4,12},{6,14},{8,0},{10,2},{12,4},{14,6},{16,24},{18,... | collective-permute-start | bytes 49160 | tf_op jit(solution)/shard_map/variance_4/ppermute | solution.py:104
  (133 shorter events, 41.9 us)
Async XLA Ops:
  5.1 36.1 %collective-permute-start.2 = (bf16[256,2048]{1,0:T(8,128)(2,1)}, bf16[256,2048]{1,0:T(8,128)(2,1)S(1)}, u32[]{:S(2)}, u32[]{:S(2)}) collective-permute-start(bf16[256,2048]{1,0:T(8,128)(2,1)} %refs_0_.1), channel_id=1, source_target_pairs={{0,4},{2,6},{4,0},{6,2},{8,12},{10,14},{12,8},{14,10},{16,20},{18,... | collective-permute-start | bytes 3145736 | tf_op jit(solution)/shard_map/inv_y/ppermute | solution.py:104
  7.7 33.5 %collective-permute-start.5 = (bf16[256,2048]{1,0:T(8,128)(2,1)}, bf16[256,2048]{1,0:T(8,128)(2,1)S(1)}, u32[]{:S(2)}, u32[]{:S(2)}) collective-permute-start(bf16[256,2048]{1,0:T(8,128)(2,1)} %refs_0_.1), channel_id=1, source_target_pairs={{0,1},{1,0},{2,3},{3,2},{4,5},{5,4},{6,7},{7,6},{8,9},{9,8},{10,11... | collective-permute-start | bytes 3145736 | tf_op jit(solution)/shard_map/inv_swap/ppermute | solution.py:98
  9.1 32.1 %collective-permute-start.3 = (bf16[192,2048]{1,0:T(8,128)(2,1)S(1)}, bf16[192,2048]{1,0:T(8,128)(2,1)S(1)}, u32[]{:S(2)}, u32[]{:S(2)}) collective-permute-start(bf16[192,2048]{1,0:T(8,128)(2,1)S(1)} %slice.54), channel_id=1, source_target_pairs={{0,8},{2,10},{4,12},{6,14},{8,0},{10,2},{12,4},{14,6},{16,24},{18,... | collective-permute-start | bytes 2359304 | tf_op jit(solution)/shard_map/inv_z0/ppermute | solution.py:104
  11.7 28.6 %collective-permute-start = (bf16[1024,256]{1,0:T(8,128)(2,1)S(1)}, bf16[1024,256]{1,0:T(8,128)(2,1)S(1)}, u32[]{:S(2)}, u32[]{:S(2)}) collective-permute-start(bf16[1024,256]{1,0:T(8,128)(2,1)S(1)} %pack_first.1.f0), channel_id=1, source_target_pairs={{0,16},{2,18},{4,20},{6,22},{8,24},{10,26},{12,28},{14,30},{16,0},... | collective-permute-start | bytes 1572872 | tf_op jit(solution)/shard_map/first_z/ppermute | solution.py:104
  14.3 26.0 %collective-permute-start.1 = (bf16[1024,256]{1,0:T(8,128)(2,1)S(1)}, bf16[1024,256]{1,0:T(8,128)(2,1)S(1)}, u32[]{:S(2)}, u32[]{:S(2)}) collective-permute-start(bf16[1024,256]{1,0:T(8,128)(2,1)S(1)} %pack_first.1.f0), channel_id=1, source_target_pairs={{0,2},{2,0},{4,6},{6,4},{8,10},{10,8},{12,14},{14,12},{16,18},{18,... | collective-permute-start | bytes 1572872 | tf_op jit(solution)/shard_map/first_x/ppermute | solution.py:104
  42.1 32.6 %collective-permute-start.8 = (bf16[192,2048]{1,0:T(8,128)(2,1)S(1)}, bf16[192,2048]{1,0:T(8,128)(2,1)S(1)}, u32[]{:S(2)}, u32[]{:S(2)}) collective-permute-start(bf16[192,2048]{1,0:T(8,128)(2,1)S(1)} %collective-permute-done.3), channel_id=1, source_target_pairs={{0,4},{2,6},{4,0},{6,2},{8,12},{10,14},{12,8},{14,10},{16,20},{18,... | collective-permute-start | bytes 2359304 | tf_op jit(solution)/shard_map/inv_yz0/ppermute | solution.py:104
  44.7 12.0 %collective-permute-start.9 = (bf16[64,2048]{1,0:T(8,128)(2,1)S(1)}, bf16[64,2048]{1,0:T(8,128)(2,1)S(1)}, u32[]{:S(2)}, u32[]{:S(2)}) collective-permute-start(bf16[64,2048]{1,0:T(8,128)(2,1)S(1)} %slice.55), channel_id=1, source_target_pairs={{0,8},{2,10},{4,12},{6,14},{8,0},{10,2},{12,4},{14,6},{16,24},{18,... | collective-permute-start | bytes 786440 | tf_op jit(solution)/shard_map/inv_z1/ppermute | solution.py:104
  48.2 18.7 %collective-permute-start.11 = (bf16[2048,128]{1,0:T(8,128)(2,1)S(1)}, bf16[2048,128]{1,0:T(8,128)(2,1)S(1)}, u32[]{:S(2)}, u32[]{:S(2)}) collective-permute-start(bf16[2048,128]{1,0:T(8,128)(2,1)S(1)} %get-tuple-element.47.r0), channel_id=1, source_target_pairs={{0,2},{2,0},{4,6},{6,4},{8,10},{10,8},{12,14},{14,12},{16,18},{18,... | collective-permute-start | bytes 1572872 | tf_op jit(solution)/shard_map/rest0_x/ppermute | solution.py:104
  49.7 22.6 %collective-permute-start.7 = (bf16[1024,256]{1,0:T(8,128)(2,1)S(1)}, bf16[1024,256]{1,0:T(8,128)(2,1)S(1)}, u32[]{:S(2)}, u32[]{:S(2)}) collective-permute-start(bf16[1024,256]{1,0:T(8,128)(2,1)S(1)} %collective-permute-done.f0), channel_id=1, source_target_pairs={{0,2},{2,0},{4,6},{6,4},{8,10},{10,8},{12,14},{14,12},{16,18},{18,... | collective-permute-start | bytes 1572872 | tf_op jit(solution)/shard_map/first_xz/ppermute | solution.py:104
  50.2 24.5 %collective-permute-start.6 = (bf16[2048,128]{1,0:T(8,128)(2,1)S(1)}, bf16[2048,128]{1,0:T(8,128)(2,1)}, u32[]{:S(2)}, u32[]{:S(2)}) collective-permute-start(bf16[2048,128]{1,0:T(8,128)(2,1)S(1)} %get-tuple-element.47.r0), channel_id=1, source_target_pairs={{0,16},{2,18},{4,20},{6,22},{8,24},{10,26},{12,28},{14,30},{16,0},... | collective-permute-start | bytes 1572872 | tf_op jit(solution)/shard_map/rest0_z/ppermute | solution.py:104
  56.7 10.2 %collective-permute-start.10 = (bf16[64,2048]{1,0:T(8,128)(2,1)S(1)}, bf16[64,2048]{1,0:T(8,128)(2,1)S(1)}, u32[]{:S(2)}, u32[]{:S(2)}) collective-permute-start(bf16[64,2048]{1,0:T(8,128)(2,1)S(1)} %collective-permute-done.9), channel_id=1, source_target_pairs={{0,4},{2,6},{4,0},{6,2},{8,12},{10,14},{12,8},{14,10},{16,20},{18,... | collective-permute-start | bytes 786440 | tf_op jit(solution)/shard_map/inv_yz1/ppermute | solution.py:104
  75.0 5.9 %collective-permute-start.12 = (bf16[768,2048]{1,0:T(8,128)(2,1)S(1)}, bf16[768,2048]{1,0:T(8,128)(2,1)}, u32[]{:S(2)}, u32[]{:S(2)}) collective-permute-start(bf16[768,2048]{1,0:T(8,128)(2,1)S(1)} %constant_dynamic-update-slice_fusion.refs_1_), channel_id=1, source_target_pairs={{0,1},{1,0},{2,3},{3,2},{4,5},{5,4},{6,7},{7,6},{8,9},{9,8},{10,11... | collective-permute-start | bytes 9437192 | tf_op jit(solution)/shard_map/inv_swap_more/ppermute | solution.py:98
  75.1 15.2 %collective-permute-start.16 = (bf16[2048,128]{1,0:T(8,128)(2,1)}, bf16[2048,128]{1,0:T(8,128)(2,1)}, u32[]{:S(2)}, u32[]{:S(2)}) collective-permute-start(bf16[2048,128]{1,0:T(8,128)(2,1)} %collective-permute-done.6.r0), channel_id=1, source_target_pairs={{0,2},{2,0},{4,6},{6,4},{8,10},{10,8},{12,14},{14,12},{16,18},{18,... | collective-permute-start | bytes 1572872 | tf_op jit(solution)/shard_map/rest0_xz/ppermute | solution.py:104
  76.7 25.2 %collective-permute-start.14 = (bf16[2048,128]{1,0:T(8,128)(2,1)}, bf16[2048,128]{1,0:T(8,128)(2,1)}, u32[]{:S(2)}, u32[]{:S(2)}) collective-permute-start(bf16[2048,128]{1,0:T(8,128)(2,1)} %copy-done.17), channel_id=1, source_target_pairs={{0,16},{2,18},{4,20},{6,22},{8,24},{10,26},{12,28},{14,30},{16,0},... | collective-permute-start | bytes 1572872 | tf_op jit(solution)/shard_map/rest1_z/ppermute | solution.py:104
  96.0 7.9 %collective-permute-start.17 = (bf16[4,2,128,256]{3,2,1,0:T(8,128)(2,1)}, bf16[4,2,128,256]{3,2,1,0:T(8,128)(2,1)}, u32[]{:S(2)}, u32[]{:S(2)}) collective-permute-start(bf16[4,2,128,256]{3,2,1,0:T(8,128)(2,1)} %get-tuple-element.75), channel_id=1, source_target_pairs={{0,1},{1,0},{2,3},{3,2},{4,5},{5,4},{6,7},{7,6},{8,9},{9,8},{10,11... | collective-permute-start | bytes 1572872 | tf_op jit(solution)/shard_map/cross0_swap/ppermute | solution.py:98
  101.8 31.8 %collective-permute-start.15 = (bf16[2048,128]{1,0:T(8,128)(2,1)}, bf16[2048,128]{1,0:T(8,128)(2,1)S(1)}, u32[]{:S(2)}, u32[]{:S(2)}) collective-permute-start(bf16[2048,128]{1,0:T(8,128)(2,1)} %collective-permute-done.14.r0), channel_id=1, source_target_pairs={{0,2},{2,0},{4,6},{6,4},{8,10},{10,8},{12,14},{14,12},{16,18},{18,... | collective-permute-start | bytes 1572872 | tf_op jit(solution)/shard_map/rest1_xz/ppermute | solution.py:104
  102.4 24.8 %collective-permute-start.13 = (bf16[2048,128]{1,0:T(8,128)(2,1)S(1)}, bf16[2048,128]{1,0:T(8,128)(2,1)S(1)}, u32[]{:S(2)}, u32[]{:S(2)}) collective-permute-start(bf16[2048,128]{1,0:T(8,128)(2,1)S(1)} %copy-done.18), channel_id=1, source_target_pairs={{0,2},{2,0},{4,6},{6,4},{8,10},{10,8},{12,14},{14,12},{16,18},{18,... | collective-permute-start | bytes 1572872 | tf_op jit(solution)/shard_map/rest1_x/ppermute | solution.py:104
  105.1 28.6 %collective-permute-start.20 = (bf16[2,2,128,256]{3,2,1,0:T(8,128)(2,1)S(1)}, bf16[2,2,128,256]{3,2,1,0:T(8,128)(2,1)S(1)}, u32[]{:S(2)}, u32[]{:S(2)}) collective-permute-start(bf16[2,2,128,256]{3,2,1,0:T(8,128)(2,1)S(1)} %pad_maximum_fusion.3), channel_id=1, source_target_pairs={{0,12},{2,14},{4,8},{6,10},{8,4},{10,6},{12,0},{14,2},{16,28},{18,... | collective-permute-start | bytes 786440 | tf_op jit(solution)/shard_map/cross0_3/ppermute | solution.py:104
  105.2 28.4 %collective-permute-start.19 = (bf16[2,2,128,256]{3,2,1,0:T(8,128)(2,1)S(1)}, bf16[2,2,128,256]{3,2,1,0:T(8,128)(2,1)S(1)}, u32[]{:S(2)}, u32[]{:S(2)}) collective-permute-start(bf16[2,2,128,256]{3,2,1,0:T(8,128)(2,1)S(1)} %pad_maximum_fusion.2), channel_id=1, source_target_pairs={{0,8},{2,10},{4,12},{6,14},{8,0},{10,2},{12,4},{14,6},{16,24},{18,... | collective-permute-start | bytes 786440 | tf_op jit(solution)/shard_map/cross0_2/ppermute | solution.py:104
  107.2 26.4 %collective-permute-start.18 = (bf16[2,2,128,256]{3,2,1,0:T(8,128)(2,1)S(1)}, bf16[2,2,128,256]{3,2,1,0:T(8,128)(2,1)S(1)}, u32[]{:S(2)}, u32[]{:S(2)}) collective-permute-start(bf16[2,2,128,256]{3,2,1,0:T(8,128)(2,1)S(1)} %pad_maximum_fusion.1), channel_id=1, source_target_pairs={{0,4},{2,6},{4,0},{6,2},{8,12},{10,14},{12,8},{14,10},{16,20},{18,... | collective-permute-start | bytes 786440 | tf_op jit(solution)/shard_map/cross0_1/ppermute | solution.py:104
  140.6 22.8 %collective-permute-start.24 = (bf16[2,2,128,256]{3,2,1,0:T(8,128)(2,1)S(1)}, bf16[2,2,128,256]{3,2,1,0:T(8,128)(2,1)S(1)}, u32[]{:S(2)}, u32[]{:S(2)}) collective-permute-start(bf16[2,2,128,256]{3,2,1,0:T(8,128)(2,1)S(1)} %pad_maximum_fusion.7), channel_id=1, source_target_pairs={{0,12},{2,14},{4,8},{6,10},{8,4},{10,6},{12,0},{14,2},{16,28},{18,... | collective-permute-start | bytes 786440 | tf_op jit(solution)/shard_map/cross1_3/ppermute | solution.py:104
  140.7 22.7 %collective-permute-start.23 = (bf16[2,2,128,256]{3,2,1,0:T(8,128)(2,1)S(1)}, bf16[2,2,128,256]{3,2,1,0:T(8,128)(2,1)S(1)}, u32[]{:S(2)}, u32[]{:S(2)}) collective-permute-start(bf16[2,2,128,256]{3,2,1,0:T(8,128)(2,1)S(1)} %pad_maximum_fusion.6), channel_id=1, source_target_pairs={{0,8},{2,10},{4,12},{6,14},{8,0},{10,2},{12,4},{14,6},{16,24},{18,... | collective-permute-start | bytes 786440 | tf_op jit(solution)/shard_map/cross1_2/ppermute | solution.py:104
  142.8 20.6 %collective-permute-start.22 = (bf16[2,2,128,256]{3,2,1,0:T(8,128)(2,1)S(1)}, bf16[2,2,128,256]{3,2,1,0:T(8,128)(2,1)S(1)}, u32[]{:S(2)}, u32[]{:S(2)}) collective-permute-start(bf16[2,2,128,256]{3,2,1,0:T(8,128)(2,1)S(1)} %pad_maximum_fusion.5), channel_id=1, source_target_pairs={{0,4},{2,6},{4,0},{6,2},{8,12},{10,14},{12,8},{14,10},{16,20},{18,... | collective-permute-start | bytes 786440 | tf_op jit(solution)/shard_map/cross1_1/ppermute | solution.py:104
  156.9 5.8 %collective-permute-start.29 = (f32[2,2048]{1,0:T(2,128)S(1)}, f32[2,2048]{1,0:T(2,128)S(1)}, u32[]{:S(2)}, u32[]{:S(2)}) collective-permute-start(f32[2,2048]{1,0:T(2,128)S(1)} %add.24), channel_id=1, source_target_pairs={{0,8},{2,10},{4,12},{6,14},{8,0},{10,2},{12,4},{14,6},{16,24},{18,... | collective-permute-start | bytes 49160 | tf_op jit(solution)/shard_map/variance_4/ppermute | solution.py:104
  (31 other events, 194.0 us)

commit v4 on v3

--- a/solution.py
+++ b/solution.py
@@ -90,7 +90,7 @@
 
 X, Y, ZL, ZH = 1, 2, 4, 8
 NGRP = 4
-SPLIT = 192
+MIB = 1024 * 1024
 
 
 def swap_cores(value, name):
@@ -128,7 +128,7 @@
         out_shape=jax.ShapeDtypeStruct((first * BLK, panel.shape[2]), panel.dtype),
         in_specs=[SMEM, VMEM],
         out_specs=VMEM,
-        compiler_params=pltpu.CompilerParams(vmem_limit_bytes=6 * 1024 * 1024),
+        compiler_params=pltpu.CompilerParams(vmem_limit_bytes=6 * MIB),
         name="pack_first",
     )(structure, panel)
 
@@ -161,51 +161,49 @@
         out_shape=(shape, shape),
         in_specs=[SMEM, VMEM, VMEM],
         out_specs=[VMEM, VMEM],
-        compiler_params=pltpu.CompilerParams(vmem_limit_bytes=8 * 1024 * 1024),
+        compiler_params=pltpu.CompilerParams(vmem_limit_bytes=8 * MIB),
         name="pack_rest",
     )(structure, panel, other)
 
 
-def pack_inverse(structure, owns, others, first):
+def pack_inverse(structure, own, other, first):
     nblocks = structure.shape[1]
-    half_blocks = owns[0].shape[1] // BLK
-    count = len(owns)
-
-    def body(st, *refs):
-        own_refs, oth_refs, out = refs[:count], refs[count : 2 * count], refs[2 * count]
-        n = lax.axis_index("narrow")
+    half_blocks = own.shape[2] // BLK
+
+    def body(st, own_ref, oth_ref, out):
+        n = lax.axis_index("narrow")
+        group = lax.rem(lax.div(lax.axis_index("wide"), Y), NGRP)
         for j in range(nblocks):
             b = pick(st, n, j, first)
             col = pl.multiple_of(lax.rem(b, half_blocks) * BLK, BLK)
             mine = lax.div(b, half_blocks) == n
 
-            def move(sources, j=j, col=col):
-                d = 0
-                for source in sources:
-                    for at in range(0, source.shape[0], BLK):
-                        out[d, :, j * BLK : (j + 1) * BLK] = source[at : at + BLK, pl.ds(col, BLK)]
-                        d += 1
-
-            pl.when(mine)(lambda move=move: move(own_refs))
-            pl.when(jnp.logical_not(mine))(lambda move=move: move(oth_refs))
-
-    return pl.pallas_call(
-        body,
-        out_shape=jax.ShapeDtypeStruct((NGRP, BLK, nblocks * BLK), owns[0].dtype),
-        in_specs=[SMEM] + [VMEM] * (2 * count),
+            def move(source, j=j, col=col):
+                for d in range(NGRP):
+                    out[d, :, j * BLK : (j + 1) * BLK] = source[
+                        lax.bitwise_xor(group, d), :, pl.ds(col, BLK)
+                    ]
+
+            pl.when(mine)(lambda move=move: move(own_ref))
+            pl.when(jnp.logical_not(mine))(lambda move=move: move(oth_ref))
+
+    return pl.pallas_call(
+        body,
+        out_shape=jax.ShapeDtypeStruct((NGRP, BLK, nblocks * BLK), own.dtype),
+        in_specs=[SMEM, VMEM, VMEM],
         out_specs=VMEM,
-        compiler_params=pltpu.CompilerParams(vmem_limit_bytes=20 * 1024 * 1024),
+        compiler_params=pltpu.CompilerParams(vmem_limit_bytes=18 * MIB),
         name="pack_inverse",
-    )(structure, *owns, *others)
-
-
-def products(structure, sel, firsts, rests, chunk, dz):
+    )(structure, own, other)
+
+
+def products(structure, sel, firsts, rests, chunk, near=None):
     nblocks = structure.shape[1]
     early = firsts[0].shape[0]
     late = rests[0].shape[0]
     first = early // BLK
 
-    def body(st, sel_ref, f0, f1, r0, r1, out_ref, sum_ref):
+    def body(st, sel_ref, f0, f1, r0, r1, *refs):
         d = pl.program_id(0)
         n = lax.axis_index("narrow")
         w = lax.axis_index("wide")
@@ -219,53 +217,76 @@
             pos = pos + j * hit
             inside = inside + hit
 
-        @pl.when(d == 0)
+        def compute(out_ref, sum_ref):
+            @pl.when(d == 0)
+            def _():
+                sum_ref[...] = jnp.zeros_like(sum_ref)
+
+            @pl.when(inside == 0)
+            def _():
+                out_ref[...] = jnp.zeros_like(out_ref)
+
+            @pl.when(inside > 0)
+            def _():
+                acc = jnp.dot(
+                    sel_ref[0, :, :early],
+                    jnp.concatenate([f0[...], f1[...]], axis=1),
+                    preferred_element_type=jnp.float32,
+                ) + jnp.dot(
+                    sel_ref[0, :, early:],
+                    jnp.concatenate([r0[...], r1[...]], axis=1),
+                    preferred_element_type=jnp.float32,
+                )
+                for dx in range(2):
+                    part = acc[:, dx * LANES : (dx + 1) * LANES]
+                    slot = lax.bitwise_xor(x, dx)
+
+                    def weigh(rows, part=part, slot=slot):
+                        total = jnp.sum(part * rows.astype(jnp.float32), axis=0, keepdims=True)
+                        sum_ref[slot] += total
+
+                    @pl.when(pos < first)
+                    def _():
+                        at = pl.multiple_of(pos * BLK, BLK)
+                        weigh((f0, f1)[dx][pl.ds(at, BLK), :])
+
+                    @pl.when(pos >= first)
+                    def _():
+                        at = pl.multiple_of((pos - first) * BLK, BLK)
+                        weigh((r0, r1)[dx][pl.ds(at, BLK), :])
+
+                    out_ref[0, slot] = (-part).T.astype(out_ref.dtype)
+
+        if near is None:
+            compute(*refs)
+            return
+        near_ref, near_sum, kept, sent, kept_sum, sent_sum = refs
+        stay = n == lax.div(w, ZH)
+
+        @pl.when(stay)
         def _():
-            sum_ref[...] = jnp.zeros_like(sum_ref)
-
-        @pl.when(inside == 0)
+            kept[...] = near_ref[...]
+            kept_sum[...] = near_sum[...]
+            compute(sent, sent_sum)
+
+        @pl.when(jnp.logical_not(stay))
         def _():
-            out_ref[...] = jnp.zeros_like(out_ref)
-
-        @pl.when(inside > 0)
-        def _():
-            acc = jnp.dot(
-                sel_ref[0, :, :early],
-                jnp.concatenate([f0[...], f1[...]], axis=1),
-                preferred_element_type=jnp.float32,
-            ) + jnp.dot(
-                sel_ref[0, :, early:],
-                jnp.concatenate([r0[...], r1[...]], axis=1),
-                preferred_element_type=jnp.float32,
-            )
-            for dx in range(2):
-                part = acc[:, dx * LANES : (dx + 1) * LANES]
-                slot = lax.bitwise_xor(x, dx)
-
-                def weigh(rows, part=part, slot=slot):
-                    total = jnp.sum(part * rows.astype(jnp.float32), axis=0, keepdims=True)
-                    sum_ref[slot] += total
-
-                @pl.when(pos < first)
-                def _():
-                    at = pl.multiple_of(pos * BLK, BLK)
-                    weigh((f0, f1)[dx][pl.ds(at, BLK), :])
-
-                @pl.when(pos >= first)
-                def _():
-                    at = pl.multiple_of((pos - first) * BLK, BLK)
-                    weigh((r0, r1)[dx][pl.ds(at, BLK), :])
-
-                out_ref[0, slot] = (-part).T.astype(out_ref.dtype)
+            sent[...] = near_ref[...]
+            sent_sum[...] = near_sum[...]
+            compute(kept, kept_sum)
 
     front = pl.BlockSpec((early, LANES), lambda d, st: (0, chunk))
     back = pl.BlockSpec((late, LANES), lambda d, st: (0, 0))
-    return pl.pallas_call(
-        body,
-        out_shape=(
-            jax.ShapeDtypeStruct((NGRP, 2, LANES, BLK), sel.dtype),
-            jax.ShapeDtypeStruct((2, 1, LANES), jnp.float32),
-        ),
+    block = pl.BlockSpec((1, 2, LANES, BLK), lambda d, st: (d, 0, 0, 0))
+    total = pl.BlockSpec((2, 1, LANES), lambda d, st: (0, 0, 0))
+    outs = [
+        jax.ShapeDtypeStruct((NGRP, 2, LANES, BLK), sel.dtype),
+        jax.ShapeDtypeStruct((2, 1, LANES), jnp.float32),
+    ]
+    again = () if near is None else tuple(near)
+    return pl.pallas_call(
+        body,
+        out_shape=outs if near is None else [outs[0], outs[0], outs[1], outs[1]],
         grid_spec=pltpu.PrefetchScalarGridSpec(
             num_scalar_prefetch=1,
             grid=(NGRP,),
@@ -275,16 +296,75 @@
                 front,
                 back,
                 back,
-            ],
-            out_specs=[
-                pl.BlockSpec((1, 2, LANES, BLK), lambda d, st: (d, 0, 0, 0)),
-                pl.BlockSpec((2, 1, LANES), lambda d, st: (0, 0, 0)),
-            ],
+            ]
+            + [block, total][: len(again)],
+            out_specs=[block, total] if near is None else [block, block, total, total],
         ),
-        compiler_params=pltpu.CompilerParams(vmem_limit_bytes=16 * 1024 * 1024),
+        compiler_params=pltpu.CompilerParams(vmem_limit_bytes=14 * MIB),
         cost_estimate=pl.CostEstimate(flops=0, bytes_accessed=0, transcendentals=0),
         name="products",
-    )(structure, sel, *firsts, *rests)
+    )(structure, sel, *firsts, *rests, *again)
+
+
+def bundle(kept, back):
+    def body(kept_ref, back_ref, *outs):
+        for d, out in enumerate(outs):
+            out[0] = kept_ref[d]
+            out[1] = back_ref[d]
+
+    shape = jax.ShapeDtypeStruct((2, *kept.shape[1:]), kept.dtype)
+    return pl.pallas_call(
+        body,
+        out_shape=[shape] * NGRP,
+        in_specs=[VMEM, VMEM],
+        out_specs=[VMEM] * NGRP,
+        compiler_params=pltpu.CompilerParams(vmem_limit_bytes=8 * MIB),
+        name="bundle",
+    )(kept, back)
+
+
+def squares(factor_inv):
+    sups, rows, cols = factor_inv.shape
+    half = cols // 2
+
+    def body(in_ref, out_ref):
+        for k in range(sups):
+            value = in_ref[k].astype(jnp.float32)
+            out_ref[k : k + 1, :] = jnp.sum(value * value, axis=0, keepdims=True)
+
+    return pl.pallas_call(
+        body,
+        out_shape=jax.ShapeDtypeStruct((sups, cols), jnp.float32),
+        grid=(2,),
+        in_specs=[pl.BlockSpec((sups, rows, half), lambda c: (0, 0, c))],
+        out_specs=pl.BlockSpec((sups, half), lambda c: (0, c)),
+        compiler_params=pltpu.CompilerParams(vmem_limit_bytes=8 * MIB),
+        name="squares",
+    )(factor_inv)
+
+
+def place_sums(linv, kept, back):
+    cols = linv.shape[1]
+
+    def body(linv_ref, kept0, kept1, back0, back1, out):
+        n = lax.axis_index("narrow")
+        group = lax.rem(lax.div(lax.axis_index("wide"), Y), NGRP)
+        out[...] = linv_ref[...]
+        for c, (ours, theirs) in enumerate(((kept0, back0), (kept1, back1))):
+            for xx in range(2):
+                at = pl.multiple_of(group * (cols // NGRP) + (2 * xx + c) * LANES, LANES)
+                for k in range(2):
+                    value = jnp.where(n == k, ours[xx], theirs[xx])
+                    out[k : k + 1, pl.ds(at, LANES)] += value
+
+    return pl.pallas_call(
+        body,
+        out_shape=jax.ShapeDtypeStruct(linv.shape, jnp.float32),
+        in_specs=[VMEM] * 5,
+        out_specs=VMEM,
+        compiler_params=pltpu.CompilerParams(vmem_limit_bytes=4 * MIB),
+        name="place_sums",
+    )(linv, *kept, *back)
 
 
 def assemble(messages, chunk, held):
@@ -330,80 +410,59 @@
             pltpu.SemaphoreType.DMA((2 * NGRP,)),
         ],
         input_output_aliases={NGRP: 0} if extra else {},
-        compiler_params=pltpu.CompilerParams(vmem_limit_bytes=16 * 1024 * 1024),
+        compiler_params=pltpu.CompilerParams(vmem_limit_bytes=8 * MIB),
         name="assemble",
     )(*messages, *extra)
 
 
 def per_device_grid(inverse, panel, factor_inv, structure):
     n = lax.axis_index("narrow")
-    w = lax.axis_index("wide")
-    zh = lax.div(w, ZH)
     first = structure.shape[1] - panel.shape[1] // BLK
+    size = lax.axis_size("wide")
+    groups = [
+        [base + spot * Y for spot in range(NGRP)] for base in range(size) if base & (Y | ZL) == 0
+    ]
     f_own = pack_first(structure, panel, first)
-    other = swap_cores(
-        lax.dynamic_index_in_dim(after(panel, f_own), 1 - n, 0, keepdims=False), "panel_swap"
-    )
+    other = swap_cores(lax.dynamic_index_in_dim(panel, 1 - n, 0, keepdims=False), "panel_swap")
     r_own = pack_rest(structure, panel, other, first)
+    with jax.named_scope("inverse_rows"):
+        own = lax.all_gather(inverse, "wide", axis_index_groups=groups)
+    linv = squares(factor_inv)
     f_z = hop(f_own, ZH, "first_z")
     f_x = hop(f_own, X, "first_x")
-    ahead = after(inverse, f_own)
-    top, bottom = ahead[:SPLIT], ahead[SPLIT:]
-    a_y = hop(ahead, Y, "inv_y")
-    a_z0 = hop(top, ZL, "inv_z0")
-    s_own = swap_cores(after(inverse, other), "inv_swap")
-    f_z, f_x, a_y, a_z0, s_own, *r_own = lax.optimization_barrier(
-        (f_z, f_x, a_y, a_z0, s_own, *r_own)
-    )
+    f_z, f_x, linv, *r_own = lax.optimization_barrier((f_z, f_x, linv, *r_own))
     r_z0 = hop(r_own[0], ZH, "rest0_z")
-    a_z1 = hop(after(bottom, f_z), ZL, "inv_z1")
     f_xz = hop(f_z, X, "first_xz")
-    a_yz0 = hop(a_z0, Y, "inv_yz0")
-    a_yz1 = hop(a_z1, Y, "inv_yz1")
-    r_x0 = hop(after(r_own[0], f_z), X, "rest0_x")
-    r_z0, f_xz, a_yz0, a_yz1, r_x0 = lax.optimization_barrier((r_z0, f_xz, a_yz0, a_yz1, r_x0))
-    r_z1 = hop(after(r_own[1], r_z0), ZH, "rest1_z")
+    r_x0 = hop(r_own[0], X, "rest0_x")
+    r_z0, f_xz, r_x0, own, *r_own = lax.optimization_barrier((r_z0, f_xz, r_x0, own, *r_own))
+    r_z1 = hop(r_own[1], ZH, "rest1_z")
     r_xz0 = hop(r_z0, X, "rest0_xz")
-    more = jnp.concatenate([after(a_y, r_z0), a_z0, a_z1, a_yz0, a_yz1])
-    s_more = swap_cores(more, "inv_swap_more")
-    owns = [inverse, more]
-    others = [s_own, s_more]
-    linv_part = jnp.sum(jnp.square(factor_inv.astype(jnp.float32)), axis=1)
-    sel = pack_inverse(structure, owns, others, first)
-    stay = n == zh
-
-    def parts(near, far):
-        return jnp.where(stay, near, far), jnp.where(stay, far, near)
-
-    def deliver(near, far, c):
-        kept, sent = parts(near, far)
-        back = swap_cores(sent, f"cross{c}_swap")
-        messages = [jnp.stack([kept[d], back[d]]) for d in range(NGRP)]
-        return messages[:1] + [
+    r_x1 = hop(r_own[1], X, "rest1_x")
+    sel = pack_inverse(structure, own, swap_cores(own, "inverse_swap"), first)
+
+    def deliver(kept, sent, c):
+        messages = bundle(kept, swap_cores(sent, f"cross{c}_swap"))
+        return [messages[0]] + [
             hop(messages[d], (d % 2) * Y + (d // 2) * ZL, f"cross{c}_{d}") for d in range(1, NGRP)
         ]
 
-    near, near_sum = products(structure, sel, (f_own, f_x), (r_own[0], r_x0), 0, 0)
-    far, far_sum = products(structure, sel, (f_z, f_xz), (r_z0, r_xz0), 0, 1)
-    sums = [parts(near_sum, far_sum)]
-    messages = deliver(near, far, 0)
-    r_x1 = hop(after(r_own[1], sel), X, "rest1_x")
-    near, near_sum = products(structure, sel, (f_own, f_x), (r_own[1], r_x1), 1, 0)
+    near = products(structure, sel, (f_own, f_x), (r_own[0], r_x0), 0)
+    kept, sent, kept_sum0, sent_sum0 = products(
+        structure, sel, (f_z, f_xz), (r_z0, r_xz0), 0, near
+    )
+    messages = deliver(kept, sent, 0)
     r_xz1 = hop(r_z1, X, "rest1_xz")
+    near = products(structure, sel, (f_own, f_x), (r_own[1], r_x1), 1)
     r_xz1, *messages = lax.optimization_barrier((r_xz1, *messages))
-    far, far_sum = products(structure, sel, (f_z, f_xz), (r_z1, r_xz1), 1, 1)
-    sums.append(parts(near_sum, far_sum))
+    kept, sent, kept_sum1, sent_sum1 = products(
+        structure, sel, (f_z, f_xz), (r_z1, r_xz1), 1, near
+    )
     held = assemble(messages, 0, None)
-    held = assemble(deliver(near, far, 1), 1, held)
-    half = panel.shape[2] * lax.axis_size("wide") // 2
+    held = assemble(deliver(kept, sent, 1), 1, held)
+    half = panel.shape[2] * size // 2
     cross = held.reshape(half, 2, 2, LANES).transpose(0, 2, 1, 3).reshape(half, 2, BLK)
-    kept, sent = [jnp.concatenate([sums[0][i], sums[1][i]], axis=1).reshape(-1) for i in (0, 1)]
-    back = swap_cores(sent, "sums_swap")
-    pair = jnp.where(n == 0, jnp.stack([kept, back]), jnp.stack([back, kept]))
-    group = lax.rem(lax.div(w, Y), NGRP)
-    spots = jnp.arange(NGRP, dtype=jnp.int32)[None, :, None] == group
-    placed = jnp.where(spots, pair[:, None, :], 0.0).reshape(2, half)
-    variance = linv_part + placed
+    back = [swap_cores(total, "sums_swap") for total in (sent_sum0, sent_sum1)]
+    variance = place_sums(linv, (kept_sum0, kept_sum1), back)
     for mask in (X, ZH, Y, ZL):
         variance = variance + hop(variance, mask, f"variance_{mask}")
     return cross, variance

time: 165 us -> 175 us (1.061)
  waiting for transfers between devices: 81 us -> 99.1 us
  between operations: 1.16 us -> 14.3 us
  local copies, waits for them, and re-layouts: 17.4 us -> 6.89 us
  starting transfers between devices: 37.5 us -> 33.5 us
  other arithmetic: 3.98 us -> 0.65 us
  Pallas kernels: 23.6 us -> 21.5 us
    all_gather x0 -> x1, waiting for transfers between devices: none -> 25.7 us  [per_device_grid(): own = lax.all_gather(inverse, 'wide', axis_index_groups=groups)]
    ppermute x24 -> x19, waiting for transfers between devices: 75.3 us -> 66.5 us  [hop(): return lax.ppermute(value, 'wide', [(i, i ^ mask) for i in range(size)])]
    unnamed x58 -> x24, local copies, waits for them, and re-layouts: 13.9 us -> 5.45 us
    ppermute x24 -> x19, starting transfers between devices: 36.1 us -> 32.3 us  [hop(): return lax.ppermute(value, 'wide', [(i, i ^ mask) for i in range(size)])]
    slice x6 -> x0, local copies, waits for them, and re-layouts: 3.4 us -> none  [the longest x2 2.16 us: per_device_grid(): top, bottom = (ahead[:SPLIT], ahead[SPLIT:])]
    reduce_sum x1 -> x0, other arithmetic: 2.12 us -> none  [per_device_grid(): linv_part = jnp.sum(jnp.square(factor_inv.astype(jnp.float32)), axis=1)]
    pallas_call x4 -> x8, Pallas kernels: 16.6 us -> 16.1 us  [the longest x4 15.7 us: products(): pl.pallas_call(body, out_shape=outs if near is None else [outs[0], outs[0...]
  transfers between devices with their start and end apart: 30 -> 26, of which waited for: 14 -> 14; matrix products, arithmetic and copies ran while one was open for 4% -> 1% of each run, Pallas kernels for 10% -> 9%
where the time goes in v4:
time: 175 us; the launch traced here: 176 us
  waiting for transfers between devices  99.1 us (57%)
  starting transfers between devices  33.5 us (19%)
  Pallas kernels  21.5 us (12%)
  between operations  14.3 us (8%)
  local copies, waits for them, and re-layouts  6.89 us (4%)
    ppermute x19, waiting for transfers between devices, hop(): return lax.ppermute(value, 'wide', [(i, i ^ mask) for i in range(size)])  66.5 us
    ppermute x19, starting transfers between devices, hop(): return lax.ppermute(value, 'wide', [(i, i ^ mask) for i in range(size)])  32.3 us
    all_gather x1, waiting for transfers between devices, per_device_grid(): own = lax.all_gather(inverse, 'wide', axis_index_groups=groups)  25.7 us
    pallas_call x4, Pallas kernels, products(): pl.pallas_call(body, out_shape=outs if near is None else [outs[0], outs[0...  15.7 us
    ppermute x6, waiting for transfers between devices, swap_cores(): return lax.ppermute(value, 'narrow', [(0, 1), (1, 0)])  6.21 us
    unnamed x24, local copies, waits for them, and re-layouts  5.45 us
  transfers between devices with their start and end apart: 26, of which 14 were waited for; matrix products, arithmetic and copies ran while one was open for 1% of the time, Pallas kernels for 9%

profile of v4, /device:TPU:0, one launch (start us, length us, event | category | flops | bytes accessed | tf_op | source)
XLA Modules:
  0.0 176.0 jit_solution(15395864419625111116)
XLA Ops:
  10.5 3.7 %collective-permute-start = (bf16[1024,256]{1,0:T(8,128)(2,1)S(1)}, bf16[1024,256]{1,0:T(8,128)(2,1)S(1)}, u32[]{:S(2)}, u32[]{:S(2)}) collective-permute-start(bf16[1024,256]{1,0:T(8,128)(2,1)S(1)} %pack_first.1.f0), channel_id=1, source_target_pairs={{0,16},{2,18},{4,20},{6,22},{8,24},{10,26},{12,28},{14,30},{16,0},... | collective-permute-start | bytes 1572872 | tf_op jit(solution)/shard_map/first_z/ppermute | solution.py:104
  17.8 20.2 %collective-permute-done.f0 = bf16[1024,256]{1,0:T(8,128)(2,1)S(1)} collective-permute-done((bf16[1024,256]{1,0:T(8,128)(2,1)S(1)}, bf16[1024,256]{1,0:T(8,128)(2,1)S(1)}, u32[]{:S(2)}, u32[]{:S(2)}) %collective-permute-start) | collective-permute-done | bytes 524320 | tf_op jit(solution)/shard_map/first_z/ppermute | solution.py:104
  41.7 22.9 %collective-permute-done.3.r0 = bf16[2048,128]{1,0:T(8,128)(2,1)} collective-permute-done((bf16[2048,128]{1,0:T(8,128)(2,1)S(1)}, bf16[2048,128]{1,0:T(8,128)(2,1)}, u32[]{:S(2)}, u32[]{:S(2)}) %collective-permute-start.3) | collective-permute-done | bytes 524320 | tf_op jit(solution)/shard_map/rest0_z/ppermute | solution.py:104
  65.4 25.7 %all-gather.3.cloned.1.call-done = bf16[1024,2048]{1,0:T(8,128)(2,1)} async-done(((bf16[256,2048]{1,0:T(8,128)(2,1)}), bf16[1024,2048]{1,0:T(8,128)(2,1)}) %all-gather.3.cloned.1.call-update) | async-done | bytes 4194320 | tf_op jit(solution)/shard_map/inverse_rows/all_gather | solution.py:429
  92.6 2.4 %collective-permute-start.7 = (bf16[2048,128]{1,0:T(8,128)(2,1)}, bf16[2048,128]{1,0:T(8,128)(2,1)S(1)}, u32[]{:S(2)}, u32[]{:S(2)}) collective-permute-start(bf16[2048,128]{1,0:T(8,128)(2,1)} %copy-done.5), channel_id=1, source_target_pairs={{0,16},{2,18},{4,20},{6,22},{8,24},{10,26},{12,28},{14,30},{16,0},... | collective-permute-start | bytes 1572872 | tf_op jit(solution)/shard_map/rest1_z/ppermute | solution.py:104
  95.0 3.5 %collective-permute-done.6.oth_ref = bf16[4,256,2048]{2,1,0:T(8,128)(2,1)S(1)} collective-permute-done((bf16[4,256,2048]{2,1,0:T(8,128)(2,1)}, bf16[4,256,2048]{2,1,0:T(8,128)(2,1)S(1)}, u32[]{:S(2)}, u32[]{:S(2)}) %collective-permute-start.6) | collective-permute-done | bytes 4194336 | tf_op jit(solution)/shard_map/inverse_swap/ppermute | solution.py:98
  98.5 2.2 %copy-done.1 = bf16[1024,2048]{1,0:T(8,128)(2,1)S(1)} copy-done((bf16[1024,2048]{1,0:T(8,128)(2,1)S(1)}, bf16[1024,2048]{1,0:T(8,128)(2,1)}, u32[]{:S(2)}) %copy-start.1) | copy-done | bytes 4194328
  102.5 3.6 %products.4 = (bf16[4,2,128,256]{3,2,1,0:T(8,128)(2,1)S(1)}, f32[2,1,128]{2,1,0:T(1,128)S(1)}) custom-call(s32[2,12]{1,0:T(2,128)S(1)} %copy-done.11, bf16[4,256,3072]{2,1,0:T(8,128)(2,1)S(1)} %pack_inverse.1.sel_ref, bf16[1024,256]{1,0:T(8,128)(2,1)S(1)} %pack_first.1.f0, bf16[1024,256]{1,0:T(8,128)(2,1)S(1)} %copy-done.3, bf16[2048,128]{1,0:T(8,128)(2,1)S(1)} %copy-done.8, ...), custom_call_target="tpu_custom_call" | custom-call | tf_op jit(solution)/shard_map/products/pallas_call | solution.py:287
  106.1 4.7 %products.5 = (bf16[4,2,128,256]{3,2,1,0:T(8,128)(2,1)S(1)}, bf16[4,2,128,256]{3,2,1,0:T(8,128)(2,1)S(1)}, f32[2,1,128]{2,1,0:T(1,128)S(1)}, f32[2,1,128]{2,1,0:T(1,128)S(1)}) custom-call(s32[2,12]{1,0:T(2,128)S(1)} %copy-done.11, bf16[4,256,3072]{2,1,0:T(8,128)(2,1)S(1)} %pack_inverse.1.sel_ref, bf16[1024,256]{1,0:T(8,128)(2,1)S(1)} %collective-permute-done.f0, ...), custom_call_target="tpu_custom_call" | custom-call | tf_op jit(solution)/shard_map/products/pallas_call | solution.py:287
  110.9 3.3 %collective-permute-start.14 = (bf16[2048,128]{1,0:T(8,128)(2,1)S(1)}, bf16[2048,128]{1,0:T(8,128)(2,1)S(1)}, u32[]{:S(2)}, u32[]{:S(2)}) collective-permute-start(bf16[2048,128]{1,0:T(8,128)(2,1)S(1)} %copy-done.6), channel_id=1, source_target_pairs={{0,2},{2,0},{4,6},{6,4},{8,10},{10,8},{12,14},{14,12},{16,18},{18,... | collective-permute-start | bytes 1572872 | tf_op jit(solution)/shard_map/rest1_x/ppermute | solution.py:104
  114.2 4.8 %collective-permute-done.7.r0 = bf16[2048,128]{1,0:T(8,128)(2,1)S(1)} collective-permute-done((bf16[2048,128]{1,0:T(8,128)(2,1)}, bf16[2048,128]{1,0:T(8,128)(2,1)S(1)}, u32[]{:S(2)}, u32[]{:S(2)}) %collective-permute-start.7) | collective-permute-done | bytes 524320 | tf_op jit(solution)/shard_map/rest1_z/ppermute | solution.py:104
  120.2 2.9 %collective-permute-start.13 = (bf16[2,2,128,256]{3,2,1,0:T(8,128)(2,1)S(1)}, bf16[2,2,128,256]{3,2,1,0:T(8,128)(2,1)S(1)}, u32[]{:S(2)}, u32[]{:S(2)}) collective-permute-start(bf16[2,2,128,256]{3,2,1,0:T(8,128)(2,1)S(1)} %get-tuple-element.59), channel_id=1, source_target_pairs={{0,12},{2,14},{4,8},{6,10},{8,4},{10,6},{12,0},{14,2},{16,28},{18,... | collective-permute-start | bytes 786440 | tf_op jit(solution)/shard_map/cross0_3/ppermute | solution.py:104
  123.2 3.7 %collective-permute-done.14.r1 = bf16[2048,128]{1,0:T(8,128)(2,1)S(1)} collective-permute-done((bf16[2048,128]{1,0:T(8,128)(2,1)S(1)}, bf16[2048,128]{1,0:T(8,128)(2,1)S(1)}, u32[]{:S(2)}, u32[]{:S(2)}) %collective-permute-start.14) | collective-permute-done | bytes 524320 | tf_op jit(solution)/shard_map/rest1_x/ppermute | solution.py:104
  126.9 3.6 %products.6 = (bf16[4,2,128,256]{3,2,1,0:T(8,128)(2,1)S(1)}, f32[2,1,128]{2,1,0:T(1,128)S(1)}) custom-call(s32[2,12]{1,0:T(2,128)S(1)} %copy-done.11, bf16[4,256,3072]{2,1,0:T(8,128)(2,1)S(1)} %pack_inverse.1.sel_ref, bf16[1024,256]{1,0:T(8,128)(2,1)S(1)} %pack_first.1.f0, bf16[1024,256]{1,0:T(8,128)(2,1)S(1)} %copy-done.3, bf16[2048,128]{1,0:T(8,128)(2,1)S(1)} %copy-done.6, ...), custom_call_target="tpu_custom_call" | custom-call | tf_op jit(solution)/shard_map/products/pallas_call | solution.py:287
  130.6 7.1 %collective-permute-done.8.r1 = bf16[2048,128]{1,0:T(8,128)(2,1)S(1)} collective-permute-done((bf16[2048,128]{1,0:T(8,128)(2,1)S(1)}, bf16[2048,128]{1,0:T(8,128)(2,1)S(1)}, u32[]{:S(2)}, u32[]{:S(2)}) %collective-permute-start.8) | collective-permute-done | bytes 524320 | tf_op jit(solution)/shard_map/rest1_xz/ppermute | solution.py:104
  137.6 3.7 %products.7 = (bf16[4,2,128,256]{3,2,1,0:T(8,128)(2,1)S(1)}, bf16[4,2,128,256]{3,2,1,0:T(8,128)(2,1)S(1)}, f32[2,1,128]{2,1,0:T(1,128)S(1)}, f32[2,1,128]{2,1,0:T(1,128)S(1)}) custom-call(s32[2,12]{1,0:T(2,128)S(1)} %copy-done.11, bf16[4,256,3072]{2,1,0:T(8,128)(2,1)S(1)} %pack_inverse.1.sel_ref, bf16[1024,256]{1,0:T(8,128)(2,1)S(1)} %collective-permute-done.f0, ...), custom_call_target="tpu_custom_call" | custom-call | tf_op jit(solution)/shard_map/products/pallas_call | solution.py:287
  141.4 1.9 %collective-permute-done.15.back_ref = bf16[4,2,128,256]{3,2,1,0:T(8,128)(2,1)S(1)} collective-permute-done((bf16[4,2,128,256]{3,2,1,0:T(8,128)(2,1)S(1)}, bf16[4,2,128,256]{3,2,1,0:T(8,128)(2,1)S(1)}, u32[]{:S(2)}, u32[]{:S(2)}) %collective-permute-start.15) | collective-permute-done | bytes 524320 | tf_op jit(solution)/shard_map/cross1_swap/ppermute | solution.py:98
  144.9 2.1 %collective-permute-start.18 = (bf16[2,2,128,256]{3,2,1,0:T(8,128)(2,1)S(1)}, bf16[2,2,128,256]{3,2,1,0:T(8,128)(2,1)S(1)}, u32[]{:S(2)}, u32[]{:S(2)}) collective-permute-start(bf16[2,2,128,256]{3,2,1,0:T(8,128)(2,1)S(1)} %get-tuple-element.68), channel_id=1, source_target_pairs={{0,12},{2,14},{4,8},{6,10},{8,4},{10,6},{12,0},{14,2},{16,28},{18,... | collective-permute-start | bytes 786440 | tf_op jit(solution)/shard_map/cross1_3/ppermute | solution.py:104
  148.3 1.8 %collective-permute-start.21 = (f32[2,2048]{1,0:T(2,128)S(1)}, f32[2,2048]{1,0:T(2,128)S(1)}, u32[]{:S(2)}, u32[]{:S(2)}) collective-permute-start(f32[2,2048]{1,0:T(2,128)S(1)} %place_sums.1), channel_id=1, source_target_pairs={{0,2},{2,0},{4,6},{6,4},{8,10},{10,8},{12,14},{14,12},{16,18},{18,... | collective-permute-start | bytes 49160 | tf_op jit(solution)/shard_map/variance_1/ppermute | solution.py:104
  150.1 2.0 %collective-permute-done.21 = f32[2,2048]{1,0:T(2,128)S(1)} collective-permute-done((f32[2,2048]{1,0:T(2,128)S(1)}, f32[2,2048]{1,0:T(2,128)S(1)}, u32[]{:S(2)}, u32[]{:S(2)}) %collective-permute-start.21) | collective-permute-done | bytes 16416 | tf_op jit(solution)/shard_map/variance_1/ppermute | solution.py:104
  152.1 4.0 %collective-permute-start.22 = (f32[2,2048]{1,0:T(2,128)S(1)}, f32[2,2048]{1,0:T(2,128)S(1)}, u32[]{:S(2)}, u32[]{:S(2)}) collective-permute-start(f32[2,2048]{1,0:T(2,128)S(1)} %add.18), channel_id=1, source_target_pairs={{0,16},{2,18},{4,20},{6,22},{8,24},{10,26},{12,28},{14,30},{16,0},... | collective-permute-start | bytes 49160 | tf_op jit(solution)/shard_map/variance_8/ppermute | solution.py:104
  156.1 1.8 %collective-permute-done.22 = f32[2,2048]{1,0:T(2,128)S(1)} collective-permute-done((f32[2,2048]{1,0:T(2,128)S(1)}, f32[2,2048]{1,0:T(2,128)S(1)}, u32[]{:S(2)}, u32[]{:S(2)}) %collective-permute-start.22) | collective-permute-done | bytes 16416 | tf_op jit(solution)/shard_map/variance_8/ppermute | solution.py:104
  158.3 3.3 %collective-permute-done.23 = f32[2,2048]{1,0:T(2,128)S(1)} collective-permute-done((f32[2,2048]{1,0:T(2,128)S(1)}, f32[2,2048]{1,0:T(2,128)S(1)}, u32[]{:S(2)}, u32[]{:S(2)}) %collective-permute-start.23) | collective-permute-done | bytes 16416 | tf_op jit(solution)/shard_map/variance_2/ppermute | solution.py:104
  161.7 4.0 %collective-permute-start.24 = (f32[2,2048]{1,0:T(2,128)S(1)}, f32[2,2048]{1,0:T(2,128)S(1)}, u32[]{:S(2)}, u32[]{:S(2)}) collective-permute-start(f32[2,2048]{1,0:T(2,128)S(1)} %add.20), channel_id=1, source_target_pairs={{0,8},{2,10},{4,12},{6,14},{8,0},{10,2},{12,4},{14,6},{16,24},{18,... | collective-permute-start | bytes 49160 | tf_op jit(solution)/shard_map/variance_4/ppermute | solution.py:104
  (71 shorter events, 22.7 us)
Async XLA Ops:
  7.2 83.9 %all-gather.3.cloned.1.call-start = ((), (), s32[]{:S(2)}) async-start(), calls=%async_computation | async-start | bytes 5242880 | tf_op jit(solution)/shard_map/inverse_rows/all_gather | solution.py:429
  9.4 6.6 %collective-permute-start.2 = (bf16[2048,256]{1,0:T(8,128)(2,1)S(1)}, bf16[2048,256]{1,0:T(8,128)(2,1)S(1)}, u32[]{:S(2)}, u32[]{:S(2)}) collective-permute-start(bf16[2048,256]{1,0:T(8,128)(2,1)S(1)} %dynamic-slice_bitcast_fusion), channel_id=1, source_target_pairs={{0,1},{1,0},{2,3},{3,2},{4,5},{5,4},{6,7},{7,6},{8,9},{9,8},{10,11... | collective-permute-start | bytes 3145736 | tf_op jit(solution)/shard_map/panel_swap/ppermute | solution.py:98
  10.5 27.5 %collective-permute-start = (bf16[1024,256]{1,0:T(8,128)(2,1)S(1)}, bf16[1024,256]{1,0:T(8,128)(2,1)S(1)}, u32[]{:S(2)}, u32[]{:S(2)}) collective-permute-start(bf16[1024,256]{1,0:T(8,128)(2,1)S(1)} %pack_first.1.f0), channel_id=1, source_target_pairs={{0,16},{2,18},{4,20},{6,22},{8,24},{10,26},{12,28},{14,30},{16,0},... | collective-permute-start | bytes 1572872 | tf_op jit(solution)/shard_map/first_z/ppermute | solution.py:104
  14.2 23.8 %collective-permute-start.1 = (bf16[1024,256]{1,0:T(8,128)(2,1)S(1)}, bf16[1024,256]{1,0:T(8,128)(2,1)S(1)}, u32[]{:S(2)}, u32[]{:S(2)}) collective-permute-start(bf16[1024,256]{1,0:T(8,128)(2,1)S(1)} %pack_first.1.f0), channel_id=1, source_target_pairs={{0,2},{2,0},{4,6},{6,4},{8,10},{10,8},{12,14},{14,12},{16,18},{18,... | collective-permute-start | bytes 1572872 | tf_op jit(solution)/shard_map/first_x/ppermute | solution.py:104
  38.8 25.7 %collective-permute-start.3 = (bf16[2048,128]{1,0:T(8,128)(2,1)S(1)}, bf16[2048,128]{1,0:T(8,128)(2,1)}, u32[]{:S(2)}, u32[]{:S(2)}) collective-permute-start(bf16[2048,128]{1,0:T(8,128)(2,1)S(1)} %get-tuple-element.50.r0), channel_id=1, source_target_pairs={{0,16},{2,18},{4,20},{6,22},{8,24},{10,26},{12,28},{14,30},{16,0},... | collective-permute-start | bytes 1572872 | tf_op jit(solution)/shard_map/rest0_z/ppermute | solution.py:104
  38.9 25.7 %collective-permute-start.4 = (bf16[1024,256]{1,0:T(8,128)(2,1)S(1)}, bf16[1024,256]{1,0:T(8,128)(2,1)S(1)}, u32[]{:S(2)}, u32[]{:S(2)}) collective-permute-start(bf16[1024,256]{1,0:T(8,128)(2,1)S(1)} %collective-permute-done.f0), channel_id=1, source_target_pairs={{0,2},{2,0},{4,6},{6,4},{8,10},{10,8},{12,14},{14,12},{16,18},{18,... | collective-permute-start | bytes 1572872 | tf_op jit(solution)/shard_map/first_xz/ppermute | solution.py:104
  40.4 24.2 %collective-permute-start.5 = (bf16[2048,128]{1,0:T(8,128)(2,1)S(1)}, bf16[2048,128]{1,0:T(8,128)(2,1)S(1)}, u32[]{:S(2)}, u32[]{:S(2)}) collective-permute-start(bf16[2048,128]{1,0:T(8,128)(2,1)S(1)} %get-tuple-element.50.r0), channel_id=1, source_target_pairs={{0,2},{2,0},{4,6},{6,4},{8,10},{10,8},{12,14},{14,12},{16,18},{18,... | collective-permute-start | bytes 1572872 | tf_op jit(solution)/shard_map/rest0_x/ppermute | solution.py:104
  91.1 7.4 %collective-permute-start.6 = (bf16[4,256,2048]{2,1,0:T(8,128)(2,1)}, bf16[4,256,2048]{2,1,0:T(8,128)(2,1)S(1)}, u32[]{:S(2)}, u32[]{:S(2)}) collective-permute-start(bf16[4,256,2048]{2,1,0:T(8,128)(2,1)} %bitcast.8), channel_id=1, source_target_pairs={{0,1},{1,0},{2,3},{3,2},{4,5},{5,4},{6,7},{7,6},{8,9},{9,8},{10,11... | collective-permute-start | bytes 12582920 | tf_op jit(solution)/shard_map/inverse_swap/ppermute | solution.py:98
  91.1 15.0 %collective-permute-start.9 = (bf16[2048,128]{1,0:T(8,128)(2,1)}, bf16[2048,128]{1,0:T(8,128)(2,1)S(1)}, u32[]{:S(2)}, u32[]{:S(2)}) collective-permute-start(bf16[2048,128]{1,0:T(8,128)(2,1)} %collective-permute-done.3.r0), channel_id=1, source_target_pairs={{0,2},{2,0},{4,6},{6,4},{8,10},{10,8},{12,14},{14,12},{16,18},{18,... | collective-permute-start | bytes 1572872 | tf_op jit(solution)/shard_map/rest0_xz/ppermute | solution.py:104
  92.6 26.4 %collective-permute-start.7 = (bf16[2048,128]{1,0:T(8,128)(2,1)}, bf16[2048,128]{1,0:T(8,128)(2,1)S(1)}, u32[]{:S(2)}, u32[]{:S(2)}) collective-permute-start(bf16[2048,128]{1,0:T(8,128)(2,1)} %copy-done.5), channel_id=1, source_target_pairs={{0,16},{2,18},{4,20},{6,22},{8,24},{10,26},{12,28},{14,30},{16,0},... | collective-permute-start | bytes 1572872 | tf_op jit(solution)/shard_map/rest1_z/ppermute | solution.py:104
  110.8 8.7 %collective-permute-start.10 = (bf16[4,2,128,256]{3,2,1,0:T(8,128)(2,1)S(1)}, bf16[4,2,128,256]{3,2,1,0:T(8,128)(2,1)S(1)}, u32[]{:S(2)}, u32[]{:S(2)}) collective-permute-start(bf16[4,2,128,256]{3,2,1,0:T(8,128)(2,1)S(1)} %get-tuple-element.55), channel_id=1, source_target_pairs={{0,1},{1,0},{2,3},{3,2},{4,5},{5,4},{6,7},{7,6},{8,9},{9,8},{10,11... | collective-permute-start | bytes 1572872 | tf_op jit(solution)/shard_map/cross0_swap/ppermute | solution.py:98
  110.9 16.0 %collective-permute-start.14 = (bf16[2048,128]{1,0:T(8,128)(2,1)S(1)}, bf16[2048,128]{1,0:T(8,128)(2,1)S(1)}, u32[]{:S(2)}, u32[]{:S(2)}) collective-permute-start(bf16[2048,128]{1,0:T(8,128)(2,1)S(1)} %copy-done.6), channel_id=1, source_target_pairs={{0,2},{2,0},{4,6},{6,4},{8,10},{10,8},{12,14},{14,12},{16,18},{18,... | collective-permute-start | bytes 1572872 | tf_op jit(solution)/shard_map/rest1_x/ppermute | solution.py:104
  119.0 18.6 %collective-permute-start.8 = (bf16[2048,128]{1,0:T(8,128)(2,1)S(1)}, bf16[2048,128]{1,0:T(8,128)(2,1)S(1)}, u32[]{:S(2)}, u32[]{:S(2)}) collective-permute-start(bf16[2048,128]{1,0:T(8,128)(2,1)S(1)} %collective-permute-done.7.r0), channel_id=1, source_target_pairs={{0,2},{2,0},{4,6},{6,4},{8,10},{10,8},{12,14},{14,12},{16,18},{18,... | collective-permute-start | bytes 1572872 | tf_op jit(solution)/shard_map/rest1_xz/ppermute | solution.py:104
  119.6 18.0 %collective-permute-start.11 = (bf16[2,2,128,256]{3,2,1,0:T(8,128)(2,1)S(1)}, bf16[2,2,128,256]{3,2,1,0:T(8,128)(2,1)S(1)}, u32[]{:S(2)}, u32[]{:S(2)}) collective-permute-start(bf16[2,2,128,256]{3,2,1,0:T(8,128)(2,1)S(1)} %get-tuple-element.57), channel_id=1, source_target_pairs={{0,4},{2,6},{4,0},{6,2},{8,12},{10,14},{12,8},{14,10},{16,20},{18,... | collective-permute-start | bytes 786440 | tf_op jit(solution)/shard_map/cross0_1/ppermute | solution.py:104
  119.7 17.9 %collective-permute-start.12 = (bf16[2,2,128,256]{3,2,1,0:T(8,128)(2,1)S(1)}, bf16[2,2,128,256]{3,2,1,0:T(8,128)(2,1)S(1)}, u32[]{:S(2)}, u32[]{:S(2)}) collective-permute-start(bf16[2,2,128,256]{3,2,1,0:T(8,128)(2,1)S(1)} %get-tuple-element.58), channel_id=1, source_target_pairs={{0,8},{2,10},{4,12},{6,14},{8,0},{10,2},{12,4},{14,6},{16,24},{18,... | collective-permute-start | bytes 786440 | tf_op jit(solution)/shard_map/cross0_2/ppermute | solution.py:104
  120.2 17.4 %collective-permute-start.13 = (bf16[2,2,128,256]{3,2,1,0:T(8,128)(2,1)S(1)}, bf16[2,2,128,256]{3,2,1,0:T(8,128)(2,1)S(1)}, u32[]{:S(2)}, u32[]{:S(2)}) collective-permute-start(bf16[2,2,128,256]{3,2,1,0:T(8,128)(2,1)S(1)} %get-tuple-element.59), channel_id=1, source_target_pairs={{0,12},{2,14},{4,8},{6,10},{8,4},{10,6},{12,0},{14,2},{16,28},{18,... | collective-permute-start | bytes 786440 | tf_op jit(solution)/shard_map/cross0_3/ppermute | solution.py:104
  141.3 2.0 %collective-permute-start.15 = (bf16[4,2,128,256]{3,2,1,0:T(8,128)(2,1)S(1)}, bf16[4,2,128,256]{3,2,1,0:T(8,128)(2,1)S(1)}, u32[]{:S(2)}, u32[]{:S(2)}) collective-permute-start(bf16[4,2,128,256]{3,2,1,0:T(8,128)(2,1)S(1)} %get-tuple-element.64), channel_id=1, source_target_pairs={{0,1},{1,0},{2,3},{3,2},{4,5},{5,4},{6,7},{7,6},{8,9},{9,8},{10,11... | collective-permute-start | bytes 1572872 | tf_op jit(solution)/shard_map/cross1_swap/ppermute | solution.py:98
  143.4 24.6 %collective-permute-start.16 = (bf16[2,2,128,256]{3,2,1,0:T(8,128)(2,1)S(1)}, bf16[2,2,128,256]{3,2,1,0:T(8,128)(2,1)S(1)}, u32[]{:S(2)}, u32[]{:S(2)}) collective-permute-start(bf16[2,2,128,256]{3,2,1,0:T(8,128)(2,1)S(1)} %get-tuple-element.66), channel_id=1, source_target_pairs={{0,4},{2,6},{4,0},{6,2},{8,12},{10,14},{12,8},{14,10},{16,20},{18,... | collective-permute-start | bytes 786440 | tf_op jit(solution)/shard_map/cross1_1/ppermute | solution.py:104
  143.5 24.5 %collective-permute-start.17 = (bf16[2,2,128,256]{3,2,1,0:T(8,128)(2,1)S(1)}, bf16[2,2,128,256]{3,2,1,0:T(8,128)(2,1)S(1)}, u32[]{:S(2)}, u32[]{:S(2)}) collective-permute-start(bf16[2,2,128,256]{3,2,1,0:T(8,128)(2,1)S(1)} %get-tuple-element.67), channel_id=1, source_target_pairs={{0,8},{2,10},{4,12},{6,14},{8,0},{10,2},{12,4},{14,6},{16,24},{18,... | collective-permute-start | bytes 786440 | tf_op jit(solution)/shard_map/cross1_2/ppermute | solution.py:104
  144.9 23.1 %collective-permute-start.18 = (bf16[2,2,128,256]{3,2,1,0:T(8,128)(2,1)S(1)}, bf16[2,2,128,256]{3,2,1,0:T(8,128)(2,1)S(1)}, u32[]{:S(2)}, u32[]{:S(2)}) collective-permute-start(bf16[2,2,128,256]{3,2,1,0:T(8,128)(2,1)S(1)} %get-tuple-element.68), channel_id=1, source_target_pairs={{0,12},{2,14},{4,8},{6,10},{8,4},{10,6},{12,0},{14,2},{16,28},{18,... | collective-permute-start | bytes 786440 | tf_op jit(solution)/shard_map/cross1_3/ppermute | solution.py:104
  148.3 3.8 %collective-permute-start.21 = (f32[2,2048]{1,0:T(2,128)S(1)}, f32[2,2048]{1,0:T(2,128)S(1)}, u32[]{:S(2)}, u32[]{:S(2)}) collective-permute-start(f32[2,2048]{1,0:T(2,128)S(1)} %place_sums.1), channel_id=1, source_target_pairs={{0,2},{2,0},{4,6},{6,4},{8,10},{10,8},{12,14},{14,12},{16,18},{18,... | collective-permute-start | bytes 49160 | tf_op jit(solution)/shard_map/variance_1/ppermute | solution.py:104
  152.1 5.7 %collective-permute-start.22 = (f32[2,2048]{1,0:T(2,128)S(1)}, f32[2,2048]{1,0:T(2,128)S(1)}, u32[]{:S(2)}, u32[]{:S(2)}) collective-permute-start(f32[2,2048]{1,0:T(2,128)S(1)} %add.18), channel_id=1, source_target_pairs={{0,16},{2,18},{4,20},{6,22},{8,24},{10,26},{12,28},{14,30},{16,0},... | collective-permute-start | bytes 49160 | tf_op jit(solution)/shard_map/variance_8/ppermute | solution.py:104
  157.9 3.8 %collective-permute-start.23 = (f32[2,2048]{1,0:T(2,128)S(1)}, f32[2,2048]{1,0:T(2,128)S(1)}, u32[]{:S(2)}, u32[]{:S(2)}) collective-permute-start(f32[2,2048]{1,0:T(2,128)S(1)} %add.19), channel_id=1, source_target_pairs={{0,4},{2,6},{4,0},{6,2},{8,12},{10,14},{12,8},{14,10},{16,20},{18,... | collective-permute-start | bytes 49160 | tf_op jit(solution)/shard_map/variance_2/ppermute | solution.py:104
  161.7 5.7 %collective-permute-start.24 = (f32[2,2048]{1,0:T(2,128)S(1)}, f32[2,2048]{1,0:T(2,128)S(1)}, u32[]{:S(2)}, u32[]{:S(2)}) collective-permute-start(f32[2,2048]{1,0:T(2,128)S(1)} %add.20), channel_id=1, source_target_pairs={{0,8},{2,10},{4,12},{6,14},{8,0},{10,2},{12,4},{14,6},{16,24},{18,... | collective-permute-start | bytes 49160 | tf_op jit(solution)/shard_map/variance_4/ppermute | solution.py:104
  (14 other events, 31.2 us)
Sparse Core Ops, SparseCore 0:
  9.6 81.4 all-gather.2

commit v5 on v4

--- a/solution.py
+++ b/solution.py
@@ -166,35 +166,33 @@
     )(structure, panel, other)
 
 
-def pack_inverse(structure, own, other, first):
+def pack_inverse(structure, owns, others, first):
     nblocks = structure.shape[1]
-    half_blocks = own.shape[2] // BLK
-
-    def body(st, own_ref, oth_ref, out):
-        n = lax.axis_index("narrow")
-        group = lax.rem(lax.div(lax.axis_index("wide"), Y), NGRP)
+    half_blocks = owns[0].shape[1] // BLK
+
+    def body(st, *refs):
+        own_refs, oth_refs, out = refs[:NGRP], refs[NGRP : 2 * NGRP], refs[2 * NGRP]
+        n = lax.axis_index("narrow")
         for j in range(nblocks):
             b = pick(st, n, j, first)
             col = pl.multiple_of(lax.rem(b, half_blocks) * BLK, BLK)
             mine = lax.div(b, half_blocks) == n
 
-            def move(source, j=j, col=col):
+            def move(sources, j=j, col=col):
                 for d in range(NGRP):
-                    out[d, :, j * BLK : (j + 1) * BLK] = source[
-                        lax.bitwise_xor(group, d), :, pl.ds(col, BLK)
-                    ]
-
-            pl.when(mine)(lambda move=move: move(own_ref))
-            pl.when(jnp.logical_not(mine))(lambda move=move: move(oth_ref))
-
-    return pl.pallas_call(
-        body,
-        out_shape=jax.ShapeDtypeStruct((NGRP, BLK, nblocks * BLK), own.dtype),
-        in_specs=[SMEM, VMEM, VMEM],
+                    out[d, :, j * BLK : (j + 1) * BLK] = sources[d][:, pl.ds(col, BLK)]
+
+            pl.when(mine)(lambda move=move: move(own_refs))
+            pl.when(jnp.logical_not(mine))(lambda move=move: move(oth_refs))
+
+    return pl.pallas_call(
+        body,
+        out_shape=jax.ShapeDtypeStruct((NGRP, BLK, nblocks * BLK), owns[0].dtype),
+        in_specs=[SMEM] + [VMEM] * (2 * NGRP),
         out_specs=VMEM,
         compiler_params=pltpu.CompilerParams(vmem_limit_bytes=18 * MIB),
         name="pack_inverse",
-    )(structure, own, other)
+    )(structure, *owns, *others)
 
 
 def products(structure, sel, firsts, rests, chunk, near=None):
@@ -419,26 +417,31 @@
     n = lax.axis_index("narrow")
     first = structure.shape[1] - panel.shape[1] // BLK
     size = lax.axis_size("wide")
-    groups = [
-        [base + spot * Y for spot in range(NGRP)] for base in range(size) if base & (Y | ZL) == 0
-    ]
     f_own = pack_first(structure, panel, first)
     other = swap_cores(lax.dynamic_index_in_dim(panel, 1 - n, 0, keepdims=False), "panel_swap")
     r_own = pack_rest(structure, panel, other, first)
-    with jax.named_scope("inverse_rows"):
-        own = lax.all_gather(inverse, "wide", axis_index_groups=groups)
     linv = squares(factor_inv)
+    a_z = hop(inverse, ZL, "inv_z")
+    a_y = hop(inverse, Y, "inv_y")
     f_z = hop(f_own, ZH, "first_z")
     f_x = hop(f_own, X, "first_x")
-    f_z, f_x, linv, *r_own = lax.optimization_barrier((f_z, f_x, linv, *r_own))
+    r_x0 = hop(r_own[0], X, "rest0_x")
+    a_y, a_z, f_z, f_x, r_x0, linv, *r_own = lax.optimization_barrier(
+        (a_y, a_z, f_z, f_x, r_x0, linv, *r_own)
+    )
     r_z0 = hop(r_own[0], ZH, "rest0_z")
     f_xz = hop(f_z, X, "first_xz")
-    r_x0 = hop(r_own[0], X, "rest0_x")
-    r_z0, f_xz, r_x0, own, *r_own = lax.optimization_barrier((r_z0, f_xz, r_x0, own, *r_own))
+    r_x1 = hop(r_own[1], X, "rest1_x")
+    a_yz = hop(a_z, Y, "inv_yz")
+    s_own = swap_cores(after(inverse, a_y), "inv_swap")
+    r_z0, f_xz, r_x1, a_yz, a_y, a_z, s_own, *r_own = lax.optimization_barrier(
+        (r_z0, f_xz, r_x1, a_yz, a_y, a_z, s_own, *r_own)
+    )
     r_z1 = hop(r_own[1], ZH, "rest1_z")
     r_xz0 = hop(r_z0, X, "rest0_xz")
-    r_x1 = hop(r_own[1], X, "rest1_x")
-    sel = pack_inverse(structure, own, swap_cores(own, "inverse_swap"), first)
+    owns = [inverse, a_y, a_z, a_yz]
+    others = [s_own] + [swap_cores(a, "inv_swap") for a in owns[1:]]
+    sel = pack_inverse(structure, owns, others, first)
 
     def deliver(kept, sent, c):
         messages = bundle(kept, swap_cores(sent, f"cross{c}_swap"))
@@ -458,13 +461,13 @@
         structure, sel, (f_z, f_xz), (r_z1, r_xz1), 1, near
     )
     held = assemble(messages, 0, None)
+    back = [swap_cores(total, "sums_swap") for total in (sent_sum0, sent_sum1)]
+    variance = place_sums(linv, (kept_sum0, kept_sum1), back)
+    for group in ((X, ZH, X | ZH), (Y, ZL, Y | ZL)):
+        variance = sum((hop(variance, mask, f"variance_{mask}") for mask in group), variance)
     held = assemble(deliver(kept, sent, 1), 1, held)
     half = panel.shape[2] * size // 2
     cross = held.reshape(half, 2, 2, LANES).transpose(0, 2, 1, 3).reshape(half, 2, BLK)
-    back = [swap_cores(total, "sums_swap") for total in (sent_sum0, sent_sum1)]
-    variance = place_sums(linv, (kept_sum0, kept_sum1), back)
-    for mask in (X, ZH, Y, ZL):
-        variance = variance + hop(variance, mask, f"variance_{mask}")
     return cross, variance
 
 

time: 175 us -> 146 us (0.83)
  between operations: 14.3 us -> 0.84 us
  waiting for transfers between devices: 99.1 us -> 91.3 us
  local copies, waits for them, and re-layouts: 6.89 us -> 1.46 us
  Pallas kernels: 21.5 us -> 17.3 us
    all_gather x1 -> x0, waiting for transfers between devices: 25.7 us -> none  [per_device_grid(): own = lax.all_gather(inverse, 'wide', axis_index_groups=groups)]
    ppermute x19 -> x24, waiting for transfers between devices: 66.5 us -> 86.8 us  [hop(): return lax.ppermute(value, 'wide', [(i, i ^ mask) for i in range(size)])]
    unnamed x24 -> x8, local copies, waits for them, and re-layouts: 5.45 us -> 0.02 us
    pallas_call x4, Pallas kernels: 15.7 us -> 11.4 us  [products(): pl.pallas_call(body, out_shape=outs if near is None else [outs[0], outs[0...]
    ppermute x6 -> x9, waiting for transfers between devices: 6.21 us -> 4.52 us  [swap_cores(): return lax.ppermute(value, 'narrow', [(0, 1), (1, 0)])]
    ppermute x19 -> x24, starting transfers between devices: 32.3 us -> 32.6 us  [hop(): return lax.ppermute(value, 'wide', [(i, i ^ mask) for i in range(size)])]
  transfers between devices with their start and end apart: 26 -> 33, of which waited for: 14 -> 17; matrix products, arithmetic and copies ran while one was open for 1% -> 0% of each run, Pallas kernels for 9% -> 9%
where the time goes in v5:
time: 146 us
  waiting for transfers between devices  91.3 us (63%)
  starting transfers between devices  34.5 us (24%)
  Pallas kernels  17.3 us (12%)
  local copies, waits for them, and re-layouts  1.46 us (1%)
    ppermute x24, waiting for transfers between devices, hop(): return lax.ppermute(value, 'wide', [(i, i ^ mask) for i in range(size)])  86.8 us
    ppermute x24, starting transfers between devices, hop(): return lax.ppermute(value, 'wide', [(i, i ^ mask) for i in range(size)])  32.6 us
    pallas_call x4, Pallas kernels, products(): pl.pallas_call(body, out_shape=outs if near is None else [outs[0], outs[0...  11.4 us
    ppermute x9, waiting for transfers between devices, swap_cores(): return lax.ppermute(value, 'narrow', [(0, 1), (1, 0)])  4.52 us
  transfers between devices with their start and end apart: 33, of which 17 were waited for; matrix products, arithmetic and copies ran while one was open for 0% of the time, Pallas kernels for 9%

profile of v5, /device:TPU:0, one launch (start us, length us, event | category | flops | bytes accessed | tf_op | source)
XLA Modules:
  0.0 146.1 jit_solution(2419161142839900112)
XLA Ops:
  2.6 2.6 %collective-permute-start = (bf16[256,2048]{1,0:T(8,128)(2,1)}, bf16[256,2048]{1,0:T(8,128)(2,1)S(1)}, u32[]{:S(2)}, u32[]{:S(2)}) collective-permute-start(bf16[256,2048]{1,0:T(8,128)(2,1)} %refs_0_.1), channel_id=1, source_target_pairs={{0,4},{2,6},{4,0},{6,2},{8,12},{10,14},{12,8},{14,10},{16,20},{18,... | collective-permute-start | bytes 3145736 | tf_op jit(solution)/shard_map/inv_y/ppermute | solution.py:104
  7.4 2.7 %collective-permute-start.2 = (bf16[1024,256]{1,0:T(8,128)(2,1)S(1)}, bf16[1024,256]{1,0:T(8,128)(2,1)S(1)}, u32[]{:S(2)}, u32[]{:S(2)}) collective-permute-start(bf16[1024,256]{1,0:T(8,128)(2,1)S(1)} %pack_first.1.f0), channel_id=1, source_target_pairs={{0,16},{2,18},{4,20},{6,22},{8,24},{10,26},{12,28},{14,30},{16,0},... | collective-permute-start | bytes 1572872 | tf_op jit(solution)/shard_map/first_z/ppermute | solution.py:104
  13.4 27.5 %collective-permute-done.2.f0 = bf16[1024,256]{1,0:T(8,128)(2,1)S(1)} collective-permute-done((bf16[1024,256]{1,0:T(8,128)(2,1)S(1)}, bf16[1024,256]{1,0:T(8,128)(2,1)S(1)}, u32[]{:S(2)}, u32[]{:S(2)}) %collective-permute-start.2) | collective-permute-done | bytes 524320 | tf_op jit(solution)/shard_map/first_z/ppermute | solution.py:104
  42.3 1.6 %collective-permute-start.7 = (bf16[1024,256]{1,0:T(8,128)(2,1)S(1)}, bf16[1024,256]{1,0:T(8,128)(2,1)S(1)}, u32[]{:S(2)}, u32[]{:S(2)}) collective-permute-start(bf16[1024,256]{1,0:T(8,128)(2,1)S(1)} %collective-permute-done.2.f0), channel_id=1, source_target_pairs={{0,2},{2,0},{4,6},{6,4},{8,10},{10,8},{12,14},{14,12},{16,18},{18,... | collective-permute-start | bytes 1572872 | tf_op jit(solution)/shard_map/first_xz/ppermute | solution.py:104
  44.0 2.6 %collective-permute-start.6 = (bf16[2048,128]{1,0:T(8,128)(2,1)S(1)}, bf16[2048,128]{1,0:T(8,128)(2,1)S(1)}, u32[]{:S(2)}, u32[]{:S(2)}) collective-permute-start(bf16[2048,128]{1,0:T(8,128)(2,1)S(1)} %get-tuple-element.63.r0), channel_id=1, source_target_pairs={{0,16},{2,18},{4,20},{6,22},{8,24},{10,26},{12,28},{14,30},{16,0},... | collective-permute-start | bytes 1572872 | tf_op jit(solution)/shard_map/rest0_z/ppermute | solution.py:104
  47.1 10.0 %collective-permute-done.7.f1 = bf16[1024,256]{1,0:T(8,128)(2,1)S(1)} collective-permute-done((bf16[1024,256]{1,0:T(8,128)(2,1)S(1)}, bf16[1024,256]{1,0:T(8,128)(2,1)S(1)}, u32[]{:S(2)}, u32[]{:S(2)}) %collective-permute-start.7) | collective-permute-done | bytes 524320 | tf_op jit(solution)/shard_map/first_xz/ppermute | solution.py:104
  57.1 12.7 %collective-permute-done.6.r0 = bf16[2048,128]{1,0:T(8,128)(2,1)S(1)} collective-permute-done((bf16[2048,128]{1,0:T(8,128)(2,1)S(1)}, bf16[2048,128]{1,0:T(8,128)(2,1)S(1)}, u32[]{:S(2)}, u32[]{:S(2)}) %collective-permute-start.6) | collective-permute-done | bytes 524320 | tf_op jit(solution)/shard_map/rest0_z/ppermute | solution.py:104
  75.5 1.8 %pack_inverse.1.sel_ref = bf16[4,256,3072]{2,1,0:T(8,128)(2,1)S(1)} custom-call(s32[2,12]{1,0:T(2,128)S(1)} %copy-done.3, bf16[256,2048]{1,0:T(8,128)(2,1)S(1)} %copy-done.2, bf16[256,2048]{1,0:T(8,128)(2,1)S(1)} %collective-permute-done.refs_1_, bf16[256,2048]{1,0:T(8,128)(2,1)S(1)} %collective-permute-done.1.refs_2_, ...), custom_call_target="tpu_custom_call" | custom-call | tf_op jit(solution)/shard_map/pack_inverse/pallas_call | solution.py:188
  77.4 2.8 %products.4 = (bf16[4,2,128,256]{3,2,1,0:T(8,128)(2,1)S(1)}, f32[2,1,128]{2,1,0:T(1,128)S(1)}) custom-call(s32[2,12]{1,0:T(2,128)S(1)} %copy-done.3, bf16[4,256,3072]{2,1,0:T(8,128)(2,1)S(1)} %pack_inverse.1.sel_ref, bf16[1024,256]{1,0:T(8,128)(2,1)S(1)} %pack_first.1.f0, bf16[1024,256]{1,0:T(8,128)(2,1)S(1)} %collective-permute-done.3.f1, ...), custom_call_target="tpu_custom_call" | custom-call | tf_op jit(solution)/shard_map/products/pallas_call | solution.py:285
  80.2 4.6 %collective-permute-done.16.r1 = bf16[2048,128]{1,0:T(8,128)(2,1)S(1)} collective-permute-done((bf16[2048,128]{1,0:T(8,128)(2,1)S(1)}, bf16[2048,128]{1,0:T(8,128)(2,1)S(1)}, u32[]{:S(2)}, u32[]{:S(2)}) %collective-permute-start.16) | collective-permute-done | bytes 524320 | tf_op jit(solution)/shard_map/rest0_xz/ppermute | solution.py:104
  84.7 2.9 %products.5 = (bf16[4,2,128,256]{3,2,1,0:T(8,128)(2,1)S(1)}, bf16[4,2,128,256]{3,2,1,0:T(8,128)(2,1)S(1)}, f32[2,1,128]{2,1,0:T(1,128)S(1)}, f32[2,1,128]{2,1,0:T(1,128)S(1)}) custom-call(s32[2,12]{1,0:T(2,128)S(1)} %copy-done.3, bf16[4,256,3072]{2,1,0:T(8,128)(2,1)S(1)} %pack_inverse.1.sel_ref, bf16[1024,256]{1,0:T(8,128)(2,1)S(1)} %collective-permute-done.2.f0, ...), custom_call_target="tpu_custom_call" | custom-call | tf_op jit(solution)/shard_map/products/pallas_call | solution.py:285
  87.7 9.4 %collective-permute-done.14.r0 = bf16[2048,128]{1,0:T(8,128)(2,1)S(1)} collective-permute-done((bf16[2048,128]{1,0:T(8,128)(2,1)S(1)}, bf16[2048,128]{1,0:T(8,128)(2,1)S(1)}, u32[]{:S(2)}, u32[]{:S(2)}) %collective-permute-start.14) | collective-permute-done | bytes 524320 | tf_op jit(solution)/shard_map/rest1_z/ppermute | solution.py:104
  100.3 2.0 %collective-permute-start.20 = (bf16[2,2,128,256]{3,2,1,0:T(8,128)(2,1)S(1)}, bf16[2,2,128,256]{3,2,1,0:T(8,128)(2,1)S(1)}, u32[]{:S(2)}, u32[]{:S(2)}) collective-permute-start(bf16[2,2,128,256]{3,2,1,0:T(8,128)(2,1)S(1)} %get-tuple-element.72), channel_id=1, source_target_pairs={{0,12},{2,14},{4,8},{6,10},{8,4},{10,6},{12,0},{14,2},{16,28},{18,... | collective-permute-start | bytes 786440 | tf_op jit(solution)/shard_map/cross0_3/ppermute | solution.py:104
  102.3 2.8 %products.6 = (bf16[4,2,128,256]{3,2,1,0:T(8,128)(2,1)S(1)}, f32[2,1,128]{2,1,0:T(1,128)S(1)}) custom-call(s32[2,12]{1,0:T(2,128)S(1)} %copy-done.3, bf16[4,256,3072]{2,1,0:T(8,128)(2,1)S(1)} %pack_inverse.1.sel_ref, bf16[1024,256]{1,0:T(8,128)(2,1)S(1)} %pack_first.1.f0, bf16[1024,256]{1,0:T(8,128)(2,1)S(1)} %collective-permute-done.3.f1, ...), custom_call_target="tpu_custom_call" | custom-call | tf_op jit(solution)/shard_map/products/pallas_call | solution.py:285
  105.1 5.2 %collective-permute-done.15.r1 = bf16[2048,128]{1,0:T(8,128)(2,1)S(1)} collective-permute-done((bf16[2048,128]{1,0:T(8,128)(2,1)S(1)}, bf16[2048,128]{1,0:T(8,128)(2,1)S(1)}, u32[]{:S(2)}, u32[]{:S(2)}) %collective-permute-start.15) | collective-permute-done | bytes 524320 | tf_op jit(solution)/shard_map/rest1_xz/ppermute | solution.py:104
  110.2 2.6 %collective-permute-done.20.refs_3_ = bf16[2,2,128,256]{3,2,1,0:T(8,128)(2,1)S(1)} collective-permute-done((bf16[2,2,128,256]{3,2,1,0:T(8,128)(2,1)S(1)}, bf16[2,2,128,256]{3,2,1,0:T(8,128)(2,1)S(1)}, u32[]{:S(2)}, u32[]{:S(2)}) %collective-permute-start.20) | collective-permute-done | bytes 262176 | tf_op jit(solution)/shard_map/cross0_3/ppermute | solution.py:104
  112.8 2.9 %products.7 = (bf16[4,2,128,256]{3,2,1,0:T(8,128)(2,1)S(1)}, bf16[4,2,128,256]{3,2,1,0:T(8,128)(2,1)S(1)}, f32[2,1,128]{2,1,0:T(1,128)S(1)}, f32[2,1,128]{2,1,0:T(1,128)S(1)}) custom-call(s32[2,12]{1,0:T(2,128)S(1)} %copy-done.3, bf16[4,256,3072]{2,1,0:T(8,128)(2,1)S(1)} %pack_inverse.1.sel_ref, bf16[1024,256]{1,0:T(8,128)(2,1)S(1)} %collective-permute-done.2.f0, ...), custom_call_target="tpu_custom_call" | custom-call | tf_op jit(solution)/shard_map/products/pallas_call | solution.py:285
  119.1 2.7 %collective-permute-start.28 = (f32[2,2048]{1,0:T(2,128)S(1)}, f32[2,2048]{1,0:T(2,128)S(1)}, u32[]{:S(2)}, u32[]{:S(2)}) collective-permute-start(f32[2,2048]{1,0:T(2,128)S(1)} %place_sums.1), channel_id=1, source_target_pairs={{0,16},{2,18},{4,20},{6,22},{8,24},{10,26},{12,28},{14,30},{16,0},... | collective-permute-start | bytes 49160 | tf_op jit(solution)/shard_map/variance_8/ppermute | solution.py:104
  123.8 3.6 %collective-permute-done.29 = f32[2,2048]{1,0:T(2,128)S(1)} collective-permute-done((f32[2,2048]{1,0:T(2,128)S(1)}, f32[2,2048]{1,0:T(2,128)S(1)}, u32[]{:S(2)}, u32[]{:S(2)}) %collective-permute-start.29) | collective-permute-done | bytes 16416 | tf_op jit(solution)/shard_map/variance_9/ppermute | solution.py:104
  129.0 1.7 %collective-permute-start.31 = (f32[2,2048]{1,0:T(2,128)S(1)}, f32[2,2048]{1,0:T(2,128)S(1)}, u32[]{:S(2)}, u32[]{:S(2)}) collective-permute-start(f32[2,2048]{1,0:T(2,128)S(1)} %add_add_fusion.1), channel_id=1, source_target_pairs={{0,8},{2,10},{4,12},{6,14},{8,0},{10,2},{12,4},{14,6},{16,24},{18,... | collective-permute-start | bytes 49160 | tf_op jit(solution)/shard_map/variance_4/ppermute | solution.py:104
  132.1 1.6 %collective-permute-start.22 = (bf16[2,2,128,256]{3,2,1,0:T(8,128)(2,1)S(1)}, bf16[2,2,128,256]{3,2,1,0:T(8,128)(2,1)S(1)}, u32[]{:S(2)}, u32[]{:S(2)}) collective-permute-start(bf16[2,2,128,256]{3,2,1,0:T(8,128)(2,1)S(1)} %get-tuple-element.80), channel_id=1, source_target_pairs={{0,4},{2,6},{4,0},{6,2},{8,12},{10,14},{12,8},{14,10},{16,20},{18,... | collective-permute-start | bytes 786440 | tf_op jit(solution)/shard_map/cross1_1/ppermute | solution.py:104
  133.7 1.7 %collective-permute-start.23 = (bf16[2,2,128,256]{3,2,1,0:T(8,128)(2,1)S(1)}, bf16[2,2,128,256]{3,2,1,0:T(8,128)(2,1)S(1)}, u32[]{:S(2)}, u32[]{:S(2)}) collective-permute-start(bf16[2,2,128,256]{3,2,1,0:T(8,128)(2,1)S(1)} %get-tuple-element.81), channel_id=1, source_target_pairs={{0,8},{2,10},{4,12},{6,14},{8,0},{10,2},{12,4},{14,6},{16,24},{18,... | collective-permute-start | bytes 786440 | tf_op jit(solution)/shard_map/cross1_2/ppermute | solution.py:104
  136.3 4.9 %collective-permute-done.22.refs_1_ = bf16[2,2,128,256]{3,2,1,0:T(8,128)(2,1)S(1)} collective-permute-done((bf16[2,2,128,256]{3,2,1,0:T(8,128)(2,1)S(1)}, bf16[2,2,128,256]{3,2,1,0:T(8,128)(2,1)S(1)}, u32[]{:S(2)}, u32[]{:S(2)}) %collective-permute-start.22) | collective-permute-done | bytes 262176 | tf_op jit(solution)/shard_map/cross1_1/ppermute | solution.py:104
  142.2 2.8 %collective-permute-done.24.refs_3_ = bf16[2,2,128,256]{3,2,1,0:T(8,128)(2,1)S(1)} collective-permute-done((bf16[2,2,128,256]{3,2,1,0:T(8,128)(2,1)S(1)}, bf16[2,2,128,256]{3,2,1,0:T(8,128)(2,1)S(1)}, u32[]{:S(2)}, u32[]{:S(2)}) %collective-permute-start.24) | collective-permute-done | bytes 262176 | tf_op jit(solution)/shard_map/cross1_3/ppermute | solution.py:104
  (66 shorter events, 29.6 us)
Async XLA Ops:
  2.1 9.5 %collective-permute-start.4 = (bf16[2048,256]{1,0:T(8,128)(2,1)S(1)}, bf16[2048,256]{1,0:T(8,128)(2,1)S(1)}, u32[]{:S(2)}, u32[]{:S(2)}) collective-permute-start(bf16[2048,256]{1,0:T(8,128)(2,1)S(1)} %dynamic-slice_bitcast_fusion), channel_id=1, source_target_pairs={{0,1},{1,0},{2,3},{3,2},{4,5},{5,4},{6,7},{7,6},{8,9},{9,8},{10,11... | collective-permute-start | bytes 3145736 | tf_op jit(solution)/shard_map/panel_swap/ppermute | solution.py:98
  2.6 38.4 %collective-permute-start = (bf16[256,2048]{1,0:T(8,128)(2,1)}, bf16[256,2048]{1,0:T(8,128)(2,1)S(1)}, u32[]{:S(2)}, u32[]{:S(2)}) collective-permute-start(bf16[256,2048]{1,0:T(8,128)(2,1)} %refs_0_.1), channel_id=1, source_target_pairs={{0,4},{2,6},{4,0},{6,2},{8,12},{10,14},{12,8},{14,10},{16,20},{18,... | collective-permute-start | bytes 3145736 | tf_op jit(solution)/shard_map/inv_y/ppermute | solution.py:104
  5.2 36.7 %collective-permute-start.1 = (bf16[256,2048]{1,0:T(8,128)(2,1)}, bf16[256,2048]{1,0:T(8,128)(2,1)S(1)}, u32[]{:S(2)}, u32[]{:S(2)}) collective-permute-start(bf16[256,2048]{1,0:T(8,128)(2,1)} %refs_0_.1), channel_id=1, source_target_pairs={{0,8},{2,10},{4,12},{6,14},{8,0},{10,2},{12,4},{14,6},{16,24},{18,... | collective-permute-start | bytes 3145736 | tf_op jit(solution)/shard_map/inv_z/ppermute | solution.py:104
  7.4 33.5 %collective-permute-start.2 = (bf16[1024,256]{1,0:T(8,128)(2,1)S(1)}, bf16[1024,256]{1,0:T(8,128)(2,1)S(1)}, u32[]{:S(2)}, u32[]{:S(2)}) collective-permute-start(bf16[1024,256]{1,0:T(8,128)(2,1)S(1)} %pack_first.1.f0), channel_id=1, source_target_pairs={{0,16},{2,18},{4,20},{6,22},{8,24},{10,26},{12,28},{14,30},{16,0},... | collective-permute-start | bytes 1572872 | tf_op jit(solution)/shard_map/first_z/ppermute | solution.py:104
  10.1 30.9 %collective-permute-start.3 = (bf16[1024,256]{1,0:T(8,128)(2,1)S(1)}, bf16[1024,256]{1,0:T(8,128)(2,1)S(1)}, u32[]{:S(2)}, u32[]{:S(2)}) collective-permute-start(bf16[1024,256]{1,0:T(8,128)(2,1)S(1)} %pack_first.1.f0), channel_id=1, source_target_pairs={{0,2},{2,0},{4,6},{6,4},{8,10},{10,8},{12,14},{14,12},{16,18},{18,... | collective-permute-start | bytes 1572872 | tf_op jit(solution)/shard_map/first_x/ppermute | solution.py:104
  12.5 29.4 %collective-permute-start.5 = (bf16[2048,128]{1,0:T(8,128)(2,1)S(1)}, bf16[2048,128]{1,0:T(8,128)(2,1)S(1)}, u32[]{:S(2)}, u32[]{:S(2)}) collective-permute-start(bf16[2048,128]{1,0:T(8,128)(2,1)S(1)} %get-tuple-element.63.r0), channel_id=1, source_target_pairs={{0,2},{2,0},{4,6},{6,4},{8,10},{10,8},{12,14},{14,12},{16,18},{18,... | collective-permute-start | bytes 1572872 | tf_op jit(solution)/shard_map/rest0_x/ppermute | solution.py:104
  41.9 27.9 %collective-permute-start.10 = (bf16[256,2048]{1,0:T(8,128)(2,1)S(1)}, bf16[256,2048]{1,0:T(8,128)(2,1)S(1)}, u32[]{:S(2)}, u32[]{:S(2)}) collective-permute-start(bf16[256,2048]{1,0:T(8,128)(2,1)S(1)} %copy-done.2), channel_id=1, source_target_pairs={{0,1},{1,0},{2,3},{3,2},{4,5},{5,4},{6,7},{7,6},{8,9},{9,8},{10,11... | collective-permute-start | bytes 3145736 | tf_op jit(solution)/shard_map/inv_swap/ppermute | solution.py:98
  41.9 27.9 %collective-permute-start.9 = (bf16[256,2048]{1,0:T(8,128)(2,1)S(1)}, bf16[256,2048]{1,0:T(8,128)(2,1)S(1)}, u32[]{:S(2)}, u32[]{:S(2)}) collective-permute-start(bf16[256,2048]{1,0:T(8,128)(2,1)S(1)} %collective-permute-done.1.refs_2_), channel_id=1, source_target_pairs={{0,4},{2,6},{4,0},{6,2},{8,12},{10,14},{12,8},{14,10},{16,20},{18,... | collective-permute-start | bytes 3145736 | tf_op jit(solution)/shard_map/inv_yz/ppermute | solution.py:104
  42.3 14.8 %collective-permute-start.7 = (bf16[1024,256]{1,0:T(8,128)(2,1)S(1)}, bf16[1024,256]{1,0:T(8,128)(2,1)S(1)}, u32[]{:S(2)}, u32[]{:S(2)}) collective-permute-start(bf16[1024,256]{1,0:T(8,128)(2,1)S(1)} %collective-permute-done.2.f0), channel_id=1, source_target_pairs={{0,2},{2,0},{4,6},{6,4},{8,10},{10,8},{12,14},{14,12},{16,18},{18,... | collective-permute-start | bytes 1572872 | tf_op jit(solution)/shard_map/first_xz/ppermute | solution.py:104
  44.0 25.8 %collective-permute-start.6 = (bf16[2048,128]{1,0:T(8,128)(2,1)S(1)}, bf16[2048,128]{1,0:T(8,128)(2,1)S(1)}, u32[]{:S(2)}, u32[]{:S(2)}) collective-permute-start(bf16[2048,128]{1,0:T(8,128)(2,1)S(1)} %get-tuple-element.63.r0), channel_id=1, source_target_pairs={{0,16},{2,18},{4,20},{6,22},{8,24},{10,26},{12,28},{14,30},{16,0},... | collective-permute-start | bytes 1572872 | tf_op jit(solution)/shard_map/rest0_z/ppermute | solution.py:104
  46.5 23.3 %collective-permute-start.8 = (bf16[2048,128]{1,0:T(8,128)(2,1)S(1)}, bf16[2048,128]{1,0:T(8,128)(2,1)S(1)}, u32[]{:S(2)}, u32[]{:S(2)}) collective-permute-start(bf16[2048,128]{1,0:T(8,128)(2,1)S(1)} %get-tuple-element.60.r0), channel_id=1, source_target_pairs={{0,2},{2,0},{4,6},{6,4},{8,10},{10,8},{12,14},{14,12},{16,18},{18,... | collective-permute-start | bytes 1572872 | tf_op jit(solution)/shard_map/rest1_x/ppermute | solution.py:104
  70.5 14.3 %collective-permute-start.16 = (bf16[2048,128]{1,0:T(8,128)(2,1)S(1)}, bf16[2048,128]{1,0:T(8,128)(2,1)S(1)}, u32[]{:S(2)}, u32[]{:S(2)}) collective-permute-start(bf16[2048,128]{1,0:T(8,128)(2,1)S(1)} %collective-permute-done.6.r0), channel_id=1, source_target_pairs={{0,2},{2,0},{4,6},{6,4},{8,10},{10,8},{12,14},{14,12},{16,18},{18,... | collective-permute-start | bytes 1572872 | tf_op jit(solution)/shard_map/rest0_xz/ppermute | solution.py:104
  70.9 26.1 %collective-permute-start.14 = (bf16[2048,128]{1,0:T(8,128)(2,1)S(1)}, bf16[2048,128]{1,0:T(8,128)(2,1)S(1)}, u32[]{:S(2)}, u32[]{:S(2)}) collective-permute-start(bf16[2048,128]{1,0:T(8,128)(2,1)S(1)} %get-tuple-element.60.r0), channel_id=1, source_target_pairs={{0,16},{2,18},{4,20},{6,22},{8,24},{10,26},{12,28},{14,30},{16,0},... | collective-permute-start | bytes 1572872 | tf_op jit(solution)/shard_map/rest1_z/ppermute | solution.py:104
  87.6 11.0 %collective-permute-start.17 = (bf16[4,2,128,256]{3,2,1,0:T(8,128)(2,1)S(1)}, bf16[4,2,128,256]{3,2,1,0:T(8,128)(2,1)S(1)}, u32[]{:S(2)}, u32[]{:S(2)}) collective-permute-start(bf16[4,2,128,256]{3,2,1,0:T(8,128)(2,1)S(1)} %get-tuple-element.68), channel_id=1, source_target_pairs={{0,1},{1,0},{2,3},{3,2},{4,5},{5,4},{6,7},{7,6},{8,9},{9,8},{10,11... | collective-permute-start | bytes 1572872 | tf_op jit(solution)/shard_map/cross0_swap/ppermute | solution.py:98
  97.1 13.2 %collective-permute-start.15 = (bf16[2048,128]{1,0:T(8,128)(2,1)S(1)}, bf16[2048,128]{1,0:T(8,128)(2,1)S(1)}, u32[]{:S(2)}, u32[]{:S(2)}) collective-permute-start(bf16[2048,128]{1,0:T(8,128)(2,1)S(1)} %collective-permute-done.14.r0), channel_id=1, source_target_pairs={{0,2},{2,0},{4,6},{6,4},{8,10},{10,8},{12,14},{14,12},{16,18},{18,... | collective-permute-start | bytes 1572872 | tf_op jit(solution)/shard_map/rest1_xz/ppermute | solution.py:104
  98.7 11.5 %collective-permute-start.18 = (bf16[2,2,128,256]{3,2,1,0:T(8,128)(2,1)S(1)}, bf16[2,2,128,256]{3,2,1,0:T(8,128)(2,1)S(1)}, u32[]{:S(2)}, u32[]{:S(2)}) collective-permute-start(bf16[2,2,128,256]{3,2,1,0:T(8,128)(2,1)S(1)} %get-tuple-element.70), channel_id=1, source_target_pairs={{0,4},{2,6},{4,0},{6,2},{8,12},{10,14},{12,8},{14,10},{16,20},{18,... | collective-permute-start | bytes 786440 | tf_op jit(solution)/shard_map/cross0_1/ppermute | solution.py:104
  100.3 10.0 %collective-permute-start.19 = (bf16[2,2,128,256]{3,2,1,0:T(8,128)(2,1)S(1)}, bf16[2,2,128,256]{3,2,1,0:T(8,128)(2,1)S(1)}, u32[]{:S(2)}, u32[]{:S(2)}) collective-permute-start(bf16[2,2,128,256]{3,2,1,0:T(8,128)(2,1)S(1)} %get-tuple-element.71), channel_id=1, source_target_pairs={{0,8},{2,10},{4,12},{6,14},{8,0},{10,2},{12,4},{14,6},{16,24},{18,... | collective-permute-start | bytes 786440 | tf_op jit(solution)/shard_map/cross0_2/ppermute | solution.py:104
  100.3 12.5 %collective-permute-start.20 = (bf16[2,2,128,256]{3,2,1,0:T(8,128)(2,1)S(1)}, bf16[2,2,128,256]{3,2,1,0:T(8,128)(2,1)S(1)}, u32[]{:S(2)}, u32[]{:S(2)}) collective-permute-start(bf16[2,2,128,256]{3,2,1,0:T(8,128)(2,1)S(1)} %get-tuple-element.72), channel_id=1, source_target_pairs={{0,12},{2,14},{4,8},{6,10},{8,4},{10,6},{12,0},{14,2},{16,28},{18,... | collective-permute-start | bytes 786440 | tf_op jit(solution)/shard_map/cross0_3/ppermute | solution.py:104
  115.7 16.3 %collective-permute-start.21 = (bf16[4,2,128,256]{3,2,1,0:T(8,128)(2,1)S(1)}, bf16[4,2,128,256]{3,2,1,0:T(8,128)(2,1)S(1)}, u32[]{:S(2)}, u32[]{:S(2)}) collective-permute-start(bf16[4,2,128,256]{3,2,1,0:T(8,128)(2,1)S(1)} %get-tuple-element.78), channel_id=1, source_target_pairs={{0,1},{1,0},{2,3},{3,2},{4,5},{5,4},{6,7},{7,6},{8,9},{9,8},{10,11... | collective-permute-start | bytes 1572872 | tf_op jit(solution)/shard_map/cross1_swap/ppermute | solution.py:98
  127.4 8.1 %collective-permute-start.30 = (f32[2,2048]{1,0:T(2,128)S(1)}, f32[2,2048]{1,0:T(2,128)S(1)}, u32[]{:S(2)}, u32[]{:S(2)}) collective-permute-start(f32[2,2048]{1,0:T(2,128)S(1)} %add_add_fusion.1), channel_id=1, source_target_pairs={{0,4},{2,6},{4,0},{6,2},{8,12},{10,14},{12,8},{14,10},{16,20},{18,... | collective-permute-start | bytes 49160 | tf_op jit(solution)/shard_map/variance_2/ppermute | solution.py:104
  129.0 6.7 %collective-permute-start.31 = (f32[2,2048]{1,0:T(2,128)S(1)}, f32[2,2048]{1,0:T(2,128)S(1)}, u32[]{:S(2)}, u32[]{:S(2)}) collective-permute-start(f32[2,2048]{1,0:T(2,128)S(1)} %add_add_fusion.1), channel_id=1, source_target_pairs={{0,8},{2,10},{4,12},{6,14},{8,0},{10,2},{12,4},{14,6},{16,24},{18,... | collective-permute-start | bytes 49160 | tf_op jit(solution)/shard_map/variance_4/ppermute | solution.py:104
  132.1 9.1 %collective-permute-start.22 = (bf16[2,2,128,256]{3,2,1,0:T(8,128)(2,1)S(1)}, bf16[2,2,128,256]{3,2,1,0:T(8,128)(2,1)S(1)}, u32[]{:S(2)}, u32[]{:S(2)}) collective-permute-start(bf16[2,2,128,256]{3,2,1,0:T(8,128)(2,1)S(1)} %get-tuple-element.80), channel_id=1, source_target_pairs={{0,4},{2,6},{4,0},{6,2},{8,12},{10,14},{12,8},{14,10},{16,20},{18,... | collective-permute-start | bytes 786440 | tf_op jit(solution)/shard_map/cross1_1/ppermute | solution.py:104
  133.7 8.5 %collective-permute-start.23 = (bf16[2,2,128,256]{3,2,1,0:T(8,128)(2,1)S(1)}, bf16[2,2,128,256]{3,2,1,0:T(8,128)(2,1)S(1)}, u32[]{:S(2)}, u32[]{:S(2)}) collective-permute-start(bf16[2,2,128,256]{3,2,1,0:T(8,128)(2,1)S(1)} %get-tuple-element.81), channel_id=1, source_target_pairs={{0,8},{2,10},{4,12},{6,14},{8,0},{10,2},{12,4},{14,6},{16,24},{18,... | collective-permute-start | bytes 786440 | tf_op jit(solution)/shard_map/cross1_2/ppermute | solution.py:104
  135.4 9.6 %collective-permute-start.24 = (bf16[2,2,128,256]{3,2,1,0:T(8,128)(2,1)S(1)}, bf16[2,2,128,256]{3,2,1,0:T(8,128)(2,1)S(1)}, u32[]{:S(2)}, u32[]{:S(2)}) collective-permute-start(bf16[2,2,128,256]{3,2,1,0:T(8,128)(2,1)S(1)} %get-tuple-element.82), channel_id=1, source_target_pairs={{0,12},{2,14},{4,8},{6,10},{8,4},{10,6},{12,0},{14,2},{16,28},{18,... | collective-permute-start | bytes 786440 | tf_op jit(solution)/shard_map/cross1_3/ppermute | solution.py:104
  (13 other events, 87.4 us)

commit v6 on v5

--- a/solution.py
+++ b/solution.py
@@ -461,11 +461,14 @@
         structure, sel, (f_z, f_xz), (r_z1, r_xz1), 1, near
     )
     held = assemble(messages, 0, None)
-    back = [swap_cores(total, "sums_swap") for total in (sent_sum0, sent_sum1)]
+    messages = deliver(kept, sent, 1)
+    back = [
+        swap_cores(after(total, messages[0]), "sums_swap") for total in (sent_sum0, sent_sum1)
+    ]
+    held = assemble(messages, 1, held)
     variance = place_sums(linv, (kept_sum0, kept_sum1), back)
-    for group in ((X, ZH, X | ZH), (Y, ZL, Y | ZL)):
-        variance = sum((hop(variance, mask, f"variance_{mask}") for mask in group), variance)
-    held = assemble(deliver(kept, sent, 1), 1, held)
+    for mask in (X, ZH, Y, ZL):
+        variance = variance + hop(variance, mask, f"variance_{mask}")
     half = panel.shape[2] * size // 2
     cross = held.reshape(half, 2, 2, LANES).transpose(0, 2, 1, 3).reshape(half, 2, BLK)
     return cross, variance

time: 146 us -> 143 us (0.979)
  waiting for transfers between devices: 91.3 us -> 86.6 us
  starting transfers between devices: 34.5 us -> 36.5 us
    ppermute x24 -> x22, waiting for transfers between devices: 86.8 us -> 80.6 us  [hop(): return lax.ppermute(value, 'wide', [(i, i ^ mask) for i in range(size)])]
    ppermute x24 -> x22, starting transfers between devices: 32.6 us -> 34.1 us  [hop(): return lax.ppermute(value, 'wide', [(i, i ^ mask) for i in range(size)])]
  transfers between devices with their start and end apart: 33 -> 31, of which waited for: 17 -> 18; matrix products, arithmetic and copies ran while one was open for 0% -> 0% of each run, Pallas kernels for 9% -> 9%
where the time goes in v6:
time: 143 us
  waiting for transfers between devices  86.6 us (61%)
  starting transfers between devices  36.5 us (26%)
  Pallas kernels  17.3 us (12%)
  local copies, waits for them, and re-layouts  1.46 us (1%)
    ppermute x22, waiting for transfers between devices, hop(): return lax.ppermute(value, 'wide', [(i, i ^ mask) for i in range(size)])  80.6 us
    ppermute x22, starting transfers between devices, hop(): return lax.ppermute(value, 'wide', [(i, i ^ mask) for i in range(size)])  34.1 us
    pallas_call x4, Pallas kernels, products(): pl.pallas_call(body, out_shape=outs if near is None else [outs[0], outs[0...  11.3 us
    ppermute x9, waiting for transfers between devices, swap_cores(): return lax.ppermute(value, 'narrow', [(0, 1), (1, 0)])  5.91 us
  transfers between devices with their start and end apart: 31, of which 18 were waited for; matrix products, arithmetic and copies ran while one was open for 0% of the time, Pallas kernels for 9%

profile of v6, /device:TPU:0, one launch (start us, length us, event | category | flops | bytes accessed | tf_op | source)
XLA Modules:
  0.0 143.3 jit_solution(7157941160352715676)
XLA Ops:
  2.6 2.6 %collective-permute-start = (bf16[256,2048]{1,0:T(8,128)(2,1)}, bf16[256,2048]{1,0:T(8,128)(2,1)S(1)}, u32[]{:S(2)}, u32[]{:S(2)}) collective-permute-start(bf16[256,2048]{1,0:T(8,128)(2,1)} %refs_0_.1), channel_id=1, source_target_pairs={{0,4},{2,6},{4,0},{6,2},{8,12},{10,14},{12,8},{14,10},{16,20},{18,... | collective-permute-start | bytes 3145736 | tf_op jit(solution)/shard_map/inv_y/ppermute | solution.py:104
  7.4 2.7 %collective-permute-start.2 = (bf16[1024,256]{1,0:T(8,128)(2,1)S(1)}, bf16[1024,256]{1,0:T(8,128)(2,1)S(1)}, u32[]{:S(2)}, u32[]{:S(2)}) collective-permute-start(bf16[1024,256]{1,0:T(8,128)(2,1)S(1)} %pack_first.1.f0), channel_id=1, source_target_pairs={{0,16},{2,18},{4,20},{6,22},{8,24},{10,26},{12,28},{14,30},{16,0},... | collective-permute-start | bytes 1572872 | tf_op jit(solution)/shard_map/first_z/ppermute | solution.py:104
  13.4 27.5 %collective-permute-done.2.f0 = bf16[1024,256]{1,0:T(8,128)(2,1)S(1)} collective-permute-done((bf16[1024,256]{1,0:T(8,128)(2,1)S(1)}, bf16[1024,256]{1,0:T(8,128)(2,1)S(1)}, u32[]{:S(2)}, u32[]{:S(2)}) %collective-permute-start.2) | collective-permute-done | bytes 524320 | tf_op jit(solution)/shard_map/first_z/ppermute | solution.py:104
  42.3 1.6 %collective-permute-start.7 = (bf16[1024,256]{1,0:T(8,128)(2,1)S(1)}, bf16[1024,256]{1,0:T(8,128)(2,1)S(1)}, u32[]{:S(2)}, u32[]{:S(2)}) collective-permute-start(bf16[1024,256]{1,0:T(8,128)(2,1)S(1)} %collective-permute-done.2.f0), channel_id=1, source_target_pairs={{0,2},{2,0},{4,6},{6,4},{8,10},{10,8},{12,14},{14,12},{16,18},{18,... | collective-permute-start | bytes 1572872 | tf_op jit(solution)/shard_map/first_xz/ppermute | solution.py:104
  44.0 2.6 %collective-permute-start.6 = (bf16[2048,128]{1,0:T(8,128)(2,1)S(1)}, bf16[2048,128]{1,0:T(8,128)(2,1)S(1)}, u32[]{:S(2)}, u32[]{:S(2)}) collective-permute-start(bf16[2048,128]{1,0:T(8,128)(2,1)S(1)} %get-tuple-element.65.r0), channel_id=1, source_target_pairs={{0,16},{2,18},{4,20},{6,22},{8,24},{10,26},{12,28},{14,30},{16,0},... | collective-permute-start | bytes 1572872 | tf_op jit(solution)/shard_map/rest0_z/ppermute | solution.py:104
  47.1 10.0 %collective-permute-done.7.f1 = bf16[1024,256]{1,0:T(8,128)(2,1)S(1)} collective-permute-done((bf16[1024,256]{1,0:T(8,128)(2,1)S(1)}, bf16[1024,256]{1,0:T(8,128)(2,1)S(1)}, u32[]{:S(2)}, u32[]{:S(2)}) %collective-permute-start.7) | collective-permute-done | bytes 524320 | tf_op jit(solution)/shard_map/first_xz/ppermute | solution.py:104
  57.1 12.7 %collective-permute-done.6.r0 = bf16[2048,128]{1,0:T(8,128)(2,1)S(1)} collective-permute-done((bf16[2048,128]{1,0:T(8,128)(2,1)S(1)}, bf16[2048,128]{1,0:T(8,128)(2,1)S(1)}, u32[]{:S(2)}, u32[]{:S(2)}) %collective-permute-start.6) | collective-permute-done | bytes 524320 | tf_op jit(solution)/shard_map/rest0_z/ppermute | solution.py:104
  75.5 1.8 %pack_inverse.1.sel_ref = bf16[4,256,3072]{2,1,0:T(8,128)(2,1)S(1)} custom-call(s32[2,12]{1,0:T(2,128)S(1)} %copy-done.3, bf16[256,2048]{1,0:T(8,128)(2,1)S(1)} %copy-done.2, bf16[256,2048]{1,0:T(8,128)(2,1)S(1)} %collective-permute-done.refs_1_, bf16[256,2048]{1,0:T(8,128)(2,1)S(1)} %collective-permute-done.1.refs_2_, ...), custom_call_target="tpu_custom_call" | custom-call | tf_op jit(solution)/shard_map/pack_inverse/pallas_call | solution.py:188
  77.4 2.8 %products.4 = (bf16[4,2,128,256]{3,2,1,0:T(8,128)(2,1)S(1)}, f32[2,1,128]{2,1,0:T(1,128)S(1)}) custom-call(s32[2,12]{1,0:T(2,128)S(1)} %copy-done.3, bf16[4,256,3072]{2,1,0:T(8,128)(2,1)S(1)} %pack_inverse.1.sel_ref, bf16[1024,256]{1,0:T(8,128)(2,1)S(1)} %pack_first.1.f0, bf16[1024,256]{1,0:T(8,128)(2,1)S(1)} %collective-permute-done.3.f1, ...), custom_call_target="tpu_custom_call" | custom-call | tf_op jit(solution)/shard_map/products/pallas_call | solution.py:285
  80.2 4.6 %collective-permute-done.16.r1 = bf16[2048,128]{1,0:T(8,128)(2,1)S(1)} collective-permute-done((bf16[2048,128]{1,0:T(8,128)(2,1)S(1)}, bf16[2048,128]{1,0:T(8,128)(2,1)S(1)}, u32[]{:S(2)}, u32[]{:S(2)}) %collective-permute-start.16) | collective-permute-done | bytes 524320 | tf_op jit(solution)/shard_map/rest0_xz/ppermute | solution.py:104
  84.7 2.9 %products.5 = (bf16[4,2,128,256]{3,2,1,0:T(8,128)(2,1)S(1)}, bf16[4,2,128,256]{3,2,1,0:T(8,128)(2,1)S(1)}, f32[2,1,128]{2,1,0:T(1,128)S(1)}, f32[2,1,128]{2,1,0:T(1,128)S(1)}) custom-call(s32[2,12]{1,0:T(2,128)S(1)} %copy-done.3, bf16[4,256,3072]{2,1,0:T(8,128)(2,1)S(1)} %pack_inverse.1.sel_ref, bf16[1024,256]{1,0:T(8,128)(2,1)S(1)} %collective-permute-done.2.f0, ...), custom_call_target="tpu_custom_call" | custom-call | tf_op jit(solution)/shard_map/products/pallas_call | solution.py:285
  88.2 8.8 %collective-permute-done.14.r0 = bf16[2048,128]{1,0:T(8,128)(2,1)S(1)} collective-permute-done((bf16[2048,128]{1,0:T(8,128)(2,1)S(1)}, bf16[2048,128]{1,0:T(8,128)(2,1)S(1)}, u32[]{:S(2)}, u32[]{:S(2)}) %collective-permute-start.14) | collective-permute-done | bytes 524320 | tf_op jit(solution)/shard_map/rest1_z/ppermute | solution.py:104
  100.3 2.0 %collective-permute-start.20 = (bf16[2,2,128,256]{3,2,1,0:T(8,128)(2,1)S(1)}, bf16[2,2,128,256]{3,2,1,0:T(8,128)(2,1)S(1)}, u32[]{:S(2)}, u32[]{:S(2)}) collective-permute-start(bf16[2,2,128,256]{3,2,1,0:T(8,128)(2,1)S(1)} %get-tuple-element.74), channel_id=1, source_target_pairs={{0,12},{2,14},{4,8},{6,10},{8,4},{10,6},{12,0},{14,2},{16,28},{18,... | collective-permute-start | bytes 786440 | tf_op jit(solution)/shard_map/cross0_3/ppermute | solution.py:104
  102.3 2.8 %products.6 = (bf16[4,2,128,256]{3,2,1,0:T(8,128)(2,1)S(1)}, f32[2,1,128]{2,1,0:T(1,128)S(1)}) custom-call(s32[2,12]{1,0:T(2,128)S(1)} %copy-done.3, bf16[4,256,3072]{2,1,0:T(8,128)(2,1)S(1)} %pack_inverse.1.sel_ref, bf16[1024,256]{1,0:T(8,128)(2,1)S(1)} %pack_first.1.f0, bf16[1024,256]{1,0:T(8,128)(2,1)S(1)} %collective-permute-done.3.f1, ...), custom_call_target="tpu_custom_call" | custom-call | tf_op jit(solution)/shard_map/products/pallas_call | solution.py:285
  105.1 5.2 %collective-permute-done.15.r1 = bf16[2048,128]{1,0:T(8,128)(2,1)S(1)} collective-permute-done((bf16[2048,128]{1,0:T(8,128)(2,1)S(1)}, bf16[2048,128]{1,0:T(8,128)(2,1)S(1)}, u32[]{:S(2)}, u32[]{:S(2)}) %collective-permute-start.15) | collective-permute-done | bytes 524320 | tf_op jit(solution)/shard_map/rest1_xz/ppermute | solution.py:104
  110.2 2.6 %collective-permute-done.20.refs_3_ = bf16[2,2,128,256]{3,2,1,0:T(8,128)(2,1)S(1)} collective-permute-done((bf16[2,2,128,256]{3,2,1,0:T(8,128)(2,1)S(1)}, bf16[2,2,128,256]{3,2,1,0:T(8,128)(2,1)S(1)}, u32[]{:S(2)}, u32[]{:S(2)}) %collective-permute-start.20) | collective-permute-done | bytes 262176 | tf_op jit(solution)/shard_map/cross0_3/ppermute | solution.py:104
  112.8 2.9 %products.7 = (bf16[4,2,128,256]{3,2,1,0:T(8,128)(2,1)S(1)}, bf16[4,2,128,256]{3,2,1,0:T(8,128)(2,1)S(1)}, f32[2,1,128]{2,1,0:T(1,128)S(1)}, f32[2,1,128]{2,1,0:T(1,128)S(1)}) custom-call(s32[2,12]{1,0:T(2,128)S(1)} %copy-done.3, bf16[4,256,3072]{2,1,0:T(8,128)(2,1)S(1)} %pack_inverse.1.sel_ref, bf16[1024,256]{1,0:T(8,128)(2,1)S(1)} %collective-permute-done.2.f0, ...), custom_call_target="tpu_custom_call" | custom-call | tf_op jit(solution)/shard_map/products/pallas_call | solution.py:285
  115.8 1.9 %collective-permute-done.21.back_ref = bf16[4,2,128,256]{3,2,1,0:T(8,128)(2,1)S(1)} collective-permute-done((bf16[4,2,128,256]{3,2,1,0:T(8,128)(2,1)S(1)}, bf16[4,2,128,256]{3,2,1,0:T(8,128)(2,1)S(1)}, u32[]{:S(2)}, u32[]{:S(2)}) %collective-permute-start.21) | collective-permute-done | bytes 524320 | tf_op jit(solution)/shard_map/cross1_swap/ppermute | solution.py:98
  119.6 1.7 %collective-permute-start.24 = (bf16[2,2,128,256]{3,2,1,0:T(8,128)(2,1)S(1)}, bf16[2,2,128,256]{3,2,1,0:T(8,128)(2,1)S(1)}, u32[]{:S(2)}, u32[]{:S(2)}) collective-permute-start(bf16[2,2,128,256]{3,2,1,0:T(8,128)(2,1)S(1)} %get-tuple-element.84), channel_id=1, source_target_pairs={{0,12},{2,14},{4,8},{6,10},{8,4},{10,6},{12,0},{14,2},{16,28},{18,... | collective-permute-start | bytes 786440 | tf_op jit(solution)/shard_map/cross1_3/ppermute | solution.py:104
  123.2 3.3 %collective-permute-done.27 = f32[2,2048]{1,0:T(2,128)S(1)} collective-permute-done((f32[2,2048]{1,0:T(2,128)S(1)}, f32[2,2048]{1,0:T(2,128)S(1)}, u32[]{:S(2)}, u32[]{:S(2)}) %collective-permute-start.27) | collective-permute-done | bytes 16416 | tf_op jit(solution)/shard_map/variance_1/ppermute | solution.py:104
  126.5 2.6 %collective-permute-start.28 = (f32[2,2048]{1,0:T(2,128)S(1)}, f32[2,2048]{1,0:T(2,128)S(1)}, u32[]{:S(2)}, u32[]{:S(2)}) collective-permute-start(f32[2,2048]{1,0:T(2,128)S(1)} %add.18), channel_id=1, source_target_pairs={{0,16},{2,18},{4,20},{6,22},{8,24},{10,26},{12,28},{14,30},{16,0},... | collective-permute-start | bytes 49160 | tf_op jit(solution)/shard_map/variance_8/ppermute | solution.py:104
  129.1 2.2 %collective-permute-done.28 = f32[2,2048]{1,0:T(2,128)S(1)} collective-permute-done((f32[2,2048]{1,0:T(2,128)S(1)}, f32[2,2048]{1,0:T(2,128)S(1)}, u32[]{:S(2)}, u32[]{:S(2)}) %collective-permute-start.28) | collective-permute-done | bytes 16416 | tf_op jit(solution)/shard_map/variance_8/ppermute | solution.py:104
  132.9 2.2 %collective-permute-done.29 = f32[2,2048]{1,0:T(2,128)S(1)} collective-permute-done((f32[2,2048]{1,0:T(2,128)S(1)}, f32[2,2048]{1,0:T(2,128)S(1)}, u32[]{:S(2)}, u32[]{:S(2)}) %collective-permute-start.29) | collective-permute-done | bytes 16416 | tf_op jit(solution)/shard_map/variance_2/ppermute | solution.py:104
  135.1 4.7 %collective-permute-start.30 = (f32[2,2048]{1,0:T(2,128)S(1)}, f32[2,2048]{1,0:T(2,128)S(1)}, u32[]{:S(2)}, u32[]{:S(2)}) collective-permute-start(f32[2,2048]{1,0:T(2,128)S(1)} %add.20), channel_id=1, source_target_pairs={{0,8},{2,10},{4,12},{6,14},{8,0},{10,2},{12,4},{14,6},{16,24},{18,... | collective-permute-start | bytes 49160 | tf_op jit(solution)/shard_map/variance_4/ppermute | solution.py:104
  (64 shorter events, 27.9 us)
Async XLA Ops:
  2.1 9.5 %collective-permute-start.4 = (bf16[2048,256]{1,0:T(8,128)(2,1)S(1)}, bf16[2048,256]{1,0:T(8,128)(2,1)S(1)}, u32[]{:S(2)}, u32[]{:S(2)}) collective-permute-start(bf16[2048,256]{1,0:T(8,128)(2,1)S(1)} %dynamic-slice_bitcast_fusion), channel_id=1, source_target_pairs={{0,1},{1,0},{2,3},{3,2},{4,5},{5,4},{6,7},{7,6},{8,9},{9,8},{10,11... | collective-permute-start | bytes 3145736 | tf_op jit(solution)/shard_map/panel_swap/ppermute | solution.py:98
  2.6 38.4 %collective-permute-start = (bf16[256,2048]{1,0:T(8,128)(2,1)}, bf16[256,2048]{1,0:T(8,128)(2,1)S(1)}, u32[]{:S(2)}, u32[]{:S(2)}) collective-permute-start(bf16[256,2048]{1,0:T(8,128)(2,1)} %refs_0_.1), channel_id=1, source_target_pairs={{0,4},{2,6},{4,0},{6,2},{8,12},{10,14},{12,8},{14,10},{16,20},{18,... | collective-permute-start | bytes 3145736 | tf_op jit(solution)/shard_map/inv_y/ppermute | solution.py:104
  5.2 36.7 %collective-permute-start.1 = (bf16[256,2048]{1,0:T(8,128)(2,1)}, bf16[256,2048]{1,0:T(8,128)(2,1)S(1)}, u32[]{:S(2)}, u32[]{:S(2)}) collective-permute-start(bf16[256,2048]{1,0:T(8,128)(2,1)} %refs_0_.1), channel_id=1, source_target_pairs={{0,8},{2,10},{4,12},{6,14},{8,0},{10,2},{12,4},{14,6},{16,24},{18,... | collective-permute-start | bytes 3145736 | tf_op jit(solution)/shard_map/inv_z/ppermute | solution.py:104
  7.4 33.5 %collective-permute-start.2 = (bf16[1024,256]{1,0:T(8,128)(2,1)S(1)}, bf16[1024,256]{1,0:T(8,128)(2,1)S(1)}, u32[]{:S(2)}, u32[]{:S(2)}) collective-permute-start(bf16[1024,256]{1,0:T(8,128)(2,1)S(1)} %pack_first.1.f0), channel_id=1, source_target_pairs={{0,16},{2,18},{4,20},{6,22},{8,24},{10,26},{12,28},{14,30},{16,0},... | collective-permute-start | bytes 1572872 | tf_op jit(solution)/shard_map/first_z/ppermute | solution.py:104
  10.1 30.9 %collective-permute-start.3 = (bf16[1024,256]{1,0:T(8,128)(2,1)S(1)}, bf16[1024,256]{1,0:T(8,128)(2,1)S(1)}, u32[]{:S(2)}, u32[]{:S(2)}) collective-permute-start(bf16[1024,256]{1,0:T(8,128)(2,1)S(1)} %pack_first.1.f0), channel_id=1, source_target_pairs={{0,2},{2,0},{4,6},{6,4},{8,10},{10,8},{12,14},{14,12},{16,18},{18,... | collective-permute-start | bytes 1572872 | tf_op jit(solution)/shard_map/first_x/ppermute | solution.py:104
  12.5 29.4 %collective-permute-start.5 = (bf16[2048,128]{1,0:T(8,128)(2,1)S(1)}, bf16[2048,128]{1,0:T(8,128)(2,1)S(1)}, u32[]{:S(2)}, u32[]{:S(2)}) collective-permute-start(bf16[2048,128]{1,0:T(8,128)(2,1)S(1)} %get-tuple-element.65.r0), channel_id=1, source_target_pairs={{0,2},{2,0},{4,6},{6,4},{8,10},{10,8},{12,14},{14,12},{16,18},{18,... | collective-permute-start | bytes 1572872 | tf_op jit(solution)/shard_map/rest0_x/ppermute | solution.py:104
  41.9 27.9 %collective-permute-start.10 = (bf16[256,2048]{1,0:T(8,128)(2,1)S(1)}, bf16[256,2048]{1,0:T(8,128)(2,1)S(1)}, u32[]{:S(2)}, u32[]{:S(2)}) collective-permute-start(bf16[256,2048]{1,0:T(8,128)(2,1)S(1)} %copy-done.2), channel_id=1, source_target_pairs={{0,1},{1,0},{2,3},{3,2},{4,5},{5,4},{6,7},{7,6},{8,9},{9,8},{10,11... | collective-permute-start | bytes 3145736 | tf_op jit(solution)/shard_map/inv_swap/ppermute | solution.py:98
  41.9 27.9 %collective-permute-start.9 = (bf16[256,2048]{1,0:T(8,128)(2,1)S(1)}, bf16[256,2048]{1,0:T(8,128)(2,1)S(1)}, u32[]{:S(2)}, u32[]{:S(2)}) collective-permute-start(bf16[256,2048]{1,0:T(8,128)(2,1)S(1)} %collective-permute-done.1.refs_2_), channel_id=1, source_target_pairs={{0,4},{2,6},{4,0},{6,2},{8,12},{10,14},{12,8},{14,10},{16,20},{18,... | collective-permute-start | bytes 3145736 | tf_op jit(solution)/shard_map/inv_yz/ppermute | solution.py:104
  42.3 14.8 %collective-permute-start.7 = (bf16[1024,256]{1,0:T(8,128)(2,1)S(1)}, bf16[1024,256]{1,0:T(8,128)(2,1)S(1)}, u32[]{:S(2)}, u32[]{:S(2)}) collective-permute-start(bf16[1024,256]{1,0:T(8,128)(2,1)S(1)} %collective-permute-done.2.f0), channel_id=1, source_target_pairs={{0,2},{2,0},{4,6},{6,4},{8,10},{10,8},{12,14},{14,12},{16,18},{18,... | collective-permute-start | bytes 1572872 | tf_op jit(solution)/shard_map/first_xz/ppermute | solution.py:104
  44.0 25.8 %collective-permute-start.6 = (bf16[2048,128]{1,0:T(8,128)(2,1)S(1)}, bf16[2048,128]{1,0:T(8,128)(2,1)S(1)}, u32[]{:S(2)}, u32[]{:S(2)}) collective-permute-start(bf16[2048,128]{1,0:T(8,128)(2,1)S(1)} %get-tuple-element.65.r0), channel_id=1, source_target_pairs={{0,16},{2,18},{4,20},{6,22},{8,24},{10,26},{12,28},{14,30},{16,0},... | collective-permute-start | bytes 1572872 | tf_op jit(solution)/shard_map/rest0_z/ppermute | solution.py:104
  46.5 23.3 %collective-permute-start.8 = (bf16[2048,128]{1,0:T(8,128)(2,1)S(1)}, bf16[2048,128]{1,0:T(8,128)(2,1)S(1)}, u32[]{:S(2)}, u32[]{:S(2)}) collective-permute-start(bf16[2048,128]{1,0:T(8,128)(2,1)S(1)} %get-tuple-element.62.r0), channel_id=1, source_target_pairs={{0,2},{2,0},{4,6},{6,4},{8,10},{10,8},{12,14},{14,12},{16,18},{18,... | collective-permute-start | bytes 1572872 | tf_op jit(solution)/shard_map/rest1_x/ppermute | solution.py:104
  70.4 5.1 %collective-permute-start.13 = (bf16[256,2048]{1,0:T(8,128)(2,1)S(1)}, bf16[256,2048]{1,0:T(8,128)(2,1)S(1)}, u32[]{:S(2)}, u32[]{:S(2)}) collective-permute-start(bf16[256,2048]{1,0:T(8,128)(2,1)S(1)} %collective-permute-done.9.refs_3_), channel_id=1, source_target_pairs={{0,1},{1,0},{2,3},{3,2},{4,5},{5,4},{6,7},{7,6},{8,9},{9,8},{10,11... | collective-permute-start | bytes 3145736 | tf_op jit(solution)/shard_map/inv_swap/ppermute | solution.py:98
  70.5 14.3 %collective-permute-start.16 = (bf16[2048,128]{1,0:T(8,128)(2,1)S(1)}, bf16[2048,128]{1,0:T(8,128)(2,1)S(1)}, u32[]{:S(2)}, u32[]{:S(2)}) collective-permute-start(bf16[2048,128]{1,0:T(8,128)(2,1)S(1)} %collective-permute-done.6.r0), channel_id=1, source_target_pairs={{0,2},{2,0},{4,6},{6,4},{8,10},{10,8},{12,14},{14,12},{16,18},{18,... | collective-permute-start | bytes 1572872 | tf_op jit(solution)/shard_map/rest0_xz/ppermute | solution.py:104
  70.9 26.1 %collective-permute-start.14 = (bf16[2048,128]{1,0:T(8,128)(2,1)S(1)}, bf16[2048,128]{1,0:T(8,128)(2,1)S(1)}, u32[]{:S(2)}, u32[]{:S(2)}) collective-permute-start(bf16[2048,128]{1,0:T(8,128)(2,1)S(1)} %get-tuple-element.62.r0), channel_id=1, source_target_pairs={{0,16},{2,18},{4,20},{6,22},{8,24},{10,26},{12,28},{14,30},{16,0},... | collective-permute-start | bytes 1572872 | tf_op jit(solution)/shard_map/rest1_z/ppermute | solution.py:104
  87.6 11.0 %collective-permute-start.17 = (bf16[4,2,128,256]{3,2,1,0:T(8,128)(2,1)S(1)}, bf16[4,2,128,256]{3,2,1,0:T(8,128)(2,1)S(1)}, u32[]{:S(2)}, u32[]{:S(2)}) collective-permute-start(bf16[4,2,128,256]{3,2,1,0:T(8,128)(2,1)S(1)} %get-tuple-element.70), channel_id=1, source_target_pairs={{0,1},{1,0},{2,3},{3,2},{4,5},{5,4},{6,7},{7,6},{8,9},{9,8},{10,11... | collective-permute-start | bytes 1572872 | tf_op jit(solution)/shard_map/cross0_swap/ppermute | solution.py:98
  97.1 13.2 %collective-permute-start.15 = (bf16[2048,128]{1,0:T(8,128)(2,1)S(1)}, bf16[2048,128]{1,0:T(8,128)(2,1)S(1)}, u32[]{:S(2)}, u32[]{:S(2)}) collective-permute-start(bf16[2048,128]{1,0:T(8,128)(2,1)S(1)} %collective-permute-done.14.r0), channel_id=1, source_target_pairs={{0,2},{2,0},{4,6},{6,4},{8,10},{10,8},{12,14},{14,12},{16,18},{18,... | collective-permute-start | bytes 1572872 | tf_op jit(solution)/shard_map/rest1_xz/ppermute | solution.py:104
  98.7 11.5 %collective-permute-start.18 = (bf16[2,2,128,256]{3,2,1,0:T(8,128)(2,1)S(1)}, bf16[2,2,128,256]{3,2,1,0:T(8,128)(2,1)S(1)}, u32[]{:S(2)}, u32[]{:S(2)}) collective-permute-start(bf16[2,2,128,256]{3,2,1,0:T(8,128)(2,1)S(1)} %get-tuple-element.72), channel_id=1, source_target_pairs={{0,4},{2,6},{4,0},{6,2},{8,12},{10,14},{12,8},{14,10},{16,20},{18,... | collective-permute-start | bytes 786440 | tf_op jit(solution)/shard_map/cross0_1/ppermute | solution.py:104
  100.3 10.0 %collective-permute-start.19 = (bf16[2,2,128,256]{3,2,1,0:T(8,128)(2,1)S(1)}, bf16[2,2,128,256]{3,2,1,0:T(8,128)(2,1)S(1)}, u32[]{:S(2)}, u32[]{:S(2)}) collective-permute-start(bf16[2,2,128,256]{3,2,1,0:T(8,128)(2,1)S(1)} %get-tuple-element.73), channel_id=1, source_target_pairs={{0,8},{2,10},{4,12},{6,14},{8,0},{10,2},{12,4},{14,6},{16,24},{18,... | collective-permute-start | bytes 786440 | tf_op jit(solution)/shard_map/cross0_2/ppermute | solution.py:104
  100.3 12.5 %collective-permute-start.20 = (bf16[2,2,128,256]{3,2,1,0:T(8,128)(2,1)S(1)}, bf16[2,2,128,256]{3,2,1,0:T(8,128)(2,1)S(1)}, u32[]{:S(2)}, u32[]{:S(2)}) collective-permute-start(bf16[2,2,128,256]{3,2,1,0:T(8,128)(2,1)S(1)} %get-tuple-element.74), channel_id=1, source_target_pairs={{0,12},{2,14},{4,8},{6,10},{8,4},{10,6},{12,0},{14,2},{16,28},{18,... | collective-permute-start | bytes 786440 | tf_op jit(solution)/shard_map/cross0_3/ppermute | solution.py:104
  117.8 24.4 %collective-permute-start.22 = (bf16[2,2,128,256]{3,2,1,0:T(8,128)(2,1)S(1)}, bf16[2,2,128,256]{3,2,1,0:T(8,128)(2,1)S(1)}, u32[]{:S(2)}, u32[]{:S(2)}) collective-permute-start(bf16[2,2,128,256]{3,2,1,0:T(8,128)(2,1)S(1)} %get-tuple-element.82), channel_id=1, source_target_pairs={{0,4},{2,6},{4,0},{6,2},{8,12},{10,14},{12,8},{14,10},{16,20},{18,... | collective-permute-start | bytes 786440 | tf_op jit(solution)/shard_map/cross1_1/ppermute | solution.py:104
  119.4 22.8 %collective-permute-start.23 = (bf16[2,2,128,256]{3,2,1,0:T(8,128)(2,1)S(1)}, bf16[2,2,128,256]{3,2,1,0:T(8,128)(2,1)S(1)}, u32[]{:S(2)}, u32[]{:S(2)}) collective-permute-start(bf16[2,2,128,256]{3,2,1,0:T(8,128)(2,1)S(1)} %get-tuple-element.83), channel_id=1, source_target_pairs={{0,8},{2,10},{4,12},{6,14},{8,0},{10,2},{12,4},{14,6},{16,24},{18,... | collective-permute-start | bytes 786440 | tf_op jit(solution)/shard_map/cross1_2/ppermute | solution.py:104
  119.6 22.6 %collective-permute-start.24 = (bf16[2,2,128,256]{3,2,1,0:T(8,128)(2,1)S(1)}, bf16[2,2,128,256]{3,2,1,0:T(8,128)(2,1)S(1)}, u32[]{:S(2)}, u32[]{:S(2)}) collective-permute-start(bf16[2,2,128,256]{3,2,1,0:T(8,128)(2,1)S(1)} %get-tuple-element.84), channel_id=1, source_target_pairs={{0,12},{2,14},{4,8},{6,10},{8,4},{10,6},{12,0},{14,2},{16,28},{18,... | collective-permute-start | bytes 786440 | tf_op jit(solution)/shard_map/cross1_3/ppermute | solution.py:104
  126.5 4.8 %collective-permute-start.28 = (f32[2,2048]{1,0:T(2,128)S(1)}, f32[2,2048]{1,0:T(2,128)S(1)}, u32[]{:S(2)}, u32[]{:S(2)}) collective-permute-start(f32[2,2048]{1,0:T(2,128)S(1)} %add.18), channel_id=1, source_target_pairs={{0,16},{2,18},{4,20},{6,22},{8,24},{10,26},{12,28},{14,30},{16,0},... | collective-permute-start | bytes 49160 | tf_op jit(solution)/shard_map/variance_8/ppermute | solution.py:104
  135.1 6.4 %collective-permute-start.30 = (f32[2,2048]{1,0:T(2,128)S(1)}, f32[2,2048]{1,0:T(2,128)S(1)}, u32[]{:S(2)}, u32[]{:S(2)}) collective-permute-start(f32[2,2048]{1,0:T(2,128)S(1)} %add.20), channel_id=1, source_target_pairs={{0,8},{2,10},{4,12},{6,14},{8,0},{10,2},{12,4},{14,6},{16,24},{18,... | collective-permute-start | bytes 49160 | tf_op jit(solution)/shard_map/variance_4/ppermute | solution.py:104
  (11 other events, 71.4 us)

commit v7 on v6

--- a/solution.py
+++ b/solution.py
@@ -90,6 +90,7 @@
 
 X, Y, ZL, ZH = 1, 2, 4, 8
 NGRP = 4
+SPLIT = 192
 MIB = 1024 * 1024
 
 
@@ -114,23 +115,30 @@
     return structure_ref[n, lax.rem(start + j, nblocks)]
 
 
-def pack_first(structure, panel, first):
+def pack_first(structure, panel, inverse, first):
     half_blocks = panel.shape[1] // BLK
 
-    def body(st, panel_ref, out):
+    def body(st, panel_ref, inv_ref, out, *pieces):
         n = lax.axis_index("narrow")
         for j in range(first):
             row = pl.multiple_of(lax.rem(pick(st, n, j, first), half_blocks) * BLK, BLK)
             out[j * BLK : (j + 1) * BLK, :] = panel_ref[n, pl.ds(row, BLK), :]
-
-    return pl.pallas_call(
-        body,
-        out_shape=jax.ShapeDtypeStruct((first * BLK, panel.shape[2]), panel.dtype),
-        in_specs=[SMEM, VMEM],
-        out_specs=VMEM,
-        compiler_params=pltpu.CompilerParams(vmem_limit_bytes=6 * MIB),
+        pieces[0][...] = inv_ref[:SPLIT, :]
+        pieces[1][...] = inv_ref[SPLIT:, :]
+
+    width = inverse.shape[1]
+    return pl.pallas_call(
+        body,
+        out_shape=[
+            jax.ShapeDtypeStruct((first * BLK, panel.shape[2]), panel.dtype),
+            jax.ShapeDtypeStruct((SPLIT, width), inverse.dtype),
+            jax.ShapeDtypeStruct((BLK - SPLIT, width), inverse.dtype),
+        ],
+        in_specs=[SMEM, VMEM, VMEM],
+        out_specs=[VMEM] * 3,
+        compiler_params=pltpu.CompilerParams(vmem_limit_bytes=8 * MIB),
         name="pack_first",
-    )(structure, panel)
+    )(structure, panel, inverse)
 
 
 def pack_rest(structure, panel, other, first):
@@ -166,12 +174,39 @@
     )(structure, panel, other)
 
 
+def stack_rows(pieces):
+    rows = sum(piece.shape[0] for piece in pieces)
+
+    def body(*refs):
+        at = 0
+        for ref in refs[:-1]:
+            refs[-1][at : at + ref.shape[0], :] = ref[...]
+            at += ref.shape[0]
+
+    return pl.pallas_call(
+        body,
+        out_shape=jax.ShapeDtypeStruct((rows, pieces[0].shape[1]), pieces[0].dtype),
+        in_specs=[VMEM] * len(pieces),
+        out_specs=VMEM,
+        compiler_params=pltpu.CompilerParams(vmem_limit_bytes=8 * MIB),
+        name="stack_rows",
+    )(*pieces)
+
+
 def pack_inverse(structure, owns, others, first):
     nblocks = structure.shape[1]
     half_blocks = owns[0].shape[1] // BLK
+    count = len(owns)
+    runs, row = [], 0
+    for p, own in enumerate(owns):
+        at = 0
+        while at < own.shape[0]:
+            rows = min(own.shape[0] - at, BLK - row % BLK)
+            runs.append((p, at, row // BLK, row % BLK, rows))
+            at, row = at + rows, row + rows
 
     def body(st, *refs):
-        own_refs, oth_refs, out = refs[:NGRP], refs[NGRP : 2 * NGRP], refs[2 * NGRP]
+        out = refs[2 * count]
         n = lax.axis_index("narrow")
         for j in range(nblocks):
             b = pick(st, n, j, first)
@@ -179,16 +214,18 @@
             mine = lax.div(b, half_blocks) == n
 
             def move(sources, j=j, col=col):
-                for d in range(NGRP):
-                    out[d, :, j * BLK : (j + 1) * BLK] = sources[d][:, pl.ds(col, BLK)]
-
-            pl.when(mine)(lambda move=move: move(own_refs))
-            pl.when(jnp.logical_not(mine))(lambda move=move: move(oth_refs))
+                for p, at, d, top, rows in runs:
+                    out[d, top : top + rows, j * BLK : (j + 1) * BLK] = sources[p][
+                        at : at + rows, pl.ds(col, BLK)
+                    ]
+
+            pl.when(mine)(lambda move=move: move(refs[:count]))
+            pl.when(jnp.logical_not(mine))(lambda move=move: move(refs[count : 2 * count]))
 
     return pl.pallas_call(
         body,
         out_shape=jax.ShapeDtypeStruct((NGRP, BLK, nblocks * BLK), owns[0].dtype),
-        in_specs=[SMEM] + [VMEM] * (2 * NGRP),
+        in_specs=[SMEM] + [VMEM] * (2 * count),
         out_specs=VMEM,
         compiler_params=pltpu.CompilerParams(vmem_limit_bytes=18 * MIB),
         name="pack_inverse",
@@ -417,31 +454,35 @@
     n = lax.axis_index("narrow")
     first = structure.shape[1] - panel.shape[1] // BLK
     size = lax.axis_size("wide")
-    f_own = pack_first(structure, panel, first)
+    f_own, top, bottom = pack_first(structure, panel, inverse, first)
     other = swap_cores(lax.dynamic_index_in_dim(panel, 1 - n, 0, keepdims=False), "panel_swap")
     r_own = pack_rest(structure, panel, other, first)
     linv = squares(factor_inv)
-    a_z = hop(inverse, ZL, "inv_z")
-    a_y = hop(inverse, Y, "inv_y")
     f_z = hop(f_own, ZH, "first_z")
     f_x = hop(f_own, X, "first_x")
+    a_z0 = hop(top, ZL, "inv_z0")
+    a_y = hop(inverse, Y, "inv_y")
     r_x0 = hop(r_own[0], X, "rest0_x")
-    a_y, a_z, f_z, f_x, r_x0, linv, *r_own = lax.optimization_barrier(
-        (a_y, a_z, f_z, f_x, r_x0, linv, *r_own)
+    a_y, a_z0, f_z, f_x, r_x0, linv, *r_own = lax.optimization_barrier(
+        (a_y, a_z0, f_z, f_x, r_x0, linv, *r_own)
     )
     r_z0 = hop(r_own[0], ZH, "rest0_z")
+    a_z1 = hop(after(bottom, f_z), ZL, "inv_z1")
     f_xz = hop(f_z, X, "first_xz")
-    r_x1 = hop(r_own[1], X, "rest1_x")
-    a_yz = hop(a_z, Y, "inv_yz")
-    s_own = swap_cores(after(inverse, a_y), "inv_swap")
-    r_z0, f_xz, r_x1, a_yz, a_y, a_z, s_own, *r_own = lax.optimization_barrier(
-        (r_z0, f_xz, r_x1, a_yz, a_y, a_z, s_own, *r_own)
+    a_yz0 = hop(a_z0, Y, "inv_yz0")
+    a_yz1 = hop(a_z1, Y, "inv_yz1")
+    most = stack_rows([inverse, a_y, a_z0])
+    s_most = swap_cores(most, "inv_swap")
+    r_z0, f_xz, a_z1, a_yz0, a_yz1, s_most, *r_own = lax.optimization_barrier(
+        (r_z0, f_xz, a_z1, a_yz0, a_yz1, s_most, *r_own)
     )
     r_z1 = hop(r_own[1], ZH, "rest1_z")
     r_xz0 = hop(r_z0, X, "rest0_xz")
-    owns = [inverse, a_y, a_z, a_yz]
-    others = [s_own] + [swap_cores(a, "inv_swap") for a in owns[1:]]
-    sel = pack_inverse(structure, owns, others, first)
+    r_x1 = hop(r_own[1], X, "rest1_x")
+    more = stack_rows([a_z1, a_yz0, a_yz1])
+    s_more = swap_cores(more, "inv_swap_more")
+    sel = pack_inverse(structure, (most, more), (s_most, s_more), first)
+    r_z1, r_x1 = lax.optimization_barrier((r_z1, r_x1))
 
     def deliver(kept, sent, c):
         messages = bundle(kept, swap_cores(sent, f"cross{c}_swap"))

time: 143 us -> 140 us (0.979)
  waiting for transfers between devices: 86.6 us -> 79.6 us
  starting transfers between devices: 36.5 us -> 38 us
    ppermute x22 -> x24, waiting for transfers between devices: 80.6 us -> 76.2 us  [hop(): return lax.ppermute(value, 'wide', [(i, i ^ mask) for i in range(size)])]
    ppermute x9 -> x7, waiting for transfers between devices: 5.91 us -> 3.47 us  [swap_cores(): return lax.ppermute(value, 'narrow', [(0, 1), (1, 0)])]
    ppermute x22 -> x24, starting transfers between devices: 34.1 us -> 35.5 us  [hop(): return lax.ppermute(value, 'wide', [(i, i ^ mask) for i in range(size)])]
  transfers between devices with their start and end apart: 31 -> 31, of which waited for: 18 -> 17; matrix products, arithmetic and copies ran while one was open for 0% -> 0% of each run, Pallas kernels for 9% -> 10%
where the time goes in v7:
time: 140 us
  waiting for transfers between devices  79.6 us (57%)
  starting transfers between devices  38 us (27%)
  Pallas kernels  17.7 us (13%)
  local copies, waits for them, and re-layouts  2.71 us (2%)
    ppermute x24, waiting for transfers between devices, hop(): return lax.ppermute(value, 'wide', [(i, i ^ mask) for i in range(size)])  76.2 us
    ppermute x24, starting transfers between devices, hop(): return lax.ppermute(value, 'wide', [(i, i ^ mask) for i in range(size)])  35.5 us
    pallas_call x4, Pallas kernels, products(): pl.pallas_call(body, out_shape=outs if near is None else [outs[0], outs[0...  11.4 us
    ppermute x7, waiting for transfers between devices, swap_cores(): return lax.ppermute(value, 'narrow', [(0, 1), (1, 0)])  3.47 us
  transfers between devices with their start and end apart: 31, of which 17 were waited for; matrix products, arithmetic and copies ran while one was open for 0% of the time, Pallas kernels for 10%

profile of v7, /device:TPU:0, one launch (start us, length us, event | category | flops | bytes accessed | tf_op | source)
XLA Modules:
  0.0 139.5 jit_solution(9717895072019910942)
XLA Ops:
  2.6 2.6 %collective-permute-start = (bf16[256,2048]{1,0:T(8,128)(2,1)}, bf16[256,2048]{1,0:T(8,128)(2,1)S(1)}, u32[]{:S(2)}, u32[]{:S(2)}) collective-permute-start(bf16[256,2048]{1,0:T(8,128)(2,1)} %refs_0_.1), channel_id=1, source_target_pairs={{0,4},{2,6},{4,0},{6,2},{8,12},{10,14},{12,8},{14,10},{16,20},{18,... | collective-permute-start | bytes 3145736 | tf_op jit(solution)/shard_map/inv_y/ppermute | solution.py:105
  7.1 1.6 %collective-permute-start.1 = (bf16[192,2048]{1,0:T(8,128)(2,1)S(1)}, bf16[192,2048]{1,0:T(8,128)(2,1)S(1)}, u32[]{:S(2)}, u32[]{:S(2)}) collective-permute-start(bf16[192,2048]{1,0:T(8,128)(2,1)S(1)} %get-tuple-element.53), channel_id=1, source_target_pairs={{0,8},{2,10},{4,12},{6,14},{8,0},{10,2},{12,4},{14,6},{16,24},{18,... | collective-permute-start | bytes 2359304 | tf_op jit(solution)/shard_map/inv_z0/ppermute | solution.py:105
  8.8 2.6 %collective-permute-start.2 = (bf16[1024,256]{1,0:T(8,128)(2,1)S(1)}, bf16[1024,256]{1,0:T(8,128)(2,1)S(1)}, u32[]{:S(2)}, u32[]{:S(2)}) collective-permute-start(bf16[1024,256]{1,0:T(8,128)(2,1)S(1)} %get-tuple-element.54.f0), channel_id=1, source_target_pairs={{0,16},{2,18},{4,20},{6,22},{8,24},{10,26},{12,28},{14,30},{16,0},... | collective-permute-start | bytes 1572872 | tf_op jit(solution)/shard_map/first_z/ppermute | solution.py:105
  14.7 22.4 %collective-permute-done.2.f0 = bf16[1024,256]{1,0:T(8,128)(2,1)S(1)} collective-permute-done((bf16[1024,256]{1,0:T(8,128)(2,1)S(1)}, bf16[1024,256]{1,0:T(8,128)(2,1)S(1)}, u32[]{:S(2)}, u32[]{:S(2)}) %collective-permute-start.2) | collective-permute-done | bytes 524320 | tf_op jit(solution)/shard_map/first_z/ppermute | solution.py:105
  38.7 2.8 %collective-permute-start.8 = (bf16[64,2048]{1,0:T(8,128)(2,1)S(1)}, bf16[64,2048]{1,0:T(8,128)(2,1)S(1)}, u32[]{:S(2)}, u32[]{:S(2)}) collective-permute-start(bf16[64,2048]{1,0:T(8,128)(2,1)S(1)} %get-tuple-element.62), channel_id=1, source_target_pairs={{0,8},{2,10},{4,12},{6,14},{8,0},{10,2},{12,4},{14,6},{16,24},{18,... | collective-permute-start | bytes 786440 | tf_op jit(solution)/shard_map/inv_z1/ppermute | solution.py:105
  44.6 8.0 %collective-permute-done.8.refs_0_ = bf16[64,2048]{1,0:T(8,128)(2,1)S(1)} collective-permute-done((bf16[64,2048]{1,0:T(8,128)(2,1)S(1)}, bf16[64,2048]{1,0:T(8,128)(2,1)S(1)}, u32[]{:S(2)}, u32[]{:S(2)}) %collective-permute-start.8) | collective-permute-done | bytes 262176 | tf_op jit(solution)/shard_map/inv_z1/ppermute | solution.py:105
  54.1 9.9 %collective-permute-done.10.refs_2_ = bf16[64,2048]{1,0:T(8,128)(2,1)S(1)} collective-permute-done((bf16[64,2048]{1,0:T(8,128)(2,1)S(1)}, bf16[64,2048]{1,0:T(8,128)(2,1)S(1)}, u32[]{:S(2)}, u32[]{:S(2)}) %collective-permute-start.10) | collective-permute-done | bytes 262176 | tf_op jit(solution)/shard_map/inv_yz1/ppermute | solution.py:105
  63.9 3.5 %collective-permute-done.6.r0 = bf16[2048,128]{1,0:T(8,128)(2,1)S(1)} collective-permute-done((bf16[2048,128]{1,0:T(8,128)(2,1)S(1)}, bf16[2048,128]{1,0:T(8,128)(2,1)S(1)}, u32[]{:S(2)}, u32[]{:S(2)}) %collective-permute-start.6) | collective-permute-done | bytes 524320 | tf_op jit(solution)/shard_map/rest0_z/ppermute | solution.py:105
  70.6 1.9 %pack_inverse.1.sel_ref = bf16[4,256,3072]{2,1,0:T(8,128)(2,1)S(1)} custom-call(s32[2,12]{1,0:T(2,128)S(1)} %copy-done.4, bf16[704,2048]{1,0:T(8,128)(2,1)S(1)} %stack_rows.2.refs_0_, bf16[320,2048]{1,0:T(8,128)(2,1)S(1)} %stack_rows.3.refs_1_, bf16[704,2048]{1,0:T(8,128)(2,1)S(1)} %collective-permute-done.11.refs_2_, ...), custom_call_target="tpu_custom_call" | custom-call | tf_op jit(solution)/shard_map/pack_inverse/pallas_call | solution.py:225
  72.5 2.8 %products.4 = (bf16[4,2,128,256]{3,2,1,0:T(8,128)(2,1)S(1)}, f32[2,1,128]{2,1,0:T(1,128)S(1)}) custom-call(s32[2,12]{1,0:T(2,128)S(1)} %copy-done.4, bf16[4,256,3072]{2,1,0:T(8,128)(2,1)S(1)} %pack_inverse.1.sel_ref, bf16[1024,256]{1,0:T(8,128)(2,1)S(1)} %get-tuple-element.54.f0, bf16[1024,256]{1,0:T(8,128)(2,1)S(1)} %collective-permute-done.3.f1, ...), custom_call_target="tpu_custom_call" | custom-call | tf_op jit(solution)/shard_map/products/pallas_call | solution.py:322
  75.3 7.1 %collective-permute-done.16.r1 = bf16[2048,128]{1,0:T(8,128)(2,1)S(1)} collective-permute-done((bf16[2048,128]{1,0:T(8,128)(2,1)S(1)}, bf16[2048,128]{1,0:T(8,128)(2,1)S(1)}, u32[]{:S(2)}, u32[]{:S(2)}) %collective-permute-start.16) | collective-permute-done | bytes 524320 | tf_op jit(solution)/shard_map/rest0_xz/ppermute | solution.py:105
  82.4 2.9 %products.5 = (bf16[4,2,128,256]{3,2,1,0:T(8,128)(2,1)S(1)}, bf16[4,2,128,256]{3,2,1,0:T(8,128)(2,1)S(1)}, f32[2,1,128]{2,1,0:T(1,128)S(1)}, f32[2,1,128]{2,1,0:T(1,128)S(1)}) custom-call(s32[2,12]{1,0:T(2,128)S(1)} %copy-done.4, bf16[4,256,3072]{2,1,0:T(8,128)(2,1)S(1)} %pack_inverse.1.sel_ref, bf16[1024,256]{1,0:T(8,128)(2,1)S(1)} %collective-permute-done.2.f0, ...), custom_call_target="tpu_custom_call" | custom-call | tf_op jit(solution)/shard_map/products/pallas_call | solution.py:322
  86.3 7.7 %collective-permute-done.13.r0 = bf16[2048,128]{1,0:T(8,128)(2,1)S(1)} collective-permute-done((bf16[2048,128]{1,0:T(8,128)(2,1)S(1)}, bf16[2048,128]{1,0:T(8,128)(2,1)S(1)}, u32[]{:S(2)}, u32[]{:S(2)}) %collective-permute-start.13) | collective-permute-done | bytes 524320 | tf_op jit(solution)/shard_map/rest1_z/ppermute | solution.py:105
  96.3 2.0 %collective-permute-start.20 = (bf16[2,2,128,256]{3,2,1,0:T(8,128)(2,1)S(1)}, bf16[2,2,128,256]{3,2,1,0:T(8,128)(2,1)S(1)}, u32[]{:S(2)}, u32[]{:S(2)}) collective-permute-start(bf16[2,2,128,256]{3,2,1,0:T(8,128)(2,1)S(1)} %get-tuple-element.82), channel_id=1, source_target_pairs={{0,12},{2,14},{4,8},{6,10},{8,4},{10,6},{12,0},{14,2},{16,28},{18,... | collective-permute-start | bytes 786440 | tf_op jit(solution)/shard_map/cross0_3/ppermute | solution.py:105
  98.3 2.8 %products.6 = (bf16[4,2,128,256]{3,2,1,0:T(8,128)(2,1)S(1)}, f32[2,1,128]{2,1,0:T(1,128)S(1)}) custom-call(s32[2,12]{1,0:T(2,128)S(1)} %copy-done.4, bf16[4,256,3072]{2,1,0:T(8,128)(2,1)S(1)} %pack_inverse.1.sel_ref, bf16[1024,256]{1,0:T(8,128)(2,1)S(1)} %get-tuple-element.54.f0, bf16[1024,256]{1,0:T(8,128)(2,1)S(1)} %collective-permute-done.3.f1, ...), custom_call_target="tpu_custom_call" | custom-call | tf_op jit(solution)/shard_map/products/pallas_call | solution.py:322
  101.1 6.8 %collective-permute-done.15.r1 = bf16[2048,128]{1,0:T(8,128)(2,1)S(1)} collective-permute-done((bf16[2048,128]{1,0:T(8,128)(2,1)S(1)}, bf16[2048,128]{1,0:T(8,128)(2,1)S(1)}, u32[]{:S(2)}, u32[]{:S(2)}) %collective-permute-start.15) | collective-permute-done | bytes 524320 | tf_op jit(solution)/shard_map/rest1_xz/ppermute | solution.py:105
  109.4 2.9 %products.7 = (bf16[4,2,128,256]{3,2,1,0:T(8,128)(2,1)S(1)}, bf16[4,2,128,256]{3,2,1,0:T(8,128)(2,1)S(1)}, f32[2,1,128]{2,1,0:T(1,128)S(1)}, f32[2,1,128]{2,1,0:T(1,128)S(1)}) custom-call(s32[2,12]{1,0:T(2,128)S(1)} %copy-done.4, bf16[4,256,3072]{2,1,0:T(8,128)(2,1)S(1)} %pack_inverse.1.sel_ref, bf16[1024,256]{1,0:T(8,128)(2,1)S(1)} %collective-permute-done.2.f0, ...), custom_call_target="tpu_custom_call" | custom-call | tf_op jit(solution)/shard_map/products/pallas_call | solution.py:322
  112.6 1.7 %collective-permute-done.21.back_ref = bf16[4,2,128,256]{3,2,1,0:T(8,128)(2,1)S(1)} collective-permute-done((bf16[4,2,128,256]{3,2,1,0:T(8,128)(2,1)S(1)}, bf16[4,2,128,256]{3,2,1,0:T(8,128)(2,1)S(1)}, u32[]{:S(2)}, u32[]{:S(2)}) %collective-permute-start.21) | collective-permute-done | bytes 524320 | tf_op jit(solution)/shard_map/cross1_swap/ppermute | solution.py:99
  114.4 1.6 %collective-permute-start.22 = (bf16[2,2,128,256]{3,2,1,0:T(8,128)(2,1)S(1)}, bf16[2,2,128,256]{3,2,1,0:T(8,128)(2,1)S(1)}, u32[]{:S(2)}, u32[]{:S(2)}) collective-permute-start(bf16[2,2,128,256]{3,2,1,0:T(8,128)(2,1)S(1)} %get-tuple-element.90), channel_id=1, source_target_pairs={{0,4},{2,6},{4,0},{6,2},{8,12},{10,14},{12,8},{14,10},{16,20},{18,... | collective-permute-start | bytes 786440 | tf_op jit(solution)/shard_map/cross1_1/ppermute | solution.py:105
  119.3 3.3 %collective-permute-start.27 = (f32[2,2048]{1,0:T(2,128)S(1)}, f32[2,2048]{1,0:T(2,128)S(1)}, u32[]{:S(2)}, u32[]{:S(2)}) collective-permute-start(f32[2,2048]{1,0:T(2,128)S(1)} %place_sums.1), channel_id=1, source_target_pairs={{0,2},{2,0},{4,6},{6,4},{8,10},{10,8},{12,14},{14,12},{16,18},{18,... | collective-permute-start | bytes 49160 | tf_op jit(solution)/shard_map/variance_1/ppermute | solution.py:105
  122.6 1.7 %collective-permute-done.27 = f32[2,2048]{1,0:T(2,128)S(1)} collective-permute-done((f32[2,2048]{1,0:T(2,128)S(1)}, f32[2,2048]{1,0:T(2,128)S(1)}, u32[]{:S(2)}, u32[]{:S(2)}) %collective-permute-start.27) | collective-permute-done | bytes 16416 | tf_op jit(solution)/shard_map/variance_1/ppermute | solution.py:105
  125.4 3.8 %collective-permute-done.28 = f32[2,2048]{1,0:T(2,128)S(1)} collective-permute-done((f32[2,2048]{1,0:T(2,128)S(1)}, f32[2,2048]{1,0:T(2,128)S(1)}, u32[]{:S(2)}, u32[]{:S(2)}) %collective-permute-start.28) | collective-permute-done | bytes 16416 | tf_op jit(solution)/shard_map/variance_8/ppermute | solution.py:105
  130.7 2.3 %collective-permute-done.29 = f32[2,2048]{1,0:T(2,128)S(1)} collective-permute-done((f32[2,2048]{1,0:T(2,128)S(1)}, f32[2,2048]{1,0:T(2,128)S(1)}, u32[]{:S(2)}, u32[]{:S(2)}) %collective-permute-start.29) | collective-permute-done | bytes 16416 | tf_op jit(solution)/shard_map/variance_2/ppermute | solution.py:105
  133.0 3.1 %collective-permute-start.30 = (f32[2,2048]{1,0:T(2,128)S(1)}, f32[2,2048]{1,0:T(2,128)S(1)}, u32[]{:S(2)}, u32[]{:S(2)}) collective-permute-start(f32[2,2048]{1,0:T(2,128)S(1)} %add.20), channel_id=1, source_target_pairs={{0,8},{2,10},{4,12},{6,14},{8,0},{10,2},{12,4},{14,6},{16,24},{18,... | collective-permute-start | bytes 49160 | tf_op jit(solution)/shard_map/variance_4/ppermute | solution.py:105
  (68 shorter events, 31.1 us)
Async XLA Ops:
  2.1 10.8 %collective-permute-start.4 = (bf16[2048,256]{1,0:T(8,128)(2,1)S(1)}, bf16[2048,256]{1,0:T(8,128)(2,1)S(1)}, u32[]{:S(2)}, u32[]{:S(2)}) collective-permute-start(bf16[2048,256]{1,0:T(8,128)(2,1)S(1)} %dynamic-slice_bitcast_fusion), channel_id=1, source_target_pairs={{0,1},{1,0},{2,3},{3,2},{4,5},{5,4},{6,7},{7,6},{8,9},{9,8},{10,11... | collective-permute-start | bytes 3145736 | tf_op jit(solution)/shard_map/panel_swap/ppermute | solution.py:99
  2.6 35.4 %collective-permute-start = (bf16[256,2048]{1,0:T(8,128)(2,1)}, bf16[256,2048]{1,0:T(8,128)(2,1)S(1)}, u32[]{:S(2)}, u32[]{:S(2)}) collective-permute-start(bf16[256,2048]{1,0:T(8,128)(2,1)} %refs_0_.1), channel_id=1, source_target_pairs={{0,4},{2,6},{4,0},{6,2},{8,12},{10,14},{12,8},{14,10},{16,20},{18,... | collective-permute-start | bytes 3145736 | tf_op jit(solution)/shard_map/inv_y/ppermute | solution.py:105
  7.1 30.9 %collective-permute-start.1 = (bf16[192,2048]{1,0:T(8,128)(2,1)S(1)}, bf16[192,2048]{1,0:T(8,128)(2,1)S(1)}, u32[]{:S(2)}, u32[]{:S(2)}) collective-permute-start(bf16[192,2048]{1,0:T(8,128)(2,1)S(1)} %get-tuple-element.53), channel_id=1, source_target_pairs={{0,8},{2,10},{4,12},{6,14},{8,0},{10,2},{12,4},{14,6},{16,24},{18,... | collective-permute-start | bytes 2359304 | tf_op jit(solution)/shard_map/inv_z0/ppermute | solution.py:105
  8.8 28.4 %collective-permute-start.2 = (bf16[1024,256]{1,0:T(8,128)(2,1)S(1)}, bf16[1024,256]{1,0:T(8,128)(2,1)S(1)}, u32[]{:S(2)}, u32[]{:S(2)}) collective-permute-start(bf16[1024,256]{1,0:T(8,128)(2,1)S(1)} %get-tuple-element.54.f0), channel_id=1, source_target_pairs={{0,16},{2,18},{4,20},{6,22},{8,24},{10,26},{12,28},{14,30},{16,0},... | collective-permute-start | bytes 1572872 | tf_op jit(solution)/shard_map/first_z/ppermute | solution.py:105
  11.4 25.8 %collective-permute-start.3 = (bf16[1024,256]{1,0:T(8,128)(2,1)S(1)}, bf16[1024,256]{1,0:T(8,128)(2,1)S(1)}, u32[]{:S(2)}, u32[]{:S(2)}) collective-permute-start(bf16[1024,256]{1,0:T(8,128)(2,1)S(1)} %get-tuple-element.54.f0), channel_id=1, source_target_pairs={{0,2},{2,0},{4,6},{6,4},{8,10},{10,8},{12,14},{14,12},{16,18},{18,... | collective-permute-start | bytes 1572872 | tf_op jit(solution)/shard_map/first_x/ppermute | solution.py:105
  13.8 24.3 %collective-permute-start.5 = (bf16[2048,128]{1,0:T(8,128)(2,1)S(1)}, bf16[2048,128]{1,0:T(8,128)(2,1)S(1)}, u32[]{:S(2)}, u32[]{:S(2)}) collective-permute-start(bf16[2048,128]{1,0:T(8,128)(2,1)S(1)} %get-tuple-element.73.r0), channel_id=1, source_target_pairs={{0,2},{2,0},{4,6},{6,4},{8,10},{10,8},{12,14},{14,12},{16,18},{18,... | collective-permute-start | bytes 1572872 | tf_op jit(solution)/shard_map/rest0_x/ppermute | solution.py:105
  38.3 29.2 %collective-permute-start.11 = (bf16[704,2048]{1,0:T(8,128)(2,1)S(1)}, bf16[704,2048]{1,0:T(8,128)(2,1)S(1)}, u32[]{:S(2)}, u32[]{:S(2)}) collective-permute-start(bf16[704,2048]{1,0:T(8,128)(2,1)S(1)} %stack_rows.2.refs_0_), channel_id=1, source_target_pairs={{0,1},{1,0},{2,3},{3,2},{4,5},{5,4},{6,7},{7,6},{8,9},{9,8},{10,11... | collective-permute-start | bytes 8650760 | tf_op jit(solution)/shard_map/inv_swap/ppermute | solution.py:99
  38.3 29.1 %collective-permute-start.9 = (bf16[192,2048]{1,0:T(8,128)(2,1)S(1)}, bf16[192,2048]{1,0:T(8,128)(2,1)S(1)}, u32[]{:S(2)}, u32[]{:S(2)}) collective-permute-start(bf16[192,2048]{1,0:T(8,128)(2,1)S(1)} %collective-permute-done.1.refs_2_), channel_id=1, source_target_pairs={{0,4},{2,6},{4,0},{6,2},{8,12},{10,14},{12,8},{14,10},{16,20},{18,... | collective-permute-start | bytes 2359304 | tf_op jit(solution)/shard_map/inv_yz0/ppermute | solution.py:105
  38.7 13.8 %collective-permute-start.8 = (bf16[64,2048]{1,0:T(8,128)(2,1)S(1)}, bf16[64,2048]{1,0:T(8,128)(2,1)S(1)}, u32[]{:S(2)}, u32[]{:S(2)}) collective-permute-start(bf16[64,2048]{1,0:T(8,128)(2,1)S(1)} %get-tuple-element.62), channel_id=1, source_target_pairs={{0,8},{2,10},{4,12},{6,14},{8,0},{10,2},{12,4},{14,6},{16,24},{18,... | collective-permute-start | bytes 786440 | tf_op jit(solution)/shard_map/inv_z1/ppermute | solution.py:105
  41.5 25.9 %collective-permute-start.6 = (bf16[2048,128]{1,0:T(8,128)(2,1)S(1)}, bf16[2048,128]{1,0:T(8,128)(2,1)S(1)}, u32[]{:S(2)}, u32[]{:S(2)}) collective-permute-start(bf16[2048,128]{1,0:T(8,128)(2,1)S(1)} %get-tuple-element.73.r0), channel_id=1, source_target_pairs={{0,16},{2,18},{4,20},{6,22},{8,24},{10,26},{12,28},{14,30},{16,0},... | collective-permute-start | bytes 1572872 | tf_op jit(solution)/shard_map/rest0_z/ppermute | solution.py:105
  43.1 24.3 %collective-permute-start.7 = (bf16[1024,256]{1,0:T(8,128)(2,1)S(1)}, bf16[1024,256]{1,0:T(8,128)(2,1)S(1)}, u32[]{:S(2)}, u32[]{:S(2)}) collective-permute-start(bf16[1024,256]{1,0:T(8,128)(2,1)S(1)} %collective-permute-done.2.f0), channel_id=1, source_target_pairs={{0,2},{2,0},{4,6},{6,4},{8,10},{10,8},{12,14},{14,12},{16,18},{18,... | collective-permute-start | bytes 1572872 | tf_op jit(solution)/shard_map/first_xz/ppermute | solution.py:105
  52.5 11.4 %collective-permute-start.10 = (bf16[64,2048]{1,0:T(8,128)(2,1)S(1)}, bf16[64,2048]{1,0:T(8,128)(2,1)S(1)}, u32[]{:S(2)}, u32[]{:S(2)}) collective-permute-start(bf16[64,2048]{1,0:T(8,128)(2,1)S(1)} %collective-permute-done.8.refs_0_), channel_id=1, source_target_pairs={{0,4},{2,6},{4,0},{6,2},{8,12},{10,14},{12,8},{14,10},{16,20},{18,... | collective-permute-start | bytes 786440 | tf_op jit(solution)/shard_map/inv_yz1/ppermute | solution.py:105
  67.6 14.8 %collective-permute-start.16 = (bf16[2048,128]{1,0:T(8,128)(2,1)S(1)}, bf16[2048,128]{1,0:T(8,128)(2,1)S(1)}, u32[]{:S(2)}, u32[]{:S(2)}) collective-permute-start(bf16[2048,128]{1,0:T(8,128)(2,1)S(1)} %collective-permute-done.6.r0), channel_id=1, source_target_pairs={{0,2},{2,0},{4,6},{6,4},{8,10},{10,8},{12,14},{14,12},{16,18},{18,... | collective-permute-start | bytes 1572872 | tf_op jit(solution)/shard_map/rest0_xz/ppermute | solution.py:105
  69.2 24.8 %collective-permute-start.13 = (bf16[2048,128]{1,0:T(8,128)(2,1)S(1)}, bf16[2048,128]{1,0:T(8,128)(2,1)S(1)}, u32[]{:S(2)}, u32[]{:S(2)}) collective-permute-start(bf16[2048,128]{1,0:T(8,128)(2,1)S(1)} %get-tuple-element.69.r0), channel_id=1, source_target_pairs={{0,16},{2,18},{4,20},{6,22},{8,24},{10,26},{12,28},{14,30},{16,0},... | collective-permute-start | bytes 1572872 | tf_op jit(solution)/shard_map/rest1_z/ppermute | solution.py:105
  69.2 24.8 %collective-permute-start.14 = (bf16[2048,128]{1,0:T(8,128)(2,1)S(1)}, bf16[2048,128]{1,0:T(8,128)(2,1)S(1)}, u32[]{:S(2)}, u32[]{:S(2)}) collective-permute-start(bf16[2048,128]{1,0:T(8,128)(2,1)S(1)} %get-tuple-element.69.r0), channel_id=1, source_target_pairs={{0,2},{2,0},{4,6},{6,4},{8,10},{10,8},{12,14},{14,12},{16,18},{18,... | collective-permute-start | bytes 1572872 | tf_op jit(solution)/shard_map/rest1_x/ppermute | solution.py:105
  85.3 9.4 %collective-permute-start.17 = (bf16[4,2,128,256]{3,2,1,0:T(8,128)(2,1)S(1)}, bf16[4,2,128,256]{3,2,1,0:T(8,128)(2,1)S(1)}, u32[]{:S(2)}, u32[]{:S(2)}) collective-permute-start(bf16[4,2,128,256]{3,2,1,0:T(8,128)(2,1)S(1)} %get-tuple-element.78), channel_id=1, source_target_pairs={{0,1},{1,0},{2,3},{3,2},{4,5},{5,4},{6,7},{7,6},{8,9},{9,8},{10,11... | collective-permute-start | bytes 1572872 | tf_op jit(solution)/shard_map/cross0_swap/ppermute | solution.py:99
  94.0 13.9 %collective-permute-start.15 = (bf16[2048,128]{1,0:T(8,128)(2,1)S(1)}, bf16[2048,128]{1,0:T(8,128)(2,1)S(1)}, u32[]{:S(2)}, u32[]{:S(2)}) collective-permute-start(bf16[2048,128]{1,0:T(8,128)(2,1)S(1)} %collective-permute-done.13.r0), channel_id=1, source_target_pairs={{0,2},{2,0},{4,6},{6,4},{8,10},{10,8},{12,14},{14,12},{16,18},{18,... | collective-permute-start | bytes 1572872 | tf_op jit(solution)/shard_map/rest1_xz/ppermute | solution.py:105
  94.7 13.1 %collective-permute-start.18 = (bf16[2,2,128,256]{3,2,1,0:T(8,128)(2,1)S(1)}, bf16[2,2,128,256]{3,2,1,0:T(8,128)(2,1)S(1)}, u32[]{:S(2)}, u32[]{:S(2)}) collective-permute-start(bf16[2,2,128,256]{3,2,1,0:T(8,128)(2,1)S(1)} %get-tuple-element.80), channel_id=1, source_target_pairs={{0,4},{2,6},{4,0},{6,2},{8,12},{10,14},{12,8},{14,10},{16,20},{18,... | collective-permute-start | bytes 786440 | tf_op jit(solution)/shard_map/cross0_1/ppermute | solution.py:105
  96.3 11.5 %collective-permute-start.19 = (bf16[2,2,128,256]{3,2,1,0:T(8,128)(2,1)S(1)}, bf16[2,2,128,256]{3,2,1,0:T(8,128)(2,1)S(1)}, u32[]{:S(2)}, u32[]{:S(2)}) collective-permute-start(bf16[2,2,128,256]{3,2,1,0:T(8,128)(2,1)S(1)} %get-tuple-element.81), channel_id=1, source_target_pairs={{0,8},{2,10},{4,12},{6,14},{8,0},{10,2},{12,4},{14,6},{16,24},{18,... | collective-permute-start | bytes 786440 | tf_op jit(solution)/shard_map/cross0_2/ppermute | solution.py:105
  96.3 13.1 %collective-permute-start.20 = (bf16[2,2,128,256]{3,2,1,0:T(8,128)(2,1)S(1)}, bf16[2,2,128,256]{3,2,1,0:T(8,128)(2,1)S(1)}, u32[]{:S(2)}, u32[]{:S(2)}) collective-permute-start(bf16[2,2,128,256]{3,2,1,0:T(8,128)(2,1)S(1)} %get-tuple-element.82), channel_id=1, source_target_pairs={{0,12},{2,14},{4,8},{6,10},{8,4},{10,6},{12,0},{14,2},{16,28},{18,... | collective-permute-start | bytes 786440 | tf_op jit(solution)/shard_map/cross0_3/ppermute | solution.py:105
  114.4 24.1 %collective-permute-start.22 = (bf16[2,2,128,256]{3,2,1,0:T(8,128)(2,1)S(1)}, bf16[2,2,128,256]{3,2,1,0:T(8,128)(2,1)S(1)}, u32[]{:S(2)}, u32[]{:S(2)}) collective-permute-start(bf16[2,2,128,256]{3,2,1,0:T(8,128)(2,1)S(1)} %get-tuple-element.90), channel_id=1, source_target_pairs={{0,4},{2,6},{4,0},{6,2},{8,12},{10,14},{12,8},{14,10},{16,20},{18,... | collective-permute-start | bytes 786440 | tf_op jit(solution)/shard_map/cross1_1/ppermute | solution.py:105
  116.0 22.5 %collective-permute-start.23 = (bf16[2,2,128,256]{3,2,1,0:T(8,128)(2,1)S(1)}, bf16[2,2,128,256]{3,2,1,0:T(8,128)(2,1)S(1)}, u32[]{:S(2)}, u32[]{:S(2)}) collective-permute-start(bf16[2,2,128,256]{3,2,1,0:T(8,128)(2,1)S(1)} %get-tuple-element.91), channel_id=1, source_target_pairs={{0,8},{2,10},{4,12},{6,14},{8,0},{10,2},{12,4},{14,6},{16,24},{18,... | collective-permute-start | bytes 786440 | tf_op jit(solution)/shard_map/cross1_2/ppermute | solution.py:105
  116.4 22.1 %collective-permute-start.24 = (bf16[2,2,128,256]{3,2,1,0:T(8,128)(2,1)S(1)}, bf16[2,2,128,256]{3,2,1,0:T(8,128)(2,1)S(1)}, u32[]{:S(2)}, u32[]{:S(2)}) collective-permute-start(bf16[2,2,128,256]{3,2,1,0:T(8,128)(2,1)S(1)} %get-tuple-element.92), channel_id=1, source_target_pairs={{0,12},{2,14},{4,8},{6,10},{8,4},{10,6},{12,0},{14,2},{16,28},{18,... | collective-permute-start | bytes 786440 | tf_op jit(solution)/shard_map/cross1_3/ppermute | solution.py:105
  119.3 5.0 %collective-permute-start.27 = (f32[2,2048]{1,0:T(2,128)S(1)}, f32[2,2048]{1,0:T(2,128)S(1)}, u32[]{:S(2)}, u32[]{:S(2)}) collective-permute-start(f32[2,2048]{1,0:T(2,128)S(1)} %place_sums.1), channel_id=1, source_target_pairs={{0,2},{2,0},{4,6},{6,4},{8,10},{10,8},{12,14},{14,12},{16,18},{18,... | collective-permute-start | bytes 49160 | tf_op jit(solution)/shard_map/variance_1/ppermute | solution.py:105
  (12 other events, 68.0 us)

commit v8 on v7

--- a/solution.py
+++ b/solution.py
@@ -462,24 +462,24 @@
     f_x = hop(f_own, X, "first_x")
     a_z0 = hop(top, ZL, "inv_z0")
     a_y = hop(inverse, Y, "inv_y")
-    r_x0 = hop(r_own[0], X, "rest0_x")
-    a_y, a_z0, f_z, f_x, r_x0, linv, *r_own = lax.optimization_barrier(
-        (a_y, a_z0, f_z, f_x, r_x0, linv, *r_own)
+    a_y, a_z0, f_z, f_x, linv, *r_own = lax.optimization_barrier(
+        (a_y, a_z0, f_z, f_x, linv, *r_own)
     )
     r_z0 = hop(r_own[0], ZH, "rest0_z")
     a_z1 = hop(after(bottom, f_z), ZL, "inv_z1")
     f_xz = hop(f_z, X, "first_xz")
+    r_x0 = hop(r_own[0], X, "rest0_x")
     a_yz0 = hop(a_z0, Y, "inv_yz0")
     a_yz1 = hop(a_z1, Y, "inv_yz1")
     most = stack_rows([inverse, a_y, a_z0])
-    s_most = swap_cores(most, "inv_swap")
-    r_z0, f_xz, a_z1, a_yz0, a_yz1, s_most, *r_own = lax.optimization_barrier(
-        (r_z0, f_xz, a_z1, a_yz0, a_yz1, s_most, *r_own)
+    r_z0, r_x0, f_xz, a_z1, a_yz0, a_yz1, most, *r_own = lax.optimization_barrier(
+        (r_z0, r_x0, f_xz, a_z1, a_yz0, a_yz1, most, *r_own)
     )
     r_z1 = hop(r_own[1], ZH, "rest1_z")
     r_xz0 = hop(r_z0, X, "rest0_xz")
     r_x1 = hop(r_own[1], X, "rest1_x")
     more = stack_rows([a_z1, a_yz0, a_yz1])
+    s_most = swap_cores(most, "inv_swap")
     s_more = swap_cores(more, "inv_swap_more")
     sel = pack_inverse(structure, (most, more), (s_most, s_more), first)
     r_z1, r_x1 = lax.optimization_barrier((r_z1, r_x1))
@@ -502,13 +502,11 @@
         structure, sel, (f_z, f_xz), (r_z1, r_xz1), 1, near
     )
     held = assemble(messages, 0, None)
-    messages = deliver(kept, sent, 1)
-    back = [
-        swap_cores(after(total, messages[0]), "sums_swap") for total in (sent_sum0, sent_sum1)
-    ]
-    held = assemble(messages, 1, held)
+    back = [swap_cores(total, "sums_swap") for total in (sent_sum0, sent_sum1)]
     variance = place_sums(linv, (kept_sum0, kept_sum1), back)
-    for mask in (X, ZH, Y, ZL):
+    variance = variance + hop(variance, X, "variance_x")
+    held = assemble(deliver(after(kept, variance), sent, 1), 1, held)
+    for mask in (ZH, Y, ZL):
         variance = variance + hop(variance, mask, f"variance_{mask}")
     half = panel.shape[2] * size // 2
     cross = held.reshape(half, 2, 2, LANES).transpose(0, 2, 1, 3).reshape(half, 2, BLK)

time: 140 us -> 141 us (level)
  Pallas kernels: 17.7 us -> 24.7 us
  starting transfers between devices: 38 us -> 34.3 us
  waiting for transfers between devices: 79.6 us -> 77 us
    pallas_call x4, Pallas kernels: 11.4 us -> 18.3 us  [products(): pl.pallas_call(body, out_shape=outs if near is None else [outs[0], outs[0...]
    ppermute x24, starting transfers between devices: 35.5 us -> 32.5 us  [hop(): return lax.ppermute(value, 'wide', [(i, i ^ mask) for i in range(size)])]
    ppermute x24, waiting for transfers between devices: 76.2 us -> 73.3 us  [hop(): return lax.ppermute(value, 'wide', [(i, i ^ mask) for i in range(size)])]
  transfers between devices with their start and end apart: 31 -> 31, of which waited for: 17 -> 15; matrix products, arithmetic and copies ran while one was open for 0% -> 0% of each run, Pallas kernels for 10% -> 14%
where the time goes in v8:
time: 141 us; the launch traced here: 140 us
  waiting for transfers between devices  77 us (55%)
  starting transfers between devices  34.3 us (24%)
  Pallas kernels  24.7 us (18%)
  local copies, waits for them, and re-layouts  2.71 us (2%)
    ppermute x24, waiting for transfers between devices, hop(): return lax.ppermute(value, 'wide', [(i, i ^ mask) for i in range(size)])  73.3 us
    ppermute x24, starting transfers between devices, hop(): return lax.ppermute(value, 'wide', [(i, i ^ mask) for i in range(size)])  32.5 us
    pallas_call x4, Pallas kernels, products(): pl.pallas_call(body, out_shape=outs if near is None else [outs[0], outs[0...  18.3 us
    ppermute x7, waiting for transfers between devices, swap_cores(): return lax.ppermute(value, 'narrow', [(0, 1), (1, 0)])  3.69 us
  transfers between devices with their start and end apart: 31, of which 15 were waited for; matrix products, arithmetic and copies ran while one was open for 0% of the time, Pallas kernels for 14%

profile of v8, /device:TPU:0, one launch (start us, length us, event | category | flops | bytes accessed | tf_op | source)
XLA Modules:
  0.0 140.3 jit_solution(13196364025186964943)
XLA Ops:
  2.6 2.6 %collective-permute-start = (bf16[256,2048]{1,0:T(8,128)(2,1)}, bf16[256,2048]{1,0:T(8,128)(2,1)S(1)}, u32[]{:S(2)}, u32[]{:S(2)}) collective-permute-start(bf16[256,2048]{1,0:T(8,128)(2,1)} %refs_0_.1), channel_id=1, source_target_pairs={{0,4},{2,6},{4,0},{6,2},{8,12},{10,14},{12,8},{14,10},{16,20},{18,... | collective-permute-start | bytes 3145736 | tf_op jit(solution)/shard_map/inv_y/ppermute | solution.py:105
  7.1 1.6 %collective-permute-start.1 = (bf16[192,2048]{1,0:T(8,128)(2,1)S(1)}, bf16[192,2048]{1,0:T(8,128)(2,1)S(1)}, u32[]{:S(2)}, u32[]{:S(2)}) collective-permute-start(bf16[192,2048]{1,0:T(8,128)(2,1)S(1)} %get-tuple-element.52), channel_id=1, source_target_pairs={{0,8},{2,10},{4,12},{6,14},{8,0},{10,2},{12,4},{14,6},{16,24},{18,... | collective-permute-start | bytes 2359304 | tf_op jit(solution)/shard_map/inv_z0/ppermute | solution.py:105
  8.8 2.6 %collective-permute-start.2 = (bf16[1024,256]{1,0:T(8,128)(2,1)S(1)}, bf16[1024,256]{1,0:T(8,128)(2,1)S(1)}, u32[]{:S(2)}, u32[]{:S(2)}) collective-permute-start(bf16[1024,256]{1,0:T(8,128)(2,1)S(1)} %get-tuple-element.53.f0), channel_id=1, source_target_pairs={{0,16},{2,18},{4,20},{6,22},{8,24},{10,26},{12,28},{14,30},{16,0},... | collective-permute-start | bytes 1572872 | tf_op jit(solution)/shard_map/first_z/ppermute | solution.py:105
  14.1 23.0 %collective-permute-done.2.f0 = bf16[1024,256]{1,0:T(8,128)(2,1)S(1)} collective-permute-done((bf16[1024,256]{1,0:T(8,128)(2,1)S(1)}, bf16[1024,256]{1,0:T(8,128)(2,1)S(1)}, u32[]{:S(2)}, u32[]{:S(2)}) %collective-permute-start.2) | collective-permute-done | bytes 524320 | tf_op jit(solution)/shard_map/first_z/ppermute | solution.py:105
  38.4 2.7 %collective-permute-start.5 = (bf16[2048,128]{1,0:T(8,128)(2,1)S(1)}, bf16[2048,128]{1,0:T(8,128)(2,1)S(1)}, u32[]{:S(2)}, u32[]{:S(2)}) collective-permute-start(bf16[2048,128]{1,0:T(8,128)(2,1)S(1)} %get-tuple-element.72.r0), channel_id=1, source_target_pairs={{0,16},{2,18},{4,20},{6,22},{8,24},{10,26},{12,28},{14,30},{16,0},... | collective-permute-start | bytes 1572872 | tf_op jit(solution)/shard_map/rest0_z/ppermute | solution.py:105
  42.6 1.6 %collective-permute-start.8 = (bf16[64,2048]{1,0:T(8,128)(2,1)S(1)}, bf16[64,2048]{1,0:T(8,128)(2,1)S(1)}, u32[]{:S(2)}, u32[]{:S(2)}) collective-permute-start(bf16[64,2048]{1,0:T(8,128)(2,1)S(1)} %get-tuple-element.59), channel_id=1, source_target_pairs={{0,8},{2,10},{4,12},{6,14},{8,0},{10,2},{12,4},{14,6},{16,24},{18,... | collective-permute-start | bytes 786440 | tf_op jit(solution)/shard_map/inv_z1/ppermute | solution.py:105
  44.7 12.4 %collective-permute-done.8.refs_0_ = bf16[64,2048]{1,0:T(8,128)(2,1)S(1)} collective-permute-done((bf16[64,2048]{1,0:T(8,128)(2,1)S(1)}, bf16[64,2048]{1,0:T(8,128)(2,1)S(1)}, u32[]{:S(2)}, u32[]{:S(2)}) %collective-permute-start.8) | collective-permute-done | bytes 262176 | tf_op jit(solution)/shard_map/inv_z1/ppermute | solution.py:105
  58.9 4.6 %collective-permute-done.5.r0 = bf16[2048,128]{1,0:T(8,128)(2,1)S(1)} collective-permute-done((bf16[2048,128]{1,0:T(8,128)(2,1)S(1)}, bf16[2048,128]{1,0:T(8,128)(2,1)S(1)}, u32[]{:S(2)}, u32[]{:S(2)}) %collective-permute-start.5) | collective-permute-done | bytes 524320 | tf_op jit(solution)/shard_map/rest0_z/ppermute | solution.py:105
  67.1 2.1 %collective-permute-start.13 = (bf16[2048,128]{1,0:T(8,128)(2,1)S(1)}, bf16[2048,128]{1,0:T(8,128)(2,1)S(1)}, u32[]{:S(2)}, u32[]{:S(2)}) collective-permute-start(bf16[2048,128]{1,0:T(8,128)(2,1)S(1)} %get-tuple-element.68.r0), channel_id=1, source_target_pairs={{0,16},{2,18},{4,20},{6,22},{8,24},{10,26},{12,28},{14,30},{16,0},... | collective-permute-start | bytes 1572872 | tf_op jit(solution)/shard_map/rest1_z/ppermute | solution.py:105
  69.8 2.4 %collective-permute-done.12.refs_3_ = bf16[320,2048]{1,0:T(8,128)(2,1)S(1)} collective-permute-done((bf16[320,2048]{1,0:T(8,128)(2,1)S(1)}, bf16[320,2048]{1,0:T(8,128)(2,1)S(1)}, u32[]{:S(2)}, u32[]{:S(2)}) %collective-permute-start.12) | collective-permute-done | bytes 1310752 | tf_op jit(solution)/shard_map/inv_swap_more/ppermute | solution.py:99
  72.1 1.9 %pack_inverse.1.sel_ref = bf16[4,256,3072]{2,1,0:T(8,128)(2,1)S(1)} custom-call(s32[2,12]{1,0:T(2,128)S(1)} %copy-done.4, bf16[704,2048]{1,0:T(8,128)(2,1)S(1)} %stack_rows.2.refs_0_, bf16[320,2048]{1,0:T(8,128)(2,1)S(1)} %stack_rows.3.refs_1_, bf16[704,2048]{1,0:T(8,128)(2,1)S(1)} %collective-permute-done.11.refs_2_, ...), custom_call_target="tpu_custom_call" | custom-call | tf_op jit(solution)/shard_map/pack_inverse/pallas_call | solution.py:225
  74.0 4.6 %products.4 = (bf16[4,2,128,256]{3,2,1,0:T(8,128)(2,1)S(1)}, f32[2,1,128]{2,1,0:T(1,128)S(1)}) custom-call(s32[2,12]{1,0:T(2,128)S(1)} %copy-done.4, bf16[4,256,3072]{2,1,0:T(8,128)(2,1)S(1)} %pack_inverse.1.sel_ref, bf16[1024,256]{1,0:T(8,128)(2,1)S(1)} %get-tuple-element.53.f0, bf16[1024,256]{1,0:T(8,128)(2,1)S(1)} %collective-permute-done.3.f1, ...), custom_call_target="tpu_custom_call" | custom-call | tf_op jit(solution)/shard_map/products/pallas_call | solution.py:322
  78.6 1.8 %collective-permute-done.16.r1 = bf16[2048,128]{1,0:T(8,128)(2,1)S(1)} collective-permute-done((bf16[2048,128]{1,0:T(8,128)(2,1)S(1)}, bf16[2048,128]{1,0:T(8,128)(2,1)S(1)}, u32[]{:S(2)}, u32[]{:S(2)}) %collective-permute-start.16) | collective-permute-done | bytes 524320 | tf_op jit(solution)/shard_map/rest0_xz/ppermute | solution.py:105
  80.4 4.6 %products.5 = (bf16[4,2,128,256]{3,2,1,0:T(8,128)(2,1)S(1)}, bf16[4,2,128,256]{3,2,1,0:T(8,128)(2,1)S(1)}, f32[2,1,128]{2,1,0:T(1,128)S(1)}, f32[2,1,128]{2,1,0:T(1,128)S(1)}) custom-call(s32[2,12]{1,0:T(2,128)S(1)} %copy-done.4, bf16[4,256,3072]{2,1,0:T(8,128)(2,1)S(1)} %pack_inverse.1.sel_ref, bf16[1024,256]{1,0:T(8,128)(2,1)S(1)} %collective-permute-done.2.f0, ...), custom_call_target="tpu_custom_call" | custom-call | tf_op jit(solution)/shard_map/products/pallas_call | solution.py:322
  85.1 7.8 %collective-permute-done.13.r0 = bf16[2048,128]{1,0:T(8,128)(2,1)S(1)} collective-permute-done((bf16[2048,128]{1,0:T(8,128)(2,1)S(1)}, bf16[2048,128]{1,0:T(8,128)(2,1)S(1)}, u32[]{:S(2)}, u32[]{:S(2)}) %collective-permute-start.13) | collective-permute-done | bytes 524320 | tf_op jit(solution)/shard_map/rest1_z/ppermute | solution.py:105
  93.5 1.6 %collective-permute-start.18 = (bf16[2,2,128,256]{3,2,1,0:T(8,128)(2,1)S(1)}, bf16[2,2,128,256]{3,2,1,0:T(8,128)(2,1)S(1)}, u32[]{:S(2)}, u32[]{:S(2)}) collective-permute-start(bf16[2,2,128,256]{3,2,1,0:T(8,128)(2,1)S(1)} %get-tuple-element.79), channel_id=1, source_target_pairs={{0,4},{2,6},{4,0},{6,2},{8,12},{10,14},{12,8},{14,10},{16,20},{18,... | collective-permute-start | bytes 786440 | tf_op jit(solution)/shard_map/cross0_1/ppermute | solution.py:105
  97.0 4.6 %products.6 = (bf16[4,2,128,256]{3,2,1,0:T(8,128)(2,1)S(1)}, f32[2,1,128]{2,1,0:T(1,128)S(1)}) custom-call(s32[2,12]{1,0:T(2,128)S(1)} %copy-done.4, bf16[4,256,3072]{2,1,0:T(8,128)(2,1)S(1)} %pack_inverse.1.sel_ref, bf16[1024,256]{1,0:T(8,128)(2,1)S(1)} %get-tuple-element.53.f0, bf16[1024,256]{1,0:T(8,128)(2,1)S(1)} %collective-permute-done.3.f1, ...), custom_call_target="tpu_custom_call" | custom-call | tf_op jit(solution)/shard_map/products/pallas_call | solution.py:322
  101.6 4.0 %collective-permute-done.15.r1 = bf16[2048,128]{1,0:T(8,128)(2,1)S(1)} collective-permute-done((bf16[2048,128]{1,0:T(8,128)(2,1)S(1)}, bf16[2048,128]{1,0:T(8,128)(2,1)S(1)}, u32[]{:S(2)}, u32[]{:S(2)}) %collective-permute-start.15) | collective-permute-done | bytes 524320 | tf_op jit(solution)/shard_map/rest1_xz/ppermute | solution.py:105
  107.2 4.6 %products.7 = (bf16[4,2,128,256]{3,2,1,0:T(8,128)(2,1)S(1)}, bf16[4,2,128,256]{3,2,1,0:T(8,128)(2,1)S(1)}, f32[2,1,128]{2,1,0:T(1,128)S(1)}, f32[2,1,128]{2,1,0:T(1,128)S(1)}) custom-call(s32[2,12]{1,0:T(2,128)S(1)} %copy-done.4, bf16[4,256,3072]{2,1,0:T(8,128)(2,1)S(1)} %pack_inverse.1.sel_ref, bf16[1024,256]{1,0:T(8,128)(2,1)S(1)} %collective-permute-done.2.f0, ...), custom_call_target="tpu_custom_call" | custom-call | tf_op jit(solution)/shard_map/products/pallas_call | solution.py:322
  114.5 3.1 %collective-permute-done.23 = f32[2,2048]{1,0:T(2,128)S(1)} collective-permute-done((f32[2,2048]{1,0:T(2,128)S(1)}, f32[2,2048]{1,0:T(2,128)S(1)}, u32[]{:S(2)}, u32[]{:S(2)}) %collective-permute-start.23) | collective-permute-done | bytes 16416 | tf_op jit(solution)/shard_map/variance_x/ppermute | solution.py:105
  117.8 1.6 %collective-permute-start.25 = (bf16[2,2,128,256]{3,2,1,0:T(8,128)(2,1)S(1)}, bf16[2,2,128,256]{3,2,1,0:T(8,128)(2,1)S(1)}, u32[]{:S(2)}, u32[]{:S(2)}) collective-permute-start(bf16[2,2,128,256]{3,2,1,0:T(8,128)(2,1)S(1)} %get-tuple-element.95), channel_id=1, source_target_pairs={{0,4},{2,6},{4,0},{6,2},{8,12},{10,14},{12,8},{14,10},{16,20},{18,... | collective-permute-start | bytes 786440 | tf_op jit(solution)/shard_map/cross1_1/ppermute | solution.py:105
  121.8 8.7 %collective-permute-done.28 = f32[2,2048]{1,0:T(2,128)S(1)} collective-permute-done((f32[2,2048]{1,0:T(2,128)S(1)}, f32[2,2048]{1,0:T(2,128)S(1)}, u32[]{:S(2)}, u32[]{:S(2)}) %collective-permute-start.28) | collective-permute-done | bytes 16416 | tf_op jit(solution)/shard_map/variance_8/ppermute | solution.py:105
  131.1 3.2 %collective-permute-done.29 = f32[2,2048]{1,0:T(2,128)S(1)} collective-permute-done((f32[2,2048]{1,0:T(2,128)S(1)}, f32[2,2048]{1,0:T(2,128)S(1)}, u32[]{:S(2)}, u32[]{:S(2)}) %collective-permute-start.29) | collective-permute-done | bytes 16416 | tf_op jit(solution)/shard_map/variance_2/ppermute | solution.py:105
  134.3 2.5 %collective-permute-start.30 = (f32[2,2048]{1,0:T(2,128)S(1)}, f32[2,2048]{1,0:T(2,128)S(1)}, u32[]{:S(2)}, u32[]{:S(2)}) collective-permute-start(f32[2,2048]{1,0:T(2,128)S(1)} %add.20), channel_id=1, source_target_pairs={{0,8},{2,10},{4,12},{6,14},{8,0},{10,2},{12,4},{14,6},{16,24},{18,... | collective-permute-start | bytes 49160 | tf_op jit(solution)/shard_map/variance_4/ppermute | solution.py:105
  (68 shorter events, 29.2 us)
Async XLA Ops:
  2.1 11.1 %collective-permute-start.4 = (bf16[2048,256]{1,0:T(8,128)(2,1)S(1)}, bf16[2048,256]{1,0:T(8,128)(2,1)S(1)}, u32[]{:S(2)}, u32[]{:S(2)}) collective-permute-start(bf16[2048,256]{1,0:T(8,128)(2,1)S(1)} %dynamic-slice_bitcast_fusion), channel_id=1, source_target_pairs={{0,1},{1,0},{2,3},{3,2},{4,5},{5,4},{6,7},{7,6},{8,9},{9,8},{10,11... | collective-permute-start | bytes 3145736 | tf_op jit(solution)/shard_map/panel_swap/ppermute | solution.py:99
  2.6 35.4 %collective-permute-start = (bf16[256,2048]{1,0:T(8,128)(2,1)}, bf16[256,2048]{1,0:T(8,128)(2,1)S(1)}, u32[]{:S(2)}, u32[]{:S(2)}) collective-permute-start(bf16[256,2048]{1,0:T(8,128)(2,1)} %refs_0_.1), channel_id=1, source_target_pairs={{0,4},{2,6},{4,0},{6,2},{8,12},{10,14},{12,8},{14,10},{16,20},{18,... | collective-permute-start | bytes 3145736 | tf_op jit(solution)/shard_map/inv_y/ppermute | solution.py:105
  7.1 30.9 %collective-permute-start.1 = (bf16[192,2048]{1,0:T(8,128)(2,1)S(1)}, bf16[192,2048]{1,0:T(8,128)(2,1)S(1)}, u32[]{:S(2)}, u32[]{:S(2)}) collective-permute-start(bf16[192,2048]{1,0:T(8,128)(2,1)S(1)} %get-tuple-element.52), channel_id=1, source_target_pairs={{0,8},{2,10},{4,12},{6,14},{8,0},{10,2},{12,4},{14,6},{16,24},{18,... | collective-permute-start | bytes 2359304 | tf_op jit(solution)/shard_map/inv_z0/ppermute | solution.py:105
  8.8 28.4 %collective-permute-start.2 = (bf16[1024,256]{1,0:T(8,128)(2,1)S(1)}, bf16[1024,256]{1,0:T(8,128)(2,1)S(1)}, u32[]{:S(2)}, u32[]{:S(2)}) collective-permute-start(bf16[1024,256]{1,0:T(8,128)(2,1)S(1)} %get-tuple-element.53.f0), channel_id=1, source_target_pairs={{0,16},{2,18},{4,20},{6,22},{8,24},{10,26},{12,28},{14,30},{16,0},... | collective-permute-start | bytes 1572872 | tf_op jit(solution)/shard_map/first_z/ppermute | solution.py:105
  11.4 25.8 %collective-permute-start.3 = (bf16[1024,256]{1,0:T(8,128)(2,1)S(1)}, bf16[1024,256]{1,0:T(8,128)(2,1)S(1)}, u32[]{:S(2)}, u32[]{:S(2)}) collective-permute-start(bf16[1024,256]{1,0:T(8,128)(2,1)S(1)} %get-tuple-element.53.f0), channel_id=1, source_target_pairs={{0,2},{2,0},{4,6},{6,4},{8,10},{10,8},{12,14},{14,12},{16,18},{18,... | collective-permute-start | bytes 1572872 | tf_op jit(solution)/shard_map/first_x/ppermute | solution.py:105
  38.0 26.9 %collective-permute-start.9 = (bf16[192,2048]{1,0:T(8,128)(2,1)S(1)}, bf16[192,2048]{1,0:T(8,128)(2,1)S(1)}, u32[]{:S(2)}, u32[]{:S(2)}) collective-permute-start(bf16[192,2048]{1,0:T(8,128)(2,1)S(1)} %collective-permute-done.1.refs_2_), channel_id=1, source_target_pairs={{0,4},{2,6},{4,0},{6,2},{8,12},{10,14},{12,8},{14,10},{16,20},{18,... | collective-permute-start | bytes 2359304 | tf_op jit(solution)/shard_map/inv_yz0/ppermute | solution.py:105
  38.4 25.1 %collective-permute-start.5 = (bf16[2048,128]{1,0:T(8,128)(2,1)S(1)}, bf16[2048,128]{1,0:T(8,128)(2,1)S(1)}, u32[]{:S(2)}, u32[]{:S(2)}) collective-permute-start(bf16[2048,128]{1,0:T(8,128)(2,1)S(1)} %get-tuple-element.72.r0), channel_id=1, source_target_pairs={{0,16},{2,18},{4,20},{6,22},{8,24},{10,26},{12,28},{14,30},{16,0},... | collective-permute-start | bytes 1572872 | tf_op jit(solution)/shard_map/rest0_z/ppermute | solution.py:105
  41.1 22.4 %collective-permute-start.6 = (bf16[2048,128]{1,0:T(8,128)(2,1)S(1)}, bf16[2048,128]{1,0:T(8,128)(2,1)S(1)}, u32[]{:S(2)}, u32[]{:S(2)}) collective-permute-start(bf16[2048,128]{1,0:T(8,128)(2,1)S(1)} %get-tuple-element.72.r0), channel_id=1, source_target_pairs={{0,2},{2,0},{4,6},{6,4},{8,10},{10,8},{12,14},{14,12},{16,18},{18,... | collective-permute-start | bytes 1572872 | tf_op jit(solution)/shard_map/rest0_x/ppermute | solution.py:105
  42.6 14.6 %collective-permute-start.8 = (bf16[64,2048]{1,0:T(8,128)(2,1)S(1)}, bf16[64,2048]{1,0:T(8,128)(2,1)S(1)}, u32[]{:S(2)}, u32[]{:S(2)}) collective-permute-start(bf16[64,2048]{1,0:T(8,128)(2,1)S(1)} %get-tuple-element.59), channel_id=1, source_target_pairs={{0,8},{2,10},{4,12},{6,14},{8,0},{10,2},{12,4},{14,6},{16,24},{18,... | collective-permute-start | bytes 786440 | tf_op jit(solution)/shard_map/inv_z1/ppermute | solution.py:105
  44.2 20.7 %collective-permute-start.7 = (bf16[1024,256]{1,0:T(8,128)(2,1)S(1)}, bf16[1024,256]{1,0:T(8,128)(2,1)S(1)}, u32[]{:S(2)}, u32[]{:S(2)}) collective-permute-start(bf16[1024,256]{1,0:T(8,128)(2,1)S(1)} %collective-permute-done.2.f0), channel_id=1, source_target_pairs={{0,2},{2,0},{4,6},{6,4},{8,10},{10,8},{12,14},{14,12},{16,18},{18,... | collective-permute-start | bytes 1572872 | tf_op jit(solution)/shard_map/first_xz/ppermute | solution.py:105
  57.2 7.8 %collective-permute-start.10 = (bf16[64,2048]{1,0:T(8,128)(2,1)S(1)}, bf16[64,2048]{1,0:T(8,128)(2,1)S(1)}, u32[]{:S(2)}, u32[]{:S(2)}) collective-permute-start(bf16[64,2048]{1,0:T(8,128)(2,1)S(1)} %collective-permute-done.8.refs_0_), channel_id=1, source_target_pairs={{0,4},{2,6},{4,0},{6,2},{8,12},{10,14},{12,8},{14,10},{16,20},{18,... | collective-permute-start | bytes 786440 | tf_op jit(solution)/shard_map/inv_yz1/ppermute | solution.py:105
  65.0 7.2 %collective-permute-start.11 = (bf16[704,2048]{1,0:T(8,128)(2,1)S(1)}, bf16[704,2048]{1,0:T(8,128)(2,1)S(1)}, u32[]{:S(2)}, u32[]{:S(2)}) collective-permute-start(bf16[704,2048]{1,0:T(8,128)(2,1)S(1)} %stack_rows.2.refs_0_), channel_id=1, source_target_pairs={{0,1},{1,0},{2,3},{3,2},{4,5},{5,4},{6,7},{7,6},{8,9},{9,8},{10,11... | collective-permute-start | bytes 8650760 | tf_op jit(solution)/shard_map/inv_swap/ppermute | solution.py:99
  65.6 14.8 %collective-permute-start.16 = (bf16[2048,128]{1,0:T(8,128)(2,1)S(1)}, bf16[2048,128]{1,0:T(8,128)(2,1)S(1)}, u32[]{:S(2)}, u32[]{:S(2)}) collective-permute-start(bf16[2048,128]{1,0:T(8,128)(2,1)S(1)} %collective-permute-done.5.r0), channel_id=1, source_target_pairs={{0,2},{2,0},{4,6},{6,4},{8,10},{10,8},{12,14},{14,12},{16,18},{18,... | collective-permute-start | bytes 1572872 | tf_op jit(solution)/shard_map/rest0_xz/ppermute | solution.py:105
  67.1 25.8 %collective-permute-start.13 = (bf16[2048,128]{1,0:T(8,128)(2,1)S(1)}, bf16[2048,128]{1,0:T(8,128)(2,1)S(1)}, u32[]{:S(2)}, u32[]{:S(2)}) collective-permute-start(bf16[2048,128]{1,0:T(8,128)(2,1)S(1)} %get-tuple-element.68.r0), channel_id=1, source_target_pairs={{0,16},{2,18},{4,20},{6,22},{8,24},{10,26},{12,28},{14,30},{16,0},... | collective-permute-start | bytes 1572872 | tf_op jit(solution)/shard_map/rest1_z/ppermute | solution.py:105
  69.2 23.7 %collective-permute-start.14 = (bf16[2048,128]{1,0:T(8,128)(2,1)S(1)}, bf16[2048,128]{1,0:T(8,128)(2,1)S(1)}, u32[]{:S(2)}, u32[]{:S(2)}) collective-permute-start(bf16[2048,128]{1,0:T(8,128)(2,1)S(1)} %get-tuple-element.68.r0), channel_id=1, source_target_pairs={{0,2},{2,0},{4,6},{6,4},{8,10},{10,8},{12,14},{14,12},{16,18},{18,... | collective-permute-start | bytes 1572872 | tf_op jit(solution)/shard_map/rest1_x/ppermute | solution.py:105
  85.0 8.4 %collective-permute-start.17 = (bf16[4,2,128,256]{3,2,1,0:T(8,128)(2,1)S(1)}, bf16[4,2,128,256]{3,2,1,0:T(8,128)(2,1)S(1)}, u32[]{:S(2)}, u32[]{:S(2)}) collective-permute-start(bf16[4,2,128,256]{3,2,1,0:T(8,128)(2,1)S(1)} %get-tuple-element.77), channel_id=1, source_target_pairs={{0,1},{1,0},{2,3},{3,2},{4,5},{5,4},{6,7},{7,6},{8,9},{9,8},{10,11... | collective-permute-start | bytes 1572872 | tf_op jit(solution)/shard_map/cross0_swap/ppermute | solution.py:99
  92.9 12.8 %collective-permute-start.15 = (bf16[2048,128]{1,0:T(8,128)(2,1)S(1)}, bf16[2048,128]{1,0:T(8,128)(2,1)S(1)}, u32[]{:S(2)}, u32[]{:S(2)}) collective-permute-start(bf16[2048,128]{1,0:T(8,128)(2,1)S(1)} %collective-permute-done.13.r0), channel_id=1, source_target_pairs={{0,2},{2,0},{4,6},{6,4},{8,10},{10,8},{12,14},{14,12},{16,18},{18,... | collective-permute-start | bytes 1572872 | tf_op jit(solution)/shard_map/rest1_xz/ppermute | solution.py:105
  93.5 12.2 %collective-permute-start.18 = (bf16[2,2,128,256]{3,2,1,0:T(8,128)(2,1)S(1)}, bf16[2,2,128,256]{3,2,1,0:T(8,128)(2,1)S(1)}, u32[]{:S(2)}, u32[]{:S(2)}) collective-permute-start(bf16[2,2,128,256]{3,2,1,0:T(8,128)(2,1)S(1)} %get-tuple-element.79), channel_id=1, source_target_pairs={{0,4},{2,6},{4,0},{6,2},{8,12},{10,14},{12,8},{14,10},{16,20},{18,... | collective-permute-start | bytes 786440 | tf_op jit(solution)/shard_map/cross0_1/ppermute | solution.py:105
  95.1 10.6 %collective-permute-start.19 = (bf16[2,2,128,256]{3,2,1,0:T(8,128)(2,1)S(1)}, bf16[2,2,128,256]{3,2,1,0:T(8,128)(2,1)S(1)}, u32[]{:S(2)}, u32[]{:S(2)}) collective-permute-start(bf16[2,2,128,256]{3,2,1,0:T(8,128)(2,1)S(1)} %get-tuple-element.80), channel_id=1, source_target_pairs={{0,8},{2,10},{4,12},{6,14},{8,0},{10,2},{12,4},{14,6},{16,24},{18,... | collective-permute-start | bytes 786440 | tf_op jit(solution)/shard_map/cross0_2/ppermute | solution.py:105
  95.5 11.7 %collective-permute-start.20 = (bf16[2,2,128,256]{3,2,1,0:T(8,128)(2,1)S(1)}, bf16[2,2,128,256]{3,2,1,0:T(8,128)(2,1)S(1)}, u32[]{:S(2)}, u32[]{:S(2)}) collective-permute-start(bf16[2,2,128,256]{3,2,1,0:T(8,128)(2,1)S(1)} %get-tuple-element.81), channel_id=1, source_target_pairs={{0,12},{2,14},{4,8},{6,10},{8,4},{10,6},{12,0},{14,2},{16,28},{18,... | collective-permute-start | bytes 786440 | tf_op jit(solution)/shard_map/cross0_3/ppermute | solution.py:105
  117.8 21.4 %collective-permute-start.25 = (bf16[2,2,128,256]{3,2,1,0:T(8,128)(2,1)S(1)}, bf16[2,2,128,256]{3,2,1,0:T(8,128)(2,1)S(1)}, u32[]{:S(2)}, u32[]{:S(2)}) collective-permute-start(bf16[2,2,128,256]{3,2,1,0:T(8,128)(2,1)S(1)} %get-tuple-element.95), channel_id=1, source_target_pairs={{0,4},{2,6},{4,0},{6,2},{8,12},{10,14},{12,8},{14,10},{16,20},{18,... | collective-permute-start | bytes 786440 | tf_op jit(solution)/shard_map/cross1_1/ppermute | solution.py:105
  119.3 19.9 %collective-permute-start.26 = (bf16[2,2,128,256]{3,2,1,0:T(8,128)(2,1)S(1)}, bf16[2,2,128,256]{3,2,1,0:T(8,128)(2,1)S(1)}, u32[]{:S(2)}, u32[]{:S(2)}) collective-permute-start(bf16[2,2,128,256]{3,2,1,0:T(8,128)(2,1)S(1)} %get-tuple-element.96), channel_id=1, source_target_pairs={{0,8},{2,10},{4,12},{6,14},{8,0},{10,2},{12,4},{14,6},{16,24},{18,... | collective-permute-start | bytes 786440 | tf_op jit(solution)/shard_map/cross1_2/ppermute | solution.py:105
  120.1 19.1 %collective-permute-start.27 = (bf16[2,2,128,256]{3,2,1,0:T(8,128)(2,1)S(1)}, bf16[2,2,128,256]{3,2,1,0:T(8,128)(2,1)S(1)}, u32[]{:S(2)}, u32[]{:S(2)}) collective-permute-start(bf16[2,2,128,256]{3,2,1,0:T(8,128)(2,1)S(1)} %get-tuple-element.97), channel_id=1, source_target_pairs={{0,12},{2,14},{4,8},{6,10},{8,4},{10,6},{12,0},{14,2},{16,28},{18,... | collective-permute-start | bytes 786440 | tf_op jit(solution)/shard_map/cross1_3/ppermute | solution.py:105
  121.3 9.2 %collective-permute-start.28 = (f32[2,2048]{1,0:T(2,128)S(1)}, f32[2,2048]{1,0:T(2,128)S(1)}, u32[]{:S(2)}, u32[]{:S(2)}) collective-permute-start(f32[2,2048]{1,0:T(2,128)S(1)} %add.18), channel_id=1, source_target_pairs={{0,16},{2,18},{4,20},{6,22},{8,24},{10,26},{12,28},{14,30},{16,0},... | collective-permute-start | bytes 49160 | tf_op jit(solution)/shard_map/variance_8/ppermute | solution.py:105
  (12 other events, 90.3 us)

commit v9 on v8

--- a/solution.py
+++ b/solution.py
@@ -91,6 +91,7 @@
 X, Y, ZL, ZH = 1, 2, 4, 8
 NGRP = 4
 SPLIT = 192
+TAIL = 16
 MIB = 1024 * 1024
 
 
@@ -235,40 +236,36 @@
 def products(structure, sel, firsts, rests, chunk, near=None):
     nblocks = structure.shape[1]
     early = firsts[0].shape[0]
-    late = rests[0].shape[0]
     first = early // BLK
+    spot = slice(chunk * LANES, (chunk + 1) * LANES)
 
     def body(st, sel_ref, f0, f1, r0, r1, *refs):
-        d = pl.program_id(0)
+        result, total = refs[-2:]
         n = lax.axis_index("narrow")
         w = lax.axis_index("wide")
         x = lax.bitwise_and(w, 1)
-        mask = lax.rem(d, 2) * Y + lax.div(d, 2) * ZL
-        row = lax.bitwise_xor(w, mask)
-        pos = jnp.int32(0)
-        inside = jnp.int32(0)
-        for j in range(nblocks):
-            hit = (pick(st, n, j, first) == row).astype(jnp.int32)
-            pos = pos + j * hit
-            inside = inside + hit
-
-        def compute(out_ref, sum_ref):
-            @pl.when(d == 0)
-            def _():
-                sum_ref[...] = jnp.zeros_like(sum_ref)
+        total[...] = jnp.zeros_like(total)
+        for d in range(NGRP):
+            row = lax.bitwise_xor(w, (d % 2) * Y + (d // 2) * ZL)
+            pos = jnp.int32(0)
+            inside = jnp.int32(0)
+            for j in range(nblocks):
+                hit = (pick(st, n, j, first) == row).astype(jnp.int32)
+                pos = pos + j * hit
+                inside = inside + hit
 
             @pl.when(inside == 0)
-            def _():
-                out_ref[...] = jnp.zeros_like(out_ref)
+            def _(d=d):
+                result[d] = jnp.zeros(result.shape[1:], result.dtype)
 
             @pl.when(inside > 0)
-            def _():
+            def _(d=d, pos=pos):
                 acc = jnp.dot(
-                    sel_ref[0, :, :early],
-                    jnp.concatenate([f0[...], f1[...]], axis=1),
+                    sel_ref[d, :, :early],
+                    jnp.concatenate([f0[:, spot], f1[:, spot]], axis=1),
                     preferred_element_type=jnp.float32,
                 ) + jnp.dot(
-                    sel_ref[0, :, early:],
+                    sel_ref[d, :, early:],
                     jnp.concatenate([r0[...], r1[...]], axis=1),
                     preferred_element_type=jnp.float32,
                 )
@@ -277,65 +274,58 @@
                     slot = lax.bitwise_xor(x, dx)
 
                     def weigh(rows, part=part, slot=slot):
-                        total = jnp.sum(part * rows.astype(jnp.float32), axis=0, keepdims=True)
-                        sum_ref[slot] += total
+                        added = jnp.sum(part * rows.astype(jnp.float32), axis=0, keepdims=True)
+                        total[slot] += added
 
                     @pl.when(pos < first)
                     def _():
                         at = pl.multiple_of(pos * BLK, BLK)
-                        weigh((f0, f1)[dx][pl.ds(at, BLK), :])
+                        weigh((f0, f1)[dx][pl.ds(at, BLK), spot])
 
                     @pl.when(pos >= first)
                     def _():
                         at = pl.multiple_of((pos - first) * BLK, BLK)
                         weigh((r0, r1)[dx][pl.ds(at, BLK), :])
 
-                    out_ref[0, slot] = (-part).T.astype(out_ref.dtype)
-
+                    at = pl.multiple_of(slot * LANES, LANES)
+                    result[d, pl.ds(at, LANES), :] = (-part).T.astype(result.dtype)
+
+        for slot in range(2):
+            left, terms = total[slot], []
+            for _ in range(3):
+                term = left.astype(result.dtype).astype(jnp.float32)
+                terms.append(term)
+                left = left - term
+            tile = jnp.concatenate(terms + [jnp.zeros((TAIL - 3, LANES), jnp.float32)], axis=0)
+            for d in range(NGRP):
+                result[d, 2 * LANES :, slot * LANES : (slot + 1) * LANES] = tile.astype(
+                    result.dtype
+                )
         if near is None:
-            compute(*refs)
+            refs[0][...] = result[...]
             return
-        near_ref, near_sum, kept, sent, kept_sum, sent_sum = refs
+        near_ref, kept, sent = refs[:3]
         stay = n == lax.div(w, ZH)
 
         @pl.when(stay)
         def _():
             kept[...] = near_ref[...]
-            kept_sum[...] = near_sum[...]
-            compute(sent, sent_sum)
+            sent[...] = result[...]
 
         @pl.when(jnp.logical_not(stay))
         def _():
+            kept[...] = result[...]
             sent[...] = near_ref[...]
-            sent_sum[...] = near_sum[...]
-            compute(kept, kept_sum)
-
-    front = pl.BlockSpec((early, LANES), lambda d, st: (0, chunk))
-    back = pl.BlockSpec((late, LANES), lambda d, st: (0, 0))
-    block = pl.BlockSpec((1, 2, LANES, BLK), lambda d, st: (d, 0, 0, 0))
-    total = pl.BlockSpec((2, 1, LANES), lambda d, st: (0, 0, 0))
-    outs = [
-        jax.ShapeDtypeStruct((NGRP, 2, LANES, BLK), sel.dtype),
-        jax.ShapeDtypeStruct((2, 1, LANES), jnp.float32),
-    ]
-    again = () if near is None else tuple(near)
-    return pl.pallas_call(
-        body,
-        out_shape=outs if near is None else [outs[0], outs[0], outs[1], outs[1]],
-        grid_spec=pltpu.PrefetchScalarGridSpec(
-            num_scalar_prefetch=1,
-            grid=(NGRP,),
-            in_specs=[
-                pl.BlockSpec((1, BLK, early + late), lambda d, st: (d, 0, 0)),
-                front,
-                front,
-                back,
-                back,
-            ]
-            + [block, total][: len(again)],
-            out_specs=[block, total] if near is None else [block, block, total, total],
-        ),
-        compiler_params=pltpu.CompilerParams(vmem_limit_bytes=14 * MIB),
+
+    out = jax.ShapeDtypeStruct((NGRP, 2 * LANES + TAIL, BLK), sel.dtype)
+    again = () if near is None else (near,)
+    return pl.pallas_call(
+        body,
+        out_shape=out if near is None else [out, out],
+        in_specs=[SMEM] + [VMEM] * (5 + len(again)),
+        out_specs=VMEM if near is None else [VMEM, VMEM],
+        scratch_shapes=[pltpu.VMEM(out.shape, out.dtype), pltpu.VMEM((2, 1, LANES), jnp.float32)],
+        compiler_params=pltpu.CompilerParams(vmem_limit_bytes=16 * MIB),
         cost_estimate=pl.CostEstimate(flops=0, bytes_accessed=0, transcendentals=0),
         name="products",
     )(structure, sel, *firsts, *rests, *again)
@@ -378,28 +368,33 @@
     )(factor_inv)
 
 
-def place_sums(linv, kept, back):
-    cols = linv.shape[1]
-
-    def body(linv_ref, kept0, kept1, back0, back1, out):
+def add_sums(base, messages, chunk):
+    cols = base.shape[1]
+
+    def body(base_ref, *refs):
+        out = refs[-1]
         n = lax.axis_index("narrow")
         group = lax.rem(lax.div(lax.axis_index("wide"), Y), NGRP)
-        out[...] = linv_ref[...]
-        for c, (ours, theirs) in enumerate(((kept0, back0), (kept1, back1))):
-            for xx in range(2):
-                at = pl.multiple_of(group * (cols // NGRP) + (2 * xx + c) * LANES, LANES)
-                for k in range(2):
-                    value = jnp.where(n == k, ours[xx], theirs[xx])
-                    out[k : k + 1, pl.ds(at, LANES)] += value
-
-    return pl.pallas_call(
-        body,
-        out_shape=jax.ShapeDtypeStruct(linv.shape, jnp.float32),
-        in_specs=[VMEM] * 5,
+        out[...] = base_ref[...]
+        for d in range(NGRP):
+            source = lax.bitwise_xor(group, d)
+            for k in range(2):
+                which = (n != k).astype(jnp.int32)
+                tile = refs[d][which, 2 * LANES :, :].astype(jnp.float32)
+                value = tile[0:1] + (tile[1:2] + tile[2:3])
+                for xx in range(2):
+                    at = source * (cols // NGRP) + (2 * xx + chunk) * LANES
+                    spot = pl.ds(pl.multiple_of(at, LANES), LANES)
+                    out[k : k + 1, spot] += value[:, xx * LANES : (xx + 1) * LANES]
+
+    return pl.pallas_call(
+        body,
+        out_shape=jax.ShapeDtypeStruct(base.shape, jnp.float32),
+        in_specs=[VMEM] * (1 + NGRP),
         out_specs=VMEM,
         compiler_params=pltpu.CompilerParams(vmem_limit_bytes=4 * MIB),
-        name="place_sums",
-    )(linv, *kept, *back)
+        name="add_sums",
+    )(base, *messages)
 
 
 def assemble(messages, chunk, held):
@@ -418,7 +413,9 @@
                 slot = 2 * d + xx
                 for k in range(2):
                     which = (n != k).astype(jnp.int32)
-                    value = msg_refs[d][which, xx].astype(jnp.float32)
+                    value = msg_refs[d][which, xx * LANES : (xx + 1) * LANES, :].astype(
+                        jnp.float32
+                    )
                     for lt in range(2):
                         wide_buf[slot, pl.ds(2 * lt + k, LANES, stride=4), :] = value[
                             :, lt * LANES : (lt + 1) * LANES
@@ -472,8 +469,8 @@
     a_yz0 = hop(a_z0, Y, "inv_yz0")
     a_yz1 = hop(a_z1, Y, "inv_yz1")
     most = stack_rows([inverse, a_y, a_z0])
-    r_z0, r_x0, f_xz, a_z1, a_yz0, a_yz1, most, *r_own = lax.optimization_barrier(
-        (r_z0, r_x0, f_xz, a_z1, a_yz0, a_yz1, most, *r_own)
+    r_z0, r_x0, f_xz, a_z1, a_yz0, a_yz1, most, linv, *r_own = lax.optimization_barrier(
+        (r_z0, r_x0, f_xz, a_z1, a_yz0, a_yz1, most, linv, *r_own)
     )
     r_z1 = hop(r_own[1], ZH, "rest1_z")
     r_xz0 = hop(r_z0, X, "rest0_xz")
@@ -482,7 +479,9 @@
     s_most = swap_cores(most, "inv_swap")
     s_more = swap_cores(more, "inv_swap_more")
     sel = pack_inverse(structure, (most, more), (s_most, s_more), first)
-    r_z1, r_x1 = lax.optimization_barrier((r_z1, r_x1))
+    for mask in (Y, ZL):
+        linv = linv + hop(linv, mask, f"squares_{mask}")
+    r_z1, r_x1, linv = lax.optimization_barrier((r_z1, r_x1, linv))
 
     def deliver(kept, sent, c):
         messages = bundle(kept, swap_cores(sent, f"cross{c}_swap"))
@@ -491,23 +490,19 @@
         ]
 
     near = products(structure, sel, (f_own, f_x), (r_own[0], r_x0), 0)
-    kept, sent, kept_sum0, sent_sum0 = products(
-        structure, sel, (f_z, f_xz), (r_z0, r_xz0), 0, near
-    )
+    kept, sent = products(structure, sel, (f_z, f_xz), (r_z0, r_xz0), 0, near)
     messages = deliver(kept, sent, 0)
     r_xz1 = hop(r_z1, X, "rest1_xz")
     near = products(structure, sel, (f_own, f_x), (r_own[1], r_x1), 1)
     r_xz1, *messages = lax.optimization_barrier((r_xz1, *messages))
-    kept, sent, kept_sum1, sent_sum1 = products(
-        structure, sel, (f_z, f_xz), (r_z1, r_xz1), 1, near
-    )
+    kept, sent = products(structure, sel, (f_z, f_xz), (r_z1, r_xz1), 1, near)
     held = assemble(messages, 0, None)
-    back = [swap_cores(total, "sums_swap") for total in (sent_sum0, sent_sum1)]
-    variance = place_sums(linv, (kept_sum0, kept_sum1), back)
-    variance = variance + hop(variance, X, "variance_x")
-    held = assemble(deliver(after(kept, variance), sent, 1), 1, held)
-    for mask in (ZH, Y, ZL):
-        variance = variance + hop(variance, mask, f"variance_{mask}")
+    variance = add_sums(linv, messages, 0)
+    messages = deliver(kept, sent, 1)
+    variance = add_sums(variance, messages, 1)
+    held = assemble(messages, 1, held)
+    hops = [hop(variance, mask, f"variance_{mask}") for mask in (X, ZH, X | ZH)]
+    variance = variance + hops[0] + hops[1] + hops[2]
     half = panel.shape[2] * size // 2
     cross = held.reshape(half, 2, 2, LANES).transpose(0, 2, 1, 3).reshape(half, 2, BLK)
     return cross, variance

time: 141 us -> 141 us (level)
  waiting for transfers between devices: 77 us -> 85.6 us
  Pallas kernels: 24.7 us -> 16.5 us
    pallas_call x5 -> x6, Pallas kernels: 18.4 us -> 10.3 us  [the longest x4 10.2 us: products(): pl.pallas_call(body, out_shape=out if near is None else [out, out], in_sp...]
    ppermute x24 -> x25, waiting for transfers between devices: 73.3 us -> 79.2 us  [hop(): return lax.ppermute(value, 'wide', [(i, i ^ mask) for i in range(size)])]
    ppermute x7 -> x5, waiting for transfers between devices: 3.69 us -> 6.42 us  [swap_cores(): return lax.ppermute(value, 'narrow', [(0, 1), (1, 0)])]
    ppermute x24 -> x25, starting transfers between devices: 32.5 us -> 33.3 us  [hop(): return lax.ppermute(value, 'wide', [(i, i ^ mask) for i in range(size)])]
  transfers between devices with their start and end apart: 31 -> 30, of which waited for: 15 -> 15; matrix products, arithmetic and copies ran while one was open for 0% -> 0% of each run, Pallas kernels for 14% -> 10%
where the time goes in v9:
time: 141 us
  waiting for transfers between devices  85.6 us (61%)
  starting transfers between devices  34.6 us (25%)
  Pallas kernels  16.5 us (12%)
  local copies, waits for them, and re-layouts  2.71 us (2%)
    ppermute x25, waiting for transfers between devices, hop(): return lax.ppermute(value, 'wide', [(i, i ^ mask) for i in range(size)])  79.2 us
    ppermute x25, starting transfers between devices, hop(): return lax.ppermute(value, 'wide', [(i, i ^ mask) for i in range(size)])  33.3 us
    pallas_call x4, Pallas kernels, products(): pl.pallas_call(body, out_shape=out if near is None else [out, out], in_sp...  10.2 us
    ppermute x5, waiting for transfers between devices, swap_cores(): return lax.ppermute(value, 'narrow', [(0, 1), (1, 0)])  6.42 us
  transfers between devices with their start and end apart: 30, of which 15 were waited for; matrix products, arithmetic and copies ran while one was open for 0% of the time, Pallas kernels for 10%

profile of v9, /device:TPU:0, one launch (start us, length us, event | category | flops | bytes accessed | tf_op | source)
XLA Modules:
  0.0 140.9 jit_solution(4480405899146253502)
XLA Ops:
  2.6 2.6 %collective-permute-start = (bf16[256,2048]{1,0:T(8,128)(2,1)}, bf16[256,2048]{1,0:T(8,128)(2,1)S(1)}, u32[]{:S(2)}, u32[]{:S(2)}) collective-permute-start(bf16[256,2048]{1,0:T(8,128)(2,1)} %refs_0_.1), channel_id=1, source_target_pairs={{0,4},{2,6},{4,0},{6,2},{8,12},{10,14},{12,8},{14,10},{16,20},{18,... | collective-permute-start | bytes 3145736 | tf_op jit(solution)/shard_map/inv_y/ppermute | solution.py:106
  8.8 2.6 %collective-permute-start.2 = (bf16[1024,256]{1,0:T(8,128)(2,1)S(1)}, bf16[1024,256]{1,0:T(8,128)(2,1)S(1)}, u32[]{:S(2)}, u32[]{:S(2)}) collective-permute-start(bf16[1024,256]{1,0:T(8,128)(2,1)S(1)} %get-tuple-element.46.f0), channel_id=1, source_target_pairs={{0,16},{2,18},{4,20},{6,22},{8,24},{10,26},{12,28},{14,30},{16,0},... | collective-permute-start | bytes 1572872 | tf_op jit(solution)/shard_map/first_z/ppermute | solution.py:106
  14.1 23.0 %collective-permute-done.2.f0 = bf16[1024,256]{1,0:T(8,128)(2,1)S(1)} collective-permute-done((bf16[1024,256]{1,0:T(8,128)(2,1)S(1)}, bf16[1024,256]{1,0:T(8,128)(2,1)S(1)}, u32[]{:S(2)}, u32[]{:S(2)}) %collective-permute-start.2) | collective-permute-done | bytes 524320 | tf_op jit(solution)/shard_map/first_z/ppermute | solution.py:106
  40.0 2.7 %collective-permute-start.8 = (bf16[64,2048]{1,0:T(8,128)(2,1)S(1)}, bf16[64,2048]{1,0:T(8,128)(2,1)S(1)}, u32[]{:S(2)}, u32[]{:S(2)}) collective-permute-start(bf16[64,2048]{1,0:T(8,128)(2,1)S(1)} %get-tuple-element.52), channel_id=1, source_target_pairs={{0,8},{2,10},{4,12},{6,14},{8,0},{10,2},{12,4},{14,6},{16,24},{18,... | collective-permute-start | bytes 786440 | tf_op jit(solution)/shard_map/inv_z1/ppermute | solution.py:106
  44.7 7.6 %collective-permute-done.8.refs_0_ = bf16[64,2048]{1,0:T(8,128)(2,1)S(1)} collective-permute-done((bf16[64,2048]{1,0:T(8,128)(2,1)S(1)}, bf16[64,2048]{1,0:T(8,128)(2,1)S(1)}, u32[]{:S(2)}, u32[]{:S(2)}) %collective-permute-start.8) | collective-permute-done | bytes 262176 | tf_op jit(solution)/shard_map/inv_z1/ppermute | solution.py:106
  54.1 13.2 %collective-permute-done.5.r0 = bf16[2048,128]{1,0:T(8,128)(2,1)S(1)} collective-permute-done((bf16[2048,128]{1,0:T(8,128)(2,1)S(1)}, bf16[2048,128]{1,0:T(8,128)(2,1)S(1)}, u32[]{:S(2)}, u32[]{:S(2)}) %collective-permute-start.5) | collective-permute-done | bytes 524320 | tf_op jit(solution)/shard_map/rest0_z/ppermute | solution.py:106
  70.0 4.5 %collective-permute-done.12.refs_3_ = bf16[320,2048]{1,0:T(8,128)(2,1)S(1)} collective-permute-done((bf16[320,2048]{1,0:T(8,128)(2,1)S(1)}, bf16[320,2048]{1,0:T(8,128)(2,1)S(1)}, u32[]{:S(2)}, u32[]{:S(2)}) %collective-permute-start.12) | collective-permute-done | bytes 1310752 | tf_op jit(solution)/shard_map/inv_swap_more/ppermute | solution.py:100
  74.5 1.7 %pack_inverse.1.sel_ref = bf16[4,256,3072]{2,1,0:T(8,128)(2,1)S(1)} custom-call(s32[2,12]{1,0:T(2,128)S(1)} %copy-done.4, bf16[704,2048]{1,0:T(8,128)(2,1)S(1)} %stack_rows.2.refs_0_, bf16[320,2048]{1,0:T(8,128)(2,1)S(1)} %stack_rows.3.refs_1_, bf16[704,2048]{1,0:T(8,128)(2,1)S(1)} %collective-permute-done.11.refs_2_, ...), custom_call_target="tpu_custom_call" | custom-call | tf_op jit(solution)/shard_map/pack_inverse/pallas_call | solution.py:226
  76.2 2.5 %products.4.refs_0_ = bf16[4,272,256]{2,1,0:T(8,128)(2,1)S(1)} custom-call(s32[2,12]{1,0:T(2,128)S(1)} %copy-done.4, bf16[4,256,3072]{2,1,0:T(8,128)(2,1)S(1)} %pack_inverse.1.sel_ref, bf16[1024,256]{1,0:T(8,128)(2,1)S(1)} %get-tuple-element.46.f0, bf16[1024,256]{1,0:T(8,128)(2,1)S(1)} %collective-permute-done.3.f1, ...), custom_call_target="tpu_custom_call" | custom-call | tf_op jit(solution)/shard_map/products/pallas_call | solution.py:322
  78.7 4.1 %collective-permute-done.18.r1 = bf16[2048,128]{1,0:T(8,128)(2,1)S(1)} collective-permute-done((bf16[2048,128]{1,0:T(8,128)(2,1)S(1)}, bf16[2048,128]{1,0:T(8,128)(2,1)S(1)}, u32[]{:S(2)}, u32[]{:S(2)}) %collective-permute-start.18) | collective-permute-done | bytes 524320 | tf_op jit(solution)/shard_map/rest0_xz/ppermute | solution.py:106
  82.7 2.5 %products.5 = (bf16[4,272,256]{2,1,0:T(8,128)(2,1)S(1)}, bf16[4,272,256]{2,1,0:T(8,128)(2,1)S(1)}) custom-call(s32[2,12]{1,0:T(2,128)S(1)} %copy-done.4, bf16[4,256,3072]{2,1,0:T(8,128)(2,1)S(1)} %pack_inverse.1.sel_ref, bf16[1024,256]{1,0:T(8,128)(2,1)S(1)} %collective-permute-done.2.f0, bf16[1024,256]{1,0:T(8,128)(2,1)S(1)} %collective-permute-done.7.f1, ...), custom_call_target="tpu_custom_call" | custom-call | tf_op jit(solution)/shard_map/products/pallas_call | solution.py:322
  86.9 2.2 %collective-permute-done.15 = f32[2,2048]{1,0:T(2,128)S(1)} collective-permute-done((f32[2,2048]{1,0:T(2,128)S(1)}, f32[2,2048]{1,0:T(2,128)S(1)}, u32[]{:S(2)}, u32[]{:S(2)}) %collective-permute-start.15) | collective-permute-done | bytes 16416 | tf_op jit(solution)/shard_map/squares_2/ppermute | solution.py:106
  89.2 4.1 %collective-permute-done.16 = f32[2,2048]{1,0:T(2,128)S(1)} collective-permute-done((f32[2,2048]{1,0:T(2,128)S(1)}, f32[2,2048]{1,0:T(2,128)S(1)}, u32[]{:S(2)}, u32[]{:S(2)}) %collective-permute-start.16) | collective-permute-done | bytes 16416 | tf_op jit(solution)/shard_map/squares_4/ppermute | solution.py:106
  96.6 2.0 %collective-permute-start.22 = (bf16[2,272,256]{2,1,0:T(8,128)(2,1)S(1)}, bf16[2,272,256]{2,1,0:T(8,128)(2,1)S(1)}, u32[]{:S(2)}, u32[]{:S(2)}) collective-permute-start(bf16[2,272,256]{2,1,0:T(8,128)(2,1)S(1)} %get-tuple-element.74), channel_id=1, source_target_pairs={{0,12},{2,14},{4,8},{6,10},{8,4},{10,6},{12,0},{14,2},{16,28},{18,... | collective-permute-start | bytes 835592 | tf_op jit(solution)/shard_map/cross0_3/ppermute | solution.py:106
  98.5 2.7 %products.6.refs_0_ = bf16[4,272,256]{2,1,0:T(8,128)(2,1)S(1)} custom-call(s32[2,12]{1,0:T(2,128)S(1)} %copy-done.4, bf16[4,256,3072]{2,1,0:T(8,128)(2,1)S(1)} %pack_inverse.1.sel_ref, bf16[1024,256]{1,0:T(8,128)(2,1)S(1)} %get-tuple-element.46.f0, bf16[1024,256]{1,0:T(8,128)(2,1)S(1)} %collective-permute-done.3.f1, ...), custom_call_target="tpu_custom_call" | custom-call | tf_op jit(solution)/shard_map/products/pallas_call | solution.py:322
  101.2 6.1 %collective-permute-done.17.r1 = bf16[2048,128]{1,0:T(8,128)(2,1)S(1)} collective-permute-done((bf16[2048,128]{1,0:T(8,128)(2,1)S(1)}, bf16[2048,128]{1,0:T(8,128)(2,1)S(1)}, u32[]{:S(2)}, u32[]{:S(2)}) %collective-permute-start.17) | collective-permute-done | bytes 524320 | tf_op jit(solution)/shard_map/rest1_xz/ppermute | solution.py:106
  107.3 3.2 %collective-permute-done.22.refs_3_ = bf16[2,272,256]{2,1,0:T(8,128)(2,1)S(1)} collective-permute-done((bf16[2,272,256]{2,1,0:T(8,128)(2,1)S(1)}, bf16[2,272,256]{2,1,0:T(8,128)(2,1)S(1)}, u32[]{:S(2)}, u32[]{:S(2)}) %collective-permute-start.22) | collective-permute-done | bytes 278560 | tf_op jit(solution)/shard_map/cross0_3/ppermute | solution.py:106
  110.5 2.5 %products.7 = (bf16[4,272,256]{2,1,0:T(8,128)(2,1)S(1)}, bf16[4,272,256]{2,1,0:T(8,128)(2,1)S(1)}) custom-call(s32[2,12]{1,0:T(2,128)S(1)} %copy-done.4, bf16[4,256,3072]{2,1,0:T(8,128)(2,1)S(1)} %pack_inverse.1.sel_ref, bf16[1024,256]{1,0:T(8,128)(2,1)S(1)} %collective-permute-done.2.f0, bf16[1024,256]{1,0:T(8,128)(2,1)S(1)} %collective-permute-done.7.f1, ...), custom_call_target="tpu_custom_call" | custom-call | tf_op jit(solution)/shard_map/products/pallas_call | solution.py:322
  113.1 1.9 %collective-permute-done.23.back_ref = bf16[4,272,256]{2,1,0:T(8,128)(2,1)S(1)} collective-permute-done((bf16[4,272,256]{2,1,0:T(8,128)(2,1)S(1)}, bf16[4,272,256]{2,1,0:T(8,128)(2,1)S(1)}, u32[]{:S(2)}, u32[]{:S(2)}) %collective-permute-start.23) | collective-permute-done | bytes 557088 | tf_op jit(solution)/shard_map/cross1_swap/ppermute | solution.py:100
  118.7 5.2 %collective-permute-done.24.refs_1_ = bf16[2,272,256]{2,1,0:T(8,128)(2,1)S(1)} collective-permute-done((bf16[2,272,256]{2,1,0:T(8,128)(2,1)S(1)}, bf16[2,272,256]{2,1,0:T(8,128)(2,1)S(1)}, u32[]{:S(2)}, u32[]{:S(2)}) %collective-permute-start.24) | collective-permute-done | bytes 278560 | tf_op jit(solution)/shard_map/cross1_1/ppermute | solution.py:106
  123.9 2.4 %collective-permute-done.25.refs_2_ = bf16[2,272,256]{2,1,0:T(8,128)(2,1)S(1)} collective-permute-done((bf16[2,272,256]{2,1,0:T(8,128)(2,1)S(1)}, bf16[2,272,256]{2,1,0:T(8,128)(2,1)S(1)}, u32[]{:S(2)}, u32[]{:S(2)}) %collective-permute-start.25) | collective-permute-done | bytes 278560 | tf_op jit(solution)/shard_map/cross1_2/ppermute | solution.py:106
  126.3 4.8 %collective-permute-done.26.refs_3_ = bf16[2,272,256]{2,1,0:T(8,128)(2,1)S(1)} collective-permute-done((bf16[2,272,256]{2,1,0:T(8,128)(2,1)S(1)}, bf16[2,272,256]{2,1,0:T(8,128)(2,1)S(1)}, u32[]{:S(2)}, u32[]{:S(2)}) %collective-permute-start.26) | collective-permute-done | bytes 278560 | tf_op jit(solution)/shard_map/cross1_3/ppermute | solution.py:106
  132.5 2.2 %collective-permute-start.28 = (f32[2,2048]{1,0:T(2,128)S(1)}, f32[2,2048]{1,0:T(2,128)S(1)}, u32[]{:S(2)}, u32[]{:S(2)}) collective-permute-start(f32[2,2048]{1,0:T(2,128)S(1)} %add_sums.3), channel_id=1, source_target_pairs={{0,16},{2,18},{4,20},{6,22},{8,24},{10,26},{12,28},{14,30},{16,0},... | collective-permute-start | bytes 49160 | tf_op jit(solution)/shard_map/variance_8/ppermute | solution.py:106
  137.7 2.5 %collective-permute-done.29 = f32[2,2048]{1,0:T(2,128)S(1)} collective-permute-done((f32[2,2048]{1,0:T(2,128)S(1)}, f32[2,2048]{1,0:T(2,128)S(1)}, u32[]{:S(2)}, u32[]{:S(2)}) %collective-permute-start.29) | collective-permute-done | bytes 16416 | tf_op jit(solution)/shard_map/variance_9/ppermute | solution.py:106
  (66 shorter events, 31.5 us)
Async XLA Ops:
  2.1 11.1 %collective-permute-start.4 = (bf16[2048,256]{1,0:T(8,128)(2,1)S(1)}, bf16[2048,256]{1,0:T(8,128)(2,1)S(1)}, u32[]{:S(2)}, u32[]{:S(2)}) collective-permute-start(bf16[2048,256]{1,0:T(8,128)(2,1)S(1)} %dynamic-slice_bitcast_fusion), channel_id=1, source_target_pairs={{0,1},{1,0},{2,3},{3,2},{4,5},{5,4},{6,7},{7,6},{8,9},{9,8},{10,11... | collective-permute-start | bytes 3145736 | tf_op jit(solution)/shard_map/panel_swap/ppermute | solution.py:100
  2.6 35.4 %collective-permute-start = (bf16[256,2048]{1,0:T(8,128)(2,1)}, bf16[256,2048]{1,0:T(8,128)(2,1)S(1)}, u32[]{:S(2)}, u32[]{:S(2)}) collective-permute-start(bf16[256,2048]{1,0:T(8,128)(2,1)} %refs_0_.1), channel_id=1, source_target_pairs={{0,4},{2,6},{4,0},{6,2},{8,12},{10,14},{12,8},{14,10},{16,20},{18,... | collective-permute-start | bytes 3145736 | tf_op jit(solution)/shard_map/inv_y/ppermute | solution.py:106
  7.1 30.9 %collective-permute-start.1 = (bf16[192,2048]{1,0:T(8,128)(2,1)S(1)}, bf16[192,2048]{1,0:T(8,128)(2,1)S(1)}, u32[]{:S(2)}, u32[]{:S(2)}) collective-permute-start(bf16[192,2048]{1,0:T(8,128)(2,1)S(1)} %get-tuple-element.45), channel_id=1, source_target_pairs={{0,8},{2,10},{4,12},{6,14},{8,0},{10,2},{12,4},{14,6},{16,24},{18,... | collective-permute-start | bytes 2359304 | tf_op jit(solution)/shard_map/inv_z0/ppermute | solution.py:106
  8.8 28.4 %collective-permute-start.2 = (bf16[1024,256]{1,0:T(8,128)(2,1)S(1)}, bf16[1024,256]{1,0:T(8,128)(2,1)S(1)}, u32[]{:S(2)}, u32[]{:S(2)}) collective-permute-start(bf16[1024,256]{1,0:T(8,128)(2,1)S(1)} %get-tuple-element.46.f0), channel_id=1, source_target_pairs={{0,16},{2,18},{4,20},{6,22},{8,24},{10,26},{12,28},{14,30},{16,0},... | collective-permute-start | bytes 1572872 | tf_op jit(solution)/shard_map/first_z/ppermute | solution.py:106
  11.4 25.8 %collective-permute-start.3 = (bf16[1024,256]{1,0:T(8,128)(2,1)S(1)}, bf16[1024,256]{1,0:T(8,128)(2,1)S(1)}, u32[]{:S(2)}, u32[]{:S(2)}) collective-permute-start(bf16[1024,256]{1,0:T(8,128)(2,1)S(1)} %get-tuple-element.46.f0), channel_id=1, source_target_pairs={{0,2},{2,0},{4,6},{6,4},{8,10},{10,8},{12,14},{14,12},{16,18},{18,... | collective-permute-start | bytes 1572872 | tf_op jit(solution)/shard_map/first_x/ppermute | solution.py:106
  38.0 29.2 %collective-permute-start.9 = (bf16[192,2048]{1,0:T(8,128)(2,1)S(1)}, bf16[192,2048]{1,0:T(8,128)(2,1)S(1)}, u32[]{:S(2)}, u32[]{:S(2)}) collective-permute-start(bf16[192,2048]{1,0:T(8,128)(2,1)S(1)} %collective-permute-done.1.refs_2_), channel_id=1, source_target_pairs={{0,4},{2,6},{4,0},{6,2},{8,12},{10,14},{12,8},{14,10},{16,20},{18,... | collective-permute-start | bytes 2359304 | tf_op jit(solution)/shard_map/inv_yz0/ppermute | solution.py:106
  38.4 15.7 %collective-permute-start.7 = (bf16[1024,256]{1,0:T(8,128)(2,1)S(1)}, bf16[1024,256]{1,0:T(8,128)(2,1)S(1)}, u32[]{:S(2)}, u32[]{:S(2)}) collective-permute-start(bf16[1024,256]{1,0:T(8,128)(2,1)S(1)} %collective-permute-done.2.f0), channel_id=1, source_target_pairs={{0,2},{2,0},{4,6},{6,4},{8,10},{10,8},{12,14},{14,12},{16,18},{18,... | collective-permute-start | bytes 1572872 | tf_op jit(solution)/shard_map/first_xz/ppermute | solution.py:106
  40.0 12.3 %collective-permute-start.8 = (bf16[64,2048]{1,0:T(8,128)(2,1)S(1)}, bf16[64,2048]{1,0:T(8,128)(2,1)S(1)}, u32[]{:S(2)}, u32[]{:S(2)}) collective-permute-start(bf16[64,2048]{1,0:T(8,128)(2,1)S(1)} %get-tuple-element.52), channel_id=1, source_target_pairs={{0,8},{2,10},{4,12},{6,14},{8,0},{10,2},{12,4},{14,6},{16,24},{18,... | collective-permute-start | bytes 786440 | tf_op jit(solution)/shard_map/inv_z1/ppermute | solution.py:106
  42.7 24.5 %collective-permute-start.5 = (bf16[2048,128]{1,0:T(8,128)(2,1)S(1)}, bf16[2048,128]{1,0:T(8,128)(2,1)S(1)}, u32[]{:S(2)}, u32[]{:S(2)}) collective-permute-start(bf16[2048,128]{1,0:T(8,128)(2,1)S(1)} %get-tuple-element.67.r0), channel_id=1, source_target_pairs={{0,16},{2,18},{4,20},{6,22},{8,24},{10,26},{12,28},{14,30},{16,0},... | collective-permute-start | bytes 1572872 | tf_op jit(solution)/shard_map/rest0_z/ppermute | solution.py:106
  44.2 23.0 %collective-permute-start.6 = (bf16[2048,128]{1,0:T(8,128)(2,1)S(1)}, bf16[2048,128]{1,0:T(8,128)(2,1)S(1)}, u32[]{:S(2)}, u32[]{:S(2)}) collective-permute-start(bf16[2048,128]{1,0:T(8,128)(2,1)S(1)} %get-tuple-element.67.r0), channel_id=1, source_target_pairs={{0,2},{2,0},{4,6},{6,4},{8,10},{10,8},{12,14},{14,12},{16,18},{18,... | collective-permute-start | bytes 1572872 | tf_op jit(solution)/shard_map/rest0_x/ppermute | solution.py:106
  52.3 14.9 %collective-permute-start.10 = (bf16[64,2048]{1,0:T(8,128)(2,1)S(1)}, bf16[64,2048]{1,0:T(8,128)(2,1)S(1)}, u32[]{:S(2)}, u32[]{:S(2)}) collective-permute-start(bf16[64,2048]{1,0:T(8,128)(2,1)S(1)} %collective-permute-done.8.refs_0_), channel_id=1, source_target_pairs={{0,4},{2,6},{4,0},{6,2},{8,12},{10,14},{12,8},{14,10},{16,20},{18,... | collective-permute-start | bytes 786440 | tf_op jit(solution)/shard_map/inv_yz1/ppermute | solution.py:106
  67.2 7.2 %collective-permute-start.11 = (bf16[704,2048]{1,0:T(8,128)(2,1)S(1)}, bf16[704,2048]{1,0:T(8,128)(2,1)S(1)}, u32[]{:S(2)}, u32[]{:S(2)}) collective-permute-start(bf16[704,2048]{1,0:T(8,128)(2,1)S(1)} %stack_rows.2.refs_0_), channel_id=1, source_target_pairs={{0,1},{1,0},{2,3},{3,2},{4,5},{5,4},{6,7},{7,6},{8,9},{9,8},{10,11... | collective-permute-start | bytes 8650760 | tf_op jit(solution)/shard_map/inv_swap/ppermute | solution.py:100
  67.4 7.1 %collective-permute-start.12 = (bf16[320,2048]{1,0:T(8,128)(2,1)S(1)}, bf16[320,2048]{1,0:T(8,128)(2,1)S(1)}, u32[]{:S(2)}, u32[]{:S(2)}) collective-permute-start(bf16[320,2048]{1,0:T(8,128)(2,1)S(1)} %stack_rows.3.refs_1_), channel_id=1, source_target_pairs={{0,1},{1,0},{2,3},{3,2},{4,5},{5,4},{6,7},{7,6},{8,9},{9,8},{10,11... | collective-permute-start | bytes 3932168 | tf_op jit(solution)/shard_map/inv_swap_more/ppermute | solution.py:100
  68.0 14.8 %collective-permute-start.18 = (bf16[2048,128]{1,0:T(8,128)(2,1)S(1)}, bf16[2048,128]{1,0:T(8,128)(2,1)S(1)}, u32[]{:S(2)}, u32[]{:S(2)}) collective-permute-start(bf16[2048,128]{1,0:T(8,128)(2,1)S(1)} %collective-permute-done.5.r0), channel_id=1, source_target_pairs={{0,2},{2,0},{4,6},{6,4},{8,10},{10,8},{12,14},{14,12},{16,18},{18,... | collective-permute-start | bytes 1572872 | tf_op jit(solution)/shard_map/rest0_xz/ppermute | solution.py:106
  68.5 24.8 %collective-permute-start.13 = (bf16[2048,128]{1,0:T(8,128)(2,1)S(1)}, bf16[2048,128]{1,0:T(8,128)(2,1)S(1)}, u32[]{:S(2)}, u32[]{:S(2)}) collective-permute-start(bf16[2048,128]{1,0:T(8,128)(2,1)S(1)} %get-tuple-element.62.r0), channel_id=1, source_target_pairs={{0,16},{2,18},{4,20},{6,22},{8,24},{10,26},{12,28},{14,30},{16,0},... | collective-permute-start | bytes 1572872 | tf_op jit(solution)/shard_map/rest1_z/ppermute | solution.py:106
  68.5 24.8 %collective-permute-start.14 = (bf16[2048,128]{1,0:T(8,128)(2,1)S(1)}, bf16[2048,128]{1,0:T(8,128)(2,1)S(1)}, u32[]{:S(2)}, u32[]{:S(2)}) collective-permute-start(bf16[2048,128]{1,0:T(8,128)(2,1)S(1)} %get-tuple-element.62.r0), channel_id=1, source_target_pairs={{0,2},{2,0},{4,6},{6,4},{8,10},{10,8},{12,14},{14,12},{16,18},{18,... | collective-permute-start | bytes 1572872 | tf_op jit(solution)/shard_map/rest1_x/ppermute | solution.py:106
  85.3 9.6 %collective-permute-start.19 = (bf16[4,272,256]{2,1,0:T(8,128)(2,1)S(1)}, bf16[4,272,256]{2,1,0:T(8,128)(2,1)S(1)}, u32[]{:S(2)}, u32[]{:S(2)}) collective-permute-start(bf16[4,272,256]{2,1,0:T(8,128)(2,1)S(1)} %get-tuple-element.70), channel_id=1, source_target_pairs={{0,1},{1,0},{2,3},{3,2},{4,5},{5,4},{6,7},{7,6},{8,9},{9,8},{10,11... | collective-permute-start | bytes 1671176 | tf_op jit(solution)/shard_map/cross0_swap/ppermute | solution.py:100
  93.3 13.9 %collective-permute-start.17 = (bf16[2048,128]{1,0:T(8,128)(2,1)S(1)}, bf16[2048,128]{1,0:T(8,128)(2,1)S(1)}, u32[]{:S(2)}, u32[]{:S(2)}) collective-permute-start(bf16[2048,128]{1,0:T(8,128)(2,1)S(1)} %collective-permute-done.13.r0), channel_id=1, source_target_pairs={{0,2},{2,0},{4,6},{6,4},{8,10},{10,8},{12,14},{14,12},{16,18},{18,... | collective-permute-start | bytes 1572872 | tf_op jit(solution)/shard_map/rest1_xz/ppermute | solution.py:106
  95.0 12.3 %collective-permute-start.20 = (bf16[2,272,256]{2,1,0:T(8,128)(2,1)S(1)}, bf16[2,272,256]{2,1,0:T(8,128)(2,1)S(1)}, u32[]{:S(2)}, u32[]{:S(2)}) collective-permute-start(bf16[2,272,256]{2,1,0:T(8,128)(2,1)S(1)} %get-tuple-element.72), channel_id=1, source_target_pairs={{0,4},{2,6},{4,0},{6,2},{8,12},{10,14},{12,8},{14,10},{16,20},{18,... | collective-permute-start | bytes 835592 | tf_op jit(solution)/shard_map/cross0_1/ppermute | solution.py:106
  96.6 10.7 %collective-permute-start.21 = (bf16[2,272,256]{2,1,0:T(8,128)(2,1)S(1)}, bf16[2,272,256]{2,1,0:T(8,128)(2,1)S(1)}, u32[]{:S(2)}, u32[]{:S(2)}) collective-permute-start(bf16[2,272,256]{2,1,0:T(8,128)(2,1)S(1)} %get-tuple-element.73), channel_id=1, source_target_pairs={{0,8},{2,10},{4,12},{6,14},{8,0},{10,2},{12,4},{14,6},{16,24},{18,... | collective-permute-start | bytes 835592 | tf_op jit(solution)/shard_map/cross0_2/ppermute | solution.py:106
  96.6 13.9 %collective-permute-start.22 = (bf16[2,272,256]{2,1,0:T(8,128)(2,1)S(1)}, bf16[2,272,256]{2,1,0:T(8,128)(2,1)S(1)}, u32[]{:S(2)}, u32[]{:S(2)}) collective-permute-start(bf16[2,272,256]{2,1,0:T(8,128)(2,1)S(1)} %get-tuple-element.74), channel_id=1, source_target_pairs={{0,12},{2,14},{4,8},{6,10},{8,4},{10,6},{12,0},{14,2},{16,28},{18,... | collective-permute-start | bytes 835592 | tf_op jit(solution)/shard_map/cross0_3/ppermute | solution.py:106
  115.1 8.8 %collective-permute-start.24 = (bf16[2,272,256]{2,1,0:T(8,128)(2,1)S(1)}, bf16[2,272,256]{2,1,0:T(8,128)(2,1)S(1)}, u32[]{:S(2)}, u32[]{:S(2)}) collective-permute-start(bf16[2,272,256]{2,1,0:T(8,128)(2,1)S(1)} %get-tuple-element.80), channel_id=1, source_target_pairs={{0,4},{2,6},{4,0},{6,2},{8,12},{10,14},{12,8},{14,10},{16,20},{18,... | collective-permute-start | bytes 835592 | tf_op jit(solution)/shard_map/cross1_1/ppermute | solution.py:106
  116.7 9.5 %collective-permute-start.25 = (bf16[2,272,256]{2,1,0:T(8,128)(2,1)S(1)}, bf16[2,272,256]{2,1,0:T(8,128)(2,1)S(1)}, u32[]{:S(2)}, u32[]{:S(2)}) collective-permute-start(bf16[2,272,256]{2,1,0:T(8,128)(2,1)S(1)} %get-tuple-element.81), channel_id=1, source_target_pairs={{0,8},{2,10},{4,12},{6,14},{8,0},{10,2},{12,4},{14,6},{16,24},{18,... | collective-permute-start | bytes 835592 | tf_op jit(solution)/shard_map/cross1_2/ppermute | solution.py:106
  117.0 14.0 %collective-permute-start.26 = (bf16[2,272,256]{2,1,0:T(8,128)(2,1)S(1)}, bf16[2,272,256]{2,1,0:T(8,128)(2,1)S(1)}, u32[]{:S(2)}, u32[]{:S(2)}) collective-permute-start(bf16[2,272,256]{2,1,0:T(8,128)(2,1)S(1)} %get-tuple-element.82), channel_id=1, source_target_pairs={{0,12},{2,14},{4,8},{6,10},{8,4},{10,6},{12,0},{14,2},{16,28},{18,... | collective-permute-start | bytes 835592 | tf_op jit(solution)/shard_map/cross1_3/ppermute | solution.py:106
  (11 other events, 84.8 us)

commit v10 on v9

--- a/solution.py
+++ b/solution.py
@@ -119,11 +119,12 @@
 def pack_first(structure, panel, inverse, first):
     half_blocks = panel.shape[1] // BLK
 
-    def body(st, panel_ref, inv_ref, out, *pieces):
+    def body(st, panel_ref, inv_ref, out, rest, *pieces):
         n = lax.axis_index("narrow")
         for j in range(first):
             row = pl.multiple_of(lax.rem(pick(st, n, j, first), half_blocks) * BLK, BLK)
             out[j * BLK : (j + 1) * BLK, :] = panel_ref[n, pl.ds(row, BLK), :]
+        rest[...] = panel_ref[1 - n]
         pieces[0][...] = inv_ref[:SPLIT, :]
         pieces[1][...] = inv_ref[SPLIT:, :]
 
@@ -132,12 +133,13 @@
         body,
         out_shape=[
             jax.ShapeDtypeStruct((first * BLK, panel.shape[2]), panel.dtype),
+            jax.ShapeDtypeStruct(panel.shape[1:], panel.dtype),
             jax.ShapeDtypeStruct((SPLIT, width), inverse.dtype),
             jax.ShapeDtypeStruct((BLK - SPLIT, width), inverse.dtype),
         ],
         in_specs=[SMEM, VMEM, VMEM],
-        out_specs=[VMEM] * 3,
-        compiler_params=pltpu.CompilerParams(vmem_limit_bytes=8 * MIB),
+        out_specs=[VMEM] * 4,
+        compiler_params=pltpu.CompilerParams(vmem_limit_bytes=10 * MIB),
         name="pack_first",
     )(structure, panel, inverse)
 
@@ -240,11 +242,22 @@
     spot = slice(chunk * LANES, (chunk + 1) * LANES)
 
     def body(st, sel_ref, f0, f1, r0, r1, *refs):
-        result, total = refs[-2:]
+        result, total, acc = refs[-3:]
         n = lax.axis_index("narrow")
         w = lax.axis_index("wide")
         x = lax.bitwise_and(w, 1)
         total[...] = jnp.zeros_like(total)
+        depth = sel_ref.shape[2]
+        rows = sel_ref[...].reshape(NGRP * BLK, depth)
+        acc[...] = jnp.dot(
+            rows[:, :early],
+            jnp.concatenate([f0[:, spot], f1[:, spot]], axis=1),
+            preferred_element_type=jnp.float32,
+        ) + jnp.dot(
+            rows[:, early:],
+            jnp.concatenate([r0[...], r1[...]], axis=1),
+            preferred_element_type=jnp.float32,
+        )
         for d in range(NGRP):
             row = lax.bitwise_xor(w, (d % 2) * Y + (d // 2) * ZL)
             pos = jnp.int32(0)
@@ -260,17 +273,8 @@
 
             @pl.when(inside > 0)
             def _(d=d, pos=pos):
-                acc = jnp.dot(
-                    sel_ref[d, :, :early],
-                    jnp.concatenate([f0[:, spot], f1[:, spot]], axis=1),
-                    preferred_element_type=jnp.float32,
-                ) + jnp.dot(
-                    sel_ref[d, :, early:],
-                    jnp.concatenate([r0[...], r1[...]], axis=1),
-                    preferred_element_type=jnp.float32,
-                )
                 for dx in range(2):
-                    part = acc[:, dx * LANES : (dx + 1) * LANES]
+                    part = acc[d * BLK : (d + 1) * BLK, dx * LANES : (dx + 1) * LANES]
                     slot = lax.bitwise_xor(x, dx)
 
                     def weigh(rows, part=part, slot=slot):
@@ -324,7 +328,11 @@
         out_shape=out if near is None else [out, out],
         in_specs=[SMEM] + [VMEM] * (5 + len(again)),
         out_specs=VMEM if near is None else [VMEM, VMEM],
-        scratch_shapes=[pltpu.VMEM(out.shape, out.dtype), pltpu.VMEM((2, 1, LANES), jnp.float32)],
+        scratch_shapes=[
+            pltpu.VMEM(out.shape, out.dtype),
+            pltpu.VMEM((2, 1, LANES), jnp.float32),
+            pltpu.VMEM((NGRP * BLK, 2 * LANES), jnp.float32),
+        ],
         compiler_params=pltpu.CompilerParams(vmem_limit_bytes=16 * MIB),
         cost_estimate=pl.CostEstimate(flops=0, bytes_accessed=0, transcendentals=0),
         name="products",
@@ -448,20 +456,17 @@
 
 
 def per_device_grid(inverse, panel, factor_inv, structure):
-    n = lax.axis_index("narrow")
     first = structure.shape[1] - panel.shape[1] // BLK
     size = lax.axis_size("wide")
-    f_own, top, bottom = pack_first(structure, panel, inverse, first)
-    other = swap_cores(lax.dynamic_index_in_dim(panel, 1 - n, 0, keepdims=False), "panel_swap")
+    f_own, other, top, bottom = pack_first(structure, panel, inverse, first)
+    other = swap_cores(other, "panel_swap")
     r_own = pack_rest(structure, panel, other, first)
     linv = squares(factor_inv)
     f_z = hop(f_own, ZH, "first_z")
     f_x = hop(f_own, X, "first_x")
     a_z0 = hop(top, ZL, "inv_z0")
     a_y = hop(inverse, Y, "inv_y")
-    a_y, a_z0, f_z, f_x, linv, *r_own = lax.optimization_barrier(
-        (a_y, a_z0, f_z, f_x, linv, *r_own)
-    )
+    a_y, a_z0, f_z, f_x, *r_own = lax.optimization_barrier((a_y, a_z0, f_z, f_x, *r_own))
     r_z0 = hop(r_own[0], ZH, "rest0_z")
     a_z1 = hop(after(bottom, f_z), ZL, "inv_z1")
     f_xz = hop(f_z, X, "first_xz")
@@ -469,8 +474,8 @@
     a_yz0 = hop(a_z0, Y, "inv_yz0")
     a_yz1 = hop(a_z1, Y, "inv_yz1")
     most = stack_rows([inverse, a_y, a_z0])
-    r_z0, r_x0, f_xz, a_z1, a_yz0, a_yz1, most, linv, *r_own = lax.optimization_barrier(
-        (r_z0, r_x0, f_xz, a_z1, a_yz0, a_yz1, most, linv, *r_own)
+    r_z0, r_x0, f_xz, a_z1, a_yz0, a_yz1, most, *r_own = lax.optimization_barrier(
+        (r_z0, r_x0, f_xz, a_z1, a_yz0, a_yz1, most, *r_own)
     )
     r_z1 = hop(r_own[1], ZH, "rest1_z")
     r_xz0 = hop(r_z0, X, "rest0_xz")
@@ -479,15 +484,17 @@
     s_most = swap_cores(most, "inv_swap")
     s_more = swap_cores(more, "inv_swap_more")
     sel = pack_inverse(structure, (most, more), (s_most, s_more), first)
+    linv = after(linv, more)
     for mask in (Y, ZL):
         linv = linv + hop(linv, mask, f"squares_{mask}")
     r_z1, r_x1, linv = lax.optimization_barrier((r_z1, r_x1, linv))
 
     def deliver(kept, sent, c):
         messages = bundle(kept, swap_cores(sent, f"cross{c}_swap"))
-        return [messages[0]] + [
-            hop(messages[d], (d % 2) * Y + (d // 2) * ZL, f"cross{c}_{d}") for d in range(1, NGRP)
-        ]
+        hops = {
+            d: hop(messages[d], (d % 2) * Y + (d // 2) * ZL, f"cross{c}_{d}") for d in (3, 1, 2)
+        }
+        return [messages[0]] + [hops[d] for d in range(1, NGRP)]
 
     near = products(structure, sel, (f_own, f_x), (r_own[0], r_x0), 0)
     kept, sent = products(structure, sel, (f_z, f_xz), (r_z0, r_xz0), 0, near)

time: 141 us -> 141 us (level)
  Pallas kernels: 16.5 us -> 21.3 us
  waiting for transfers between devices: 85.6 us -> 81.1 us
    pallas_call x4, Pallas kernels: 10.2 us -> 14.9 us  [products(): pl.pallas_call(body, out_shape=out if near is None else [out, out], in_sp...]
    ppermute x25, waiting for transfers between devices: 79.2 us -> 74.7 us  [hop(): return lax.ppermute(value, 'wide', [(i, i ^ mask) for i in range(size)])]
    unnamed x10 -> x12, local copies, waits for them, and re-layouts: 1.27 us -> 3.5 us
    squeeze x1 -> x0, local copies, waits for them, and re-layouts: 1.44 us -> none  [per_device_grid(): lax.dynamic_index_in_dim(panel, 1 - n, 0, keepdims=False)]
  transfers between devices with their start and end apart: 30 -> 30, of which waited for: 15 -> 15; matrix products, arithmetic and copies ran while one was open for 0% -> 0% of each run, Pallas kernels for 10% -> 12%
where the time goes in v10:
time: 141 us
  waiting for transfers between devices  81.1 us (58%)
  starting transfers between devices  33.4 us (24%)
  Pallas kernels  21.3 us (15%)
  local copies, waits for them, and re-layouts  3.5 us (2%)
    ppermute x25, waiting for transfers between devices, hop(): return lax.ppermute(value, 'wide', [(i, i ^ mask) for i in range(size)])  74.7 us
    ppermute x25, starting transfers between devices, hop(): return lax.ppermute(value, 'wide', [(i, i ^ mask) for i in range(size)])  32.1 us
    pallas_call x4, Pallas kernels, products(): pl.pallas_call(body, out_shape=out if near is None else [out, out], in_sp...  14.9 us
    ppermute x5, waiting for transfers between devices, swap_cores(): return lax.ppermute(value, 'narrow', [(0, 1), (1, 0)])  6.42 us
    unnamed x12, local copies, waits for them, and re-layouts  3.5 us
  transfers between devices with their start and end apart: 30, of which 15 were waited for; matrix products, arithmetic and copies ran while one was open for 0% of the time, Pallas kernels for 12%

profile of v10, /device:TPU:0, one launch (start us, length us, event | category | flops | bytes accessed | tf_op | source)
XLA Modules:
  0.0 140.8 jit_solution(11210237999789821266)
XLA Ops:
  5.4 2.6 %collective-permute-start = (bf16[256,2048]{1,0:T(8,128)(2,1)S(1)}, bf16[256,2048]{1,0:T(8,128)(2,1)S(1)}, u32[]{:S(2)}, u32[]{:S(2)}) collective-permute-start(bf16[256,2048]{1,0:T(8,128)(2,1)S(1)} %copy-done.2), channel_id=1, source_target_pairs={{0,4},{2,6},{4,0},{6,2},{8,12},{10,14},{12,8},{14,10},{16,20},{18,... | collective-permute-start | bytes 3145736 | tf_op jit(solution)/shard_map/inv_y/ppermute | solution.py:106
  9.6 2.6 %collective-permute-start.2 = (bf16[1024,256]{1,0:T(8,128)(2,1)S(1)}, bf16[1024,256]{1,0:T(8,128)(2,1)S(1)}, u32[]{:S(2)}, u32[]{:S(2)}) collective-permute-start(bf16[1024,256]{1,0:T(8,128)(2,1)S(1)} %get-tuple-element.46.f0), channel_id=1, source_target_pairs={{0,16},{2,18},{4,20},{6,22},{8,24},{10,26},{12,28},{14,30},{16,0},... | collective-permute-start | bytes 1572872 | tf_op jit(solution)/shard_map/first_z/ppermute | solution.py:106
  14.6 23.4 %collective-permute-done.2.f0 = bf16[1024,256]{1,0:T(8,128)(2,1)S(1)} collective-permute-done((bf16[1024,256]{1,0:T(8,128)(2,1)S(1)}, bf16[1024,256]{1,0:T(8,128)(2,1)S(1)}, u32[]{:S(2)}, u32[]{:S(2)}) %collective-permute-start.2) | collective-permute-done | bytes 524320 | tf_op jit(solution)/shard_map/first_z/ppermute | solution.py:106
  40.8 2.7 %collective-permute-start.8 = (bf16[64,2048]{1,0:T(8,128)(2,1)S(1)}, bf16[64,2048]{1,0:T(8,128)(2,1)S(1)}, u32[]{:S(2)}, u32[]{:S(2)}) collective-permute-start(bf16[64,2048]{1,0:T(8,128)(2,1)S(1)} %get-tuple-element.53), channel_id=1, source_target_pairs={{0,8},{2,10},{4,12},{6,14},{8,0},{10,2},{12,4},{14,6},{16,24},{18,... | collective-permute-start | bytes 786440 | tf_op jit(solution)/shard_map/inv_z1/ppermute | solution.py:106
  45.5 7.6 %collective-permute-done.8.refs_0_ = bf16[64,2048]{1,0:T(8,128)(2,1)S(1)} collective-permute-done((bf16[64,2048]{1,0:T(8,128)(2,1)S(1)}, bf16[64,2048]{1,0:T(8,128)(2,1)S(1)}, u32[]{:S(2)}, u32[]{:S(2)}) %collective-permute-start.8) | collective-permute-done | bytes 262176 | tf_op jit(solution)/shard_map/inv_z1/ppermute | solution.py:106
  54.8 13.2 %collective-permute-done.5.r0 = bf16[2048,128]{1,0:T(8,128)(2,1)S(1)} collective-permute-done((bf16[2048,128]{1,0:T(8,128)(2,1)S(1)}, bf16[2048,128]{1,0:T(8,128)(2,1)S(1)}, u32[]{:S(2)}, u32[]{:S(2)}) %collective-permute-start.5) | collective-permute-done | bytes 524320 | tf_op jit(solution)/shard_map/rest0_z/ppermute | solution.py:106
  70.8 4.5 %collective-permute-done.12.refs_3_ = bf16[320,2048]{1,0:T(8,128)(2,1)S(1)} collective-permute-done((bf16[320,2048]{1,0:T(8,128)(2,1)S(1)}, bf16[320,2048]{1,0:T(8,128)(2,1)S(1)}, u32[]{:S(2)}, u32[]{:S(2)}) %collective-permute-start.12) | collective-permute-done | bytes 1310752 | tf_op jit(solution)/shard_map/inv_swap_more/ppermute | solution.py:100
  75.2 1.8 %pack_inverse.1.sel_ref = bf16[4,256,3072]{2,1,0:T(8,128)(2,1)S(1)} custom-call(s32[2,12]{1,0:T(2,128)S(1)} %copy-done.5, bf16[704,2048]{1,0:T(8,128)(2,1)S(1)} %stack_rows.2.refs_0_, bf16[320,2048]{1,0:T(8,128)(2,1)S(1)} %stack_rows.3.refs_1_, bf16[704,2048]{1,0:T(8,128)(2,1)S(1)} %collective-permute-done.11.refs_2_, ...), custom_call_target="tpu_custom_call" | custom-call | tf_op jit(solution)/shard_map/pack_inverse/pallas_call | solution.py:228
  77.1 3.6 %products.4.refs_0_ = bf16[4,272,256]{2,1,0:T(8,128)(2,1)S(1)} custom-call(s32[2,12]{1,0:T(2,128)S(1)} %copy-done.5, bf16[4,256,3072]{2,1,0:T(8,128)(2,1)S(1)} %pack_inverse.1.sel_ref, bf16[1024,256]{1,0:T(8,128)(2,1)S(1)} %get-tuple-element.46.f0, bf16[1024,256]{1,0:T(8,128)(2,1)S(1)} %collective-permute-done.3.f1, ...), custom_call_target="tpu_custom_call" | custom-call | tf_op jit(solution)/shard_map/products/pallas_call | solution.py:326
  80.7 2.8 %collective-permute-done.18.r1 = bf16[2048,128]{1,0:T(8,128)(2,1)S(1)} collective-permute-done((bf16[2048,128]{1,0:T(8,128)(2,1)S(1)}, bf16[2048,128]{1,0:T(8,128)(2,1)S(1)}, u32[]{:S(2)}, u32[]{:S(2)}) %collective-permute-start.18) | collective-permute-done | bytes 524320 | tf_op jit(solution)/shard_map/rest0_xz/ppermute | solution.py:106
  83.5 3.7 %products.5 = (bf16[4,272,256]{2,1,0:T(8,128)(2,1)S(1)}, bf16[4,272,256]{2,1,0:T(8,128)(2,1)S(1)}) custom-call(s32[2,12]{1,0:T(2,128)S(1)} %copy-done.5, bf16[4,256,3072]{2,1,0:T(8,128)(2,1)S(1)} %pack_inverse.1.sel_ref, bf16[1024,256]{1,0:T(8,128)(2,1)S(1)} %collective-permute-done.2.f0, bf16[1024,256]{1,0:T(8,128)(2,1)S(1)} %collective-permute-done.7.f1, ...), custom_call_target="tpu_custom_call" | custom-call | tf_op jit(solution)/shard_map/products/pallas_call | solution.py:326
  89.2 2.2 %collective-permute-done.15 = f32[2,2048]{1,0:T(2,128)S(1)} collective-permute-done((f32[2,2048]{1,0:T(2,128)S(1)}, f32[2,2048]{1,0:T(2,128)S(1)}, u32[]{:S(2)}, u32[]{:S(2)}) %collective-permute-start.15) | collective-permute-done | bytes 16416 | tf_op jit(solution)/shard_map/squares_2/ppermute | solution.py:106
  91.5 3.7 %collective-permute-done.16 = f32[2,2048]{1,0:T(2,128)S(1)} collective-permute-done((f32[2,2048]{1,0:T(2,128)S(1)}, f32[2,2048]{1,0:T(2,128)S(1)}, u32[]{:S(2)}, u32[]{:S(2)}) %collective-permute-start.16) | collective-permute-done | bytes 16416 | tf_op jit(solution)/shard_map/squares_4/ppermute | solution.py:106
  97.3 2.0 %collective-permute-start.22 = (bf16[2,272,256]{2,1,0:T(8,128)(2,1)S(1)}, bf16[2,272,256]{2,1,0:T(8,128)(2,1)S(1)}, u32[]{:S(2)}, u32[]{:S(2)}) collective-permute-start(bf16[2,272,256]{2,1,0:T(8,128)(2,1)S(1)} %get-tuple-element.74), channel_id=1, source_target_pairs={{0,12},{2,14},{4,8},{6,10},{8,4},{10,6},{12,0},{14,2},{16,28},{18,... | collective-permute-start | bytes 835592 | tf_op jit(solution)/shard_map/cross0_3/ppermute | solution.py:106
  99.3 3.8 %products.6.refs_0_ = bf16[4,272,256]{2,1,0:T(8,128)(2,1)S(1)} custom-call(s32[2,12]{1,0:T(2,128)S(1)} %copy-done.5, bf16[4,256,3072]{2,1,0:T(8,128)(2,1)S(1)} %pack_inverse.1.sel_ref, bf16[1024,256]{1,0:T(8,128)(2,1)S(1)} %get-tuple-element.46.f0, bf16[1024,256]{1,0:T(8,128)(2,1)S(1)} %collective-permute-done.3.f1, ...), custom_call_target="tpu_custom_call" | custom-call | tf_op jit(solution)/shard_map/products/pallas_call | solution.py:326
  103.1 4.8 %collective-permute-done.17.r1 = bf16[2048,128]{1,0:T(8,128)(2,1)S(1)} collective-permute-done((bf16[2048,128]{1,0:T(8,128)(2,1)S(1)}, bf16[2048,128]{1,0:T(8,128)(2,1)S(1)}, u32[]{:S(2)}, u32[]{:S(2)}) %collective-permute-start.17) | collective-permute-done | bytes 524320 | tf_op jit(solution)/shard_map/rest1_xz/ppermute | solution.py:106
  107.9 3.3 %collective-permute-done.22.refs_3_ = bf16[2,272,256]{2,1,0:T(8,128)(2,1)S(1)} collective-permute-done((bf16[2,272,256]{2,1,0:T(8,128)(2,1)S(1)}, bf16[2,272,256]{2,1,0:T(8,128)(2,1)S(1)}, u32[]{:S(2)}, u32[]{:S(2)}) %collective-permute-start.22) | collective-permute-done | bytes 278560 | tf_op jit(solution)/shard_map/cross0_3/ppermute | solution.py:106
  111.3 3.7 %products.7 = (bf16[4,272,256]{2,1,0:T(8,128)(2,1)S(1)}, bf16[4,272,256]{2,1,0:T(8,128)(2,1)S(1)}) custom-call(s32[2,12]{1,0:T(2,128)S(1)} %copy-done.5, bf16[4,256,3072]{2,1,0:T(8,128)(2,1)S(1)} %pack_inverse.1.sel_ref, bf16[1024,256]{1,0:T(8,128)(2,1)S(1)} %collective-permute-done.2.f0, bf16[1024,256]{1,0:T(8,128)(2,1)S(1)} %collective-permute-done.7.f1, ...), custom_call_target="tpu_custom_call" | custom-call | tf_op jit(solution)/shard_map/products/pallas_call | solution.py:326
  115.0 1.9 %collective-permute-done.23.back_ref = bf16[4,272,256]{2,1,0:T(8,128)(2,1)S(1)} collective-permute-done((bf16[4,272,256]{2,1,0:T(8,128)(2,1)S(1)}, bf16[4,272,256]{2,1,0:T(8,128)(2,1)S(1)}, u32[]{:S(2)}, u32[]{:S(2)}) %collective-permute-start.23) | collective-permute-done | bytes 557088 | tf_op jit(solution)/shard_map/cross1_swap/ppermute | solution.py:100
  118.9 1.7 %collective-permute-start.26 = (bf16[2,272,256]{2,1,0:T(8,128)(2,1)S(1)}, bf16[2,272,256]{2,1,0:T(8,128)(2,1)S(1)}, u32[]{:S(2)}, u32[]{:S(2)}) collective-permute-start(bf16[2,272,256]{2,1,0:T(8,128)(2,1)S(1)} %get-tuple-element.82), channel_id=1, source_target_pairs={{0,12},{2,14},{4,8},{6,10},{8,4},{10,6},{12,0},{14,2},{16,28},{18,... | collective-permute-start | bytes 835592 | tf_op jit(solution)/shard_map/cross1_3/ppermute | solution.py:106
  120.7 5.2 %collective-permute-done.24.refs_1_ = bf16[2,272,256]{2,1,0:T(8,128)(2,1)S(1)} collective-permute-done((bf16[2,272,256]{2,1,0:T(8,128)(2,1)S(1)}, bf16[2,272,256]{2,1,0:T(8,128)(2,1)S(1)}, u32[]{:S(2)}, u32[]{:S(2)}) %collective-permute-start.24) | collective-permute-done | bytes 278560 | tf_op jit(solution)/shard_map/cross1_1/ppermute | solution.py:106
  125.8 2.4 %collective-permute-done.25.refs_2_ = bf16[2,272,256]{2,1,0:T(8,128)(2,1)S(1)} collective-permute-done((bf16[2,272,256]{2,1,0:T(8,128)(2,1)S(1)}, bf16[2,272,256]{2,1,0:T(8,128)(2,1)S(1)}, u32[]{:S(2)}, u32[]{:S(2)}) %collective-permute-start.25) | collective-permute-done | bytes 278560 | tf_op jit(solution)/shard_map/cross1_2/ppermute | solution.py:106
  128.2 4.8 %collective-permute-done.26.refs_3_ = bf16[2,272,256]{2,1,0:T(8,128)(2,1)S(1)} collective-permute-done((bf16[2,272,256]{2,1,0:T(8,128)(2,1)S(1)}, bf16[2,272,256]{2,1,0:T(8,128)(2,1)S(1)}, u32[]{:S(2)}, u32[]{:S(2)}) %collective-permute-start.26) | collective-permute-done | bytes 278560 | tf_op jit(solution)/shard_map/cross1_3/ppermute | solution.py:106
  134.7 2.8 %collective-permute-start.29 = (f32[2,2048]{1,0:T(2,128)S(1)}, f32[2,2048]{1,0:T(2,128)S(1)}, u32[]{:S(2)}, u32[]{:S(2)}) collective-permute-start(f32[2,2048]{1,0:T(2,128)S(1)} %add_sums.3), channel_id=1, source_target_pairs={{0,18},{2,16},{4,22},{6,20},{8,26},{10,24},{12,30},{14,28},{16,2},... | collective-permute-start | bytes 49160 | tf_op jit(solution)/shard_map/variance_9/ppermute | solution.py:106
  (67 shorter events, 29.3 us)
Async XLA Ops:
  4.9 8.8 %collective-permute-start.4 = (bf16[2048,256]{1,0:T(8,128)(2,1)S(1)}, bf16[2048,256]{1,0:T(8,128)(2,1)S(1)}, u32[]{:S(2)}, u32[]{:S(2)}) collective-permute-start(bf16[2048,256]{1,0:T(8,128)(2,1)S(1)} %get-tuple-element.47), channel_id=1, source_target_pairs={{0,1},{1,0},{2,3},{3,2},{4,5},{5,4},{6,7},{7,6},{8,9},{9,8},{10,11... | collective-permute-start | bytes 3145736 | tf_op jit(solution)/shard_map/panel_swap/ppermute | solution.py:100
  5.4 33.4 %collective-permute-start = (bf16[256,2048]{1,0:T(8,128)(2,1)S(1)}, bf16[256,2048]{1,0:T(8,128)(2,1)S(1)}, u32[]{:S(2)}, u32[]{:S(2)}) collective-permute-start(bf16[256,2048]{1,0:T(8,128)(2,1)S(1)} %copy-done.2), channel_id=1, source_target_pairs={{0,4},{2,6},{4,0},{6,2},{8,12},{10,14},{12,8},{14,10},{16,20},{18,... | collective-permute-start | bytes 3145736 | tf_op jit(solution)/shard_map/inv_y/ppermute | solution.py:106
  8.0 30.8 %collective-permute-start.1 = (bf16[192,2048]{1,0:T(8,128)(2,1)S(1)}, bf16[192,2048]{1,0:T(8,128)(2,1)S(1)}, u32[]{:S(2)}, u32[]{:S(2)}) collective-permute-start(bf16[192,2048]{1,0:T(8,128)(2,1)S(1)} %get-tuple-element.45), channel_id=1, source_target_pairs={{0,8},{2,10},{4,12},{6,14},{8,0},{10,2},{12,4},{14,6},{16,24},{18,... | collective-permute-start | bytes 2359304 | tf_op jit(solution)/shard_map/inv_z0/ppermute | solution.py:106
  9.6 28.4 %collective-permute-start.2 = (bf16[1024,256]{1,0:T(8,128)(2,1)S(1)}, bf16[1024,256]{1,0:T(8,128)(2,1)S(1)}, u32[]{:S(2)}, u32[]{:S(2)}) collective-permute-start(bf16[1024,256]{1,0:T(8,128)(2,1)S(1)} %get-tuple-element.46.f0), channel_id=1, source_target_pairs={{0,16},{2,18},{4,20},{6,22},{8,24},{10,26},{12,28},{14,30},{16,0},... | collective-permute-start | bytes 1572872 | tf_op jit(solution)/shard_map/first_z/ppermute | solution.py:106
  12.1 25.8 %collective-permute-start.3 = (bf16[1024,256]{1,0:T(8,128)(2,1)S(1)}, bf16[1024,256]{1,0:T(8,128)(2,1)S(1)}, u32[]{:S(2)}, u32[]{:S(2)}) collective-permute-start(bf16[1024,256]{1,0:T(8,128)(2,1)S(1)} %get-tuple-element.46.f0), channel_id=1, source_target_pairs={{0,2},{2,0},{4,6},{6,4},{8,10},{10,8},{12,14},{14,12},{16,18},{18,... | collective-permute-start | bytes 1572872 | tf_op jit(solution)/shard_map/first_x/ppermute | solution.py:106
  38.8 29.2 %collective-permute-start.9 = (bf16[192,2048]{1,0:T(8,128)(2,1)S(1)}, bf16[192,2048]{1,0:T(8,128)(2,1)S(1)}, u32[]{:S(2)}, u32[]{:S(2)}) collective-permute-start(bf16[192,2048]{1,0:T(8,128)(2,1)S(1)} %collective-permute-done.1.refs_2_), channel_id=1, source_target_pairs={{0,4},{2,6},{4,0},{6,2},{8,12},{10,14},{12,8},{14,10},{16,20},{18,... | collective-permute-start | bytes 2359304 | tf_op jit(solution)/shard_map/inv_yz0/ppermute | solution.py:106
  39.2 15.7 %collective-permute-start.7 = (bf16[1024,256]{1,0:T(8,128)(2,1)S(1)}, bf16[1024,256]{1,0:T(8,128)(2,1)S(1)}, u32[]{:S(2)}, u32[]{:S(2)}) collective-permute-start(bf16[1024,256]{1,0:T(8,128)(2,1)S(1)} %collective-permute-done.2.f0), channel_id=1, source_target_pairs={{0,2},{2,0},{4,6},{6,4},{8,10},{10,8},{12,14},{14,12},{16,18},{18,... | collective-permute-start | bytes 1572872 | tf_op jit(solution)/shard_map/first_xz/ppermute | solution.py:106
  40.8 12.3 %collective-permute-start.8 = (bf16[64,2048]{1,0:T(8,128)(2,1)S(1)}, bf16[64,2048]{1,0:T(8,128)(2,1)S(1)}, u32[]{:S(2)}, u32[]{:S(2)}) collective-permute-start(bf16[64,2048]{1,0:T(8,128)(2,1)S(1)} %get-tuple-element.53), channel_id=1, source_target_pairs={{0,8},{2,10},{4,12},{6,14},{8,0},{10,2},{12,4},{14,6},{16,24},{18,... | collective-permute-start | bytes 786440 | tf_op jit(solution)/shard_map/inv_z1/ppermute | solution.py:106
  43.5 24.5 %collective-permute-start.5 = (bf16[2048,128]{1,0:T(8,128)(2,1)S(1)}, bf16[2048,128]{1,0:T(8,128)(2,1)S(1)}, u32[]{:S(2)}, u32[]{:S(2)}) collective-permute-start(bf16[2048,128]{1,0:T(8,128)(2,1)S(1)} %get-tuple-element.67.r0), channel_id=1, source_target_pairs={{0,16},{2,18},{4,20},{6,22},{8,24},{10,26},{12,28},{14,30},{16,0},... | collective-permute-start | bytes 1572872 | tf_op jit(solution)/shard_map/rest0_z/ppermute | solution.py:106
  45.0 23.0 %collective-permute-start.6 = (bf16[2048,128]{1,0:T(8,128)(2,1)S(1)}, bf16[2048,128]{1,0:T(8,128)(2,1)S(1)}, u32[]{:S(2)}, u32[]{:S(2)}) collective-permute-start(bf16[2048,128]{1,0:T(8,128)(2,1)S(1)} %get-tuple-element.67.r0), channel_id=1, source_target_pairs={{0,2},{2,0},{4,6},{6,4},{8,10},{10,8},{12,14},{14,12},{16,18},{18,... | collective-permute-start | bytes 1572872 | tf_op jit(solution)/shard_map/rest0_x/ppermute | solution.py:106
  53.1 14.9 %collective-permute-start.10 = (bf16[64,2048]{1,0:T(8,128)(2,1)S(1)}, bf16[64,2048]{1,0:T(8,128)(2,1)S(1)}, u32[]{:S(2)}, u32[]{:S(2)}) collective-permute-start(bf16[64,2048]{1,0:T(8,128)(2,1)S(1)} %collective-permute-done.8.refs_0_), channel_id=1, source_target_pairs={{0,4},{2,6},{4,0},{6,2},{8,12},{10,14},{12,8},{14,10},{16,20},{18,... | collective-permute-start | bytes 786440 | tf_op jit(solution)/shard_map/inv_yz1/ppermute | solution.py:106
  68.0 7.2 %collective-permute-start.11 = (bf16[704,2048]{1,0:T(8,128)(2,1)S(1)}, bf16[704,2048]{1,0:T(8,128)(2,1)S(1)}, u32[]{:S(2)}, u32[]{:S(2)}) collective-permute-start(bf16[704,2048]{1,0:T(8,128)(2,1)S(1)} %stack_rows.2.refs_0_), channel_id=1, source_target_pairs={{0,1},{1,0},{2,3},{3,2},{4,5},{5,4},{6,7},{7,6},{8,9},{9,8},{10,11... | collective-permute-start | bytes 8650760 | tf_op jit(solution)/shard_map/inv_swap/ppermute | solution.py:100
  68.2 7.1 %collective-permute-start.12 = (bf16[320,2048]{1,0:T(8,128)(2,1)S(1)}, bf16[320,2048]{1,0:T(8,128)(2,1)S(1)}, u32[]{:S(2)}, u32[]{:S(2)}) collective-permute-start(bf16[320,2048]{1,0:T(8,128)(2,1)S(1)} %stack_rows.3.refs_1_), channel_id=1, source_target_pairs={{0,1},{1,0},{2,3},{3,2},{4,5},{5,4},{6,7},{7,6},{8,9},{9,8},{10,11... | collective-permute-start | bytes 3932168 | tf_op jit(solution)/shard_map/inv_swap_more/ppermute | solution.py:100
  68.7 14.8 %collective-permute-start.18 = (bf16[2048,128]{1,0:T(8,128)(2,1)S(1)}, bf16[2048,128]{1,0:T(8,128)(2,1)S(1)}, u32[]{:S(2)}, u32[]{:S(2)}) collective-permute-start(bf16[2048,128]{1,0:T(8,128)(2,1)S(1)} %collective-permute-done.5.r0), channel_id=1, source_target_pairs={{0,2},{2,0},{4,6},{6,4},{8,10},{10,8},{12,14},{14,12},{16,18},{18,... | collective-permute-start | bytes 1572872 | tf_op jit(solution)/shard_map/rest0_xz/ppermute | solution.py:106
  69.3 26.0 %collective-permute-start.13 = (bf16[2048,128]{1,0:T(8,128)(2,1)S(1)}, bf16[2048,128]{1,0:T(8,128)(2,1)S(1)}, u32[]{:S(2)}, u32[]{:S(2)}) collective-permute-start(bf16[2048,128]{1,0:T(8,128)(2,1)S(1)} %get-tuple-element.62.r0), channel_id=1, source_target_pairs={{0,16},{2,18},{4,20},{6,22},{8,24},{10,26},{12,28},{14,30},{16,0},... | collective-permute-start | bytes 1572872 | tf_op jit(solution)/shard_map/rest1_z/ppermute | solution.py:106
  69.3 26.0 %collective-permute-start.14 = (bf16[2048,128]{1,0:T(8,128)(2,1)S(1)}, bf16[2048,128]{1,0:T(8,128)(2,1)S(1)}, u32[]{:S(2)}, u32[]{:S(2)}) collective-permute-start(bf16[2048,128]{1,0:T(8,128)(2,1)S(1)} %get-tuple-element.62.r0), channel_id=1, source_target_pairs={{0,2},{2,0},{4,6},{6,4},{8,10},{10,8},{12,14},{14,12},{16,18},{18,... | collective-permute-start | bytes 1572872 | tf_op jit(solution)/shard_map/rest1_x/ppermute | solution.py:106
  87.2 8.5 %collective-permute-start.19 = (bf16[4,272,256]{2,1,0:T(8,128)(2,1)S(1)}, bf16[4,272,256]{2,1,0:T(8,128)(2,1)S(1)}, u32[]{:S(2)}, u32[]{:S(2)}) collective-permute-start(bf16[4,272,256]{2,1,0:T(8,128)(2,1)S(1)} %get-tuple-element.70), channel_id=1, source_target_pairs={{0,1},{1,0},{2,3},{3,2},{4,5},{5,4},{6,7},{7,6},{8,9},{9,8},{10,11... | collective-permute-start | bytes 1671176 | tf_op jit(solution)/shard_map/cross0_swap/ppermute | solution.py:100
  95.3 12.6 %collective-permute-start.17 = (bf16[2048,128]{1,0:T(8,128)(2,1)S(1)}, bf16[2048,128]{1,0:T(8,128)(2,1)S(1)}, u32[]{:S(2)}, u32[]{:S(2)}) collective-permute-start(bf16[2048,128]{1,0:T(8,128)(2,1)S(1)} %collective-permute-done.13.r0), channel_id=1, source_target_pairs={{0,2},{2,0},{4,6},{6,4},{8,10},{10,8},{12,14},{14,12},{16,18},{18,... | collective-permute-start | bytes 1572872 | tf_op jit(solution)/shard_map/rest1_xz/ppermute | solution.py:106
  95.8 12.2 %collective-permute-start.20 = (bf16[2,272,256]{2,1,0:T(8,128)(2,1)S(1)}, bf16[2,272,256]{2,1,0:T(8,128)(2,1)S(1)}, u32[]{:S(2)}, u32[]{:S(2)}) collective-permute-start(bf16[2,272,256]{2,1,0:T(8,128)(2,1)S(1)} %get-tuple-element.72), channel_id=1, source_target_pairs={{0,4},{2,6},{4,0},{6,2},{8,12},{10,14},{12,8},{14,10},{16,20},{18,... | collective-permute-start | bytes 835592 | tf_op jit(solution)/shard_map/cross0_1/ppermute | solution.py:106
  97.3 10.6 %collective-permute-start.21 = (bf16[2,272,256]{2,1,0:T(8,128)(2,1)S(1)}, bf16[2,272,256]{2,1,0:T(8,128)(2,1)S(1)}, u32[]{:S(2)}, u32[]{:S(2)}) collective-permute-start(bf16[2,272,256]{2,1,0:T(8,128)(2,1)S(1)} %get-tuple-element.73), channel_id=1, source_target_pairs={{0,8},{2,10},{4,12},{6,14},{8,0},{10,2},{12,4},{14,6},{16,24},{18,... | collective-permute-start | bytes 835592 | tf_op jit(solution)/shard_map/cross0_2/ppermute | solution.py:106
  97.3 13.9 %collective-permute-start.22 = (bf16[2,272,256]{2,1,0:T(8,128)(2,1)S(1)}, bf16[2,272,256]{2,1,0:T(8,128)(2,1)S(1)}, u32[]{:S(2)}, u32[]{:S(2)}) collective-permute-start(bf16[2,272,256]{2,1,0:T(8,128)(2,1)S(1)} %get-tuple-element.74), channel_id=1, source_target_pairs={{0,12},{2,14},{4,8},{6,10},{8,4},{10,6},{12,0},{14,2},{16,28},{18,... | collective-permute-start | bytes 835592 | tf_op jit(solution)/shard_map/cross0_3/ppermute | solution.py:106
  117.1 8.8 %collective-permute-start.24 = (bf16[2,272,256]{2,1,0:T(8,128)(2,1)S(1)}, bf16[2,272,256]{2,1,0:T(8,128)(2,1)S(1)}, u32[]{:S(2)}, u32[]{:S(2)}) collective-permute-start(bf16[2,272,256]{2,1,0:T(8,128)(2,1)S(1)} %get-tuple-element.80), channel_id=1, source_target_pairs={{0,4},{2,6},{4,0},{6,2},{8,12},{10,14},{12,8},{14,10},{16,20},{18,... | collective-permute-start | bytes 835592 | tf_op jit(solution)/shard_map/cross1_1/ppermute | solution.py:106
  118.7 9.5 %collective-permute-start.25 = (bf16[2,272,256]{2,1,0:T(8,128)(2,1)S(1)}, bf16[2,272,256]{2,1,0:T(8,128)(2,1)S(1)}, u32[]{:S(2)}, u32[]{:S(2)}) collective-permute-start(bf16[2,272,256]{2,1,0:T(8,128)(2,1)S(1)} %get-tuple-element.81), channel_id=1, source_target_pairs={{0,8},{2,10},{4,12},{6,14},{8,0},{10,2},{12,4},{14,6},{16,24},{18,... | collective-permute-start | bytes 835592 | tf_op jit(solution)/shard_map/cross1_2/ppermute | solution.py:106
  118.9 14.1 %collective-permute-start.26 = (bf16[2,272,256]{2,1,0:T(8,128)(2,1)S(1)}, bf16[2,272,256]{2,1,0:T(8,128)(2,1)S(1)}, u32[]{:S(2)}, u32[]{:S(2)}) collective-permute-start(bf16[2,272,256]{2,1,0:T(8,128)(2,1)S(1)} %get-tuple-element.82), channel_id=1, source_target_pairs={{0,12},{2,14},{4,8},{6,10},{8,4},{10,6},{12,0},{14,2},{16,28},{18,... | collective-permute-start | bytes 835592 | tf_op jit(solution)/shard_map/cross1_3/ppermute | solution.py:106
  (12 other events, 68.2 us)

commit v11 on v10

--- a/solution.py
+++ b/solution.py
@@ -92,6 +92,7 @@
 NGRP = 4
 SPLIT = 192
 TAIL = 16
+DEST = (0, 3, 1, 2)
 MIB = 1024 * 1024
 
 
@@ -119,12 +120,11 @@
 def pack_first(structure, panel, inverse, first):
     half_blocks = panel.shape[1] // BLK
 
-    def body(st, panel_ref, inv_ref, out, rest, *pieces):
+    def body(st, panel_ref, inv_ref, out, *pieces):
         n = lax.axis_index("narrow")
         for j in range(first):
             row = pl.multiple_of(lax.rem(pick(st, n, j, first), half_blocks) * BLK, BLK)
             out[j * BLK : (j + 1) * BLK, :] = panel_ref[n, pl.ds(row, BLK), :]
-        rest[...] = panel_ref[1 - n]
         pieces[0][...] = inv_ref[:SPLIT, :]
         pieces[1][...] = inv_ref[SPLIT:, :]
 
@@ -133,13 +133,12 @@
         body,
         out_shape=[
             jax.ShapeDtypeStruct((first * BLK, panel.shape[2]), panel.dtype),
-            jax.ShapeDtypeStruct(panel.shape[1:], panel.dtype),
             jax.ShapeDtypeStruct((SPLIT, width), inverse.dtype),
             jax.ShapeDtypeStruct((BLK - SPLIT, width), inverse.dtype),
         ],
         in_specs=[SMEM, VMEM, VMEM],
-        out_specs=[VMEM] * 4,
-        compiler_params=pltpu.CompilerParams(vmem_limit_bytes=10 * MIB),
+        out_specs=[VMEM] * 3,
+        compiler_params=pltpu.CompilerParams(vmem_limit_bytes=8 * MIB),
         name="pack_first",
     )(structure, panel, inverse)
 
@@ -150,6 +149,7 @@
 
     def body(st, panel_ref, other_ref, out0, out1):
         n = lax.axis_index("narrow")
+        out0[(nblocks - first) * BLK :, :] = jnp.zeros((TAIL, LANES), out0.dtype)
         for j in range(nblocks - first):
             b = pick(st, n, first + j, first)
             row = pl.multiple_of(lax.rem(b, half_blocks) * BLK, BLK)
@@ -166,10 +166,13 @@
                 out0[rows, :] = other_ref[pl.ds(row, BLK), :LANES]
                 out1[rows, :] = other_ref[pl.ds(row, BLK), LANES:]
 
-    shape = jax.ShapeDtypeStruct(((nblocks - first) * BLK, LANES), panel.dtype)
-    return pl.pallas_call(
-        body,
-        out_shape=(shape, shape),
+    rows = (nblocks - first) * BLK
+    return pl.pallas_call(
+        body,
+        out_shape=(
+            jax.ShapeDtypeStruct((rows + TAIL, LANES), panel.dtype),
+            jax.ShapeDtypeStruct((rows, LANES), panel.dtype),
+        ),
         in_specs=[SMEM, VMEM, VMEM],
         out_specs=[VMEM, VMEM],
         compiler_params=pltpu.CompilerParams(vmem_limit_bytes=8 * MIB),
@@ -238,6 +241,7 @@
 def products(structure, sel, firsts, rests, chunk, near=None):
     nblocks = structure.shape[1]
     early = firsts[0].shape[0]
+    late = sel.shape[2] - early
     first = early // BLK
     spot = slice(chunk * LANES, (chunk + 1) * LANES)
 
@@ -255,7 +259,7 @@
             preferred_element_type=jnp.float32,
         ) + jnp.dot(
             rows[:, early:],
-            jnp.concatenate([r0[...], r1[...]], axis=1),
+            jnp.concatenate([r0[:late, :], r1[:late, :]], axis=1),
             preferred_element_type=jnp.float32,
         )
         for d in range(NGRP):
@@ -339,13 +343,13 @@
     )(structure, sel, *firsts, *rests, *again)
 
 
-def bundle(kept, back):
-    def body(kept_ref, back_ref, *outs):
-        for d, out in enumerate(outs):
-            out[0] = kept_ref[d]
-            out[1] = back_ref[d]
-
-    shape = jax.ShapeDtypeStruct((2, *kept.shape[1:]), kept.dtype)
+def bundle(ours, theirs):
+    def body(our_ref, their_ref, *outs):
+        for d, out in zip(DEST, outs):
+            out[0] = our_ref[d]
+            out[1] = their_ref[d]
+
+    shape = jax.ShapeDtypeStruct((2, *ours.shape[1:]), ours.dtype)
     return pl.pallas_call(
         body,
         out_shape=[shape] * NGRP,
@@ -353,7 +357,7 @@
         out_specs=[VMEM] * NGRP,
         compiler_params=pltpu.CompilerParams(vmem_limit_bytes=8 * MIB),
         name="bundle",
-    )(kept, back)
+    )(ours, theirs)
 
 
 def squares(factor_inv):
@@ -384,11 +388,11 @@
         n = lax.axis_index("narrow")
         group = lax.rem(lax.div(lax.axis_index("wide"), Y), NGRP)
         out[...] = base_ref[...]
-        for d in range(NGRP):
+        for d, ref in zip(DEST, refs):
             source = lax.bitwise_xor(group, d)
             for k in range(2):
                 which = (n != k).astype(jnp.int32)
-                tile = refs[d][which, 2 * LANES :, :].astype(jnp.float32)
+                tile = ref[which, 2 * LANES :, :].astype(jnp.float32)
                 value = tile[0:1] + (tile[1:2] + tile[2:3])
                 for xx in range(2):
                     at = source * (cols // NGRP) + (2 * xx + chunk) * LANES
@@ -415,13 +419,13 @@
         n = lax.axis_index("narrow")
         w = lax.axis_index("wide")
         copies = []
-        for d in range(NGRP):
+        for d, msg_ref in zip(DEST, msg_refs):
             source = lax.bitwise_xor(lax.rem(lax.div(w, Y), NGRP), d)
             for xx in range(2):
                 slot = 2 * d + xx
                 for k in range(2):
                     which = (n != k).astype(jnp.int32)
-                    value = msg_refs[d][which, xx * LANES : (xx + 1) * LANES, :].astype(
+                    value = msg_ref[which, xx * LANES : (xx + 1) * LANES, :].astype(
                         jnp.float32
                     )
                     for lt in range(2):
@@ -458,15 +462,16 @@
 def per_device_grid(inverse, panel, factor_inv, structure):
     first = structure.shape[1] - panel.shape[1] // BLK
     size = lax.axis_size("wide")
-    f_own, other, top, bottom = pack_first(structure, panel, inverse, first)
-    other = swap_cores(other, "panel_swap")
+    n = lax.axis_index("narrow")
+    f_own, top, bottom = pack_first(structure, panel, inverse, first)
+    other = swap_cores(lax.dynamic_index_in_dim(panel, 1 - n, 0, keepdims=False), "panel_swap")
     r_own = pack_rest(structure, panel, other, first)
     linv = squares(factor_inv)
     f_z = hop(f_own, ZH, "first_z")
     f_x = hop(f_own, X, "first_x")
     a_z0 = hop(top, ZL, "inv_z0")
     a_y = hop(inverse, Y, "inv_y")
-    a_y, a_z0, f_z, f_x, *r_own = lax.optimization_barrier((a_y, a_z0, f_z, f_x, *r_own))
+    a_y, f_z, f_x, *r_own = lax.optimization_barrier((a_y, f_z, f_x, *r_own))
     r_z0 = hop(r_own[0], ZH, "rest0_z")
     a_z1 = hop(after(bottom, f_z), ZL, "inv_z1")
     f_xz = hop(f_z, X, "first_xz")
@@ -491,10 +496,10 @@
 
     def deliver(kept, sent, c):
         messages = bundle(kept, swap_cores(sent, f"cross{c}_swap"))
-        hops = {
-            d: hop(messages[d], (d % 2) * Y + (d // 2) * ZL, f"cross{c}_{d}") for d in (3, 1, 2)
-        }
-        return [messages[0]] + [hops[d] for d in range(1, NGRP)]
+        return [messages[0]] + [
+            hop(message, (d % 2) * Y + (d // 2) * ZL, f"cross{c}_{d}")
+            for d, message in zip(DEST[1:], messages[1:])
+        ]
 
     near = products(structure, sel, (f_own, f_x), (r_own[0], r_x0), 0)
     kept, sent = products(structure, sel, (f_z, f_xz), (r_z0, r_xz0), 0, near)

time: 141 us -> 140 us (level)
  waiting for transfers between devices: 81.1 us -> 75.9 us
  starting transfers between devices: 33.4 us -> 38.3 us
    ppermute x25, starting transfers between devices: 32.1 us -> 37 us  [hop(): return lax.ppermute(value, 'wide', [(i, i ^ mask) for i in range(size)])]
    ppermute x25, waiting for transfers between devices: 74.7 us -> 71.6 us  [hop(): return lax.ppermute(value, 'wide', [(i, i ^ mask) for i in range(size)])]
    unnamed x12 -> x10, local copies, waits for them, and re-layouts: 3.5 us -> 1.27 us
    ppermute x5, waiting for transfers between devices: 6.42 us -> 4.31 us  [swap_cores(): return lax.ppermute(value, 'narrow', [(0, 1), (1, 0)])]
    squeeze x0 -> x1, local copies, waits for them, and re-layouts: none -> 1.44 us  [per_device_grid(): lax.dynamic_index_in_dim(panel, 1 - n, 0, keepdims=False)]
  transfers between devices with their start and end apart: 30 -> 30, of which waited for: 15 -> 14; matrix products, arithmetic and copies ran while one was open for 0% -> 0% of each run, Pallas kernels for 12% -> 12%
where the time goes in v11:
time: 140 us
  waiting for transfers between devices  75.9 us (54%)
  starting transfers between devices  38.3 us (27%)
  Pallas kernels  21.1 us (15%)
  local copies, waits for them, and re-layouts  2.72 us (2%)
    ppermute x25, waiting for transfers between devices, hop(): return lax.ppermute(value, 'wide', [(i, i ^ mask) for i in range(size)])  71.6 us
    ppermute x25, starting transfers between devices, hop(): return lax.ppermute(value, 'wide', [(i, i ^ mask) for i in range(size)])  37 us
    pallas_call x4, Pallas kernels, products(): pl.pallas_call(body, out_shape=out if near is None else [out, out], in_sp...  14.8 us
    ppermute x5, waiting for transfers between devices, swap_cores(): return lax.ppermute(value, 'narrow', [(0, 1), (1, 0)])  4.31 us
  transfers between devices with their start and end apart: 30, of which 14 were waited for; matrix products, arithmetic and copies ran while one was open for 0% of the time, Pallas kernels for 12%

profile of v11, /device:TPU:0, one launch (start us, length us, event | category | flops | bytes accessed | tf_op | source)
XLA Modules:
  0.0 139.6 jit_solution(13294845814979867277)
XLA Ops:
  2.6 2.6 %collective-permute-start = (bf16[256,2048]{1,0:T(8,128)(2,1)}, bf16[256,2048]{1,0:T(8,128)(2,1)S(1)}, u32[]{:S(2)}, u32[]{:S(2)}) collective-permute-start(bf16[256,2048]{1,0:T(8,128)(2,1)} %refs_0_.1), channel_id=1, source_target_pairs={{0,4},{2,6},{4,0},{6,2},{8,12},{10,14},{12,8},{14,10},{16,20},{18,... | collective-permute-start | bytes 3145736 | tf_op jit(solution)/shard_map/inv_y/ppermute | solution.py:107
  8.8 2.6 %collective-permute-start.1 = (bf16[1024,256]{1,0:T(8,128)(2,1)S(1)}, bf16[1024,256]{1,0:T(8,128)(2,1)S(1)}, u32[]{:S(2)}, u32[]{:S(2)}) collective-permute-start(bf16[1024,256]{1,0:T(8,128)(2,1)S(1)} %get-tuple-element.43.f0), channel_id=1, source_target_pairs={{0,16},{2,18},{4,20},{6,22},{8,24},{10,26},{12,28},{14,30},{16,0},... | collective-permute-start | bytes 1572872 | tf_op jit(solution)/shard_map/first_z/ppermute | solution.py:107
  12.9 25.2 %collective-permute-done.8.refs_2_ = bf16[192,2048]{1,0:T(8,128)(2,1)S(1)} collective-permute-done((bf16[192,2048]{1,0:T(8,128)(2,1)S(1)}, bf16[192,2048]{1,0:T(8,128)(2,1)S(1)}, u32[]{:S(2)}, u32[]{:S(2)}) %collective-permute-start.8) | collective-permute-done | bytes 786464 | tf_op jit(solution)/shard_map/inv_z0/ppermute | solution.py:107
  39.4 1.9 %collective-permute-start.4 = (bf16[2064,128]{1,0:T(8,128)(2,1)S(1)}, bf16[2064,128]{1,0:T(8,128)(2,1)S(1)}, u32[]{:S(2)}, u32[]{:S(2)}) collective-permute-start(bf16[2064,128]{1,0:T(8,128)(2,1)S(1)} %get-tuple-element.63.r0), channel_id=1, source_target_pairs={{0,16},{2,18},{4,20},{6,22},{8,24},{10,26},{12,28},{14,30},{16,0},... | collective-permute-start | bytes 1585160 | tf_op jit(solution)/shard_map/rest0_z/ppermute | solution.py:107
  42.8 2.5 %collective-permute-start.7 = (bf16[64,2048]{1,0:T(8,128)(2,1)S(1)}, bf16[64,2048]{1,0:T(8,128)(2,1)S(1)}, u32[]{:S(2)}, u32[]{:S(2)}) collective-permute-start(bf16[64,2048]{1,0:T(8,128)(2,1)S(1)} %get-tuple-element.49), channel_id=1, source_target_pairs={{0,8},{2,10},{4,12},{6,14},{8,0},{10,2},{12,4},{14,6},{16,24},{18,... | collective-permute-start | bytes 786440 | tf_op jit(solution)/shard_map/inv_z1/ppermute | solution.py:107
  45.8 11.6 %collective-permute-done.7.refs_0_ = bf16[64,2048]{1,0:T(8,128)(2,1)S(1)} collective-permute-done((bf16[64,2048]{1,0:T(8,128)(2,1)S(1)}, bf16[64,2048]{1,0:T(8,128)(2,1)S(1)}, u32[]{:S(2)}, u32[]{:S(2)}) %collective-permute-start.7) | collective-permute-done | bytes 262176 | tf_op jit(solution)/shard_map/inv_z1/ppermute | solution.py:107
  59.1 6.1 %collective-permute-done.6.f1 = bf16[1024,256]{1,0:T(8,128)(2,1)S(1)} collective-permute-done((bf16[1024,256]{1,0:T(8,128)(2,1)S(1)}, bf16[1024,256]{1,0:T(8,128)(2,1)S(1)}, u32[]{:S(2)}, u32[]{:S(2)}) %collective-permute-start.6) | collective-permute-done | bytes 524320 | tf_op jit(solution)/shard_map/first_xz/ppermute | solution.py:107
  67.4 2.1 %collective-permute-start.13 = (bf16[2048,128]{1,0:T(8,128)(2,1)S(1)}, bf16[2048,128]{1,0:T(8,128)(2,1)S(1)}, u32[]{:S(2)}, u32[]{:S(2)}) collective-permute-start(bf16[2048,128]{1,0:T(8,128)(2,1)S(1)} %get-tuple-element.58.r0), channel_id=1, source_target_pairs={{0,16},{2,18},{4,20},{6,22},{8,24},{10,26},{12,28},{14,30},{16,0},... | collective-permute-start | bytes 1572872 | tf_op jit(solution)/shard_map/rest1_z/ppermute | solution.py:107
  70.1 2.4 %collective-permute-done.12.refs_3_ = bf16[320,2048]{1,0:T(8,128)(2,1)S(1)} collective-permute-done((bf16[320,2048]{1,0:T(8,128)(2,1)S(1)}, bf16[320,2048]{1,0:T(8,128)(2,1)S(1)}, u32[]{:S(2)}, u32[]{:S(2)}) %collective-permute-start.12) | collective-permute-done | bytes 1310752 | tf_op jit(solution)/shard_map/inv_swap_more/ppermute | solution.py:101
  74.1 3.6 %products.4.refs_0_ = bf16[4,272,256]{2,1,0:T(8,128)(2,1)S(1)} custom-call(s32[2,12]{1,0:T(2,128)S(1)} %copy-done.4, bf16[4,256,3072]{2,1,0:T(8,128)(2,1)S(1)} %pack_inverse.1.sel_ref, bf16[1024,256]{1,0:T(8,128)(2,1)S(1)} %get-tuple-element.43.f0, bf16[1024,256]{1,0:T(8,128)(2,1)S(1)} %collective-permute-done.2.f1, ...), custom_call_target="tpu_custom_call" | custom-call | tf_op jit(solution)/shard_map/products/pallas_call | solution.py:330
  77.8 3.0 %collective-permute-done.18.r1 = bf16[2064,128]{1,0:T(8,128)(2,1)S(1)} collective-permute-done((bf16[2064,128]{1,0:T(8,128)(2,1)S(1)}, bf16[2064,128]{1,0:T(8,128)(2,1)S(1)}, u32[]{:S(2)}, u32[]{:S(2)}) %collective-permute-start.18) | collective-permute-done | bytes 528416 | tf_op jit(solution)/shard_map/rest0_xz/ppermute | solution.py:107
  80.8 3.7 %products.5 = (bf16[4,272,256]{2,1,0:T(8,128)(2,1)S(1)}, bf16[4,272,256]{2,1,0:T(8,128)(2,1)S(1)}) custom-call(s32[2,12]{1,0:T(2,128)S(1)} %copy-done.4, bf16[4,256,3072]{2,1,0:T(8,128)(2,1)S(1)} %pack_inverse.1.sel_ref, bf16[1024,256]{1,0:T(8,128)(2,1)S(1)} %collective-permute-done.1.f0, bf16[1024,256]{1,0:T(8,128)(2,1)S(1)} %collective-permute-done.6.f1, ...), custom_call_target="tpu_custom_call" | custom-call | tf_op jit(solution)/shard_map/products/pallas_call | solution.py:330
  86.5 2.2 %collective-permute-done.15 = f32[2,2048]{1,0:T(2,128)S(1)} collective-permute-done((f32[2,2048]{1,0:T(2,128)S(1)}, f32[2,2048]{1,0:T(2,128)S(1)}, u32[]{:S(2)}, u32[]{:S(2)}) %collective-permute-start.15) | collective-permute-done | bytes 16416 | tf_op jit(solution)/shard_map/squares_2/ppermute | solution.py:107
  88.8 2.5 %collective-permute-start.16 = (f32[2,2048]{1,0:T(2,128)S(1)}, f32[2,2048]{1,0:T(2,128)S(1)}, u32[]{:S(2)}, u32[]{:S(2)}) collective-permute-start(f32[2,2048]{1,0:T(2,128)S(1)} %add.21), channel_id=1, source_target_pairs={{0,8},{2,10},{4,12},{6,14},{8,0},{10,2},{12,4},{14,6},{16,24},{18,... | collective-permute-start | bytes 49160 | tf_op jit(solution)/shard_map/squares_4/ppermute | solution.py:107
  91.3 2.3 %collective-permute-done.16 = f32[2,2048]{1,0:T(2,128)S(1)} collective-permute-done((f32[2,2048]{1,0:T(2,128)S(1)}, f32[2,2048]{1,0:T(2,128)S(1)}, u32[]{:S(2)}, u32[]{:S(2)}) %collective-permute-start.16) | collective-permute-done | bytes 16416 | tf_op jit(solution)/shard_map/squares_4/ppermute | solution.py:107
  94.3 2.9 %collective-permute-start.20 = (bf16[2,272,256]{2,1,0:T(8,128)(2,1)S(1)}, bf16[2,272,256]{2,1,0:T(8,128)(2,1)S(1)}, u32[]{:S(2)}, u32[]{:S(2)}) collective-permute-start(bf16[2,272,256]{2,1,0:T(8,128)(2,1)S(1)} %get-tuple-element.68), channel_id=1, source_target_pairs={{0,12},{2,14},{4,8},{6,10},{8,4},{10,6},{12,0},{14,2},{16,28},{18,... | collective-permute-start | bytes 835592 | tf_op jit(solution)/shard_map/cross0_3/ppermute | solution.py:107
  97.8 3.8 %products.6.refs_0_ = bf16[4,272,256]{2,1,0:T(8,128)(2,1)S(1)} custom-call(s32[2,12]{1,0:T(2,128)S(1)} %copy-done.4, bf16[4,256,3072]{2,1,0:T(8,128)(2,1)S(1)} %pack_inverse.1.sel_ref, bf16[1024,256]{1,0:T(8,128)(2,1)S(1)} %get-tuple-element.43.f0, bf16[1024,256]{1,0:T(8,128)(2,1)S(1)} %collective-permute-done.2.f1, ...), custom_call_target="tpu_custom_call" | custom-call | tf_op jit(solution)/shard_map/products/pallas_call | solution.py:330
  101.7 5.8 %collective-permute-done.17.r1 = bf16[2048,128]{1,0:T(8,128)(2,1)S(1)} collective-permute-done((bf16[2048,128]{1,0:T(8,128)(2,1)S(1)}, bf16[2048,128]{1,0:T(8,128)(2,1)S(1)}, u32[]{:S(2)}, u32[]{:S(2)}) %collective-permute-start.17) | collective-permute-done | bytes 524320 | tf_op jit(solution)/shard_map/rest1_xz/ppermute | solution.py:107
  107.5 2.0 %collective-permute-done.21.refs_2_ = bf16[2,272,256]{2,1,0:T(8,128)(2,1)S(1)} collective-permute-done((bf16[2,272,256]{2,1,0:T(8,128)(2,1)S(1)}, bf16[2,272,256]{2,1,0:T(8,128)(2,1)S(1)}, u32[]{:S(2)}, u32[]{:S(2)}) %collective-permute-start.21) | collective-permute-done | bytes 278560 | tf_op jit(solution)/shard_map/cross0_1/ppermute | solution.py:107
  109.6 3.7 %products.7 = (bf16[4,272,256]{2,1,0:T(8,128)(2,1)S(1)}, bf16[4,272,256]{2,1,0:T(8,128)(2,1)S(1)}) custom-call(s32[2,12]{1,0:T(2,128)S(1)} %copy-done.4, bf16[4,256,3072]{2,1,0:T(8,128)(2,1)S(1)} %pack_inverse.1.sel_ref, bf16[1024,256]{1,0:T(8,128)(2,1)S(1)} %collective-permute-done.1.f0, bf16[1024,256]{1,0:T(8,128)(2,1)S(1)} %collective-permute-done.6.f1, ...), custom_call_target="tpu_custom_call" | custom-call | tf_op jit(solution)/shard_map/products/pallas_call | solution.py:330
  113.4 1.9 %collective-permute-done.23.their_ref = bf16[4,272,256]{2,1,0:T(8,128)(2,1)S(1)} collective-permute-done((bf16[4,272,256]{2,1,0:T(8,128)(2,1)S(1)}, bf16[4,272,256]{2,1,0:T(8,128)(2,1)S(1)}, u32[]{:S(2)}, u32[]{:S(2)}) %collective-permute-start.23) | collective-permute-done | bytes 557088 | tf_op jit(solution)/shard_map/cross1_swap/ppermute | solution.py:101
  119.0 6.9 %collective-permute-done.24.refs_1_ = bf16[2,272,256]{2,1,0:T(8,128)(2,1)S(1)} collective-permute-done((bf16[2,272,256]{2,1,0:T(8,128)(2,1)S(1)}, bf16[2,272,256]{2,1,0:T(8,128)(2,1)S(1)}, u32[]{:S(2)}, u32[]{:S(2)}) %collective-permute-start.24) | collective-permute-done | bytes 278560 | tf_op jit(solution)/shard_map/cross1_3/ppermute | solution.py:107
  125.9 5.1 %collective-permute-done.25.refs_2_ = bf16[2,272,256]{2,1,0:T(8,128)(2,1)S(1)} collective-permute-done((bf16[2,272,256]{2,1,0:T(8,128)(2,1)S(1)}, bf16[2,272,256]{2,1,0:T(8,128)(2,1)S(1)}, u32[]{:S(2)}, u32[]{:S(2)}) %collective-permute-start.25) | collective-permute-done | bytes 278560 | tf_op jit(solution)/shard_map/cross1_1/ppermute | solution.py:107
  133.4 2.1 %collective-permute-start.29 = (f32[2,2048]{1,0:T(2,128)S(1)}, f32[2,2048]{1,0:T(2,128)S(1)}, u32[]{:S(2)}, u32[]{:S(2)}) collective-permute-start(f32[2,2048]{1,0:T(2,128)S(1)} %add_sums.3), channel_id=1, source_target_pairs={{0,18},{2,16},{4,22},{6,20},{8,26},{10,24},{12,30},{14,28},{16,2},... | collective-permute-start | bytes 49160 | tf_op jit(solution)/shard_map/variance_9/ppermute | solution.py:107
  (66 shorter events, 30.1 us)
Async XLA Ops:
  2.1 36.3 %collective-permute-start.3 = (bf16[2048,256]{1,0:T(8,128)(2,1)S(1)}, bf16[2048,256]{1,0:T(8,128)(2,1)S(1)}, u32[]{:S(2)}, u32[]{:S(2)}) collective-permute-start(bf16[2048,256]{1,0:T(8,128)(2,1)S(1)} %dynamic-slice_bitcast_fusion), channel_id=1, source_target_pairs={{0,1},{1,0},{2,3},{3,2},{4,5},{5,4},{6,7},{7,6},{8,9},{9,8},{10,11... | collective-permute-start | bytes 3145736 | tf_op jit(solution)/shard_map/panel_swap/ppermute | solution.py:101
  2.6 36.7 %collective-permute-start = (bf16[256,2048]{1,0:T(8,128)(2,1)}, bf16[256,2048]{1,0:T(8,128)(2,1)S(1)}, u32[]{:S(2)}, u32[]{:S(2)}) collective-permute-start(bf16[256,2048]{1,0:T(8,128)(2,1)} %refs_0_.1), channel_id=1, source_target_pairs={{0,4},{2,6},{4,0},{6,2},{8,12},{10,14},{12,8},{14,10},{16,20},{18,... | collective-permute-start | bytes 3145736 | tf_op jit(solution)/shard_map/inv_y/ppermute | solution.py:107
  7.1 30.9 %collective-permute-start.8 = (bf16[192,2048]{1,0:T(8,128)(2,1)S(1)}, bf16[192,2048]{1,0:T(8,128)(2,1)S(1)}, u32[]{:S(2)}, u32[]{:S(2)}) collective-permute-start(bf16[192,2048]{1,0:T(8,128)(2,1)S(1)} %get-tuple-element.50), channel_id=1, source_target_pairs={{0,8},{2,10},{4,12},{6,14},{8,0},{10,2},{12,4},{14,6},{16,24},{18,... | collective-permute-start | bytes 2359304 | tf_op jit(solution)/shard_map/inv_z0/ppermute | solution.py:107
  8.8 30.5 %collective-permute-start.1 = (bf16[1024,256]{1,0:T(8,128)(2,1)S(1)}, bf16[1024,256]{1,0:T(8,128)(2,1)S(1)}, u32[]{:S(2)}, u32[]{:S(2)}) collective-permute-start(bf16[1024,256]{1,0:T(8,128)(2,1)S(1)} %get-tuple-element.43.f0), channel_id=1, source_target_pairs={{0,16},{2,18},{4,20},{6,22},{8,24},{10,26},{12,28},{14,30},{16,0},... | collective-permute-start | bytes 1572872 | tf_op jit(solution)/shard_map/first_z/ppermute | solution.py:107
  11.4 28.0 %collective-permute-start.2 = (bf16[1024,256]{1,0:T(8,128)(2,1)S(1)}, bf16[1024,256]{1,0:T(8,128)(2,1)S(1)}, u32[]{:S(2)}, u32[]{:S(2)}) collective-permute-start(bf16[1024,256]{1,0:T(8,128)(2,1)S(1)} %get-tuple-element.43.f0), channel_id=1, source_target_pairs={{0,2},{2,0},{4,6},{6,4},{8,10},{10,8},{12,14},{14,12},{16,18},{18,... | collective-permute-start | bytes 1572872 | tf_op jit(solution)/shard_map/first_x/ppermute | solution.py:107
  38.1 27.2 %collective-permute-start.9 = (bf16[192,2048]{1,0:T(8,128)(2,1)S(1)}, bf16[192,2048]{1,0:T(8,128)(2,1)S(1)}, u32[]{:S(2)}, u32[]{:S(2)}) collective-permute-start(bf16[192,2048]{1,0:T(8,128)(2,1)S(1)} %collective-permute-done.8.refs_2_), channel_id=1, source_target_pairs={{0,4},{2,6},{4,0},{6,2},{8,12},{10,14},{12,8},{14,10},{16,20},{18,... | collective-permute-start | bytes 2359304 | tf_op jit(solution)/shard_map/inv_yz0/ppermute | solution.py:107
  39.4 25.9 %collective-permute-start.4 = (bf16[2064,128]{1,0:T(8,128)(2,1)S(1)}, bf16[2064,128]{1,0:T(8,128)(2,1)S(1)}, u32[]{:S(2)}, u32[]{:S(2)}) collective-permute-start(bf16[2064,128]{1,0:T(8,128)(2,1)S(1)} %get-tuple-element.63.r0), channel_id=1, source_target_pairs={{0,16},{2,18},{4,20},{6,22},{8,24},{10,26},{12,28},{14,30},{16,0},... | collective-permute-start | bytes 1585160 | tf_op jit(solution)/shard_map/rest0_z/ppermute | solution.py:107
  41.3 23.9 %collective-permute-start.5 = (bf16[2064,128]{1,0:T(8,128)(2,1)S(1)}, bf16[2064,128]{1,0:T(8,128)(2,1)S(1)}, u32[]{:S(2)}, u32[]{:S(2)}) collective-permute-start(bf16[2064,128]{1,0:T(8,128)(2,1)S(1)} %get-tuple-element.63.r0), channel_id=1, source_target_pairs={{0,2},{2,0},{4,6},{6,4},{8,10},{10,8},{12,14},{14,12},{16,18},{18,... | collective-permute-start | bytes 1585160 | tf_op jit(solution)/shard_map/rest0_x/ppermute | solution.py:107
  42.8 14.7 %collective-permute-start.7 = (bf16[64,2048]{1,0:T(8,128)(2,1)S(1)}, bf16[64,2048]{1,0:T(8,128)(2,1)S(1)}, u32[]{:S(2)}, u32[]{:S(2)}) collective-permute-start(bf16[64,2048]{1,0:T(8,128)(2,1)S(1)} %get-tuple-element.49), channel_id=1, source_target_pairs={{0,8},{2,10},{4,12},{6,14},{8,0},{10,2},{12,4},{14,6},{16,24},{18,... | collective-permute-start | bytes 786440 | tf_op jit(solution)/shard_map/inv_z1/ppermute | solution.py:107
  45.2 20.0 %collective-permute-start.6 = (bf16[1024,256]{1,0:T(8,128)(2,1)S(1)}, bf16[1024,256]{1,0:T(8,128)(2,1)S(1)}, u32[]{:S(2)}, u32[]{:S(2)}) collective-permute-start(bf16[1024,256]{1,0:T(8,128)(2,1)S(1)} %collective-permute-done.1.f0), channel_id=1, source_target_pairs={{0,2},{2,0},{4,6},{6,4},{8,10},{10,8},{12,14},{14,12},{16,18},{18,... | collective-permute-start | bytes 1572872 | tf_op jit(solution)/shard_map/first_xz/ppermute | solution.py:107
  57.4 7.8 %collective-permute-start.10 = (bf16[64,2048]{1,0:T(8,128)(2,1)S(1)}, bf16[64,2048]{1,0:T(8,128)(2,1)S(1)}, u32[]{:S(2)}, u32[]{:S(2)}) collective-permute-start(bf16[64,2048]{1,0:T(8,128)(2,1)S(1)} %collective-permute-done.7.refs_0_), channel_id=1, source_target_pairs={{0,4},{2,6},{4,0},{6,2},{8,12},{10,14},{12,8},{14,10},{16,20},{18,... | collective-permute-start | bytes 786440 | tf_op jit(solution)/shard_map/inv_yz1/ppermute | solution.py:107
  65.2 7.2 %collective-permute-start.11 = (bf16[704,2048]{1,0:T(8,128)(2,1)S(1)}, bf16[704,2048]{1,0:T(8,128)(2,1)S(1)}, u32[]{:S(2)}, u32[]{:S(2)}) collective-permute-start(bf16[704,2048]{1,0:T(8,128)(2,1)S(1)} %stack_rows.2.refs_0_), channel_id=1, source_target_pairs={{0,1},{1,0},{2,3},{3,2},{4,5},{5,4},{6,7},{7,6},{8,9},{9,8},{10,11... | collective-permute-start | bytes 8650760 | tf_op jit(solution)/shard_map/inv_swap/ppermute | solution.py:101
  65.4 7.1 %collective-permute-start.12 = (bf16[320,2048]{1,0:T(8,128)(2,1)S(1)}, bf16[320,2048]{1,0:T(8,128)(2,1)S(1)}, u32[]{:S(2)}, u32[]{:S(2)}) collective-permute-start(bf16[320,2048]{1,0:T(8,128)(2,1)S(1)} %stack_rows.3.refs_1_), channel_id=1, source_target_pairs={{0,1},{1,0},{2,3},{3,2},{4,5},{5,4},{6,7},{7,6},{8,9},{9,8},{10,11... | collective-permute-start | bytes 3932168 | tf_op jit(solution)/shard_map/inv_swap_more/ppermute | solution.py:101
  66.0 14.9 %collective-permute-start.18 = (bf16[2064,128]{1,0:T(8,128)(2,1)S(1)}, bf16[2064,128]{1,0:T(8,128)(2,1)S(1)}, u32[]{:S(2)}, u32[]{:S(2)}) collective-permute-start(bf16[2064,128]{1,0:T(8,128)(2,1)S(1)} %collective-permute-done.4.r0), channel_id=1, source_target_pairs={{0,2},{2,0},{4,6},{6,4},{8,10},{10,8},{12,14},{14,12},{16,18},{18,... | collective-permute-start | bytes 1585160 | tf_op jit(solution)/shard_map/rest0_xz/ppermute | solution.py:107
  67.4 26.1 %collective-permute-start.13 = (bf16[2048,128]{1,0:T(8,128)(2,1)S(1)}, bf16[2048,128]{1,0:T(8,128)(2,1)S(1)}, u32[]{:S(2)}, u32[]{:S(2)}) collective-permute-start(bf16[2048,128]{1,0:T(8,128)(2,1)S(1)} %get-tuple-element.58.r0), channel_id=1, source_target_pairs={{0,16},{2,18},{4,20},{6,22},{8,24},{10,26},{12,28},{14,30},{16,0},... | collective-permute-start | bytes 1572872 | tf_op jit(solution)/shard_map/rest1_z/ppermute | solution.py:107
  69.6 24.0 %collective-permute-start.14 = (bf16[2048,128]{1,0:T(8,128)(2,1)S(1)}, bf16[2048,128]{1,0:T(8,128)(2,1)S(1)}, u32[]{:S(2)}, u32[]{:S(2)}) collective-permute-start(bf16[2048,128]{1,0:T(8,128)(2,1)S(1)} %get-tuple-element.58.r0), channel_id=1, source_target_pairs={{0,2},{2,0},{4,6},{6,4},{8,10},{10,8},{12,14},{14,12},{16,18},{18,... | collective-permute-start | bytes 1572872 | tf_op jit(solution)/shard_map/rest1_x/ppermute | solution.py:107
  84.5 9.7 %collective-permute-start.19 = (bf16[4,272,256]{2,1,0:T(8,128)(2,1)S(1)}, bf16[4,272,256]{2,1,0:T(8,128)(2,1)S(1)}, u32[]{:S(2)}, u32[]{:S(2)}) collective-permute-start(bf16[4,272,256]{2,1,0:T(8,128)(2,1)S(1)} %get-tuple-element.66), channel_id=1, source_target_pairs={{0,1},{1,0},{2,3},{3,2},{4,5},{5,4},{6,7},{7,6},{8,9},{9,8},{10,11... | collective-permute-start | bytes 1671176 | tf_op jit(solution)/shard_map/cross0_swap/ppermute | solution.py:101
  93.6 13.9 %collective-permute-start.17 = (bf16[2048,128]{1,0:T(8,128)(2,1)S(1)}, bf16[2048,128]{1,0:T(8,128)(2,1)S(1)}, u32[]{:S(2)}, u32[]{:S(2)}) collective-permute-start(bf16[2048,128]{1,0:T(8,128)(2,1)S(1)} %collective-permute-done.13.r0), channel_id=1, source_target_pairs={{0,2},{2,0},{4,6},{6,4},{8,10},{10,8},{12,14},{14,12},{16,18},{18,... | collective-permute-start | bytes 1572872 | tf_op jit(solution)/shard_map/rest1_xz/ppermute | solution.py:107
  94.3 13.2 %collective-permute-start.20 = (bf16[2,272,256]{2,1,0:T(8,128)(2,1)S(1)}, bf16[2,272,256]{2,1,0:T(8,128)(2,1)S(1)}, u32[]{:S(2)}, u32[]{:S(2)}) collective-permute-start(bf16[2,272,256]{2,1,0:T(8,128)(2,1)S(1)} %get-tuple-element.68), channel_id=1, source_target_pairs={{0,12},{2,14},{4,8},{6,10},{8,4},{10,6},{12,0},{14,2},{16,28},{18,... | collective-permute-start | bytes 835592 | tf_op jit(solution)/shard_map/cross0_3/ppermute | solution.py:107
  97.2 12.3 %collective-permute-start.21 = (bf16[2,272,256]{2,1,0:T(8,128)(2,1)S(1)}, bf16[2,272,256]{2,1,0:T(8,128)(2,1)S(1)}, u32[]{:S(2)}, u32[]{:S(2)}) collective-permute-start(bf16[2,272,256]{2,1,0:T(8,128)(2,1)S(1)} %get-tuple-element.69), channel_id=1, source_target_pairs={{0,4},{2,6},{4,0},{6,2},{8,12},{10,14},{12,8},{14,10},{16,20},{18,... | collective-permute-start | bytes 835592 | tf_op jit(solution)/shard_map/cross0_1/ppermute | solution.py:107
  97.7 11.9 %collective-permute-start.22 = (bf16[2,272,256]{2,1,0:T(8,128)(2,1)S(1)}, bf16[2,272,256]{2,1,0:T(8,128)(2,1)S(1)}, u32[]{:S(2)}, u32[]{:S(2)}) collective-permute-start(bf16[2,272,256]{2,1,0:T(8,128)(2,1)S(1)} %get-tuple-element.70), channel_id=1, source_target_pairs={{0,8},{2,10},{4,12},{6,14},{8,0},{10,2},{12,4},{14,6},{16,24},{18,... | collective-permute-start | bytes 835592 | tf_op jit(solution)/shard_map/cross0_2/ppermute | solution.py:107
  115.4 10.5 %collective-permute-start.24 = (bf16[2,272,256]{2,1,0:T(8,128)(2,1)S(1)}, bf16[2,272,256]{2,1,0:T(8,128)(2,1)S(1)}, u32[]{:S(2)}, u32[]{:S(2)}) collective-permute-start(bf16[2,272,256]{2,1,0:T(8,128)(2,1)S(1)} %get-tuple-element.76), channel_id=1, source_target_pairs={{0,12},{2,14},{4,8},{6,10},{8,4},{10,6},{12,0},{14,2},{16,28},{18,... | collective-permute-start | bytes 835592 | tf_op jit(solution)/shard_map/cross1_3/ppermute | solution.py:107
  117.0 14.1 %collective-permute-start.25 = (bf16[2,272,256]{2,1,0:T(8,128)(2,1)S(1)}, bf16[2,272,256]{2,1,0:T(8,128)(2,1)S(1)}, u32[]{:S(2)}, u32[]{:S(2)}) collective-permute-start(bf16[2,272,256]{2,1,0:T(8,128)(2,1)S(1)} %get-tuple-element.77), channel_id=1, source_target_pairs={{0,4},{2,6},{4,0},{6,2},{8,12},{10,14},{12,8},{14,10},{16,20},{18,... | collective-permute-start | bytes 835592 | tf_op jit(solution)/shard_map/cross1_1/ppermute | solution.py:107
  117.6 13.5 %collective-permute-start.26 = (bf16[2,272,256]{2,1,0:T(8,128)(2,1)S(1)}, bf16[2,272,256]{2,1,0:T(8,128)(2,1)S(1)}, u32[]{:S(2)}, u32[]{:S(2)}) collective-permute-start(bf16[2,272,256]{2,1,0:T(8,128)(2,1)S(1)} %get-tuple-element.78), channel_id=1, source_target_pairs={{0,8},{2,10},{4,12},{6,14},{8,0},{10,2},{12,4},{14,6},{16,24},{18,... | collective-permute-start | bytes 835592 | tf_op jit(solution)/shard_map/cross1_2/ppermute | solution.py:107
  (11 other events, 97.4 us)

commit v12 on v11

--- a/solution.py
+++ b/solution.py
@@ -109,6 +109,23 @@
 
 def after(value, *earlier):
     return lax.optimization_barrier((value, *earlier))[0]
+
+
+def lead(values, micros):
+    def body(*refs):
+        pass
+
+    return pl.pallas_call(
+        body,
+        out_shape=[jax.ShapeDtypeStruct(v.shape, v.dtype) for v in values],
+        in_specs=[ANY] * len(values),
+        out_specs=[ANY] * len(values),
+        input_output_aliases={i: i for i in range(len(values))},
+        cost_estimate=pl.CostEstimate(
+            flops=int(micros * 1.15e9), bytes_accessed=0, transcendentals=0
+        ),
+        name="lead",
+    )(*values)
 
 
 def pick(structure_ref, n, j, first):
@@ -472,6 +489,7 @@
     a_z0 = hop(top, ZL, "inv_z0")
     a_y = hop(inverse, Y, "inv_y")
     a_y, f_z, f_x, *r_own = lax.optimization_barrier((a_y, f_z, f_x, *r_own))
+    r_z1 = hop(r_own[1], ZH, "rest1_z")
     r_z0 = hop(r_own[0], ZH, "rest0_z")
     a_z1 = hop(after(bottom, f_z), ZL, "inv_z1")
     f_xz = hop(f_z, X, "first_xz")
@@ -482,7 +500,6 @@
     r_z0, r_x0, f_xz, a_z1, a_yz0, a_yz1, most, *r_own = lax.optimization_barrier(
         (r_z0, r_x0, f_xz, a_z1, a_yz0, a_yz1, most, *r_own)
     )
-    r_z1 = hop(r_own[1], ZH, "rest1_z")
     r_xz0 = hop(r_z0, X, "rest0_xz")
     r_x1 = hop(r_own[1], X, "rest1_x")
     more = stack_rows([a_z1, a_yz0, a_yz1])
@@ -492,7 +509,9 @@
     linv = after(linv, more)
     for mask in (Y, ZL):
         linv = linv + hop(linv, mask, f"squares_{mask}")
-    r_z1, r_x1, linv = lax.optimization_barrier((r_z1, r_x1, linv))
+    r_z1 = lead([r_z1], 20)[0]
+    r_x1 = lead([r_x1], 10)[0]
+    r_x1, linv = lax.optimization_barrier((r_x1, linv))
 
     def deliver(kept, sent, c):
         messages = bundle(kept, swap_cores(sent, f"cross{c}_swap"))
@@ -504,13 +523,13 @@
     near = products(structure, sel, (f_own, f_x), (r_own[0], r_x0), 0)
     kept, sent = products(structure, sel, (f_z, f_xz), (r_z0, r_xz0), 0, near)
     messages = deliver(kept, sent, 0)
-    r_xz1 = hop(r_z1, X, "rest1_xz")
+    r_xz1 = hop(after(r_z1, kept), X, "rest1_xz")
     near = products(structure, sel, (f_own, f_x), (r_own[1], r_x1), 1)
-    r_xz1, *messages = lax.optimization_barrier((r_xz1, *messages))
+    messages[1:] = lead(messages[1:], 5)
     kept, sent = products(structure, sel, (f_z, f_xz), (r_z1, r_xz1), 1, near)
     held = assemble(messages, 0, None)
     variance = add_sums(linv, messages, 0)
-    messages = deliver(kept, sent, 1)
+    messages = deliver(after(kept, variance), sent, 1)
     variance = add_sums(variance, messages, 1)
     held = assemble(messages, 1, held)
     hops = [hop(variance, mask, f"variance_{mask}") for mask in (X, ZH, X | ZH)]

time: 140 us -> 144 us (1.029)
  local copies, waits for them, and re-layouts: 2.72 us -> 10.7 us
  waiting for transfers between devices: 75.9 us -> 69.1 us
  Pallas kernels: 21.1 us -> 25.8 us
  starting transfers between devices: 38.3 us -> 36.4 us
    unnamed x10 -> x42, local copies, waits for them, and re-layouts: 1.27 us -> 9.28 us
    ppermute x5, waiting for transfers between devices: 4.31 us -> 0.01 us  [swap_cores(): return lax.ppermute(value, 'narrow', [(0, 1), (1, 0)])]
    ppermute x25, waiting for transfers between devices: 71.6 us -> 69.1 us  [hop(): return lax.ppermute(value, 'wide', [(i, i ^ mask) for i in range(size)])]
    pallas_call x4, Pallas kernels: 14.8 us -> 16.8 us  [products(): pl.pallas_call(body, out_shape=out if near is None else [out, out], in_sp...]
    pallas_call x2, Pallas kernels: 0.15 us -> 2.05 us  [bundle(): pl.pallas_call(body, out_shape=[shape] * NGRP, in_specs=[VMEM, VMEM], out...]
    ppermute x25, starting transfers between devices: 37 us -> 35.2 us  [hop(): return lax.ppermute(value, 'wide', [(i, i ^ mask) for i in range(size)])]
  transfers between devices with their start and end apart: 30 -> 30, of which waited for: 14 -> 10; matrix products, arithmetic and copies ran while one was open for 0% -> 0% of each run, Pallas kernels for 12% -> 18%
where the time goes in v12:
time: 144 us
  waiting for transfers between devices  69.1 us (48%)
  starting transfers between devices  36.4 us (25%)
  Pallas kernels  25.8 us (18%)
  local copies, waits for them, and re-layouts  10.7 us (7%)
    ppermute x25, waiting for transfers between devices, hop(): return lax.ppermute(value, 'wide', [(i, i ^ mask) for i in range(size)])  69.1 us
    ppermute x25, starting transfers between devices, hop(): return lax.ppermute(value, 'wide', [(i, i ^ mask) for i in range(size)])  35.2 us
    pallas_call x4, Pallas kernels, products(): pl.pallas_call(body, out_shape=out if near is None else [out, out], in_sp...  16.8 us
    unnamed x42, local copies, waits for them, and re-layouts  9.28 us
  transfers between devices with their start and end apart: 30, of which 10 were waited for; matrix products, arithmetic and copies ran while one was open for 0% of the time, Pallas kernels for 18%

profile of v12, /device:TPU:0, one launch (start us, length us, event | category | flops | bytes accessed | tf_op | source)
XLA Modules:
  0.0 143.6 jit_solution(7426643321623928771)
XLA Ops:
  2.6 2.6 %collective-permute-start = (bf16[256,2048]{1,0:T(8,128)(2,1)}, bf16[256,2048]{1,0:T(8,128)(2,1)S(1)}, u32[]{:S(2)}, u32[]{:S(2)}) collective-permute-start(bf16[256,2048]{1,0:T(8,128)(2,1)} %refs_0_.1), channel_id=1, source_target_pairs={{0,4},{2,6},{4,0},{6,2},{8,12},{10,14},{12,8},{14,10},{16,20},{18,... | collective-permute-start | bytes 3145736 | tf_op jit(solution)/shard_map/inv_y/ppermute | solution.py:107
  8.8 2.6 %collective-permute-start.1 = (bf16[1024,256]{1,0:T(8,128)(2,1)S(1)}, bf16[1024,256]{1,0:T(8,128)(2,1)S(1)}, u32[]{:S(2)}, u32[]{:S(2)}) collective-permute-start(bf16[1024,256]{1,0:T(8,128)(2,1)S(1)} %get-tuple-element.42.f0), channel_id=1, source_target_pairs={{0,16},{2,18},{4,20},{6,22},{8,24},{10,26},{12,28},{14,30},{16,0},... | collective-permute-start | bytes 1572872 | tf_op jit(solution)/shard_map/first_z/ppermute | solution.py:107
  12.9 25.2 %collective-permute-done.8.refs_2_ = bf16[192,2048]{1,0:T(8,128)(2,1)S(1)} collective-permute-done((bf16[192,2048]{1,0:T(8,128)(2,1)S(1)}, bf16[192,2048]{1,0:T(8,128)(2,1)S(1)}, u32[]{:S(2)}, u32[]{:S(2)}) %collective-permute-start.8) | collective-permute-done | bytes 786464 | tf_op jit(solution)/shard_map/inv_z0/ppermute | solution.py:107
  38.4 1.7 %pack_rest.1 = (bf16[2064,128]{1,0:T(8,128)(2,1)S(1)}, bf16[2048,128]{1,0:T(8,128)(2,1)}) custom-call(s32[2,12]{1,0:T(2,128)S(1)} %copy-done.20, bf16[2,2048,256]{2,1,0:T(8,128)(2,1)S(1)} %copy-done.3, bf16[2048,256]{1,0:T(8,128)(2,1)S(1)} %collective-permute-done.3.other_ref), custom_call_target="tpu_custom_call" | custom-call | tf_op jit(solution)/shard_map/pack_rest/pallas_call | solution.py:187
  40.1 1.9 %collective-permute-start.4 = (bf16[2064,128]{1,0:T(8,128)(2,1)S(1)}, bf16[2064,128]{1,0:T(8,128)(2,1)S(1)}, u32[]{:S(2)}, u32[]{:S(2)}) collective-permute-start(bf16[2064,128]{1,0:T(8,128)(2,1)S(1)} %get-tuple-element.59.r0), channel_id=1, source_target_pairs={{0,16},{2,18},{4,20},{6,22},{8,24},{10,26},{12,28},{14,30},{16,0},... | collective-permute-start | bytes 1585160 | tf_op jit(solution)/shard_map/rest0_z/ppermute | solution.py:107
  44.1 2.5 %collective-permute-start.7 = (bf16[64,2048]{1,0:T(8,128)(2,1)S(1)}, bf16[64,2048]{1,0:T(8,128)(2,1)S(1)}, u32[]{:S(2)}, u32[]{:S(2)}) collective-permute-start(bf16[64,2048]{1,0:T(8,128)(2,1)S(1)} %get-tuple-element.48), channel_id=1, source_target_pairs={{0,8},{2,10},{4,12},{6,14},{8,0},{10,2},{12,4},{14,6},{16,24},{18,... | collective-permute-start | bytes 786440 | tf_op jit(solution)/shard_map/inv_z1/ppermute | solution.py:107
  46.6 11.6 %collective-permute-done.7.refs_0_ = bf16[64,2048]{1,0:T(8,128)(2,1)S(1)} collective-permute-done((bf16[64,2048]{1,0:T(8,128)(2,1)S(1)}, bf16[64,2048]{1,0:T(8,128)(2,1)S(1)}, u32[]{:S(2)}, u32[]{:S(2)}) %collective-permute-start.7) | collective-permute-done | bytes 262176 | tf_op jit(solution)/shard_map/inv_z1/ppermute | solution.py:107
  59.9 6.1 %collective-permute-done.6.f1 = bf16[1024,256]{1,0:T(8,128)(2,1)S(1)} collective-permute-done((bf16[1024,256]{1,0:T(8,128)(2,1)S(1)}, bf16[1024,256]{1,0:T(8,128)(2,1)S(1)}, u32[]{:S(2)}, u32[]{:S(2)}) %collective-permute-start.6) | collective-permute-done | bytes 524320 | tf_op jit(solution)/shard_map/first_xz/ppermute | solution.py:107
  68.2 2.1 %collective-permute-start.13 = (bf16[2048,128]{1,0:T(8,128)(2,1)}, bf16[2048,128]{1,0:T(8,128)(2,1)}, u32[]{:S(2)}, u32[]{:S(2)}) collective-permute-start(bf16[2048,128]{1,0:T(8,128)(2,1)} %get-tuple-element.63.r0), channel_id=1, source_target_pairs={{0,16},{2,18},{4,20},{6,22},{8,24},{10,26},{12,28},{14,30},{16,0},... | collective-permute-start | bytes 1572872 | tf_op jit(solution)/shard_map/rest1_z/ppermute | solution.py:107
  72.2 2.2 %collective-permute-done.17 = f32[2,2048]{1,0:T(2,128)S(1)} collective-permute-done((f32[2,2048]{1,0:T(2,128)S(1)}, f32[2,2048]{1,0:T(2,128)S(1)}, u32[]{:S(2)}, u32[]{:S(2)}) %collective-permute-start.17) | collective-permute-done | bytes 16416 | tf_op jit(solution)/shard_map/squares_2/ppermute | solution.py:107
  75.8 1.7 %pack_inverse.1.sel_ref = bf16[4,256,3072]{2,1,0:T(8,128)(2,1)S(1)} custom-call(s32[2,12]{1,0:T(2,128)S(1)} %copy-done.20, bf16[704,2048]{1,0:T(8,128)(2,1)S(1)} %stack_rows.2.refs_0_, bf16[320,2048]{1,0:T(8,128)(2,1)S(1)} %stack_rows.3.refs_1_, bf16[704,2048]{1,0:T(8,128)(2,1)S(1)} %collective-permute-done.11.refs_2_, ...), custom_call_target="tpu_custom_call" | custom-call | tf_op jit(solution)/shard_map/pack_inverse/pallas_call | solution.py:248
  77.6 3.4 %products.4.refs_0_ = bf16[4,272,256]{2,1,0:T(8,128)(2,1)S(1)} custom-call(s32[2,12]{1,0:T(2,128)S(1)} %copy-done.20, bf16[4,256,3072]{2,1,0:T(8,128)(2,1)S(1)} %pack_inverse.1.sel_ref, bf16[1024,256]{1,0:T(8,128)(2,1)S(1)} %get-tuple-element.42.f0, bf16[1024,256]{1,0:T(8,128)(2,1)S(1)} %collective-permute-done.2.f1, ...), custom_call_target="tpu_custom_call" | custom-call | tf_op jit(solution)/shard_map/products/pallas_call | solution.py:347
  81.6 4.2 %products.5 = (bf16[4,272,256]{2,1,0:T(8,128)(2,1)S(1)}, bf16[4,272,256]{2,1,0:T(8,128)(2,1)}) custom-call(s32[2,12]{1,0:T(2,128)S(1)} %copy-done.20, bf16[4,256,3072]{2,1,0:T(8,128)(2,1)S(1)} %pack_inverse.1.sel_ref, bf16[1024,256]{1,0:T(8,128)(2,1)S(1)} %collective-permute-done.1.f0, bf16[1024,256]{1,0:T(8,128)(2,1)S(1)} %collective-permute-done.6.f1, ...), custom_call_target="tpu_custom_call" | custom-call | tf_op jit(solution)/shard_map/products/pallas_call | solution.py:347
  85.8 8.5 %collective-permute-done.13.refs_0_ = bf16[2048,128]{1,0:T(8,128)(2,1)} collective-permute-done((bf16[2048,128]{1,0:T(8,128)(2,1)}, bf16[2048,128]{1,0:T(8,128)(2,1)}, u32[]{:S(2)}, u32[]{:S(2)}) %collective-permute-start.13) | collective-permute-done | bytes 524320 | tf_op jit(solution)/shard_map/rest1_z/ppermute | solution.py:107
  94.9 2.0 %bundle.2 = (bf16[2,272,256]{2,1,0:T(8,128)(2,1)S(1)}, bf16[2,272,256]{2,1,0:T(8,128)(2,1)}, bf16[2,272,256]{2,1,0:T(8,128)(2,1)}, bf16[2,272,256]{2,1,0:T(8,128)(2,1)}) custom-call(bf16[4,272,256]{2,1,0:T(8,128)(2,1)S(1)} %get-tuple-element.61.our_ref, bf16[4,272,256]{2,1,0:T(8,128)(2,1)} %collective-permute-done.19.their_ref), custom_call_target="tpu_custom_call" | custom-call | tf_op jit(solution)/shard_map/bundle/pallas_call | solution.py:370
  98.4 2.0 %collective-permute-start.22 = (bf16[2,272,256]{2,1,0:T(8,128)(2,1)}, bf16[2,272,256]{2,1,0:T(8,128)(2,1)S(1)}, u32[]{:S(2)}, u32[]{:S(2)}) collective-permute-start(bf16[2,272,256]{2,1,0:T(8,128)(2,1)} %get-tuple-element.72), channel_id=1, source_target_pairs={{0,8},{2,10},{4,12},{6,14},{8,0},{10,2},{12,4},{14,6},{16,24},{18,... | collective-permute-start | bytes 835592 | tf_op jit(solution)/shard_map/cross0_2/ppermute | solution.py:107
  100.4 2.8 %copy-done.1 = bf16[4,256,3072]{2,1,0:T(8,128)(2,1)S(1)} copy-done((bf16[4,256,3072]{2,1,0:T(8,128)(2,1)S(1)}, bf16[4,256,3072]{2,1,0:T(8,128)(2,1)}, u32[]{:S(2)}) %copy-start.1) | copy-done | bytes 6291480
  103.2 4.3 %products.6.refs_0_ = bf16[4,272,256]{2,1,0:T(8,128)(2,1)S(1)} custom-call(s32[2,12]{1,0:T(2,128)S(1)} %copy-done.20, bf16[4,256,3072]{2,1,0:T(8,128)(2,1)S(1)} %copy-done.1, bf16[1024,256]{1,0:T(8,128)(2,1)S(1)} %get-tuple-element.42.f0, bf16[1024,256]{1,0:T(8,128)(2,1)S(1)} %copy-done.8, bf16[2048,128]{1,0:T(8,128)(2,1)} %get-tuple-element.63.r0, ...), custom_call_target="tpu_custom_call" | custom-call | tf_op jit(solution)/shard_map/products/pallas_call | solution.py:347
  107.6 4.9 %products.7 = (bf16[4,272,256]{2,1,0:T(8,128)(2,1)S(1)}, bf16[4,272,256]{2,1,0:T(8,128)(2,1)}) custom-call(s32[2,12]{1,0:T(2,128)S(1)} %copy-done.20, bf16[4,256,3072]{2,1,0:T(8,128)(2,1)S(1)} %copy-done.2, bf16[1024,256]{1,0:T(8,128)(2,1)S(1)} %collective-permute-done.1.f0, bf16[1024,256]{1,0:T(8,128)(2,1)S(1)} %collective-permute-done.6.f1, ...), custom_call_target="tpu_custom_call" | custom-call | tf_op jit(solution)/shard_map/products/pallas_call | solution.py:347
  117.9 2.0 %collective-permute-start.24 = (bf16[2,272,256]{2,1,0:T(8,128)(2,1)S(1)}, bf16[2,272,256]{2,1,0:T(8,128)(2,1)S(1)}, u32[]{:S(2)}, u32[]{:S(2)}) collective-permute-start(bf16[2,272,256]{2,1,0:T(8,128)(2,1)S(1)} %get-tuple-element.79), channel_id=1, source_target_pairs={{0,12},{2,14},{4,8},{6,10},{8,4},{10,6},{12,0},{14,2},{16,28},{18,... | collective-permute-start | bytes 835592 | tf_op jit(solution)/shard_map/cross1_3/ppermute | solution.py:107
  121.4 6.9 %collective-permute-done.24.refs_1_ = bf16[2,272,256]{2,1,0:T(8,128)(2,1)S(1)} collective-permute-done((bf16[2,272,256]{2,1,0:T(8,128)(2,1)S(1)}, bf16[2,272,256]{2,1,0:T(8,128)(2,1)S(1)}, u32[]{:S(2)}, u32[]{:S(2)}) %collective-permute-start.24) | collective-permute-done | bytes 278560 | tf_op jit(solution)/shard_map/cross1_3/ppermute | solution.py:107
  128.3 5.5 %collective-permute-done.25.refs_2_ = bf16[2,272,256]{2,1,0:T(8,128)(2,1)S(1)} collective-permute-done((bf16[2,272,256]{2,1,0:T(8,128)(2,1)S(1)}, bf16[2,272,256]{2,1,0:T(8,128)(2,1)S(1)}, u32[]{:S(2)}, u32[]{:S(2)}) %collective-permute-start.25) | collective-permute-done | bytes 278560 | tf_op jit(solution)/shard_map/cross1_1/ppermute | solution.py:107
  135.6 1.9 %collective-permute-start.28 = (f32[2,2048]{1,0:T(2,128)S(1)}, f32[2,2048]{1,0:T(2,128)S(1)}, u32[]{:S(2)}, u32[]{:S(2)}) collective-permute-start(f32[2,2048]{1,0:T(2,128)S(1)} %add_sums.3), channel_id=1, source_target_pairs={{0,16},{2,18},{4,20},{6,22},{8,24},{10,26},{12,28},{14,30},{16,0},... | collective-permute-start | bytes 49160 | tf_op jit(solution)/shard_map/variance_8/ppermute | solution.py:107
  140.7 2.3 %collective-permute-done.29 = f32[2,2048]{1,0:T(2,128)S(1)} collective-permute-done((f32[2,2048]{1,0:T(2,128)S(1)}, f32[2,2048]{1,0:T(2,128)S(1)}, u32[]{:S(2)}, u32[]{:S(2)}) %collective-permute-start.29) | collective-permute-done | bytes 16416 | tf_op jit(solution)/shard_map/variance_9/ppermute | solution.py:107
  (101 shorter events, 31.7 us)
Async XLA Ops:
  2.1 36.3 %collective-permute-start.3 = (bf16[2048,256]{1,0:T(8,128)(2,1)S(1)}, bf16[2048,256]{1,0:T(8,128)(2,1)S(1)}, u32[]{:S(2)}, u32[]{:S(2)}) collective-permute-start(bf16[2048,256]{1,0:T(8,128)(2,1)S(1)} %dynamic-slice_bitcast_fusion), channel_id=1, source_target_pairs={{0,1},{1,0},{2,3},{3,2},{4,5},{5,4},{6,7},{7,6},{8,9},{9,8},{10,11... | collective-permute-start | bytes 3145736 | tf_op jit(solution)/shard_map/panel_swap/ppermute | solution.py:101
  2.6 37.5 %collective-permute-start = (bf16[256,2048]{1,0:T(8,128)(2,1)}, bf16[256,2048]{1,0:T(8,128)(2,1)S(1)}, u32[]{:S(2)}, u32[]{:S(2)}) collective-permute-start(bf16[256,2048]{1,0:T(8,128)(2,1)} %refs_0_.1), channel_id=1, source_target_pairs={{0,4},{2,6},{4,0},{6,2},{8,12},{10,14},{12,8},{14,10},{16,20},{18,... | collective-permute-start | bytes 3145736 | tf_op jit(solution)/shard_map/inv_y/ppermute | solution.py:107
  7.1 30.9 %collective-permute-start.8 = (bf16[192,2048]{1,0:T(8,128)(2,1)S(1)}, bf16[192,2048]{1,0:T(8,128)(2,1)S(1)}, u32[]{:S(2)}, u32[]{:S(2)}) collective-permute-start(bf16[192,2048]{1,0:T(8,128)(2,1)S(1)} %get-tuple-element.49), channel_id=1, source_target_pairs={{0,8},{2,10},{4,12},{6,14},{8,0},{10,2},{12,4},{14,6},{16,24},{18,... | collective-permute-start | bytes 2359304 | tf_op jit(solution)/shard_map/inv_z0/ppermute | solution.py:107
  8.8 31.3 %collective-permute-start.1 = (bf16[1024,256]{1,0:T(8,128)(2,1)S(1)}, bf16[1024,256]{1,0:T(8,128)(2,1)S(1)}, u32[]{:S(2)}, u32[]{:S(2)}) collective-permute-start(bf16[1024,256]{1,0:T(8,128)(2,1)S(1)} %get-tuple-element.42.f0), channel_id=1, source_target_pairs={{0,16},{2,18},{4,20},{6,22},{8,24},{10,26},{12,28},{14,30},{16,0},... | collective-permute-start | bytes 1572872 | tf_op jit(solution)/shard_map/first_z/ppermute | solution.py:107
  11.4 28.7 %collective-permute-start.2 = (bf16[1024,256]{1,0:T(8,128)(2,1)S(1)}, bf16[1024,256]{1,0:T(8,128)(2,1)S(1)}, u32[]{:S(2)}, u32[]{:S(2)}) collective-permute-start(bf16[1024,256]{1,0:T(8,128)(2,1)S(1)} %get-tuple-element.42.f0), channel_id=1, source_target_pairs={{0,2},{2,0},{4,6},{6,4},{8,10},{10,8},{12,14},{14,12},{16,18},{18,... | collective-permute-start | bytes 1572872 | tf_op jit(solution)/shard_map/first_x/ppermute | solution.py:107
  38.1 27.9 %collective-permute-start.9 = (bf16[192,2048]{1,0:T(8,128)(2,1)S(1)}, bf16[192,2048]{1,0:T(8,128)(2,1)S(1)}, u32[]{:S(2)}, u32[]{:S(2)}) collective-permute-start(bf16[192,2048]{1,0:T(8,128)(2,1)S(1)} %collective-permute-done.8.refs_2_), channel_id=1, source_target_pairs={{0,4},{2,6},{4,0},{6,2},{8,12},{10,14},{12,8},{14,10},{16,20},{18,... | collective-permute-start | bytes 2359304 | tf_op jit(solution)/shard_map/inv_yz0/ppermute | solution.py:107
  40.1 25.9 %collective-permute-start.4 = (bf16[2064,128]{1,0:T(8,128)(2,1)S(1)}, bf16[2064,128]{1,0:T(8,128)(2,1)S(1)}, u32[]{:S(2)}, u32[]{:S(2)}) collective-permute-start(bf16[2064,128]{1,0:T(8,128)(2,1)S(1)} %get-tuple-element.59.r0), channel_id=1, source_target_pairs={{0,16},{2,18},{4,20},{6,22},{8,24},{10,26},{12,28},{14,30},{16,0},... | collective-permute-start | bytes 1585160 | tf_op jit(solution)/shard_map/rest0_z/ppermute | solution.py:107
  42.0 23.9 %collective-permute-start.5 = (bf16[2064,128]{1,0:T(8,128)(2,1)S(1)}, bf16[2064,128]{1,0:T(8,128)(2,1)S(1)}, u32[]{:S(2)}, u32[]{:S(2)}) collective-permute-start(bf16[2064,128]{1,0:T(8,128)(2,1)S(1)} %get-tuple-element.59.r0), channel_id=1, source_target_pairs={{0,2},{2,0},{4,6},{6,4},{8,10},{10,8},{12,14},{14,12},{16,18},{18,... | collective-permute-start | bytes 1585160 | tf_op jit(solution)/shard_map/rest0_x/ppermute | solution.py:107
  43.5 22.4 %collective-permute-start.6 = (bf16[1024,256]{1,0:T(8,128)(2,1)S(1)}, bf16[1024,256]{1,0:T(8,128)(2,1)S(1)}, u32[]{:S(2)}, u32[]{:S(2)}) collective-permute-start(bf16[1024,256]{1,0:T(8,128)(2,1)S(1)} %collective-permute-done.1.f0), channel_id=1, source_target_pairs={{0,2},{2,0},{4,6},{6,4},{8,10},{10,8},{12,14},{14,12},{16,18},{18,... | collective-permute-start | bytes 1572872 | tf_op jit(solution)/shard_map/first_xz/ppermute | solution.py:107
  44.1 14.1 %collective-permute-start.7 = (bf16[64,2048]{1,0:T(8,128)(2,1)S(1)}, bf16[64,2048]{1,0:T(8,128)(2,1)S(1)}, u32[]{:S(2)}, u32[]{:S(2)}) collective-permute-start(bf16[64,2048]{1,0:T(8,128)(2,1)S(1)} %get-tuple-element.48), channel_id=1, source_target_pairs={{0,8},{2,10},{4,12},{6,14},{8,0},{10,2},{12,4},{14,6},{16,24},{18,... | collective-permute-start | bytes 786440 | tf_op jit(solution)/shard_map/inv_z1/ppermute | solution.py:107
  66.0 9.8 %collective-permute-start.11 = (bf16[704,2048]{1,0:T(8,128)(2,1)S(1)}, bf16[704,2048]{1,0:T(8,128)(2,1)S(1)}, u32[]{:S(2)}, u32[]{:S(2)}) collective-permute-start(bf16[704,2048]{1,0:T(8,128)(2,1)S(1)} %stack_rows.2.refs_0_), channel_id=1, source_target_pairs={{0,1},{1,0},{2,3},{3,2},{4,5},{5,4},{6,7},{7,6},{8,9},{9,8},{10,11... | collective-permute-start | bytes 8650760 | tf_op jit(solution)/shard_map/inv_swap/ppermute | solution.py:101
  66.2 8.8 %collective-permute-start.12 = (bf16[320,2048]{1,0:T(8,128)(2,1)S(1)}, bf16[320,2048]{1,0:T(8,128)(2,1)S(1)}, u32[]{:S(2)}, u32[]{:S(2)}) collective-permute-start(bf16[320,2048]{1,0:T(8,128)(2,1)S(1)} %stack_rows.3.refs_1_), channel_id=1, source_target_pairs={{0,1},{1,0},{2,3},{3,2},{4,5},{5,4},{6,7},{7,6},{8,9},{9,8},{10,11... | collective-permute-start | bytes 3932168 | tf_op jit(solution)/shard_map/inv_swap_more/ppermute | solution.py:101
  66.7 14.9 %collective-permute-start.14 = (bf16[2064,128]{1,0:T(8,128)(2,1)S(1)}, bf16[2064,128]{1,0:T(8,128)(2,1)S(1)}, u32[]{:S(2)}, u32[]{:S(2)}) collective-permute-start(bf16[2064,128]{1,0:T(8,128)(2,1)S(1)} %collective-permute-done.4.r0), channel_id=1, source_target_pairs={{0,2},{2,0},{4,6},{6,4},{8,10},{10,8},{12,14},{14,12},{16,18},{18,... | collective-permute-start | bytes 1585160 | tf_op jit(solution)/shard_map/rest0_xz/ppermute | solution.py:107
  68.2 26.1 %collective-permute-start.13 = (bf16[2048,128]{1,0:T(8,128)(2,1)}, bf16[2048,128]{1,0:T(8,128)(2,1)}, u32[]{:S(2)}, u32[]{:S(2)}) collective-permute-start(bf16[2048,128]{1,0:T(8,128)(2,1)} %get-tuple-element.63.r0), channel_id=1, source_target_pairs={{0,16},{2,18},{4,20},{6,22},{8,24},{10,26},{12,28},{14,30},{16,0},... | collective-permute-start | bytes 1572872 | tf_op jit(solution)/shard_map/rest1_z/ppermute | solution.py:107
  74.5 25.9 %collective-permute-start.16 = (bf16[2048,128]{1,0:T(8,128)(2,1)}, bf16[2048,128]{1,0:T(8,128)(2,1)}, u32[]{:S(2)}, u32[]{:S(2)}) collective-permute-start(bf16[2048,128]{1,0:T(8,128)(2,1)} %get-tuple-element.63.r0), channel_id=1, source_target_pairs={{0,2},{2,0},{4,6},{6,4},{8,10},{10,8},{12,14},{14,12},{16,18},{18,... | collective-permute-start | bytes 1572872 | tf_op jit(solution)/shard_map/rest1_x/ppermute | solution.py:107
  75.0 19.3 %collective-permute-start.18 = (f32[2,2048]{1,0:T(2,128)S(1)}, f32[2,2048]{1,0:T(2,128)S(1)}, u32[]{:S(2)}, u32[]{:S(2)}) collective-permute-start(f32[2,2048]{1,0:T(2,128)S(1)} %add.21), channel_id=1, source_target_pairs={{0,8},{2,10},{4,12},{6,14},{8,0},{10,2},{12,4},{14,6},{16,24},{18,... | collective-permute-start | bytes 49160 | tf_op jit(solution)/shard_map/squares_4/ppermute | solution.py:107
  85.8 9.1 %collective-permute-start.19 = (bf16[4,272,256]{2,1,0:T(8,128)(2,1)}, bf16[4,272,256]{2,1,0:T(8,128)(2,1)}, u32[]{:S(2)}, u32[]{:S(2)}) collective-permute-start(bf16[4,272,256]{2,1,0:T(8,128)(2,1)} %get-tuple-element.68), channel_id=1, source_target_pairs={{0,1},{1,0},{2,3},{3,2},{4,5},{5,4},{6,7},{7,6},{8,9},{9,8},{10,11... | collective-permute-start | bytes 1671176 | tf_op jit(solution)/shard_map/cross0_swap/ppermute | solution.py:101
  94.3 13.2 %collective-permute-start.15 = (bf16[2048,128]{1,0:T(8,128)(2,1)}, bf16[2048,128]{1,0:T(8,128)(2,1)}, u32[]{:S(2)}, u32[]{:S(2)}) collective-permute-start(bf16[2048,128]{1,0:T(8,128)(2,1)} %lead.3.r0), channel_id=1, source_target_pairs={{0,2},{2,0},{4,6},{6,4},{8,10},{10,8},{12,14},{14,12},{16,18},{18,... | collective-permute-start | bytes 1572872 | tf_op jit(solution)/shard_map/rest1_xz/ppermute | solution.py:107
  96.9 16.4 %collective-permute-start.20 = (bf16[2,272,256]{2,1,0:T(8,128)(2,1)}, bf16[2,272,256]{2,1,0:T(8,128)(2,1)S(1)}, u32[]{:S(2)}, u32[]{:S(2)}) collective-permute-start(bf16[2,272,256]{2,1,0:T(8,128)(2,1)} %get-tuple-element.70), channel_id=1, source_target_pairs={{0,12},{2,14},{4,8},{6,10},{8,4},{10,6},{12,0},{14,2},{16,28},{18,... | collective-permute-start | bytes 835592 | tf_op jit(solution)/shard_map/cross0_3/ppermute | solution.py:107
  97.3 16.0 %collective-permute-start.21 = (bf16[2,272,256]{2,1,0:T(8,128)(2,1)}, bf16[2,272,256]{2,1,0:T(8,128)(2,1)S(1)}, u32[]{:S(2)}, u32[]{:S(2)}) collective-permute-start(bf16[2,272,256]{2,1,0:T(8,128)(2,1)} %get-tuple-element.71), channel_id=1, source_target_pairs={{0,4},{2,6},{4,0},{6,2},{8,12},{10,14},{12,8},{14,10},{16,20},{18,... | collective-permute-start | bytes 835592 | tf_op jit(solution)/shard_map/cross0_1/ppermute | solution.py:107
  98.4 14.9 %collective-permute-start.22 = (bf16[2,272,256]{2,1,0:T(8,128)(2,1)}, bf16[2,272,256]{2,1,0:T(8,128)(2,1)S(1)}, u32[]{:S(2)}, u32[]{:S(2)}) collective-permute-start(bf16[2,272,256]{2,1,0:T(8,128)(2,1)} %get-tuple-element.72), channel_id=1, source_target_pairs={{0,8},{2,10},{4,12},{6,14},{8,0},{10,2},{12,4},{14,6},{16,24},{18,... | collective-permute-start | bytes 835592 | tf_op jit(solution)/shard_map/cross0_2/ppermute | solution.py:107
  117.9 10.5 %collective-permute-start.24 = (bf16[2,272,256]{2,1,0:T(8,128)(2,1)S(1)}, bf16[2,272,256]{2,1,0:T(8,128)(2,1)S(1)}, u32[]{:S(2)}, u32[]{:S(2)}) collective-permute-start(bf16[2,272,256]{2,1,0:T(8,128)(2,1)S(1)} %get-tuple-element.79), channel_id=1, source_target_pairs={{0,12},{2,14},{4,8},{6,10},{8,4},{10,6},{12,0},{14,2},{16,28},{18,... | collective-permute-start | bytes 835592 | tf_op jit(solution)/shard_map/cross1_3/ppermute | solution.py:107
  119.9 14.0 %collective-permute-start.25 = (bf16[2,272,256]{2,1,0:T(8,128)(2,1)S(1)}, bf16[2,272,256]{2,1,0:T(8,128)(2,1)S(1)}, u32[]{:S(2)}, u32[]{:S(2)}) collective-permute-start(bf16[2,272,256]{2,1,0:T(8,128)(2,1)S(1)} %get-tuple-element.80), channel_id=1, source_target_pairs={{0,4},{2,6},{4,0},{6,2},{8,12},{10,14},{12,8},{14,10},{16,20},{18,... | collective-permute-start | bytes 835592 | tf_op jit(solution)/shard_map/cross1_1/ppermute | solution.py:107
  120.4 13.6 %collective-permute-start.26 = (bf16[2,272,256]{2,1,0:T(8,128)(2,1)S(1)}, bf16[2,272,256]{2,1,0:T(8,128)(2,1)S(1)}, u32[]{:S(2)}, u32[]{:S(2)}) collective-permute-start(bf16[2,272,256]{2,1,0:T(8,128)(2,1)S(1)} %get-tuple-element.81), channel_id=1, source_target_pairs={{0,8},{2,10},{4,12},{6,14},{8,0},{10,2},{12,4},{14,6},{16,24},{18,... | collective-permute-start | bytes 835592 | tf_op jit(solution)/shard_map/cross1_2/ppermute | solution.py:107
  (27 other events, 230.0 us)

commit v13 on v12

--- a/solution.py
+++ b/solution.py
@@ -121,6 +121,7 @@
         in_specs=[ANY] * len(values),
         out_specs=[ANY] * len(values),
         input_output_aliases={i: i for i in range(len(values))},
+        compiler_params=pltpu.CompilerParams(vmem_limit_bytes=2 * MIB),
         cost_estimate=pl.CostEstimate(
             flops=int(micros * 1.15e9), bytes_accessed=0, transcendentals=0
         ),

time: 144 us -> 136 us (0.944)
  local copies, waits for them, and re-layouts: 10.7 us -> 2.72 us
  waiting for transfers between devices: 69.1 us -> 76.1 us
  Pallas kernels: 25.8 us -> 18.9 us
    unnamed x42 -> x10, local copies, waits for them, and re-layouts: 9.28 us -> 1.27 us
    ppermute x25, waiting for transfers between devices: 69.1 us -> 74.3 us  [hop(): return lax.ppermute(value, 'wide', [(i, i ^ mask) for i in range(size)])]
    pallas_call x4, Pallas kernels: 16.8 us -> 12.5 us  [products(): pl.pallas_call(body, out_shape=out if near is None else [out, out], in_sp...]
    pallas_call x2, Pallas kernels: 2.05 us -> 0.15 us  [bundle(): pl.pallas_call(body, out_shape=[shape] * NGRP, in_specs=[VMEM, VMEM], out...]
    ppermute x5, waiting for transfers between devices: 0.01 us -> 1.85 us  [swap_cores(): return lax.ppermute(value, 'narrow', [(0, 1), (1, 0)])]
  transfers between devices with their start and end apart: 30 -> 30, of which waited for: 10 -> 12; matrix products, arithmetic and copies ran while one was open for 0% -> 0% of each run, Pallas kernels for 18% -> 14%
where the time goes in v13:
time: 136 us
  waiting for transfers between devices  76.1 us (56%)
  starting transfers between devices  36.6 us (27%)
  Pallas kernels  18.9 us (14%)
  local copies, waits for them, and re-layouts  2.72 us (2%)
    ppermute x25, waiting for transfers between devices, hop(): return lax.ppermute(value, 'wide', [(i, i ^ mask) for i in range(size)])  74.3 us
    ppermute x25, starting transfers between devices, hop(): return lax.ppermute(value, 'wide', [(i, i ^ mask) for i in range(size)])  35.3 us
    pallas_call x4, Pallas kernels, products(): pl.pallas_call(body, out_shape=out if near is None else [out, out], in_sp...  12.5 us
  transfers between devices with their start and end apart: 30, of which 12 were waited for; matrix products, arithmetic and copies ran while one was open for 0% of the time, Pallas kernels for 14%

profile of v13, /device:TPU:0, one launch (start us, length us, event | category | flops | bytes accessed | tf_op | source)
XLA Modules:
  0.0 135.8 jit_solution(998387356433478734)
XLA Ops:
  2.6 2.6 %collective-permute-start = (bf16[256,2048]{1,0:T(8,128)(2,1)}, bf16[256,2048]{1,0:T(8,128)(2,1)S(1)}, u32[]{:S(2)}, u32[]{:S(2)}) collective-permute-start(bf16[256,2048]{1,0:T(8,128)(2,1)} %refs_0_.1), channel_id=1, source_target_pairs={{0,4},{2,6},{4,0},{6,2},{8,12},{10,14},{12,8},{14,10},{16,20},{18,... | collective-permute-start | bytes 3145736 | tf_op jit(solution)/shard_map/inv_y/ppermute | solution.py:107
  7.1 1.6 %collective-permute-start.8 = (bf16[192,2048]{1,0:T(8,128)(2,1)S(1)}, bf16[192,2048]{1,0:T(8,128)(2,1)S(1)}, u32[]{:S(2)}, u32[]{:S(2)}) collective-permute-start(bf16[192,2048]{1,0:T(8,128)(2,1)S(1)} %get-tuple-element.49), channel_id=1, source_target_pairs={{0,8},{2,10},{4,12},{6,14},{8,0},{10,2},{12,4},{14,6},{16,24},{18,... | collective-permute-start | bytes 2359304 | tf_op jit(solution)/shard_map/inv_z0/ppermute | solution.py:107
  8.8 2.6 %collective-permute-start.1 = (bf16[1024,256]{1,0:T(8,128)(2,1)S(1)}, bf16[1024,256]{1,0:T(8,128)(2,1)S(1)}, u32[]{:S(2)}, u32[]{:S(2)}) collective-permute-start(bf16[1024,256]{1,0:T(8,128)(2,1)S(1)} %get-tuple-element.42.f0), channel_id=1, source_target_pairs={{0,16},{2,18},{4,20},{6,22},{8,24},{10,26},{12,28},{14,30},{16,0},... | collective-permute-start | bytes 1572872 | tf_op jit(solution)/shard_map/first_z/ppermute | solution.py:107
  12.9 25.2 %collective-permute-done.8.refs_2_ = bf16[192,2048]{1,0:T(8,128)(2,1)S(1)} collective-permute-done((bf16[192,2048]{1,0:T(8,128)(2,1)S(1)}, bf16[192,2048]{1,0:T(8,128)(2,1)S(1)}, u32[]{:S(2)}, u32[]{:S(2)}) %collective-permute-start.8) | collective-permute-done | bytes 786464 | tf_op jit(solution)/shard_map/inv_z0/ppermute | solution.py:107
  39.4 1.9 %collective-permute-start.4 = (bf16[2064,128]{1,0:T(8,128)(2,1)S(1)}, bf16[2064,128]{1,0:T(8,128)(2,1)S(1)}, u32[]{:S(2)}, u32[]{:S(2)}) collective-permute-start(bf16[2064,128]{1,0:T(8,128)(2,1)S(1)} %get-tuple-element.59.r0), channel_id=1, source_target_pairs={{0,16},{2,18},{4,20},{6,22},{8,24},{10,26},{12,28},{14,30},{16,0},... | collective-permute-start | bytes 1585160 | tf_op jit(solution)/shard_map/rest0_z/ppermute | solution.py:107
  43.3 2.5 %collective-permute-start.7 = (bf16[64,2048]{1,0:T(8,128)(2,1)S(1)}, bf16[64,2048]{1,0:T(8,128)(2,1)S(1)}, u32[]{:S(2)}, u32[]{:S(2)}) collective-permute-start(bf16[64,2048]{1,0:T(8,128)(2,1)S(1)} %get-tuple-element.48), channel_id=1, source_target_pairs={{0,8},{2,10},{4,12},{6,14},{8,0},{10,2},{12,4},{14,6},{16,24},{18,... | collective-permute-start | bytes 786440 | tf_op jit(solution)/shard_map/inv_z1/ppermute | solution.py:107
  45.8 11.6 %collective-permute-done.7.refs_0_ = bf16[64,2048]{1,0:T(8,128)(2,1)S(1)} collective-permute-done((bf16[64,2048]{1,0:T(8,128)(2,1)S(1)}, bf16[64,2048]{1,0:T(8,128)(2,1)S(1)}, u32[]{:S(2)}, u32[]{:S(2)}) %collective-permute-start.7) | collective-permute-done | bytes 262176 | tf_op jit(solution)/shard_map/inv_z1/ppermute | solution.py:107
  59.2 6.1 %collective-permute-done.6.f1 = bf16[1024,256]{1,0:T(8,128)(2,1)S(1)} collective-permute-done((bf16[1024,256]{1,0:T(8,128)(2,1)S(1)}, bf16[1024,256]{1,0:T(8,128)(2,1)S(1)}, u32[]{:S(2)}, u32[]{:S(2)}) %collective-permute-start.6) | collective-permute-done | bytes 524320 | tf_op jit(solution)/shard_map/first_xz/ppermute | solution.py:107
  67.4 2.1 %collective-permute-start.13 = (bf16[2048,128]{1,0:T(8,128)(2,1)S(1)}, bf16[2048,128]{1,0:T(8,128)(2,1)S(1)}, u32[]{:S(2)}, u32[]{:S(2)}) collective-permute-start(bf16[2048,128]{1,0:T(8,128)(2,1)S(1)} %get-tuple-element.63.r0), channel_id=1, source_target_pairs={{0,16},{2,18},{4,20},{6,22},{8,24},{10,26},{12,28},{14,30},{16,0},... | collective-permute-start | bytes 1572872 | tf_op jit(solution)/shard_map/rest1_z/ppermute | solution.py:107
  71.5 2.2 %collective-permute-done.17 = f32[2,2048]{1,0:T(2,128)S(1)} collective-permute-done((f32[2,2048]{1,0:T(2,128)S(1)}, f32[2,2048]{1,0:T(2,128)S(1)}, u32[]{:S(2)}, u32[]{:S(2)}) %collective-permute-start.17) | collective-permute-done | bytes 16416 | tf_op jit(solution)/shard_map/squares_2/ppermute | solution.py:107
  75.1 1.8 %pack_inverse.1.sel_ref = bf16[4,256,3072]{2,1,0:T(8,128)(2,1)S(1)} custom-call(s32[2,12]{1,0:T(2,128)S(1)} %copy-done.4, bf16[704,2048]{1,0:T(8,128)(2,1)S(1)} %stack_rows.2.refs_0_, bf16[320,2048]{1,0:T(8,128)(2,1)S(1)} %stack_rows.3.refs_1_, bf16[704,2048]{1,0:T(8,128)(2,1)S(1)} %collective-permute-done.11.refs_2_, ...), custom_call_target="tpu_custom_call" | custom-call | tf_op jit(solution)/shard_map/pack_inverse/pallas_call | solution.py:249
  76.8 3.1 %products.4.refs_0_ = bf16[4,272,256]{2,1,0:T(8,128)(2,1)S(1)} custom-call(s32[2,12]{1,0:T(2,128)S(1)} %copy-done.4, bf16[4,256,3072]{2,1,0:T(8,128)(2,1)S(1)} %pack_inverse.1.sel_ref, bf16[1024,256]{1,0:T(8,128)(2,1)S(1)} %get-tuple-element.42.f0, bf16[1024,256]{1,0:T(8,128)(2,1)S(1)} %collective-permute-done.2.f1, ...), custom_call_target="tpu_custom_call" | custom-call | tf_op jit(solution)/shard_map/products/pallas_call | solution.py:348
  80.8 3.1 %products.5 = (bf16[4,272,256]{2,1,0:T(8,128)(2,1)S(1)}, bf16[4,272,256]{2,1,0:T(8,128)(2,1)S(1)}) custom-call(s32[2,12]{1,0:T(2,128)S(1)} %copy-done.4, bf16[4,256,3072]{2,1,0:T(8,128)(2,1)S(1)} %pack_inverse.1.sel_ref, bf16[1024,256]{1,0:T(8,128)(2,1)S(1)} %collective-permute-done.1.f0, bf16[1024,256]{1,0:T(8,128)(2,1)S(1)} %collective-permute-done.6.f1, ...), custom_call_target="tpu_custom_call" | custom-call | tf_op jit(solution)/shard_map/products/pallas_call | solution.py:348
  84.0 9.2 %collective-permute-done.13.refs_0_ = bf16[2048,128]{1,0:T(8,128)(2,1)S(1)} collective-permute-done((bf16[2048,128]{1,0:T(8,128)(2,1)S(1)}, bf16[2048,128]{1,0:T(8,128)(2,1)S(1)}, u32[]{:S(2)}, u32[]{:S(2)}) %collective-permute-start.13) | collective-permute-done | bytes 524320 | tf_op jit(solution)/shard_map/rest1_z/ppermute | solution.py:107
  95.6 1.9 %collective-permute-start.22 = (bf16[2,272,256]{2,1,0:T(8,128)(2,1)S(1)}, bf16[2,272,256]{2,1,0:T(8,128)(2,1)S(1)}, u32[]{:S(2)}, u32[]{:S(2)}) collective-permute-start(bf16[2,272,256]{2,1,0:T(8,128)(2,1)S(1)} %get-tuple-element.72), channel_id=1, source_target_pairs={{0,8},{2,10},{4,12},{6,14},{8,0},{10,2},{12,4},{14,6},{16,24},{18,... | collective-permute-start | bytes 835592 | tf_op jit(solution)/shard_map/cross0_2/ppermute | solution.py:107
  97.5 3.2 %products.6.refs_0_ = bf16[4,272,256]{2,1,0:T(8,128)(2,1)S(1)} custom-call(s32[2,12]{1,0:T(2,128)S(1)} %copy-done.4, bf16[4,256,3072]{2,1,0:T(8,128)(2,1)S(1)} %pack_inverse.1.sel_ref, bf16[1024,256]{1,0:T(8,128)(2,1)S(1)} %get-tuple-element.42.f0, bf16[1024,256]{1,0:T(8,128)(2,1)S(1)} %collective-permute-done.2.f1, ...), custom_call_target="tpu_custom_call" | custom-call | tf_op jit(solution)/shard_map/products/pallas_call | solution.py:348
  100.7 5.3 %collective-permute-done.15.r1 = bf16[2048,128]{1,0:T(8,128)(2,1)S(1)} collective-permute-done((bf16[2048,128]{1,0:T(8,128)(2,1)S(1)}, bf16[2048,128]{1,0:T(8,128)(2,1)S(1)}, u32[]{:S(2)}, u32[]{:S(2)}) %collective-permute-start.15) | collective-permute-done | bytes 524320 | tf_op jit(solution)/shard_map/rest1_xz/ppermute | solution.py:107
  106.0 3.1 %products.7 = (bf16[4,272,256]{2,1,0:T(8,128)(2,1)S(1)}, bf16[4,272,256]{2,1,0:T(8,128)(2,1)S(1)}) custom-call(s32[2,12]{1,0:T(2,128)S(1)} %copy-done.4, bf16[4,256,3072]{2,1,0:T(8,128)(2,1)S(1)} %pack_inverse.1.sel_ref, bf16[1024,256]{1,0:T(8,128)(2,1)S(1)} %collective-permute-done.1.f0, bf16[1024,256]{1,0:T(8,128)(2,1)S(1)} %collective-permute-done.6.f1, ...), custom_call_target="tpu_custom_call" | custom-call | tf_op jit(solution)/shard_map/products/pallas_call | solution.py:348
  109.3 1.8 %collective-permute-done.23.their_ref = bf16[4,272,256]{2,1,0:T(8,128)(2,1)S(1)} collective-permute-done((bf16[4,272,256]{2,1,0:T(8,128)(2,1)S(1)}, bf16[4,272,256]{2,1,0:T(8,128)(2,1)S(1)}, u32[]{:S(2)}, u32[]{:S(2)}) %collective-permute-start.23) | collective-permute-done | bytes 557088 | tf_op jit(solution)/shard_map/cross1_swap/ppermute | solution.py:101
  112.9 1.9 %collective-permute-start.26 = (bf16[2,272,256]{2,1,0:T(8,128)(2,1)S(1)}, bf16[2,272,256]{2,1,0:T(8,128)(2,1)S(1)}, u32[]{:S(2)}, u32[]{:S(2)}) collective-permute-start(bf16[2,272,256]{2,1,0:T(8,128)(2,1)S(1)} %get-tuple-element.81), channel_id=1, source_target_pairs={{0,8},{2,10},{4,12},{6,14},{8,0},{10,2},{12,4},{14,6},{16,24},{18,... | collective-permute-start | bytes 835592 | tf_op jit(solution)/shard_map/cross1_2/ppermute | solution.py:107
  114.8 7.0 %collective-permute-done.24.refs_1_ = bf16[2,272,256]{2,1,0:T(8,128)(2,1)S(1)} collective-permute-done((bf16[2,272,256]{2,1,0:T(8,128)(2,1)S(1)}, bf16[2,272,256]{2,1,0:T(8,128)(2,1)S(1)}, u32[]{:S(2)}, u32[]{:S(2)}) %collective-permute-start.24) | collective-permute-done | bytes 278560 | tf_op jit(solution)/shard_map/cross1_3/ppermute | solution.py:107
  121.8 4.7 %collective-permute-done.25.refs_2_ = bf16[2,272,256]{2,1,0:T(8,128)(2,1)S(1)} collective-permute-done((bf16[2,272,256]{2,1,0:T(8,128)(2,1)S(1)}, bf16[2,272,256]{2,1,0:T(8,128)(2,1)S(1)}, u32[]{:S(2)}, u32[]{:S(2)}) %collective-permute-start.25) | collective-permute-done | bytes 278560 | tf_op jit(solution)/shard_map/cross1_1/ppermute | solution.py:107
  127.9 1.7 %collective-permute-start.28 = (f32[2,2048]{1,0:T(2,128)S(1)}, f32[2,2048]{1,0:T(2,128)S(1)}, u32[]{:S(2)}, u32[]{:S(2)}) collective-permute-start(f32[2,2048]{1,0:T(2,128)S(1)} %add_sums.3), channel_id=1, source_target_pairs={{0,16},{2,18},{4,20},{6,22},{8,24},{10,26},{12,28},{14,30},{16,0},... | collective-permute-start | bytes 49160 | tf_op jit(solution)/shard_map/variance_8/ppermute | solution.py:107
  129.6 1.9 %collective-permute-start.29 = (f32[2,2048]{1,0:T(2,128)S(1)}, f32[2,2048]{1,0:T(2,128)S(1)}, u32[]{:S(2)}, u32[]{:S(2)}) collective-permute-start(f32[2,2048]{1,0:T(2,128)S(1)} %add_sums.3), channel_id=1, source_target_pairs={{0,18},{2,16},{4,22},{6,20},{8,26},{10,24},{12,30},{14,28},{16,2},... | collective-permute-start | bytes 49160 | tf_op jit(solution)/shard_map/variance_9/ppermute | solution.py:107
  (69 shorter events, 26.8 us)
Async XLA Ops:
  2.1 36.3 %collective-permute-start.3 = (bf16[2048,256]{1,0:T(8,128)(2,1)S(1)}, bf16[2048,256]{1,0:T(8,128)(2,1)S(1)}, u32[]{:S(2)}, u32[]{:S(2)}) collective-permute-start(bf16[2048,256]{1,0:T(8,128)(2,1)S(1)} %dynamic-slice_bitcast_fusion), channel_id=1, source_target_pairs={{0,1},{1,0},{2,3},{3,2},{4,5},{5,4},{6,7},{7,6},{8,9},{9,8},{10,11... | collective-permute-start | bytes 3145736 | tf_op jit(solution)/shard_map/panel_swap/ppermute | solution.py:101
  2.6 36.7 %collective-permute-start = (bf16[256,2048]{1,0:T(8,128)(2,1)}, bf16[256,2048]{1,0:T(8,128)(2,1)S(1)}, u32[]{:S(2)}, u32[]{:S(2)}) collective-permute-start(bf16[256,2048]{1,0:T(8,128)(2,1)} %refs_0_.1), channel_id=1, source_target_pairs={{0,4},{2,6},{4,0},{6,2},{8,12},{10,14},{12,8},{14,10},{16,20},{18,... | collective-permute-start | bytes 3145736 | tf_op jit(solution)/shard_map/inv_y/ppermute | solution.py:107
  7.1 30.9 %collective-permute-start.8 = (bf16[192,2048]{1,0:T(8,128)(2,1)S(1)}, bf16[192,2048]{1,0:T(8,128)(2,1)S(1)}, u32[]{:S(2)}, u32[]{:S(2)}) collective-permute-start(bf16[192,2048]{1,0:T(8,128)(2,1)S(1)} %get-tuple-element.49), channel_id=1, source_target_pairs={{0,8},{2,10},{4,12},{6,14},{8,0},{10,2},{12,4},{14,6},{16,24},{18,... | collective-permute-start | bytes 2359304 | tf_op jit(solution)/shard_map/inv_z0/ppermute | solution.py:107
  8.8 30.5 %collective-permute-start.1 = (bf16[1024,256]{1,0:T(8,128)(2,1)S(1)}, bf16[1024,256]{1,0:T(8,128)(2,1)S(1)}, u32[]{:S(2)}, u32[]{:S(2)}) collective-permute-start(bf16[1024,256]{1,0:T(8,128)(2,1)S(1)} %get-tuple-element.42.f0), channel_id=1, source_target_pairs={{0,16},{2,18},{4,20},{6,22},{8,24},{10,26},{12,28},{14,30},{16,0},... | collective-permute-start | bytes 1572872 | tf_op jit(solution)/shard_map/first_z/ppermute | solution.py:107
  11.4 28.0 %collective-permute-start.2 = (bf16[1024,256]{1,0:T(8,128)(2,1)S(1)}, bf16[1024,256]{1,0:T(8,128)(2,1)S(1)}, u32[]{:S(2)}, u32[]{:S(2)}) collective-permute-start(bf16[1024,256]{1,0:T(8,128)(2,1)S(1)} %get-tuple-element.42.f0), channel_id=1, source_target_pairs={{0,2},{2,0},{4,6},{6,4},{8,10},{10,8},{12,14},{14,12},{16,18},{18,... | collective-permute-start | bytes 1572872 | tf_op jit(solution)/shard_map/first_x/ppermute | solution.py:107
  38.1 27.2 %collective-permute-start.9 = (bf16[192,2048]{1,0:T(8,128)(2,1)S(1)}, bf16[192,2048]{1,0:T(8,128)(2,1)S(1)}, u32[]{:S(2)}, u32[]{:S(2)}) collective-permute-start(bf16[192,2048]{1,0:T(8,128)(2,1)S(1)} %collective-permute-done.8.refs_2_), channel_id=1, source_target_pairs={{0,4},{2,6},{4,0},{6,2},{8,12},{10,14},{12,8},{14,10},{16,20},{18,... | collective-permute-start | bytes 2359304 | tf_op jit(solution)/shard_map/inv_yz0/ppermute | solution.py:107
  39.4 25.9 %collective-permute-start.4 = (bf16[2064,128]{1,0:T(8,128)(2,1)S(1)}, bf16[2064,128]{1,0:T(8,128)(2,1)S(1)}, u32[]{:S(2)}, u32[]{:S(2)}) collective-permute-start(bf16[2064,128]{1,0:T(8,128)(2,1)S(1)} %get-tuple-element.59.r0), channel_id=1, source_target_pairs={{0,16},{2,18},{4,20},{6,22},{8,24},{10,26},{12,28},{14,30},{16,0},... | collective-permute-start | bytes 1585160 | tf_op jit(solution)/shard_map/rest0_z/ppermute | solution.py:107
  41.3 23.9 %collective-permute-start.5 = (bf16[2064,128]{1,0:T(8,128)(2,1)S(1)}, bf16[2064,128]{1,0:T(8,128)(2,1)S(1)}, u32[]{:S(2)}, u32[]{:S(2)}) collective-permute-start(bf16[2064,128]{1,0:T(8,128)(2,1)S(1)} %get-tuple-element.59.r0), channel_id=1, source_target_pairs={{0,2},{2,0},{4,6},{6,4},{8,10},{10,8},{12,14},{14,12},{16,18},{18,... | collective-permute-start | bytes 1585160 | tf_op jit(solution)/shard_map/rest0_x/ppermute | solution.py:107
  42.8 22.4 %collective-permute-start.6 = (bf16[1024,256]{1,0:T(8,128)(2,1)S(1)}, bf16[1024,256]{1,0:T(8,128)(2,1)S(1)}, u32[]{:S(2)}, u32[]{:S(2)}) collective-permute-start(bf16[1024,256]{1,0:T(8,128)(2,1)S(1)} %collective-permute-done.1.f0), channel_id=1, source_target_pairs={{0,2},{2,0},{4,6},{6,4},{8,10},{10,8},{12,14},{14,12},{16,18},{18,... | collective-permute-start | bytes 1572872 | tf_op jit(solution)/shard_map/first_xz/ppermute | solution.py:107
  43.3 14.1 %collective-permute-start.7 = (bf16[64,2048]{1,0:T(8,128)(2,1)S(1)}, bf16[64,2048]{1,0:T(8,128)(2,1)S(1)}, u32[]{:S(2)}, u32[]{:S(2)}) collective-permute-start(bf16[64,2048]{1,0:T(8,128)(2,1)S(1)} %get-tuple-element.48), channel_id=1, source_target_pairs={{0,8},{2,10},{4,12},{6,14},{8,0},{10,2},{12,4},{14,6},{16,24},{18,... | collective-permute-start | bytes 786440 | tf_op jit(solution)/shard_map/inv_z1/ppermute | solution.py:107
  65.2 9.8 %collective-permute-start.11 = (bf16[704,2048]{1,0:T(8,128)(2,1)S(1)}, bf16[704,2048]{1,0:T(8,128)(2,1)S(1)}, u32[]{:S(2)}, u32[]{:S(2)}) collective-permute-start(bf16[704,2048]{1,0:T(8,128)(2,1)S(1)} %stack_rows.2.refs_0_), channel_id=1, source_target_pairs={{0,1},{1,0},{2,3},{3,2},{4,5},{5,4},{6,7},{7,6},{8,9},{9,8},{10,11... | collective-permute-start | bytes 8650760 | tf_op jit(solution)/shard_map/inv_swap/ppermute | solution.py:101
  65.4 8.9 %collective-permute-start.12 = (bf16[320,2048]{1,0:T(8,128)(2,1)S(1)}, bf16[320,2048]{1,0:T(8,128)(2,1)S(1)}, u32[]{:S(2)}, u32[]{:S(2)}) collective-permute-start(bf16[320,2048]{1,0:T(8,128)(2,1)S(1)} %stack_rows.3.refs_1_), channel_id=1, source_target_pairs={{0,1},{1,0},{2,3},{3,2},{4,5},{5,4},{6,7},{7,6},{8,9},{9,8},{10,11... | collective-permute-start | bytes 3932168 | tf_op jit(solution)/shard_map/inv_swap_more/ppermute | solution.py:101
  66.0 14.9 %collective-permute-start.14 = (bf16[2064,128]{1,0:T(8,128)(2,1)S(1)}, bf16[2064,128]{1,0:T(8,128)(2,1)S(1)}, u32[]{:S(2)}, u32[]{:S(2)}) collective-permute-start(bf16[2064,128]{1,0:T(8,128)(2,1)S(1)} %collective-permute-done.4.r0), channel_id=1, source_target_pairs={{0,2},{2,0},{4,6},{6,4},{8,10},{10,8},{12,14},{14,12},{16,18},{18,... | collective-permute-start | bytes 1585160 | tf_op jit(solution)/shard_map/rest0_xz/ppermute | solution.py:107
  67.4 25.8 %collective-permute-start.13 = (bf16[2048,128]{1,0:T(8,128)(2,1)S(1)}, bf16[2048,128]{1,0:T(8,128)(2,1)S(1)}, u32[]{:S(2)}, u32[]{:S(2)}) collective-permute-start(bf16[2048,128]{1,0:T(8,128)(2,1)S(1)} %get-tuple-element.63.r0), channel_id=1, source_target_pairs={{0,16},{2,18},{4,20},{6,22},{8,24},{10,26},{12,28},{14,30},{16,0},... | collective-permute-start | bytes 1572872 | tf_op jit(solution)/shard_map/rest1_z/ppermute | solution.py:107
  73.7 23.8 %collective-permute-start.16 = (bf16[2048,128]{1,0:T(8,128)(2,1)S(1)}, bf16[2048,128]{1,0:T(8,128)(2,1)S(1)}, u32[]{:S(2)}, u32[]{:S(2)}) collective-permute-start(bf16[2048,128]{1,0:T(8,128)(2,1)S(1)} %get-tuple-element.63.r0), channel_id=1, source_target_pairs={{0,2},{2,0},{4,6},{6,4},{8,10},{10,8},{12,14},{14,12},{16,18},{18,... | collective-permute-start | bytes 1572872 | tf_op jit(solution)/shard_map/rest1_x/ppermute | solution.py:107
  74.3 19.0 %collective-permute-start.18 = (f32[2,2048]{1,0:T(2,128)S(1)}, f32[2,2048]{1,0:T(2,128)S(1)}, u32[]{:S(2)}, u32[]{:S(2)}) collective-permute-start(f32[2,2048]{1,0:T(2,128)S(1)} %add.21), channel_id=1, source_target_pairs={{0,8},{2,10},{4,12},{6,14},{8,0},{10,2},{12,4},{14,6},{16,24},{18,... | collective-permute-start | bytes 49160 | tf_op jit(solution)/shard_map/squares_4/ppermute | solution.py:107
  83.9 9.9 %collective-permute-start.19 = (bf16[4,272,256]{2,1,0:T(8,128)(2,1)S(1)}, bf16[4,272,256]{2,1,0:T(8,128)(2,1)S(1)}, u32[]{:S(2)}, u32[]{:S(2)}) collective-permute-start(bf16[4,272,256]{2,1,0:T(8,128)(2,1)S(1)} %get-tuple-element.68), channel_id=1, source_target_pairs={{0,1},{1,0},{2,3},{3,2},{4,5},{5,4},{6,7},{7,6},{8,9},{9,8},{10,11... | collective-permute-start | bytes 1671176 | tf_op jit(solution)/shard_map/cross0_swap/ppermute | solution.py:101
  93.2 12.8 %collective-permute-start.15 = (bf16[2048,128]{1,0:T(8,128)(2,1)S(1)}, bf16[2048,128]{1,0:T(8,128)(2,1)S(1)}, u32[]{:S(2)}, u32[]{:S(2)}) collective-permute-start(bf16[2048,128]{1,0:T(8,128)(2,1)S(1)} %lead.3.r0), channel_id=1, source_target_pairs={{0,2},{2,0},{4,6},{6,4},{8,10},{10,8},{12,14},{14,12},{16,18},{18,... | collective-permute-start | bytes 1572872 | tf_op jit(solution)/shard_map/rest1_xz/ppermute | solution.py:107
  93.9 15.3 %collective-permute-start.20 = (bf16[2,272,256]{2,1,0:T(8,128)(2,1)S(1)}, bf16[2,272,256]{2,1,0:T(8,128)(2,1)S(1)}, u32[]{:S(2)}, u32[]{:S(2)}) collective-permute-start(bf16[2,272,256]{2,1,0:T(8,128)(2,1)S(1)} %get-tuple-element.70), channel_id=1, source_target_pairs={{0,12},{2,14},{4,8},{6,10},{8,4},{10,6},{12,0},{14,2},{16,28},{18,... | collective-permute-start | bytes 835592 | tf_op jit(solution)/shard_map/cross0_3/ppermute | solution.py:107
  94.4 14.9 %collective-permute-start.21 = (bf16[2,272,256]{2,1,0:T(8,128)(2,1)S(1)}, bf16[2,272,256]{2,1,0:T(8,128)(2,1)S(1)}, u32[]{:S(2)}, u32[]{:S(2)}) collective-permute-start(bf16[2,272,256]{2,1,0:T(8,128)(2,1)S(1)} %get-tuple-element.71), channel_id=1, source_target_pairs={{0,4},{2,6},{4,0},{6,2},{8,12},{10,14},{12,8},{14,10},{16,20},{18,... | collective-permute-start | bytes 835592 | tf_op jit(solution)/shard_map/cross0_1/ppermute | solution.py:107
  95.6 13.7 %collective-permute-start.22 = (bf16[2,272,256]{2,1,0:T(8,128)(2,1)S(1)}, bf16[2,272,256]{2,1,0:T(8,128)(2,1)S(1)}, u32[]{:S(2)}, u32[]{:S(2)}) collective-permute-start(bf16[2,272,256]{2,1,0:T(8,128)(2,1)S(1)} %get-tuple-element.72), channel_id=1, source_target_pairs={{0,8},{2,10},{4,12},{6,14},{8,0},{10,2},{12,4},{14,6},{16,24},{18,... | collective-permute-start | bytes 835592 | tf_op jit(solution)/shard_map/cross0_2/ppermute | solution.py:107
  111.3 10.5 %collective-permute-start.24 = (bf16[2,272,256]{2,1,0:T(8,128)(2,1)S(1)}, bf16[2,272,256]{2,1,0:T(8,128)(2,1)S(1)}, u32[]{:S(2)}, u32[]{:S(2)}) collective-permute-start(bf16[2,272,256]{2,1,0:T(8,128)(2,1)S(1)} %get-tuple-element.79), channel_id=1, source_target_pairs={{0,12},{2,14},{4,8},{6,10},{8,4},{10,6},{12,0},{14,2},{16,28},{18,... | collective-permute-start | bytes 835592 | tf_op jit(solution)/shard_map/cross1_3/ppermute | solution.py:107
  112.1 14.4 %collective-permute-start.25 = (bf16[2,272,256]{2,1,0:T(8,128)(2,1)S(1)}, bf16[2,272,256]{2,1,0:T(8,128)(2,1)S(1)}, u32[]{:S(2)}, u32[]{:S(2)}) collective-permute-start(bf16[2,272,256]{2,1,0:T(8,128)(2,1)S(1)} %get-tuple-element.80), channel_id=1, source_target_pairs={{0,4},{2,6},{4,0},{6,2},{8,12},{10,14},{12,8},{14,10},{16,20},{18,... | collective-permute-start | bytes 835592 | tf_op jit(solution)/shard_map/cross1_1/ppermute | solution.py:107
  112.9 14.1 %collective-permute-start.26 = (bf16[2,272,256]{2,1,0:T(8,128)(2,1)S(1)}, bf16[2,272,256]{2,1,0:T(8,128)(2,1)S(1)}, u32[]{:S(2)}, u32[]{:S(2)}) collective-permute-start(bf16[2,272,256]{2,1,0:T(8,128)(2,1)S(1)} %get-tuple-element.81), channel_id=1, source_target_pairs={{0,8},{2,10},{4,12},{6,14},{8,0},{10,2},{12,4},{14,6},{16,24},{18,... | collective-permute-start | bytes 835592 | tf_op jit(solution)/shard_map/cross1_2/ppermute | solution.py:107
  (11 other events, 104.2 us)

commit v14 on v13

--- a/solution.py
+++ b/solution.py
@@ -314,7 +314,7 @@
                         weigh((r0, r1)[dx][pl.ds(at, BLK), :])
 
                     at = pl.multiple_of(slot * LANES, LANES)
-                    result[d, pl.ds(at, LANES), :] = (-part).T.astype(result.dtype)
+                    result[d, pl.ds(at, LANES), :] = (-part).astype(result.dtype).T
 
         for slot in range(2):
             left, terms = total[slot], []
@@ -485,7 +485,7 @@
     other = swap_cores(lax.dynamic_index_in_dim(panel, 1 - n, 0, keepdims=False), "panel_swap")
     r_own = pack_rest(structure, panel, other, first)
     linv = squares(factor_inv)
-    f_z = hop(f_own, ZH, "first_z")
+    f_z = lead([hop(f_own, ZH, "first_z")], 10)[0]
     f_x = hop(f_own, X, "first_x")
     a_z0 = hop(top, ZL, "inv_z0")
     a_y = hop(inverse, Y, "inv_y")

time: 136 us -> 136 us (level)
  Pallas kernels: 18.9 us -> 23.7 us
  waiting for transfers between devices: 76.1 us -> 72 us
    ppermute x25, waiting for transfers between devices: 74.3 us -> 70.2 us  [hop(): return lax.ppermute(value, 'wide', [(i, i ^ mask) for i in range(size)])]
    pallas_call x2, Pallas kernels: 0.27 us -> 2.04 us  [stack_rows(): pl.pallas_call(body, out_shape=jax.ShapeDtypeStruct((rows, pieces[0].shap...]
    pallas_call x1, Pallas kernels: 0.65 us -> 2.35 us  [pack_first(): pl.pallas_call(body, out_shape=[jax.ShapeDtypeStruct((first * BLK, panel....]
    pallas_call x4, Pallas kernels: 12.5 us -> 13.9 us  [products(): pl.pallas_call(body, out_shape=out if near is None else [out, out], in_sp...]
    squeeze x1, local copies, waits for them, and re-layouts: 1.44 us -> 0.07 us  [per_device_grid(): lax.dynamic_index_in_dim(panel, 1 - n, 0, keepdims=False)]
  transfers between devices with their start and end apart: 30 -> 30, of which waited for: 12 -> 12; matrix products, arithmetic and copies ran while one was open for 0% -> 0% of each run, Pallas kernels for 14% -> 16%
where the time goes in v14:
time: 136 us
  waiting for transfers between devices  72 us (53%)
  starting transfers between devices  36.5 us (27%)
  Pallas kernels  23.7 us (17%)
  local copies, waits for them, and re-layouts  2.35 us (2%)
    ppermute x25, waiting for transfers between devices, hop(): return lax.ppermute(value, 'wide', [(i, i ^ mask) for i in range(size)])  70.2 us
    ppermute x25, starting transfers between devices, hop(): return lax.ppermute(value, 'wide', [(i, i ^ mask) for i in range(size)])  35.7 us
    pallas_call x4, Pallas kernels, products(): pl.pallas_call(body, out_shape=out if near is None else [out, out], in_sp...  13.9 us
  transfers between devices with their start and end apart: 30, of which 12 were waited for; matrix products, arithmetic and copies ran while one was open for 0% of the time, Pallas kernels for 16%

profile of v14, /device:TPU:0, one launch (start us, length us, event | category | flops | bytes accessed | tf_op | source)
XLA Modules:
  0.0 136.1 jit_solution(6611579892018602643)
XLA Ops:
  2.9 2.3 %pack_first.1 = (bf16[1024,256]{1,0:T(8,128)(2,1)S(1)}, bf16[192,2048]{1,0:T(8,128)(2,1)}, bf16[64,2048]{1,0:T(8,128)(2,1)S(1)}) custom-call(s32[2,12]{1,0:T(2,128)S(1)} %copy-done.3, bf16[2,2048,256]{2,1,0:T(8,128)(2,1)S(1)} %copy-done, bf16[256,2048]{1,0:T(8,128)(2,1)} %refs_0_.1), custom_call_target="tpu_custom_call" | custom-call | tf_op jit(solution)/shard_map/pack_first/pallas_call | solution.py:150
  5.3 3.0 %collective-permute-start.8 = (bf16[192,2048]{1,0:T(8,128)(2,1)}, bf16[192,2048]{1,0:T(8,128)(2,1)}, u32[]{:S(2)}, u32[]{:S(2)}) collective-permute-start(bf16[192,2048]{1,0:T(8,128)(2,1)} %get-tuple-element.49), channel_id=1, source_target_pairs={{0,8},{2,10},{4,12},{6,14},{8,0},{10,2},{12,4},{14,6},{16,24},{18,... | collective-permute-start | bytes 2359304 | tf_op jit(solution)/shard_map/inv_z0/ppermute | solution.py:107
  8.3 2.6 %collective-permute-start.1 = (bf16[1024,256]{1,0:T(8,128)(2,1)S(1)}, bf16[1024,256]{1,0:T(8,128)(2,1)}, u32[]{:S(2)}, u32[]{:S(2)}) collective-permute-start(bf16[1024,256]{1,0:T(8,128)(2,1)S(1)} %get-tuple-element.42.f0), channel_id=1, source_target_pairs={{0,16},{2,18},{4,20},{6,22},{8,24},{10,26},{12,28},{14,30},{16,0},... | collective-permute-start | bytes 1572872 | tf_op jit(solution)/shard_map/first_z/ppermute | solution.py:107
  14.0 23.3 %collective-permute-done.8.refs_2_ = bf16[192,2048]{1,0:T(8,128)(2,1)} collective-permute-done((bf16[192,2048]{1,0:T(8,128)(2,1)}, bf16[192,2048]{1,0:T(8,128)(2,1)}, u32[]{:S(2)}, u32[]{:S(2)}) %collective-permute-start.8) | collective-permute-done | bytes 786464 | tf_op jit(solution)/shard_map/inv_z0/ppermute | solution.py:107
  43.8 2.5 %collective-permute-start.7 = (bf16[64,2048]{1,0:T(8,128)(2,1)S(1)}, bf16[64,2048]{1,0:T(8,128)(2,1)S(1)}, u32[]{:S(2)}, u32[]{:S(2)}) collective-permute-start(bf16[64,2048]{1,0:T(8,128)(2,1)S(1)} %get-tuple-element.48), channel_id=1, source_target_pairs={{0,8},{2,10},{4,12},{6,14},{8,0},{10,2},{12,4},{14,6},{16,24},{18,... | collective-permute-start | bytes 786440 | tf_op jit(solution)/shard_map/inv_z1/ppermute | solution.py:107
  46.3 11.4 %collective-permute-done.7.refs_0_ = bf16[64,2048]{1,0:T(8,128)(2,1)S(1)} collective-permute-done((bf16[64,2048]{1,0:T(8,128)(2,1)S(1)}, bf16[64,2048]{1,0:T(8,128)(2,1)S(1)}, u32[]{:S(2)}, u32[]{:S(2)}) %collective-permute-start.7) | collective-permute-done | bytes 262176 | tf_op jit(solution)/shard_map/inv_z1/ppermute | solution.py:107
  58.6 1.9 %stack_rows.2.refs_0_ = bf16[704,2048]{1,0:T(8,128)(2,1)S(1)} custom-call(bf16[256,2048]{1,0:T(8,128)(2,1)} %refs_0_.1, bf16[256,2048]{1,0:T(8,128)(2,1)} %collective-permute-done.refs_1_, bf16[192,2048]{1,0:T(8,128)(2,1)} %collective-permute-done.8.refs_2_), custom_call_target="tpu_custom_call" | custom-call | tf_op jit(solution)/shard_map/stack_rows/pallas_call | solution.py:210
  60.6 4.9 %collective-permute-done.6.f1 = bf16[1024,256]{1,0:T(8,128)(2,1)S(1)} collective-permute-done((bf16[1024,256]{1,0:T(8,128)(2,1)}, bf16[1024,256]{1,0:T(8,128)(2,1)S(1)}, u32[]{:S(2)}, u32[]{:S(2)}) %collective-permute-start.6) | collective-permute-done | bytes 524320 | tf_op jit(solution)/shard_map/first_xz/ppermute | solution.py:107
  67.7 1.9 %collective-permute-start.13 = (bf16[2048,128]{1,0:T(8,128)(2,1)S(1)}, bf16[2048,128]{1,0:T(8,128)(2,1)S(1)}, u32[]{:S(2)}, u32[]{:S(2)}) collective-permute-start(bf16[2048,128]{1,0:T(8,128)(2,1)S(1)} %get-tuple-element.63.r0), channel_id=1, source_target_pairs={{0,16},{2,18},{4,20},{6,22},{8,24},{10,26},{12,28},{14,30},{16,0},... | collective-permute-start | bytes 1572872 | tf_op jit(solution)/shard_map/rest1_z/ppermute | solution.py:107
  71.1 2.7 %collective-permute-done.17 = f32[2,2048]{1,0:T(2,128)S(1)} collective-permute-done((f32[2,2048]{1,0:T(2,128)S(1)}, f32[2,2048]{1,0:T(2,128)S(1)}, u32[]{:S(2)}, u32[]{:S(2)}) %collective-permute-start.17) | collective-permute-done | bytes 16416 | tf_op jit(solution)/shard_map/squares_2/ppermute | solution.py:107
  75.3 1.8 %pack_inverse.1.sel_ref = bf16[4,256,3072]{2,1,0:T(8,128)(2,1)S(1)} custom-call(s32[2,12]{1,0:T(2,128)S(1)} %copy-done.4, bf16[704,2048]{1,0:T(8,128)(2,1)S(1)} %stack_rows.2.refs_0_, bf16[320,2048]{1,0:T(8,128)(2,1)S(1)} %stack_rows.3.refs_1_, bf16[704,2048]{1,0:T(8,128)(2,1)S(1)} %collective-permute-done.11.refs_2_, ...), custom_call_target="tpu_custom_call" | custom-call | tf_op jit(solution)/shard_map/pack_inverse/pallas_call | solution.py:249
  77.1 3.2 %products.4.refs_0_ = bf16[4,272,256]{2,1,0:T(8,128)(2,1)S(1)} custom-call(s32[2,12]{1,0:T(2,128)S(1)} %copy-done.4, bf16[4,256,3072]{2,1,0:T(8,128)(2,1)S(1)} %pack_inverse.1.sel_ref, bf16[1024,256]{1,0:T(8,128)(2,1)S(1)} %get-tuple-element.42.f0, bf16[1024,256]{1,0:T(8,128)(2,1)S(1)} %collective-permute-done.2.f1, ...), custom_call_target="tpu_custom_call" | custom-call | tf_op jit(solution)/shard_map/products/pallas_call | solution.py:348
  81.1 3.7 %products.5 = (bf16[4,272,256]{2,1,0:T(8,128)(2,1)S(1)}, bf16[4,272,256]{2,1,0:T(8,128)(2,1)S(1)}) custom-call(s32[2,12]{1,0:T(2,128)S(1)} %copy-done.4, bf16[4,256,3072]{2,1,0:T(8,128)(2,1)S(1)} %pack_inverse.1.sel_ref, bf16[1024,256]{1,0:T(8,128)(2,1)} %lead.4.f0, bf16[1024,256]{1,0:T(8,128)(2,1)S(1)} %collective-permute-done.6.f1, ...), custom_call_target="tpu_custom_call" | custom-call | tf_op jit(solution)/shard_map/products/pallas_call | solution.py:348
  84.9 8.6 %collective-permute-done.13.refs_0_ = bf16[2048,128]{1,0:T(8,128)(2,1)S(1)} collective-permute-done((bf16[2048,128]{1,0:T(8,128)(2,1)S(1)}, bf16[2048,128]{1,0:T(8,128)(2,1)S(1)}, u32[]{:S(2)}, u32[]{:S(2)}) %collective-permute-start.13) | collective-permute-done | bytes 524320 | tf_op jit(solution)/shard_map/rest1_z/ppermute | solution.py:107
  95.2 2.5 %collective-permute-start.22 = (bf16[2,272,256]{2,1,0:T(8,128)(2,1)S(1)}, bf16[2,272,256]{2,1,0:T(8,128)(2,1)S(1)}, u32[]{:S(2)}, u32[]{:S(2)}) collective-permute-start(bf16[2,272,256]{2,1,0:T(8,128)(2,1)S(1)} %get-tuple-element.72), channel_id=1, source_target_pairs={{0,8},{2,10},{4,12},{6,14},{8,0},{10,2},{12,4},{14,6},{16,24},{18,... | collective-permute-start | bytes 835592 | tf_op jit(solution)/shard_map/cross0_2/ppermute | solution.py:107
  97.8 3.3 %products.6.refs_0_ = bf16[4,272,256]{2,1,0:T(8,128)(2,1)S(1)} custom-call(s32[2,12]{1,0:T(2,128)S(1)} %copy-done.4, bf16[4,256,3072]{2,1,0:T(8,128)(2,1)S(1)} %pack_inverse.1.sel_ref, bf16[1024,256]{1,0:T(8,128)(2,1)S(1)} %get-tuple-element.42.f0, bf16[1024,256]{1,0:T(8,128)(2,1)S(1)} %collective-permute-done.2.f1, ...), custom_call_target="tpu_custom_call" | custom-call | tf_op jit(solution)/shard_map/products/pallas_call | solution.py:348
  101.1 5.2 %collective-permute-done.15.r1 = bf16[2048,128]{1,0:T(8,128)(2,1)S(1)} collective-permute-done((bf16[2048,128]{1,0:T(8,128)(2,1)S(1)}, bf16[2048,128]{1,0:T(8,128)(2,1)S(1)}, u32[]{:S(2)}, u32[]{:S(2)}) %collective-permute-start.15) | collective-permute-done | bytes 524320 | tf_op jit(solution)/shard_map/rest1_xz/ppermute | solution.py:107
  106.3 3.7 %products.7 = (bf16[4,272,256]{2,1,0:T(8,128)(2,1)S(1)}, bf16[4,272,256]{2,1,0:T(8,128)(2,1)S(1)}) custom-call(s32[2,12]{1,0:T(2,128)S(1)} %copy-done.4, bf16[4,256,3072]{2,1,0:T(8,128)(2,1)S(1)} %pack_inverse.1.sel_ref, bf16[1024,256]{1,0:T(8,128)(2,1)} %lead.4.f0, bf16[1024,256]{1,0:T(8,128)(2,1)S(1)} %collective-permute-done.6.f1, ...), custom_call_target="tpu_custom_call" | custom-call | tf_op jit(solution)/shard_map/products/pallas_call | solution.py:348
  110.2 1.8 %collective-permute-done.23.their_ref = bf16[4,272,256]{2,1,0:T(8,128)(2,1)S(1)} collective-permute-done((bf16[4,272,256]{2,1,0:T(8,128)(2,1)S(1)}, bf16[4,272,256]{2,1,0:T(8,128)(2,1)S(1)}, u32[]{:S(2)}, u32[]{:S(2)}) %collective-permute-start.23) | collective-permute-done | bytes 557088 | tf_op jit(solution)/shard_map/cross1_swap/ppermute | solution.py:101
  113.7 2.0 %collective-permute-start.26 = (bf16[2,272,256]{2,1,0:T(8,128)(2,1)S(1)}, bf16[2,272,256]{2,1,0:T(8,128)(2,1)S(1)}, u32[]{:S(2)}, u32[]{:S(2)}) collective-permute-start(bf16[2,272,256]{2,1,0:T(8,128)(2,1)S(1)} %get-tuple-element.81), channel_id=1, source_target_pairs={{0,8},{2,10},{4,12},{6,14},{8,0},{10,2},{12,4},{14,6},{16,24},{18,... | collective-permute-start | bytes 835592 | tf_op jit(solution)/shard_map/cross1_2/ppermute | solution.py:107
  115.7 7.0 %collective-permute-done.24.refs_1_ = bf16[2,272,256]{2,1,0:T(8,128)(2,1)S(1)} collective-permute-done((bf16[2,272,256]{2,1,0:T(8,128)(2,1)S(1)}, bf16[2,272,256]{2,1,0:T(8,128)(2,1)S(1)}, u32[]{:S(2)}, u32[]{:S(2)}) %collective-permute-start.24) | collective-permute-done | bytes 278560 | tf_op jit(solution)/shard_map/cross1_3/ppermute | solution.py:107
  122.7 4.5 %collective-permute-done.25.refs_2_ = bf16[2,272,256]{2,1,0:T(8,128)(2,1)S(1)} collective-permute-done((bf16[2,272,256]{2,1,0:T(8,128)(2,1)S(1)}, bf16[2,272,256]{2,1,0:T(8,128)(2,1)S(1)}, u32[]{:S(2)}, u32[]{:S(2)}) %collective-permute-start.25) | collective-permute-done | bytes 278560 | tf_op jit(solution)/shard_map/cross1_1/ppermute | solution.py:107
  127.7 2.3 %collective-permute-start.28 = (f32[2,2048]{1,0:T(2,128)S(1)}, f32[2,2048]{1,0:T(2,128)S(1)}, u32[]{:S(2)}, u32[]{:S(2)}) collective-permute-start(f32[2,2048]{1,0:T(2,128)S(1)} %add_sums.3), channel_id=1, source_target_pairs={{0,16},{2,18},{4,20},{6,22},{8,24},{10,26},{12,28},{14,30},{16,0},... | collective-permute-start | bytes 49160 | tf_op jit(solution)/shard_map/variance_8/ppermute | solution.py:107
  130.0 1.8 %collective-permute-start.29 = (f32[2,2048]{1,0:T(2,128)S(1)}, f32[2,2048]{1,0:T(2,128)S(1)}, u32[]{:S(2)}, u32[]{:S(2)}) collective-permute-start(f32[2,2048]{1,0:T(2,128)S(1)} %add_sums.3), channel_id=1, source_target_pairs={{0,18},{2,16},{4,22},{6,20},{8,26},{10,24},{12,30},{14,28},{16,2},... | collective-permute-start | bytes 49160 | tf_op jit(solution)/shard_map/variance_9/ppermute | solution.py:107
  (70 shorter events, 27.1 us)
Async XLA Ops:
  5.3 32.1 %collective-permute-start.8 = (bf16[192,2048]{1,0:T(8,128)(2,1)}, bf16[192,2048]{1,0:T(8,128)(2,1)}, u32[]{:S(2)}, u32[]{:S(2)}) collective-permute-start(bf16[192,2048]{1,0:T(8,128)(2,1)} %get-tuple-element.49), channel_id=1, source_target_pairs={{0,8},{2,10},{4,12},{6,14},{8,0},{10,2},{12,4},{14,6},{16,24},{18,... | collective-permute-start | bytes 2359304 | tf_op jit(solution)/shard_map/inv_z0/ppermute | solution.py:107
  8.3 30.8 %collective-permute-start.1 = (bf16[1024,256]{1,0:T(8,128)(2,1)S(1)}, bf16[1024,256]{1,0:T(8,128)(2,1)}, u32[]{:S(2)}, u32[]{:S(2)}) collective-permute-start(bf16[1024,256]{1,0:T(8,128)(2,1)S(1)} %get-tuple-element.42.f0), channel_id=1, source_target_pairs={{0,16},{2,18},{4,20},{6,22},{8,24},{10,26},{12,28},{14,30},{16,0},... | collective-permute-start | bytes 1572872 | tf_op jit(solution)/shard_map/first_z/ppermute | solution.py:107
  10.9 29.1 %collective-permute-start.2 = (bf16[1024,256]{1,0:T(8,128)(2,1)S(1)}, bf16[1024,256]{1,0:T(8,128)(2,1)S(1)}, u32[]{:S(2)}, u32[]{:S(2)}) collective-permute-start(bf16[1024,256]{1,0:T(8,128)(2,1)S(1)} %get-tuple-element.42.f0), channel_id=1, source_target_pairs={{0,2},{2,0},{4,6},{6,4},{8,10},{10,8},{12,14},{14,12},{16,18},{18,... | collective-permute-start | bytes 1572872 | tf_op jit(solution)/shard_map/first_x/ppermute | solution.py:107
  12.4 27.6 %collective-permute-start = (bf16[256,2048]{1,0:T(8,128)(2,1)}, bf16[256,2048]{1,0:T(8,128)(2,1)}, u32[]{:S(2)}, u32[]{:S(2)}) collective-permute-start(bf16[256,2048]{1,0:T(8,128)(2,1)} %refs_0_.1), channel_id=1, source_target_pairs={{0,4},{2,6},{4,0},{6,2},{8,12},{10,14},{12,8},{14,10},{16,20},{18,... | collective-permute-start | bytes 3145736 | tf_op jit(solution)/shard_map/inv_y/ppermute | solution.py:107
  14.0 25.1 %collective-permute-start.3 = (bf16[2048,256]{1,0:T(8,128)(2,1)S(1)}, bf16[2048,256]{1,0:T(8,128)(2,1)S(1)}, u32[]{:S(2)}, u32[]{:S(2)}) collective-permute-start(bf16[2048,256]{1,0:T(8,128)(2,1)S(1)} %dynamic-slice_bitcast_fusion), channel_id=1, source_target_pairs={{0,1},{1,0},{2,3},{3,2},{4,5},{5,4},{6,7},{7,6},{8,9},{9,8},{10,11... | collective-permute-start | bytes 3145736 | tf_op jit(solution)/shard_map/panel_swap/ppermute | solution.py:101
  37.4 28.1 %collective-permute-start.9 = (bf16[192,2048]{1,0:T(8,128)(2,1)}, bf16[192,2048]{1,0:T(8,128)(2,1)S(1)}, u32[]{:S(2)}, u32[]{:S(2)}) collective-permute-start(bf16[192,2048]{1,0:T(8,128)(2,1)} %collective-permute-done.8.refs_2_), channel_id=1, source_target_pairs={{0,4},{2,6},{4,0},{6,2},{8,12},{10,14},{12,8},{14,10},{16,20},{18,... | collective-permute-start | bytes 2359304 | tf_op jit(solution)/shard_map/inv_yz0/ppermute | solution.py:107
  40.0 25.5 %collective-permute-start.4 = (bf16[2064,128]{1,0:T(8,128)(2,1)S(1)}, bf16[2064,128]{1,0:T(8,128)(2,1)S(1)}, u32[]{:S(2)}, u32[]{:S(2)}) collective-permute-start(bf16[2064,128]{1,0:T(8,128)(2,1)S(1)} %get-tuple-element.59.r0), channel_id=1, source_target_pairs={{0,16},{2,18},{4,20},{6,22},{8,24},{10,26},{12,28},{14,30},{16,0},... | collective-permute-start | bytes 1585160 | tf_op jit(solution)/shard_map/rest0_z/ppermute | solution.py:107
  41.8 23.7 %collective-permute-start.5 = (bf16[2064,128]{1,0:T(8,128)(2,1)S(1)}, bf16[2064,128]{1,0:T(8,128)(2,1)S(1)}, u32[]{:S(2)}, u32[]{:S(2)}) collective-permute-start(bf16[2064,128]{1,0:T(8,128)(2,1)S(1)} %get-tuple-element.59.r0), channel_id=1, source_target_pairs={{0,2},{2,0},{4,6},{6,4},{8,10},{10,8},{12,14},{14,12},{16,18},{18,... | collective-permute-start | bytes 1585160 | tf_op jit(solution)/shard_map/rest0_x/ppermute | solution.py:107
  43.3 22.2 %collective-permute-start.6 = (bf16[1024,256]{1,0:T(8,128)(2,1)}, bf16[1024,256]{1,0:T(8,128)(2,1)S(1)}, u32[]{:S(2)}, u32[]{:S(2)}) collective-permute-start(bf16[1024,256]{1,0:T(8,128)(2,1)} %lead.4.f0), channel_id=1, source_target_pairs={{0,2},{2,0},{4,6},{6,4},{8,10},{10,8},{12,14},{14,12},{16,18},{18,... | collective-permute-start | bytes 1572872 | tf_op jit(solution)/shard_map/first_xz/ppermute | solution.py:107
  43.8 13.9 %collective-permute-start.7 = (bf16[64,2048]{1,0:T(8,128)(2,1)S(1)}, bf16[64,2048]{1,0:T(8,128)(2,1)S(1)}, u32[]{:S(2)}, u32[]{:S(2)}) collective-permute-start(bf16[64,2048]{1,0:T(8,128)(2,1)S(1)} %get-tuple-element.48), channel_id=1, source_target_pairs={{0,8},{2,10},{4,12},{6,14},{8,0},{10,2},{12,4},{14,6},{16,24},{18,... | collective-permute-start | bytes 786440 | tf_op jit(solution)/shard_map/inv_z1/ppermute | solution.py:107
  65.5 9.8 %collective-permute-start.11 = (bf16[704,2048]{1,0:T(8,128)(2,1)S(1)}, bf16[704,2048]{1,0:T(8,128)(2,1)S(1)}, u32[]{:S(2)}, u32[]{:S(2)}) collective-permute-start(bf16[704,2048]{1,0:T(8,128)(2,1)S(1)} %stack_rows.2.refs_0_), channel_id=1, source_target_pairs={{0,1},{1,0},{2,3},{3,2},{4,5},{5,4},{6,7},{7,6},{8,9},{9,8},{10,11... | collective-permute-start | bytes 8650760 | tf_op jit(solution)/shard_map/inv_swap/ppermute | solution.py:101
  65.7 8.6 %collective-permute-start.12 = (bf16[320,2048]{1,0:T(8,128)(2,1)S(1)}, bf16[320,2048]{1,0:T(8,128)(2,1)S(1)}, u32[]{:S(2)}, u32[]{:S(2)}) collective-permute-start(bf16[320,2048]{1,0:T(8,128)(2,1)S(1)} %stack_rows.3.refs_1_), channel_id=1, source_target_pairs={{0,1},{1,0},{2,3},{3,2},{4,5},{5,4},{6,7},{7,6},{8,9},{9,8},{10,11... | collective-permute-start | bytes 3932168 | tf_op jit(solution)/shard_map/inv_swap_more/ppermute | solution.py:101
  66.2 14.9 %collective-permute-start.14 = (bf16[2064,128]{1,0:T(8,128)(2,1)S(1)}, bf16[2064,128]{1,0:T(8,128)(2,1)S(1)}, u32[]{:S(2)}, u32[]{:S(2)}) collective-permute-start(bf16[2064,128]{1,0:T(8,128)(2,1)S(1)} %collective-permute-done.4.r0), channel_id=1, source_target_pairs={{0,2},{2,0},{4,6},{6,4},{8,10},{10,8},{12,14},{14,12},{16,18},{18,... | collective-permute-start | bytes 1585160 | tf_op jit(solution)/shard_map/rest0_xz/ppermute | solution.py:107
  67.7 25.8 %collective-permute-start.13 = (bf16[2048,128]{1,0:T(8,128)(2,1)S(1)}, bf16[2048,128]{1,0:T(8,128)(2,1)S(1)}, u32[]{:S(2)}, u32[]{:S(2)}) collective-permute-start(bf16[2048,128]{1,0:T(8,128)(2,1)S(1)} %get-tuple-element.63.r0), channel_id=1, source_target_pairs={{0,16},{2,18},{4,20},{6,22},{8,24},{10,26},{12,28},{14,30},{16,0},... | collective-permute-start | bytes 1572872 | tf_op jit(solution)/shard_map/rest1_z/ppermute | solution.py:107
  73.8 24.0 %collective-permute-start.16 = (bf16[2048,128]{1,0:T(8,128)(2,1)S(1)}, bf16[2048,128]{1,0:T(8,128)(2,1)S(1)}, u32[]{:S(2)}, u32[]{:S(2)}) collective-permute-start(bf16[2048,128]{1,0:T(8,128)(2,1)S(1)} %get-tuple-element.63.r0), channel_id=1, source_target_pairs={{0,2},{2,0},{4,6},{6,4},{8,10},{10,8},{12,14},{14,12},{16,18},{18,... | collective-permute-start | bytes 1572872 | tf_op jit(solution)/shard_map/rest1_x/ppermute | solution.py:107
  74.3 19.2 %collective-permute-start.18 = (f32[2,2048]{1,0:T(2,128)S(1)}, f32[2,2048]{1,0:T(2,128)S(1)}, u32[]{:S(2)}, u32[]{:S(2)}) collective-permute-start(f32[2,2048]{1,0:T(2,128)S(1)} %add.21), channel_id=1, source_target_pairs={{0,8},{2,10},{4,12},{6,14},{8,0},{10,2},{12,4},{14,6},{16,24},{18,... | collective-permute-start | bytes 49160 | tf_op jit(solution)/shard_map/squares_4/ppermute | solution.py:107
  84.8 9.3 %collective-permute-start.19 = (bf16[4,272,256]{2,1,0:T(8,128)(2,1)S(1)}, bf16[4,272,256]{2,1,0:T(8,128)(2,1)S(1)}, u32[]{:S(2)}, u32[]{:S(2)}) collective-permute-start(bf16[4,272,256]{2,1,0:T(8,128)(2,1)S(1)} %get-tuple-element.68), channel_id=1, source_target_pairs={{0,1},{1,0},{2,3},{3,2},{4,5},{5,4},{6,7},{7,6},{8,9},{9,8},{10,11... | collective-permute-start | bytes 1671176 | tf_op jit(solution)/shard_map/cross0_swap/ppermute | solution.py:101
  93.5 12.8 %collective-permute-start.15 = (bf16[2048,128]{1,0:T(8,128)(2,1)S(1)}, bf16[2048,128]{1,0:T(8,128)(2,1)S(1)}, u32[]{:S(2)}, u32[]{:S(2)}) collective-permute-start(bf16[2048,128]{1,0:T(8,128)(2,1)S(1)} %lead.5.r0), channel_id=1, source_target_pairs={{0,2},{2,0},{4,6},{6,4},{8,10},{10,8},{12,14},{14,12},{16,18},{18,... | collective-permute-start | bytes 1572872 | tf_op jit(solution)/shard_map/rest1_xz/ppermute | solution.py:107
  94.2 15.9 %collective-permute-start.20 = (bf16[2,272,256]{2,1,0:T(8,128)(2,1)S(1)}, bf16[2,272,256]{2,1,0:T(8,128)(2,1)S(1)}, u32[]{:S(2)}, u32[]{:S(2)}) collective-permute-start(bf16[2,272,256]{2,1,0:T(8,128)(2,1)S(1)} %get-tuple-element.70), channel_id=1, source_target_pairs={{0,12},{2,14},{4,8},{6,10},{8,4},{10,6},{12,0},{14,2},{16,28},{18,... | collective-permute-start | bytes 835592 | tf_op jit(solution)/shard_map/cross0_3/ppermute | solution.py:107
  94.3 15.9 %collective-permute-start.21 = (bf16[2,272,256]{2,1,0:T(8,128)(2,1)S(1)}, bf16[2,272,256]{2,1,0:T(8,128)(2,1)S(1)}, u32[]{:S(2)}, u32[]{:S(2)}) collective-permute-start(bf16[2,272,256]{2,1,0:T(8,128)(2,1)S(1)} %get-tuple-element.71), channel_id=1, source_target_pairs={{0,4},{2,6},{4,0},{6,2},{8,12},{10,14},{12,8},{14,10},{16,20},{18,... | collective-permute-start | bytes 835592 | tf_op jit(solution)/shard_map/cross0_1/ppermute | solution.py:107
  95.2 14.9 %collective-permute-start.22 = (bf16[2,272,256]{2,1,0:T(8,128)(2,1)S(1)}, bf16[2,272,256]{2,1,0:T(8,128)(2,1)S(1)}, u32[]{:S(2)}, u32[]{:S(2)}) collective-permute-start(bf16[2,272,256]{2,1,0:T(8,128)(2,1)S(1)} %get-tuple-element.72), channel_id=1, source_target_pairs={{0,8},{2,10},{4,12},{6,14},{8,0},{10,2},{12,4},{14,6},{16,24},{18,... | collective-permute-start | bytes 835592 | tf_op jit(solution)/shard_map/cross0_2/ppermute | solution.py:107
  112.2 10.5 %collective-permute-start.24 = (bf16[2,272,256]{2,1,0:T(8,128)(2,1)S(1)}, bf16[2,272,256]{2,1,0:T(8,128)(2,1)S(1)}, u32[]{:S(2)}, u32[]{:S(2)}) collective-permute-start(bf16[2,272,256]{2,1,0:T(8,128)(2,1)S(1)} %get-tuple-element.79), channel_id=1, source_target_pairs={{0,12},{2,14},{4,8},{6,10},{8,4},{10,6},{12,0},{14,2},{16,28},{18,... | collective-permute-start | bytes 835592 | tf_op jit(solution)/shard_map/cross1_3/ppermute | solution.py:107
  112.8 14.4 %collective-permute-start.25 = (bf16[2,272,256]{2,1,0:T(8,128)(2,1)S(1)}, bf16[2,272,256]{2,1,0:T(8,128)(2,1)S(1)}, u32[]{:S(2)}, u32[]{:S(2)}) collective-permute-start(bf16[2,272,256]{2,1,0:T(8,128)(2,1)S(1)} %get-tuple-element.80), channel_id=1, source_target_pairs={{0,4},{2,6},{4,0},{6,2},{8,12},{10,14},{12,8},{14,10},{16,20},{18,... | collective-permute-start | bytes 835592 | tf_op jit(solution)/shard_map/cross1_1/ppermute | solution.py:107
  113.7 13.6 %collective-permute-start.26 = (bf16[2,272,256]{2,1,0:T(8,128)(2,1)S(1)}, bf16[2,272,256]{2,1,0:T(8,128)(2,1)S(1)}, u32[]{:S(2)}, u32[]{:S(2)}) collective-permute-start(bf16[2,272,256]{2,1,0:T(8,128)(2,1)S(1)} %get-tuple-element.81), channel_id=1, source_target_pairs={{0,8},{2,10},{4,12},{6,14},{8,0},{10,2},{12,4},{14,6},{16,24},{18,... | collective-permute-start | bytes 835592 | tf_op jit(solution)/shard_map/cross1_2/ppermute | solution.py:107
  (11 other events, 79.5 us)

commit v15 on v14

--- a/solution.py
+++ b/solution.py
@@ -167,7 +167,9 @@
 
     def body(st, panel_ref, other_ref, out0, out1):
         n = lax.axis_index("narrow")
-        out0[(nblocks - first) * BLK :, :] = jnp.zeros((TAIL, LANES), out0.dtype)
+        for out in (out0, out1):
+            pad = out.shape[0] - (nblocks - first) * BLK
+            out[(nblocks - first) * BLK :, :] = jnp.zeros((pad, LANES), out.dtype)
         for j in range(nblocks - first):
             b = pick(st, n, first + j, first)
             row = pl.multiple_of(lax.rem(b, half_blocks) * BLK, BLK)
@@ -189,7 +191,7 @@
         body,
         out_shape=(
             jax.ShapeDtypeStruct((rows + TAIL, LANES), panel.dtype),
-            jax.ShapeDtypeStruct((rows, LANES), panel.dtype),
+            jax.ShapeDtypeStruct((rows + 2 * TAIL, LANES), panel.dtype),
         ),
         in_specs=[SMEM, VMEM, VMEM],
         out_specs=[VMEM, VMEM],
@@ -485,7 +487,7 @@
     other = swap_cores(lax.dynamic_index_in_dim(panel, 1 - n, 0, keepdims=False), "panel_swap")
     r_own = pack_rest(structure, panel, other, first)
     linv = squares(factor_inv)
-    f_z = lead([hop(f_own, ZH, "first_z")], 10)[0]
+    f_z = hop(f_own, ZH, "first_z")
     f_x = hop(f_own, X, "first_x")
     a_z0 = hop(top, ZL, "inv_z0")
     a_y = hop(inverse, Y, "inv_y")

time: 136 us -> 136 us (level)
  Pallas kernels: 23.7 us -> 19.2 us
  waiting for transfers between devices: 72 us -> 74.8 us
    ppermute x25, waiting for transfers between devices: 70.2 us -> 73 us  [hop(): return lax.ppermute(value, 'wide', [(i, i ^ mask) for i in range(size)])]
    pallas_call x2, Pallas kernels: 2.04 us -> 0.27 us  [stack_rows(): pl.pallas_call(body, out_shape=jax.ShapeDtypeStruct((rows, pieces[0].shap...]
    pallas_call x1, Pallas kernels: 2.35 us -> 0.65 us  [pack_first(): pl.pallas_call(body, out_shape=[jax.ShapeDtypeStruct((first * BLK, panel....]
    squeeze x1, local copies, waits for them, and re-layouts: 0.07 us -> 1.44 us  [per_device_grid(): lax.dynamic_index_in_dim(panel, 1 - n, 0, keepdims=False)]
  transfers between devices with their start and end apart: 30 -> 30, of which waited for: 12 -> 12; matrix products, arithmetic and copies ran while one was open for 0% -> 0% of each run, Pallas kernels for 16% -> 14%
where the time goes in v15:
time: 136 us
  waiting for transfers between devices  74.8 us (55%)
  starting transfers between devices  37.5 us (28%)
  Pallas kernels  19.2 us (14%)
  local copies, waits for them, and re-layouts  2.72 us (2%)
    ppermute x25, waiting for transfers between devices, hop(): return lax.ppermute(value, 'wide', [(i, i ^ mask) for i in range(size)])  73 us
    ppermute x25, starting transfers between devices, hop(): return lax.ppermute(value, 'wide', [(i, i ^ mask) for i in range(size)])  36.2 us
    pallas_call x4, Pallas kernels, products(): pl.pallas_call(body, out_shape=out if near is None else [out, out], in_sp...  13 us
  transfers between devices with their start and end apart: 30, of which 12 were waited for; matrix products, arithmetic and copies ran while one was open for 0% of the time, Pallas kernels for 14%

profile of v15, /device:TPU:0, one launch (start us, length us, event | category | flops | bytes accessed | tf_op | source)
XLA Modules:
  0.0 135.9 jit_solution(7278737519158067129)
XLA Ops:
  2.6 2.6 %collective-permute-start = (bf16[256,2048]{1,0:T(8,128)(2,1)}, bf16[256,2048]{1,0:T(8,128)(2,1)S(1)}, u32[]{:S(2)}, u32[]{:S(2)}) collective-permute-start(bf16[256,2048]{1,0:T(8,128)(2,1)} %refs_0_.1), channel_id=1, source_target_pairs={{0,4},{2,6},{4,0},{6,2},{8,12},{10,14},{12,8},{14,10},{16,20},{18,... | collective-permute-start | bytes 3145736 | tf_op jit(solution)/shard_map/inv_y/ppermute | solution.py:107
  7.1 1.6 %collective-permute-start.8 = (bf16[192,2048]{1,0:T(8,128)(2,1)S(1)}, bf16[192,2048]{1,0:T(8,128)(2,1)S(1)}, u32[]{:S(2)}, u32[]{:S(2)}) collective-permute-start(bf16[192,2048]{1,0:T(8,128)(2,1)S(1)} %get-tuple-element.49), channel_id=1, source_target_pairs={{0,8},{2,10},{4,12},{6,14},{8,0},{10,2},{12,4},{14,6},{16,24},{18,... | collective-permute-start | bytes 2359304 | tf_op jit(solution)/shard_map/inv_z0/ppermute | solution.py:107
  8.8 2.6 %collective-permute-start.1 = (bf16[1024,256]{1,0:T(8,128)(2,1)S(1)}, bf16[1024,256]{1,0:T(8,128)(2,1)S(1)}, u32[]{:S(2)}, u32[]{:S(2)}) collective-permute-start(bf16[1024,256]{1,0:T(8,128)(2,1)S(1)} %get-tuple-element.42.f0), channel_id=1, source_target_pairs={{0,16},{2,18},{4,20},{6,22},{8,24},{10,26},{12,28},{14,30},{16,0},... | collective-permute-start | bytes 1572872 | tf_op jit(solution)/shard_map/first_z/ppermute | solution.py:107
  12.9 25.2 %collective-permute-done.8.refs_2_ = bf16[192,2048]{1,0:T(8,128)(2,1)S(1)} collective-permute-done((bf16[192,2048]{1,0:T(8,128)(2,1)S(1)}, bf16[192,2048]{1,0:T(8,128)(2,1)S(1)}, u32[]{:S(2)}, u32[]{:S(2)}) %collective-permute-start.8) | collective-permute-done | bytes 786464 | tf_op jit(solution)/shard_map/inv_z0/ppermute | solution.py:107
  39.4 1.9 %collective-permute-start.4 = (bf16[2064,128]{1,0:T(8,128)(2,1)S(1)}, bf16[2064,128]{1,0:T(8,128)(2,1)S(1)}, u32[]{:S(2)}, u32[]{:S(2)}) collective-permute-start(bf16[2064,128]{1,0:T(8,128)(2,1)S(1)} %get-tuple-element.59.r0), channel_id=1, source_target_pairs={{0,16},{2,18},{4,20},{6,22},{8,24},{10,26},{12,28},{14,30},{16,0},... | collective-permute-start | bytes 1585160 | tf_op jit(solution)/shard_map/rest0_z/ppermute | solution.py:107
  43.3 2.5 %collective-permute-start.7 = (bf16[64,2048]{1,0:T(8,128)(2,1)S(1)}, bf16[64,2048]{1,0:T(8,128)(2,1)S(1)}, u32[]{:S(2)}, u32[]{:S(2)}) collective-permute-start(bf16[64,2048]{1,0:T(8,128)(2,1)S(1)} %get-tuple-element.48), channel_id=1, source_target_pairs={{0,8},{2,10},{4,12},{6,14},{8,0},{10,2},{12,4},{14,6},{16,24},{18,... | collective-permute-start | bytes 786440 | tf_op jit(solution)/shard_map/inv_z1/ppermute | solution.py:107
  45.8 11.6 %collective-permute-done.7.refs_0_ = bf16[64,2048]{1,0:T(8,128)(2,1)S(1)} collective-permute-done((bf16[64,2048]{1,0:T(8,128)(2,1)S(1)}, bf16[64,2048]{1,0:T(8,128)(2,1)S(1)}, u32[]{:S(2)}, u32[]{:S(2)}) %collective-permute-start.7) | collective-permute-done | bytes 262176 | tf_op jit(solution)/shard_map/inv_z1/ppermute | solution.py:107
  59.1 6.1 %collective-permute-done.6.f1 = bf16[1024,256]{1,0:T(8,128)(2,1)S(1)} collective-permute-done((bf16[1024,256]{1,0:T(8,128)(2,1)S(1)}, bf16[1024,256]{1,0:T(8,128)(2,1)S(1)}, u32[]{:S(2)}, u32[]{:S(2)}) %collective-permute-start.6) | collective-permute-done | bytes 524320 | tf_op jit(solution)/shard_map/first_xz/ppermute | solution.py:107
  66.0 2.1 %collective-permute-start.13 = (bf16[2080,128]{1,0:T(8,128)(2,1)S(1)}, bf16[2080,128]{1,0:T(8,128)(2,1)S(1)}, u32[]{:S(2)}, u32[]{:S(2)}) collective-permute-start(bf16[2080,128]{1,0:T(8,128)(2,1)S(1)} %get-tuple-element.63.r0), channel_id=1, source_target_pairs={{0,16},{2,18},{4,20},{6,22},{8,24},{10,26},{12,28},{14,30},{16,0},... | collective-permute-start | bytes 1597448 | tf_op jit(solution)/shard_map/rest1_z/ppermute | solution.py:107
  71.5 2.2 %collective-permute-done.17 = f32[2,2048]{1,0:T(2,128)S(1)} collective-permute-done((f32[2,2048]{1,0:T(2,128)S(1)}, f32[2,2048]{1,0:T(2,128)S(1)}, u32[]{:S(2)}, u32[]{:S(2)}) %collective-permute-start.17) | collective-permute-done | bytes 16416 | tf_op jit(solution)/shard_map/squares_2/ppermute | solution.py:107
  75.1 1.7 %pack_inverse.1.sel_ref = bf16[4,256,3072]{2,1,0:T(8,128)(2,1)S(1)} custom-call(s32[2,12]{1,0:T(2,128)S(1)} %copy-done.4, bf16[704,2048]{1,0:T(8,128)(2,1)S(1)} %stack_rows.2.refs_0_, bf16[320,2048]{1,0:T(8,128)(2,1)S(1)} %stack_rows.3.refs_1_, bf16[704,2048]{1,0:T(8,128)(2,1)S(1)} %collective-permute-done.11.refs_2_, ...), custom_call_target="tpu_custom_call" | custom-call | tf_op jit(solution)/shard_map/pack_inverse/pallas_call | solution.py:251
  76.7 3.2 %products.4.refs_0_ = bf16[4,272,256]{2,1,0:T(8,128)(2,1)S(1)} custom-call(s32[2,12]{1,0:T(2,128)S(1)} %copy-done.4, bf16[4,256,3072]{2,1,0:T(8,128)(2,1)S(1)} %pack_inverse.1.sel_ref, bf16[1024,256]{1,0:T(8,128)(2,1)S(1)} %get-tuple-element.42.f0, bf16[1024,256]{1,0:T(8,128)(2,1)S(1)} %collective-permute-done.2.f1, ...), custom_call_target="tpu_custom_call" | custom-call | tf_op jit(solution)/shard_map/products/pallas_call | solution.py:350
  79.9 3.0 %collective-permute-done.14.r1 = bf16[2064,128]{1,0:T(8,128)(2,1)S(1)} collective-permute-done((bf16[2064,128]{1,0:T(8,128)(2,1)S(1)}, bf16[2064,128]{1,0:T(8,128)(2,1)S(1)}, u32[]{:S(2)}, u32[]{:S(2)}) %collective-permute-start.14) | collective-permute-done | bytes 528416 | tf_op jit(solution)/shard_map/rest0_xz/ppermute | solution.py:107
  83.0 3.2 %products.5 = (bf16[4,272,256]{2,1,0:T(8,128)(2,1)S(1)}, bf16[4,272,256]{2,1,0:T(8,128)(2,1)S(1)}) custom-call(s32[2,12]{1,0:T(2,128)S(1)} %copy-done.4, bf16[4,256,3072]{2,1,0:T(8,128)(2,1)S(1)} %pack_inverse.1.sel_ref, bf16[1024,256]{1,0:T(8,128)(2,1)S(1)} %collective-permute-done.1.f0, bf16[1024,256]{1,0:T(8,128)(2,1)S(1)} %collective-permute-done.6.f1, ...), custom_call_target="tpu_custom_call" | custom-call | tf_op jit(solution)/shard_map/products/pallas_call | solution.py:350
  86.3 6.1 %collective-permute-done.13.refs_0_ = bf16[2080,128]{1,0:T(8,128)(2,1)S(1)} collective-permute-done((bf16[2080,128]{1,0:T(8,128)(2,1)S(1)}, bf16[2080,128]{1,0:T(8,128)(2,1)S(1)}, u32[]{:S(2)}, u32[]{:S(2)}) %collective-permute-start.13) | collective-permute-done | bytes 532512 | tf_op jit(solution)/shard_map/rest1_z/ppermute | solution.py:107
  95.7 1.9 %collective-permute-start.22 = (bf16[2,272,256]{2,1,0:T(8,128)(2,1)S(1)}, bf16[2,272,256]{2,1,0:T(8,128)(2,1)S(1)}, u32[]{:S(2)}, u32[]{:S(2)}) collective-permute-start(bf16[2,272,256]{2,1,0:T(8,128)(2,1)S(1)} %get-tuple-element.72), channel_id=1, source_target_pairs={{0,8},{2,10},{4,12},{6,14},{8,0},{10,2},{12,4},{14,6},{16,24},{18,... | collective-permute-start | bytes 835592 | tf_op jit(solution)/shard_map/cross0_2/ppermute | solution.py:107
  97.6 3.4 %products.6.refs_0_ = bf16[4,272,256]{2,1,0:T(8,128)(2,1)S(1)} custom-call(s32[2,12]{1,0:T(2,128)S(1)} %copy-done.4, bf16[4,256,3072]{2,1,0:T(8,128)(2,1)S(1)} %pack_inverse.1.sel_ref, bf16[1024,256]{1,0:T(8,128)(2,1)S(1)} %get-tuple-element.42.f0, bf16[1024,256]{1,0:T(8,128)(2,1)S(1)} %collective-permute-done.2.f1, ...), custom_call_target="tpu_custom_call" | custom-call | tf_op jit(solution)/shard_map/products/pallas_call | solution.py:350
  100.9 4.8 %collective-permute-done.15.r1 = bf16[2080,128]{1,0:T(8,128)(2,1)S(1)} collective-permute-done((bf16[2080,128]{1,0:T(8,128)(2,1)S(1)}, bf16[2080,128]{1,0:T(8,128)(2,1)S(1)}, u32[]{:S(2)}, u32[]{:S(2)}) %collective-permute-start.15) | collective-permute-done | bytes 532512 | tf_op jit(solution)/shard_map/rest1_xz/ppermute | solution.py:107
  105.7 3.2 %products.7 = (bf16[4,272,256]{2,1,0:T(8,128)(2,1)S(1)}, bf16[4,272,256]{2,1,0:T(8,128)(2,1)S(1)}) custom-call(s32[2,12]{1,0:T(2,128)S(1)} %copy-done.4, bf16[4,256,3072]{2,1,0:T(8,128)(2,1)S(1)} %pack_inverse.1.sel_ref, bf16[1024,256]{1,0:T(8,128)(2,1)S(1)} %collective-permute-done.1.f0, bf16[1024,256]{1,0:T(8,128)(2,1)S(1)} %collective-permute-done.6.f1, ...), custom_call_target="tpu_custom_call" | custom-call | tf_op jit(solution)/shard_map/products/pallas_call | solution.py:350
  109.1 1.8 %collective-permute-done.23.their_ref = bf16[4,272,256]{2,1,0:T(8,128)(2,1)S(1)} collective-permute-done((bf16[4,272,256]{2,1,0:T(8,128)(2,1)S(1)}, bf16[4,272,256]{2,1,0:T(8,128)(2,1)S(1)}, u32[]{:S(2)}, u32[]{:S(2)}) %collective-permute-start.23) | collective-permute-done | bytes 557088 | tf_op jit(solution)/shard_map/cross1_swap/ppermute | solution.py:101
  112.7 1.9 %collective-permute-start.26 = (bf16[2,272,256]{2,1,0:T(8,128)(2,1)S(1)}, bf16[2,272,256]{2,1,0:T(8,128)(2,1)S(1)}, u32[]{:S(2)}, u32[]{:S(2)}) collective-permute-start(bf16[2,272,256]{2,1,0:T(8,128)(2,1)S(1)} %get-tuple-element.81), channel_id=1, source_target_pairs={{0,8},{2,10},{4,12},{6,14},{8,0},{10,2},{12,4},{14,6},{16,24},{18,... | collective-permute-start | bytes 835592 | tf_op jit(solution)/shard_map/cross1_2/ppermute | solution.py:107
  114.6 7.0 %collective-permute-done.24.refs_1_ = bf16[2,272,256]{2,1,0:T(8,128)(2,1)S(1)} collective-permute-done((bf16[2,272,256]{2,1,0:T(8,128)(2,1)S(1)}, bf16[2,272,256]{2,1,0:T(8,128)(2,1)S(1)}, u32[]{:S(2)}, u32[]{:S(2)}) %collective-permute-start.24) | collective-permute-done | bytes 278560 | tf_op jit(solution)/shard_map/cross1_3/ppermute | solution.py:107
  121.5 4.6 %collective-permute-done.25.refs_2_ = bf16[2,272,256]{2,1,0:T(8,128)(2,1)S(1)} collective-permute-done((bf16[2,272,256]{2,1,0:T(8,128)(2,1)S(1)}, bf16[2,272,256]{2,1,0:T(8,128)(2,1)S(1)}, u32[]{:S(2)}, u32[]{:S(2)}) %collective-permute-start.25) | collective-permute-done | bytes 278560 | tf_op jit(solution)/shard_map/cross1_1/ppermute | solution.py:107
  133.4 1.8 %collective-permute-done.29 = f32[2,2048]{1,0:T(2,128)S(1)} collective-permute-done((f32[2,2048]{1,0:T(2,128)S(1)}, f32[2,2048]{1,0:T(2,128)S(1)}, u32[]{:S(2)}, u32[]{:S(2)}) %collective-permute-start.29) | collective-permute-done | bytes 16416 | tf_op jit(solution)/shard_map/variance_9/ppermute | solution.py:107
  (69 shorter events, 29.0 us)
Async XLA Ops:
  2.1 36.3 %collective-permute-start.3 = (bf16[2048,256]{1,0:T(8,128)(2,1)S(1)}, bf16[2048,256]{1,0:T(8,128)(2,1)S(1)}, u32[]{:S(2)}, u32[]{:S(2)}) collective-permute-start(bf16[2048,256]{1,0:T(8,128)(2,1)S(1)} %dynamic-slice_bitcast_fusion), channel_id=1, source_target_pairs={{0,1},{1,0},{2,3},{3,2},{4,5},{5,4},{6,7},{7,6},{8,9},{9,8},{10,11... | collective-permute-start | bytes 3145736 | tf_op jit(solution)/shard_map/panel_swap/ppermute | solution.py:101
  2.6 36.7 %collective-permute-start = (bf16[256,2048]{1,0:T(8,128)(2,1)}, bf16[256,2048]{1,0:T(8,128)(2,1)S(1)}, u32[]{:S(2)}, u32[]{:S(2)}) collective-permute-start(bf16[256,2048]{1,0:T(8,128)(2,1)} %refs_0_.1), channel_id=1, source_target_pairs={{0,4},{2,6},{4,0},{6,2},{8,12},{10,14},{12,8},{14,10},{16,20},{18,... | collective-permute-start | bytes 3145736 | tf_op jit(solution)/shard_map/inv_y/ppermute | solution.py:107
  7.1 30.9 %collective-permute-start.8 = (bf16[192,2048]{1,0:T(8,128)(2,1)S(1)}, bf16[192,2048]{1,0:T(8,128)(2,1)S(1)}, u32[]{:S(2)}, u32[]{:S(2)}) collective-permute-start(bf16[192,2048]{1,0:T(8,128)(2,1)S(1)} %get-tuple-element.49), channel_id=1, source_target_pairs={{0,8},{2,10},{4,12},{6,14},{8,0},{10,2},{12,4},{14,6},{16,24},{18,... | collective-permute-start | bytes 2359304 | tf_op jit(solution)/shard_map/inv_z0/ppermute | solution.py:107
  8.8 30.5 %collective-permute-start.1 = (bf16[1024,256]{1,0:T(8,128)(2,1)S(1)}, bf16[1024,256]{1,0:T(8,128)(2,1)S(1)}, u32[]{:S(2)}, u32[]{:S(2)}) collective-permute-start(bf16[1024,256]{1,0:T(8,128)(2,1)S(1)} %get-tuple-element.42.f0), channel_id=1, source_target_pairs={{0,16},{2,18},{4,20},{6,22},{8,24},{10,26},{12,28},{14,30},{16,0},... | collective-permute-start | bytes 1572872 | tf_op jit(solution)/shard_map/first_z/ppermute | solution.py:107
  11.4 28.0 %collective-permute-start.2 = (bf16[1024,256]{1,0:T(8,128)(2,1)S(1)}, bf16[1024,256]{1,0:T(8,128)(2,1)S(1)}, u32[]{:S(2)}, u32[]{:S(2)}) collective-permute-start(bf16[1024,256]{1,0:T(8,128)(2,1)S(1)} %get-tuple-element.42.f0), channel_id=1, source_target_pairs={{0,2},{2,0},{4,6},{6,4},{8,10},{10,8},{12,14},{14,12},{16,18},{18,... | collective-permute-start | bytes 1572872 | tf_op jit(solution)/shard_map/first_x/ppermute | solution.py:107
  38.1 27.2 %collective-permute-start.9 = (bf16[192,2048]{1,0:T(8,128)(2,1)S(1)}, bf16[192,2048]{1,0:T(8,128)(2,1)S(1)}, u32[]{:S(2)}, u32[]{:S(2)}) collective-permute-start(bf16[192,2048]{1,0:T(8,128)(2,1)S(1)} %collective-permute-done.8.refs_2_), channel_id=1, source_target_pairs={{0,4},{2,6},{4,0},{6,2},{8,12},{10,14},{12,8},{14,10},{16,20},{18,... | collective-permute-start | bytes 2359304 | tf_op jit(solution)/shard_map/inv_yz0/ppermute | solution.py:107
  39.4 25.9 %collective-permute-start.4 = (bf16[2064,128]{1,0:T(8,128)(2,1)S(1)}, bf16[2064,128]{1,0:T(8,128)(2,1)S(1)}, u32[]{:S(2)}, u32[]{:S(2)}) collective-permute-start(bf16[2064,128]{1,0:T(8,128)(2,1)S(1)} %get-tuple-element.59.r0), channel_id=1, source_target_pairs={{0,16},{2,18},{4,20},{6,22},{8,24},{10,26},{12,28},{14,30},{16,0},... | collective-permute-start | bytes 1585160 | tf_op jit(solution)/shard_map/rest0_z/ppermute | solution.py:107
  41.3 23.9 %collective-permute-start.5 = (bf16[2064,128]{1,0:T(8,128)(2,1)S(1)}, bf16[2064,128]{1,0:T(8,128)(2,1)S(1)}, u32[]{:S(2)}, u32[]{:S(2)}) collective-permute-start(bf16[2064,128]{1,0:T(8,128)(2,1)S(1)} %get-tuple-element.59.r0), channel_id=1, source_target_pairs={{0,2},{2,0},{4,6},{6,4},{8,10},{10,8},{12,14},{14,12},{16,18},{18,... | collective-permute-start | bytes 1585160 | tf_op jit(solution)/shard_map/rest0_x/ppermute | solution.py:107
  42.8 22.4 %collective-permute-start.6 = (bf16[1024,256]{1,0:T(8,128)(2,1)S(1)}, bf16[1024,256]{1,0:T(8,128)(2,1)S(1)}, u32[]{:S(2)}, u32[]{:S(2)}) collective-permute-start(bf16[1024,256]{1,0:T(8,128)(2,1)S(1)} %collective-permute-done.1.f0), channel_id=1, source_target_pairs={{0,2},{2,0},{4,6},{6,4},{8,10},{10,8},{12,14},{14,12},{16,18},{18,... | collective-permute-start | bytes 1572872 | tf_op jit(solution)/shard_map/first_xz/ppermute | solution.py:107
  43.3 14.1 %collective-permute-start.7 = (bf16[64,2048]{1,0:T(8,128)(2,1)S(1)}, bf16[64,2048]{1,0:T(8,128)(2,1)S(1)}, u32[]{:S(2)}, u32[]{:S(2)}) collective-permute-start(bf16[64,2048]{1,0:T(8,128)(2,1)S(1)} %get-tuple-element.48), channel_id=1, source_target_pairs={{0,8},{2,10},{4,12},{6,14},{8,0},{10,2},{12,4},{14,6},{16,24},{18,... | collective-permute-start | bytes 786440 | tf_op jit(solution)/shard_map/inv_z1/ppermute | solution.py:107
  57.4 7.8 %collective-permute-start.10 = (bf16[64,2048]{1,0:T(8,128)(2,1)S(1)}, bf16[64,2048]{1,0:T(8,128)(2,1)S(1)}, u32[]{:S(2)}, u32[]{:S(2)}) collective-permute-start(bf16[64,2048]{1,0:T(8,128)(2,1)S(1)} %collective-permute-done.7.refs_0_), channel_id=1, source_target_pairs={{0,4},{2,6},{4,0},{6,2},{8,12},{10,14},{12,8},{14,10},{16,20},{18,... | collective-permute-start | bytes 786440 | tf_op jit(solution)/shard_map/inv_yz1/ppermute | solution.py:107
  65.2 9.8 %collective-permute-start.11 = (bf16[704,2048]{1,0:T(8,128)(2,1)S(1)}, bf16[704,2048]{1,0:T(8,128)(2,1)S(1)}, u32[]{:S(2)}, u32[]{:S(2)}) collective-permute-start(bf16[704,2048]{1,0:T(8,128)(2,1)S(1)} %stack_rows.2.refs_0_), channel_id=1, source_target_pairs={{0,1},{1,0},{2,3},{3,2},{4,5},{5,4},{6,7},{7,6},{8,9},{9,8},{10,11... | collective-permute-start | bytes 8650760 | tf_op jit(solution)/shard_map/inv_swap/ppermute | solution.py:101
  65.4 8.8 %collective-permute-start.12 = (bf16[320,2048]{1,0:T(8,128)(2,1)S(1)}, bf16[320,2048]{1,0:T(8,128)(2,1)S(1)}, u32[]{:S(2)}, u32[]{:S(2)}) collective-permute-start(bf16[320,2048]{1,0:T(8,128)(2,1)S(1)} %stack_rows.3.refs_1_), channel_id=1, source_target_pairs={{0,1},{1,0},{2,3},{3,2},{4,5},{5,4},{6,7},{7,6},{8,9},{9,8},{10,11... | collective-permute-start | bytes 3932168 | tf_op jit(solution)/shard_map/inv_swap_more/ppermute | solution.py:101
  66.0 26.4 %collective-permute-start.13 = (bf16[2080,128]{1,0:T(8,128)(2,1)S(1)}, bf16[2080,128]{1,0:T(8,128)(2,1)S(1)}, u32[]{:S(2)}, u32[]{:S(2)}) collective-permute-start(bf16[2080,128]{1,0:T(8,128)(2,1)S(1)} %get-tuple-element.63.r0), channel_id=1, source_target_pairs={{0,16},{2,18},{4,20},{6,22},{8,24},{10,26},{12,28},{14,30},{16,0},... | collective-permute-start | bytes 1597448 | tf_op jit(solution)/shard_map/rest1_z/ppermute | solution.py:107
  68.1 14.9 %collective-permute-start.14 = (bf16[2064,128]{1,0:T(8,128)(2,1)S(1)}, bf16[2064,128]{1,0:T(8,128)(2,1)S(1)}, u32[]{:S(2)}, u32[]{:S(2)}) collective-permute-start(bf16[2064,128]{1,0:T(8,128)(2,1)S(1)} %collective-permute-done.4.r0), channel_id=1, source_target_pairs={{0,2},{2,0},{4,6},{6,4},{8,10},{10,8},{12,14},{14,12},{16,18},{18,... | collective-permute-start | bytes 1585160 | tf_op jit(solution)/shard_map/rest0_xz/ppermute | solution.py:107
  73.7 23.9 %collective-permute-start.16 = (bf16[2080,128]{1,0:T(8,128)(2,1)S(1)}, bf16[2080,128]{1,0:T(8,128)(2,1)S(1)}, u32[]{:S(2)}, u32[]{:S(2)}) collective-permute-start(bf16[2080,128]{1,0:T(8,128)(2,1)S(1)} %get-tuple-element.63.r0), channel_id=1, source_target_pairs={{0,2},{2,0},{4,6},{6,4},{8,10},{10,8},{12,14},{14,12},{16,18},{18,... | collective-permute-start | bytes 1597448 | tf_op jit(solution)/shard_map/rest1_x/ppermute | solution.py:107
  74.3 18.1 %collective-permute-start.18 = (f32[2,2048]{1,0:T(2,128)S(1)}, f32[2,2048]{1,0:T(2,128)S(1)}, u32[]{:S(2)}, u32[]{:S(2)}) collective-permute-start(f32[2,2048]{1,0:T(2,128)S(1)} %add.21), channel_id=1, source_target_pairs={{0,8},{2,10},{4,12},{6,14},{8,0},{10,2},{12,4},{14,6},{16,24},{18,... | collective-permute-start | bytes 49160 | tf_op jit(solution)/shard_map/squares_4/ppermute | solution.py:107
  92.4 13.3 %collective-permute-start.15 = (bf16[2080,128]{1,0:T(8,128)(2,1)S(1)}, bf16[2080,128]{1,0:T(8,128)(2,1)S(1)}, u32[]{:S(2)}, u32[]{:S(2)}) collective-permute-start(bf16[2080,128]{1,0:T(8,128)(2,1)S(1)} %lead.3.r0), channel_id=1, source_target_pairs={{0,2},{2,0},{4,6},{6,4},{8,10},{10,8},{12,14},{14,12},{16,18},{18,... | collective-permute-start | bytes 1597448 | tf_op jit(solution)/shard_map/rest1_xz/ppermute | solution.py:107
  94.0 15.0 %collective-permute-start.20 = (bf16[2,272,256]{2,1,0:T(8,128)(2,1)S(1)}, bf16[2,272,256]{2,1,0:T(8,128)(2,1)S(1)}, u32[]{:S(2)}, u32[]{:S(2)}) collective-permute-start(bf16[2,272,256]{2,1,0:T(8,128)(2,1)S(1)} %get-tuple-element.70), channel_id=1, source_target_pairs={{0,12},{2,14},{4,8},{6,10},{8,4},{10,6},{12,0},{14,2},{16,28},{18,... | collective-permute-start | bytes 835592 | tf_op jit(solution)/shard_map/cross0_3/ppermute | solution.py:107
  94.5 14.5 %collective-permute-start.21 = (bf16[2,272,256]{2,1,0:T(8,128)(2,1)S(1)}, bf16[2,272,256]{2,1,0:T(8,128)(2,1)S(1)}, u32[]{:S(2)}, u32[]{:S(2)}) collective-permute-start(bf16[2,272,256]{2,1,0:T(8,128)(2,1)S(1)} %get-tuple-element.71), channel_id=1, source_target_pairs={{0,4},{2,6},{4,0},{6,2},{8,12},{10,14},{12,8},{14,10},{16,20},{18,... | collective-permute-start | bytes 835592 | tf_op jit(solution)/shard_map/cross0_1/ppermute | solution.py:107
  95.7 13.3 %collective-permute-start.22 = (bf16[2,272,256]{2,1,0:T(8,128)(2,1)S(1)}, bf16[2,272,256]{2,1,0:T(8,128)(2,1)S(1)}, u32[]{:S(2)}, u32[]{:S(2)}) collective-permute-start(bf16[2,272,256]{2,1,0:T(8,128)(2,1)S(1)} %get-tuple-element.72), channel_id=1, source_target_pairs={{0,8},{2,10},{4,12},{6,14},{8,0},{10,2},{12,4},{14,6},{16,24},{18,... | collective-permute-start | bytes 835592 | tf_op jit(solution)/shard_map/cross0_2/ppermute | solution.py:107
  111.0 10.5 %collective-permute-start.24 = (bf16[2,272,256]{2,1,0:T(8,128)(2,1)S(1)}, bf16[2,272,256]{2,1,0:T(8,128)(2,1)S(1)}, u32[]{:S(2)}, u32[]{:S(2)}) collective-permute-start(bf16[2,272,256]{2,1,0:T(8,128)(2,1)S(1)} %get-tuple-element.79), channel_id=1, source_target_pairs={{0,12},{2,14},{4,8},{6,10},{8,4},{10,6},{12,0},{14,2},{16,28},{18,... | collective-permute-start | bytes 835592 | tf_op jit(solution)/shard_map/cross1_3/ppermute | solution.py:107
  111.7 14.4 %collective-permute-start.25 = (bf16[2,272,256]{2,1,0:T(8,128)(2,1)S(1)}, bf16[2,272,256]{2,1,0:T(8,128)(2,1)S(1)}, u32[]{:S(2)}, u32[]{:S(2)}) collective-permute-start(bf16[2,272,256]{2,1,0:T(8,128)(2,1)S(1)} %get-tuple-element.80), channel_id=1, source_target_pairs={{0,4},{2,6},{4,0},{6,2},{8,12},{10,14},{12,8},{14,10},{16,20},{18,... | collective-permute-start | bytes 835592 | tf_op jit(solution)/shard_map/cross1_1/ppermute | solution.py:107
  112.7 14.1 %collective-permute-start.26 = (bf16[2,272,256]{2,1,0:T(8,128)(2,1)S(1)}, bf16[2,272,256]{2,1,0:T(8,128)(2,1)S(1)}, u32[]{:S(2)}, u32[]{:S(2)}) collective-permute-start(bf16[2,272,256]{2,1,0:T(8,128)(2,1)S(1)} %get-tuple-element.81), channel_id=1, source_target_pairs={{0,8},{2,10},{4,12},{6,14},{8,0},{10,2},{12,4},{14,6},{16,24},{18,... | collective-permute-start | bytes 835592 | tf_op jit(solution)/shard_map/cross1_2/ppermute | solution.py:107
  (11 other events, 103.4 us)

commit v16 on v14

--- a/solution.py
+++ b/solution.py
@@ -485,7 +485,7 @@
     other = swap_cores(lax.dynamic_index_in_dim(panel, 1 - n, 0, keepdims=False), "panel_swap")
     r_own = pack_rest(structure, panel, other, first)
     linv = squares(factor_inv)
-    f_z = lead([hop(f_own, ZH, "first_z")], 10)[0]
+    f_z = hop(f_own, ZH, "first_z")
     f_x = hop(f_own, X, "first_x")
     a_z0 = hop(top, ZL, "inv_z0")
     a_y = hop(inverse, Y, "inv_y")

time: 136 us -> 136 us (level)
  Pallas kernels: 23.7 us -> 19.4 us
  waiting for transfers between devices: 72 us -> 75.1 us
    ppermute x25, waiting for transfers between devices: 70.2 us -> 73.2 us  [hop(): return lax.ppermute(value, 'wide', [(i, i ^ mask) for i in range(size)])]
    pallas_call x2, Pallas kernels: 2.04 us -> 0.27 us  [stack_rows(): pl.pallas_call(body, out_shape=jax.ShapeDtypeStruct((rows, pieces[0].shap...]
    pallas_call x1, Pallas kernels: 2.35 us -> 0.65 us  [pack_first(): pl.pallas_call(body, out_shape=[jax.ShapeDtypeStruct((first * BLK, panel....]
    squeeze x1, local copies, waits for them, and re-layouts: 0.07 us -> 1.44 us  [per_device_grid(): lax.dynamic_index_in_dim(panel, 1 - n, 0, keepdims=False)]
  transfers between devices with their start and end apart: 30 -> 30, of which waited for: 12 -> 12; matrix products, arithmetic and copies ran while one was open for 0% -> 0% of each run, Pallas kernels for 16% -> 14%
where the time goes in v16:
time: 136 us; the launch traced here: 135 us
  waiting for transfers between devices  75.1 us (55%)
  starting transfers between devices  36.6 us (27%)
  Pallas kernels  19.4 us (14%)
  local copies, waits for them, and re-layouts  2.72 us (2%)
    ppermute x25, waiting for transfers between devices, hop(): return lax.ppermute(value, 'wide', [(i, i ^ mask) for i in range(size)])  73.2 us
    ppermute x25, starting transfers between devices, hop(): return lax.ppermute(value, 'wide', [(i, i ^ mask) for i in range(size)])  35.3 us
    pallas_call x4, Pallas kernels, products(): pl.pallas_call(body, out_shape=out if near is None else [out, out], in_sp...  13 us
  transfers between devices with their start and end apart: 30, of which 12 were waited for; matrix products, arithmetic and copies ran while one was open for 0% of the time, Pallas kernels for 14%

profile of v16, /device:TPU:0, one launch (start us, length us, event | category | flops | bytes accessed | tf_op | source)
XLA Modules:
  0.0 135.3 jit_solution(3682811894549179117)
XLA Ops:
  2.6 2.6 %collective-permute-start = (bf16[256,2048]{1,0:T(8,128)(2,1)}, bf16[256,2048]{1,0:T(8,128)(2,1)S(1)}, u32[]{:S(2)}, u32[]{:S(2)}) collective-permute-start(bf16[256,2048]{1,0:T(8,128)(2,1)} %refs_0_.1), channel_id=1, source_target_pairs={{0,4},{2,6},{4,0},{6,2},{8,12},{10,14},{12,8},{14,10},{16,20},{18,... | collective-permute-start | bytes 3145736 | tf_op jit(solution)/shard_map/inv_y/ppermute | solution.py:107
  7.1 1.6 %collective-permute-start.8 = (bf16[192,2048]{1,0:T(8,128)(2,1)S(1)}, bf16[192,2048]{1,0:T(8,128)(2,1)S(1)}, u32[]{:S(2)}, u32[]{:S(2)}) collective-permute-start(bf16[192,2048]{1,0:T(8,128)(2,1)S(1)} %get-tuple-element.49), channel_id=1, source_target_pairs={{0,8},{2,10},{4,12},{6,14},{8,0},{10,2},{12,4},{14,6},{16,24},{18,... | collective-permute-start | bytes 2359304 | tf_op jit(solution)/shard_map/inv_z0/ppermute | solution.py:107
  8.8 2.6 %collective-permute-start.1 = (bf16[1024,256]{1,0:T(8,128)(2,1)S(1)}, bf16[1024,256]{1,0:T(8,128)(2,1)S(1)}, u32[]{:S(2)}, u32[]{:S(2)}) collective-permute-start(bf16[1024,256]{1,0:T(8,128)(2,1)S(1)} %get-tuple-element.42.f0), channel_id=1, source_target_pairs={{0,16},{2,18},{4,20},{6,22},{8,24},{10,26},{12,28},{14,30},{16,0},... | collective-permute-start | bytes 1572872 | tf_op jit(solution)/shard_map/first_z/ppermute | solution.py:107
  12.9 25.2 %collective-permute-done.8.refs_2_ = bf16[192,2048]{1,0:T(8,128)(2,1)S(1)} collective-permute-done((bf16[192,2048]{1,0:T(8,128)(2,1)S(1)}, bf16[192,2048]{1,0:T(8,128)(2,1)S(1)}, u32[]{:S(2)}, u32[]{:S(2)}) %collective-permute-start.8) | collective-permute-done | bytes 786464 | tf_op jit(solution)/shard_map/inv_z0/ppermute | solution.py:107
  39.4 1.9 %collective-permute-start.4 = (bf16[2064,128]{1,0:T(8,128)(2,1)S(1)}, bf16[2064,128]{1,0:T(8,128)(2,1)S(1)}, u32[]{:S(2)}, u32[]{:S(2)}) collective-permute-start(bf16[2064,128]{1,0:T(8,128)(2,1)S(1)} %get-tuple-element.59.r0), channel_id=1, source_target_pairs={{0,16},{2,18},{4,20},{6,22},{8,24},{10,26},{12,28},{14,30},{16,0},... | collective-permute-start | bytes 1585160 | tf_op jit(solution)/shard_map/rest0_z/ppermute | solution.py:107
  43.3 2.5 %collective-permute-start.7 = (bf16[64,2048]{1,0:T(8,128)(2,1)S(1)}, bf16[64,2048]{1,0:T(8,128)(2,1)S(1)}, u32[]{:S(2)}, u32[]{:S(2)}) collective-permute-start(bf16[64,2048]{1,0:T(8,128)(2,1)S(1)} %get-tuple-element.48), channel_id=1, source_target_pairs={{0,8},{2,10},{4,12},{6,14},{8,0},{10,2},{12,4},{14,6},{16,24},{18,... | collective-permute-start | bytes 786440 | tf_op jit(solution)/shard_map/inv_z1/ppermute | solution.py:107
  45.8 11.6 %collective-permute-done.7.refs_0_ = bf16[64,2048]{1,0:T(8,128)(2,1)S(1)} collective-permute-done((bf16[64,2048]{1,0:T(8,128)(2,1)S(1)}, bf16[64,2048]{1,0:T(8,128)(2,1)S(1)}, u32[]{:S(2)}, u32[]{:S(2)}) %collective-permute-start.7) | collective-permute-done | bytes 262176 | tf_op jit(solution)/shard_map/inv_z1/ppermute | solution.py:107
  59.2 6.1 %collective-permute-done.6.f1 = bf16[1024,256]{1,0:T(8,128)(2,1)S(1)} collective-permute-done((bf16[1024,256]{1,0:T(8,128)(2,1)S(1)}, bf16[1024,256]{1,0:T(8,128)(2,1)S(1)}, u32[]{:S(2)}, u32[]{:S(2)}) %collective-permute-start.6) | collective-permute-done | bytes 524320 | tf_op jit(solution)/shard_map/first_xz/ppermute | solution.py:107
  67.4 2.1 %collective-permute-start.13 = (bf16[2048,128]{1,0:T(8,128)(2,1)S(1)}, bf16[2048,128]{1,0:T(8,128)(2,1)S(1)}, u32[]{:S(2)}, u32[]{:S(2)}) collective-permute-start(bf16[2048,128]{1,0:T(8,128)(2,1)S(1)} %get-tuple-element.63.r0), channel_id=1, source_target_pairs={{0,16},{2,18},{4,20},{6,22},{8,24},{10,26},{12,28},{14,30},{16,0},... | collective-permute-start | bytes 1572872 | tf_op jit(solution)/shard_map/rest1_z/ppermute | solution.py:107
  71.5 2.2 %collective-permute-done.17 = f32[2,2048]{1,0:T(2,128)S(1)} collective-permute-done((f32[2,2048]{1,0:T(2,128)S(1)}, f32[2,2048]{1,0:T(2,128)S(1)}, u32[]{:S(2)}, u32[]{:S(2)}) %collective-permute-start.17) | collective-permute-done | bytes 16416 | tf_op jit(solution)/shard_map/squares_2/ppermute | solution.py:107
  75.1 1.9 %pack_inverse.1.sel_ref = bf16[4,256,3072]{2,1,0:T(8,128)(2,1)S(1)} custom-call(s32[2,12]{1,0:T(2,128)S(1)} %copy-done.4, bf16[704,2048]{1,0:T(8,128)(2,1)S(1)} %stack_rows.2.refs_0_, bf16[320,2048]{1,0:T(8,128)(2,1)S(1)} %stack_rows.3.refs_1_, bf16[704,2048]{1,0:T(8,128)(2,1)S(1)} %collective-permute-done.11.refs_2_, ...), custom_call_target="tpu_custom_call" | custom-call | tf_op jit(solution)/shard_map/pack_inverse/pallas_call | solution.py:249
  76.9 3.2 %products.4.refs_0_ = bf16[4,272,256]{2,1,0:T(8,128)(2,1)S(1)} custom-call(s32[2,12]{1,0:T(2,128)S(1)} %copy-done.4, bf16[4,256,3072]{2,1,0:T(8,128)(2,1)S(1)} %pack_inverse.1.sel_ref, bf16[1024,256]{1,0:T(8,128)(2,1)S(1)} %get-tuple-element.42.f0, bf16[1024,256]{1,0:T(8,128)(2,1)S(1)} %collective-permute-done.2.f1, ...), custom_call_target="tpu_custom_call" | custom-call | tf_op jit(solution)/shard_map/products/pallas_call | solution.py:348
  80.8 3.2 %products.5 = (bf16[4,272,256]{2,1,0:T(8,128)(2,1)S(1)}, bf16[4,272,256]{2,1,0:T(8,128)(2,1)S(1)}) custom-call(s32[2,12]{1,0:T(2,128)S(1)} %copy-done.4, bf16[4,256,3072]{2,1,0:T(8,128)(2,1)S(1)} %pack_inverse.1.sel_ref, bf16[1024,256]{1,0:T(8,128)(2,1)S(1)} %collective-permute-done.1.f0, bf16[1024,256]{1,0:T(8,128)(2,1)S(1)} %collective-permute-done.6.f1, ...), custom_call_target="tpu_custom_call" | custom-call | tf_op jit(solution)/shard_map/products/pallas_call | solution.py:348
  84.1 9.1 %collective-permute-done.13.refs_0_ = bf16[2048,128]{1,0:T(8,128)(2,1)S(1)} collective-permute-done((bf16[2048,128]{1,0:T(8,128)(2,1)S(1)}, bf16[2048,128]{1,0:T(8,128)(2,1)S(1)}, u32[]{:S(2)}, u32[]{:S(2)}) %collective-permute-start.13) | collective-permute-done | bytes 524320 | tf_op jit(solution)/shard_map/rest1_z/ppermute | solution.py:107
  95.6 1.9 %collective-permute-start.22 = (bf16[2,272,256]{2,1,0:T(8,128)(2,1)S(1)}, bf16[2,272,256]{2,1,0:T(8,128)(2,1)S(1)}, u32[]{:S(2)}, u32[]{:S(2)}) collective-permute-start(bf16[2,272,256]{2,1,0:T(8,128)(2,1)S(1)} %get-tuple-element.72), channel_id=1, source_target_pairs={{0,8},{2,10},{4,12},{6,14},{8,0},{10,2},{12,4},{14,6},{16,24},{18,... | collective-permute-start | bytes 835592 | tf_op jit(solution)/shard_map/cross0_2/ppermute | solution.py:107
  97.5 3.4 %products.6.refs_0_ = bf16[4,272,256]{2,1,0:T(8,128)(2,1)S(1)} custom-call(s32[2,12]{1,0:T(2,128)S(1)} %copy-done.4, bf16[4,256,3072]{2,1,0:T(8,128)(2,1)S(1)} %pack_inverse.1.sel_ref, bf16[1024,256]{1,0:T(8,128)(2,1)S(1)} %get-tuple-element.42.f0, bf16[1024,256]{1,0:T(8,128)(2,1)S(1)} %collective-permute-done.2.f1, ...), custom_call_target="tpu_custom_call" | custom-call | tf_op jit(solution)/shard_map/products/pallas_call | solution.py:348
  100.8 5.2 %collective-permute-done.15.r1 = bf16[2048,128]{1,0:T(8,128)(2,1)S(1)} collective-permute-done((bf16[2048,128]{1,0:T(8,128)(2,1)S(1)}, bf16[2048,128]{1,0:T(8,128)(2,1)S(1)}, u32[]{:S(2)}, u32[]{:S(2)}) %collective-permute-start.15) | collective-permute-done | bytes 524320 | tf_op jit(solution)/shard_map/rest1_xz/ppermute | solution.py:107
  106.0 3.2 %products.7 = (bf16[4,272,256]{2,1,0:T(8,128)(2,1)S(1)}, bf16[4,272,256]{2,1,0:T(8,128)(2,1)S(1)}) custom-call(s32[2,12]{1,0:T(2,128)S(1)} %copy-done.4, bf16[4,256,3072]{2,1,0:T(8,128)(2,1)S(1)} %pack_inverse.1.sel_ref, bf16[1024,256]{1,0:T(8,128)(2,1)S(1)} %collective-permute-done.1.f0, bf16[1024,256]{1,0:T(8,128)(2,1)S(1)} %collective-permute-done.6.f1, ...), custom_call_target="tpu_custom_call" | custom-call | tf_op jit(solution)/shard_map/products/pallas_call | solution.py:348
  109.5 1.8 %collective-permute-done.23.their_ref = bf16[4,272,256]{2,1,0:T(8,128)(2,1)S(1)} collective-permute-done((bf16[4,272,256]{2,1,0:T(8,128)(2,1)S(1)}, bf16[4,272,256]{2,1,0:T(8,128)(2,1)S(1)}, u32[]{:S(2)}, u32[]{:S(2)}) %collective-permute-start.23) | collective-permute-done | bytes 557088 | tf_op jit(solution)/shard_map/cross1_swap/ppermute | solution.py:101
  113.0 1.9 %collective-permute-start.26 = (bf16[2,272,256]{2,1,0:T(8,128)(2,1)S(1)}, bf16[2,272,256]{2,1,0:T(8,128)(2,1)S(1)}, u32[]{:S(2)}, u32[]{:S(2)}) collective-permute-start(bf16[2,272,256]{2,1,0:T(8,128)(2,1)S(1)} %get-tuple-element.81), channel_id=1, source_target_pairs={{0,8},{2,10},{4,12},{6,14},{8,0},{10,2},{12,4},{14,6},{16,24},{18,... | collective-permute-start | bytes 835592 | tf_op jit(solution)/shard_map/cross1_2/ppermute | solution.py:107
  114.9 7.0 %collective-permute-done.24.refs_1_ = bf16[2,272,256]{2,1,0:T(8,128)(2,1)S(1)} collective-permute-done((bf16[2,272,256]{2,1,0:T(8,128)(2,1)S(1)}, bf16[2,272,256]{2,1,0:T(8,128)(2,1)S(1)}, u32[]{:S(2)}, u32[]{:S(2)}) %collective-permute-start.24) | collective-permute-done | bytes 278560 | tf_op jit(solution)/shard_map/cross1_3/ppermute | solution.py:107
  121.9 4.7 %collective-permute-done.25.refs_2_ = bf16[2,272,256]{2,1,0:T(8,128)(2,1)S(1)} collective-permute-done((bf16[2,272,256]{2,1,0:T(8,128)(2,1)S(1)}, bf16[2,272,256]{2,1,0:T(8,128)(2,1)S(1)}, u32[]{:S(2)}, u32[]{:S(2)}) %collective-permute-start.25) | collective-permute-done | bytes 278560 | tf_op jit(solution)/shard_map/cross1_1/ppermute | solution.py:107
  127.5 1.6 %collective-permute-start.28 = (f32[2,2048]{1,0:T(2,128)S(1)}, f32[2,2048]{1,0:T(2,128)S(1)}, u32[]{:S(2)}, u32[]{:S(2)}) collective-permute-start(f32[2,2048]{1,0:T(2,128)S(1)} %add_sums.3), channel_id=1, source_target_pairs={{0,16},{2,18},{4,20},{6,22},{8,24},{10,26},{12,28},{14,30},{16,0},... | collective-permute-start | bytes 49160 | tf_op jit(solution)/shard_map/variance_8/ppermute | solution.py:107
  129.2 2.4 %collective-permute-start.29 = (f32[2,2048]{1,0:T(2,128)S(1)}, f32[2,2048]{1,0:T(2,128)S(1)}, u32[]{:S(2)}, u32[]{:S(2)}) collective-permute-start(f32[2,2048]{1,0:T(2,128)S(1)} %add_sums.3), channel_id=1, source_target_pairs={{0,18},{2,16},{4,22},{6,20},{8,26},{10,24},{12,30},{14,28},{16,2},... | collective-permute-start | bytes 49160 | tf_op jit(solution)/shard_map/variance_9/ppermute | solution.py:107
  (69 shorter events, 25.5 us)
Async XLA Ops:
  2.1 36.3 %collective-permute-start.3 = (bf16[2048,256]{1,0:T(8,128)(2,1)S(1)}, bf16[2048,256]{1,0:T(8,128)(2,1)S(1)}, u32[]{:S(2)}, u32[]{:S(2)}) collective-permute-start(bf16[2048,256]{1,0:T(8,128)(2,1)S(1)} %dynamic-slice_bitcast_fusion), channel_id=1, source_target_pairs={{0,1},{1,0},{2,3},{3,2},{4,5},{5,4},{6,7},{7,6},{8,9},{9,8},{10,11... | collective-permute-start | bytes 3145736 | tf_op jit(solution)/shard_map/panel_swap/ppermute | solution.py:101
  2.6 36.7 %collective-permute-start = (bf16[256,2048]{1,0:T(8,128)(2,1)}, bf16[256,2048]{1,0:T(8,128)(2,1)S(1)}, u32[]{:S(2)}, u32[]{:S(2)}) collective-permute-start(bf16[256,2048]{1,0:T(8,128)(2,1)} %refs_0_.1), channel_id=1, source_target_pairs={{0,4},{2,6},{4,0},{6,2},{8,12},{10,14},{12,8},{14,10},{16,20},{18,... | collective-permute-start | bytes 3145736 | tf_op jit(solution)/shard_map/inv_y/ppermute | solution.py:107
  7.1 30.9 %collective-permute-start.8 = (bf16[192,2048]{1,0:T(8,128)(2,1)S(1)}, bf16[192,2048]{1,0:T(8,128)(2,1)S(1)}, u32[]{:S(2)}, u32[]{:S(2)}) collective-permute-start(bf16[192,2048]{1,0:T(8,128)(2,1)S(1)} %get-tuple-element.49), channel_id=1, source_target_pairs={{0,8},{2,10},{4,12},{6,14},{8,0},{10,2},{12,4},{14,6},{16,24},{18,... | collective-permute-start | bytes 2359304 | tf_op jit(solution)/shard_map/inv_z0/ppermute | solution.py:107
  8.8 30.5 %collective-permute-start.1 = (bf16[1024,256]{1,0:T(8,128)(2,1)S(1)}, bf16[1024,256]{1,0:T(8,128)(2,1)S(1)}, u32[]{:S(2)}, u32[]{:S(2)}) collective-permute-start(bf16[1024,256]{1,0:T(8,128)(2,1)S(1)} %get-tuple-element.42.f0), channel_id=1, source_target_pairs={{0,16},{2,18},{4,20},{6,22},{8,24},{10,26},{12,28},{14,30},{16,0},... | collective-permute-start | bytes 1572872 | tf_op jit(solution)/shard_map/first_z/ppermute | solution.py:107
  11.4 28.0 %collective-permute-start.2 = (bf16[1024,256]{1,0:T(8,128)(2,1)S(1)}, bf16[1024,256]{1,0:T(8,128)(2,1)S(1)}, u32[]{:S(2)}, u32[]{:S(2)}) collective-permute-start(bf16[1024,256]{1,0:T(8,128)(2,1)S(1)} %get-tuple-element.42.f0), channel_id=1, source_target_pairs={{0,2},{2,0},{4,6},{6,4},{8,10},{10,8},{12,14},{14,12},{16,18},{18,... | collective-permute-start | bytes 1572872 | tf_op jit(solution)/shard_map/first_x/ppermute | solution.py:107
  38.1 27.2 %collective-permute-start.9 = (bf16[192,2048]{1,0:T(8,128)(2,1)S(1)}, bf16[192,2048]{1,0:T(8,128)(2,1)S(1)}, u32[]{:S(2)}, u32[]{:S(2)}) collective-permute-start(bf16[192,2048]{1,0:T(8,128)(2,1)S(1)} %collective-permute-done.8.refs_2_), channel_id=1, source_target_pairs={{0,4},{2,6},{4,0},{6,2},{8,12},{10,14},{12,8},{14,10},{16,20},{18,... | collective-permute-start | bytes 2359304 | tf_op jit(solution)/shard_map/inv_yz0/ppermute | solution.py:107
  39.4 25.9 %collective-permute-start.4 = (bf16[2064,128]{1,0:T(8,128)(2,1)S(1)}, bf16[2064,128]{1,0:T(8,128)(2,1)S(1)}, u32[]{:S(2)}, u32[]{:S(2)}) collective-permute-start(bf16[2064,128]{1,0:T(8,128)(2,1)S(1)} %get-tuple-element.59.r0), channel_id=1, source_target_pairs={{0,16},{2,18},{4,20},{6,22},{8,24},{10,26},{12,28},{14,30},{16,0},... | collective-permute-start | bytes 1585160 | tf_op jit(solution)/shard_map/rest0_z/ppermute | solution.py:107
  41.3 23.9 %collective-permute-start.5 = (bf16[2064,128]{1,0:T(8,128)(2,1)S(1)}, bf16[2064,128]{1,0:T(8,128)(2,1)S(1)}, u32[]{:S(2)}, u32[]{:S(2)}) collective-permute-start(bf16[2064,128]{1,0:T(8,128)(2,1)S(1)} %get-tuple-element.59.r0), channel_id=1, source_target_pairs={{0,2},{2,0},{4,6},{6,4},{8,10},{10,8},{12,14},{14,12},{16,18},{18,... | collective-permute-start | bytes 1585160 | tf_op jit(solution)/shard_map/rest0_x/ppermute | solution.py:107
  42.8 22.4 %collective-permute-start.6 = (bf16[1024,256]{1,0:T(8,128)(2,1)S(1)}, bf16[1024,256]{1,0:T(8,128)(2,1)S(1)}, u32[]{:S(2)}, u32[]{:S(2)}) collective-permute-start(bf16[1024,256]{1,0:T(8,128)(2,1)S(1)} %collective-permute-done.1.f0), channel_id=1, source_target_pairs={{0,2},{2,0},{4,6},{6,4},{8,10},{10,8},{12,14},{14,12},{16,18},{18,... | collective-permute-start | bytes 1572872 | tf_op jit(solution)/shard_map/first_xz/ppermute | solution.py:107
  43.3 14.1 %collective-permute-start.7 = (bf16[64,2048]{1,0:T(8,128)(2,1)S(1)}, bf16[64,2048]{1,0:T(8,128)(2,1)S(1)}, u32[]{:S(2)}, u32[]{:S(2)}) collective-permute-start(bf16[64,2048]{1,0:T(8,128)(2,1)S(1)} %get-tuple-element.48), channel_id=1, source_target_pairs={{0,8},{2,10},{4,12},{6,14},{8,0},{10,2},{12,4},{14,6},{16,24},{18,... | collective-permute-start | bytes 786440 | tf_op jit(solution)/shard_map/inv_z1/ppermute | solution.py:107
  65.2 9.8 %collective-permute-start.11 = (bf16[704,2048]{1,0:T(8,128)(2,1)S(1)}, bf16[704,2048]{1,0:T(8,128)(2,1)S(1)}, u32[]{:S(2)}, u32[]{:S(2)}) collective-permute-start(bf16[704,2048]{1,0:T(8,128)(2,1)S(1)} %stack_rows.2.refs_0_), channel_id=1, source_target_pairs={{0,1},{1,0},{2,3},{3,2},{4,5},{5,4},{6,7},{7,6},{8,9},{9,8},{10,11... | collective-permute-start | bytes 8650760 | tf_op jit(solution)/shard_map/inv_swap/ppermute | solution.py:101
  65.4 8.9 %collective-permute-start.12 = (bf16[320,2048]{1,0:T(8,128)(2,1)S(1)}, bf16[320,2048]{1,0:T(8,128)(2,1)S(1)}, u32[]{:S(2)}, u32[]{:S(2)}) collective-permute-start(bf16[320,2048]{1,0:T(8,128)(2,1)S(1)} %stack_rows.3.refs_1_), channel_id=1, source_target_pairs={{0,1},{1,0},{2,3},{3,2},{4,5},{5,4},{6,7},{7,6},{8,9},{9,8},{10,11... | collective-permute-start | bytes 3932168 | tf_op jit(solution)/shard_map/inv_swap_more/ppermute | solution.py:101
  66.0 14.9 %collective-permute-start.14 = (bf16[2064,128]{1,0:T(8,128)(2,1)S(1)}, bf16[2064,128]{1,0:T(8,128)(2,1)S(1)}, u32[]{:S(2)}, u32[]{:S(2)}) collective-permute-start(bf16[2064,128]{1,0:T(8,128)(2,1)S(1)} %collective-permute-done.4.r0), channel_id=1, source_target_pairs={{0,2},{2,0},{4,6},{6,4},{8,10},{10,8},{12,14},{14,12},{16,18},{18,... | collective-permute-start | bytes 1585160 | tf_op jit(solution)/shard_map/rest0_xz/ppermute | solution.py:107
  67.4 25.8 %collective-permute-start.13 = (bf16[2048,128]{1,0:T(8,128)(2,1)S(1)}, bf16[2048,128]{1,0:T(8,128)(2,1)S(1)}, u32[]{:S(2)}, u32[]{:S(2)}) collective-permute-start(bf16[2048,128]{1,0:T(8,128)(2,1)S(1)} %get-tuple-element.63.r0), channel_id=1, source_target_pairs={{0,16},{2,18},{4,20},{6,22},{8,24},{10,26},{12,28},{14,30},{16,0},... | collective-permute-start | bytes 1572872 | tf_op jit(solution)/shard_map/rest1_z/ppermute | solution.py:107
  73.7 23.8 %collective-permute-start.16 = (bf16[2048,128]{1,0:T(8,128)(2,1)S(1)}, bf16[2048,128]{1,0:T(8,128)(2,1)S(1)}, u32[]{:S(2)}, u32[]{:S(2)}) collective-permute-start(bf16[2048,128]{1,0:T(8,128)(2,1)S(1)} %get-tuple-element.63.r0), channel_id=1, source_target_pairs={{0,2},{2,0},{4,6},{6,4},{8,10},{10,8},{12,14},{14,12},{16,18},{18,... | collective-permute-start | bytes 1572872 | tf_op jit(solution)/shard_map/rest1_x/ppermute | solution.py:107
  74.3 19.0 %collective-permute-start.18 = (f32[2,2048]{1,0:T(2,128)S(1)}, f32[2,2048]{1,0:T(2,128)S(1)}, u32[]{:S(2)}, u32[]{:S(2)}) collective-permute-start(f32[2,2048]{1,0:T(2,128)S(1)} %add.21), channel_id=1, source_target_pairs={{0,8},{2,10},{4,12},{6,14},{8,0},{10,2},{12,4},{14,6},{16,24},{18,... | collective-permute-start | bytes 49160 | tf_op jit(solution)/shard_map/squares_4/ppermute | solution.py:107
  84.0 9.8 %collective-permute-start.19 = (bf16[4,272,256]{2,1,0:T(8,128)(2,1)S(1)}, bf16[4,272,256]{2,1,0:T(8,128)(2,1)S(1)}, u32[]{:S(2)}, u32[]{:S(2)}) collective-permute-start(bf16[4,272,256]{2,1,0:T(8,128)(2,1)S(1)} %get-tuple-element.68), channel_id=1, source_target_pairs={{0,1},{1,0},{2,3},{3,2},{4,5},{5,4},{6,7},{7,6},{8,9},{9,8},{10,11... | collective-permute-start | bytes 1671176 | tf_op jit(solution)/shard_map/cross0_swap/ppermute | solution.py:101
  93.2 12.8 %collective-permute-start.15 = (bf16[2048,128]{1,0:T(8,128)(2,1)S(1)}, bf16[2048,128]{1,0:T(8,128)(2,1)S(1)}, u32[]{:S(2)}, u32[]{:S(2)}) collective-permute-start(bf16[2048,128]{1,0:T(8,128)(2,1)S(1)} %lead.3.r0), channel_id=1, source_target_pairs={{0,2},{2,0},{4,6},{6,4},{8,10},{10,8},{12,14},{14,12},{16,18},{18,... | collective-permute-start | bytes 1572872 | tf_op jit(solution)/shard_map/rest1_xz/ppermute | solution.py:107
  93.9 15.4 %collective-permute-start.20 = (bf16[2,272,256]{2,1,0:T(8,128)(2,1)S(1)}, bf16[2,272,256]{2,1,0:T(8,128)(2,1)S(1)}, u32[]{:S(2)}, u32[]{:S(2)}) collective-permute-start(bf16[2,272,256]{2,1,0:T(8,128)(2,1)S(1)} %get-tuple-element.70), channel_id=1, source_target_pairs={{0,12},{2,14},{4,8},{6,10},{8,4},{10,6},{12,0},{14,2},{16,28},{18,... | collective-permute-start | bytes 835592 | tf_op jit(solution)/shard_map/cross0_3/ppermute | solution.py:107
  94.4 15.0 %collective-permute-start.21 = (bf16[2,272,256]{2,1,0:T(8,128)(2,1)S(1)}, bf16[2,272,256]{2,1,0:T(8,128)(2,1)S(1)}, u32[]{:S(2)}, u32[]{:S(2)}) collective-permute-start(bf16[2,272,256]{2,1,0:T(8,128)(2,1)S(1)} %get-tuple-element.71), channel_id=1, source_target_pairs={{0,4},{2,6},{4,0},{6,2},{8,12},{10,14},{12,8},{14,10},{16,20},{18,... | collective-permute-start | bytes 835592 | tf_op jit(solution)/shard_map/cross0_1/ppermute | solution.py:107
  95.6 13.8 %collective-permute-start.22 = (bf16[2,272,256]{2,1,0:T(8,128)(2,1)S(1)}, bf16[2,272,256]{2,1,0:T(8,128)(2,1)S(1)}, u32[]{:S(2)}, u32[]{:S(2)}) collective-permute-start(bf16[2,272,256]{2,1,0:T(8,128)(2,1)S(1)} %get-tuple-element.72), channel_id=1, source_target_pairs={{0,8},{2,10},{4,12},{6,14},{8,0},{10,2},{12,4},{14,6},{16,24},{18,... | collective-permute-start | bytes 835592 | tf_op jit(solution)/shard_map/cross0_2/ppermute | solution.py:107
  111.4 10.5 %collective-permute-start.24 = (bf16[2,272,256]{2,1,0:T(8,128)(2,1)S(1)}, bf16[2,272,256]{2,1,0:T(8,128)(2,1)S(1)}, u32[]{:S(2)}, u32[]{:S(2)}) collective-permute-start(bf16[2,272,256]{2,1,0:T(8,128)(2,1)S(1)} %get-tuple-element.79), channel_id=1, source_target_pairs={{0,12},{2,14},{4,8},{6,10},{8,4},{10,6},{12,0},{14,2},{16,28},{18,... | collective-permute-start | bytes 835592 | tf_op jit(solution)/shard_map/cross1_3/ppermute | solution.py:107
  112.2 14.4 %collective-permute-start.25 = (bf16[2,272,256]{2,1,0:T(8,128)(2,1)S(1)}, bf16[2,272,256]{2,1,0:T(8,128)(2,1)S(1)}, u32[]{:S(2)}, u32[]{:S(2)}) collective-permute-start(bf16[2,272,256]{2,1,0:T(8,128)(2,1)S(1)} %get-tuple-element.80), channel_id=1, source_target_pairs={{0,4},{2,6},{4,0},{6,2},{8,12},{10,14},{12,8},{14,10},{16,20},{18,... | collective-permute-start | bytes 835592 | tf_op jit(solution)/shard_map/cross1_1/ppermute | solution.py:107
  113.0 14.1 %collective-permute-start.26 = (bf16[2,272,256]{2,1,0:T(8,128)(2,1)S(1)}, bf16[2,272,256]{2,1,0:T(8,128)(2,1)S(1)}, u32[]{:S(2)}, u32[]{:S(2)}) collective-permute-start(bf16[2,272,256]{2,1,0:T(8,128)(2,1)S(1)} %get-tuple-element.81), channel_id=1, source_target_pairs={{0,8},{2,10},{4,12},{6,14},{8,0},{10,2},{12,4},{14,6},{16,24},{18,... | collective-permute-start | bytes 835592 | tf_op jit(solution)/shard_map/cross1_2/ppermute | solution.py:107
  (11 other events, 104.7 us)
